TPU v7x, 32 devices: a whole 2x2x4 slice. The times are simulated.
32 devices in a mesh: context: 8 (over z, y), fsdp: 4 (over x, core).
Axes of the slice: x: 2, y: 2, z: 4, core: 2. Of those that a mesh axis runs over, the one named last changes fastest.
Arguments:
- layer_input: bfloat16 [3, 2048, 1280], P(None, ('context', 'fsdp')), may hold values from -6 to 6
- output_cotangent: bfloat16 [3, 2048, 1280], P(None, ('context', 'fsdp')), may hold values from -6 to 6
- qkv_weight: bfloat16 [3, 1280, 1280], P(None, None, 'fsdp'), may hold values from -0.15625 to 0.15625
- out_weight: bfloat16 [1280, 1280], P('fsdp'), may hold values from -2 to 2
- in_weight: bfloat16 [1280, 1280], P(None, 'fsdp'), may hold values from -0.15625 to 0.15625
- down_weight: bfloat16 [1280, 1280], P('fsdp'), may hold values from -0.15625 to 0.15625
- qv_bias: float32 [2, 1280], P(None, 'fsdp'), may hold values from -0.6 to 0.6
- in_bias: float32 [1280], P('fsdp'), may hold values from -1.5 to 1.5
- out_bias: float32 [2, 1280], replicated, may hold values from -1.5 to 1.5
- norm_gains: float32 [2, 1280], replicated, may hold values from 0.5 to 1.5
- query_scale: float32 [80], replicated, may hold values from -1 to 1.5
- block_table: int32 [8, 2], replicated, may hold values from 0 to 15, as said below
- block_marks: int32 [3, 2048], replicated, may hold values from 0 to 15, never falling along the last dimension, each value on 1 to 256 neighbouring positions
Outputs:
- layer_output: bfloat16 [3, 2048, 1280], P(None, ('context', 'fsdp'))
- input_grad: bfloat16 [3, 2048, 1280], P(None, ('context', 'fsdp'))
- qkv_weight_grad: float32 [3, 1280, 1280], P(None, None, 'fsdp')
- out_weight_grad: float32 [1280, 1280], P('fsdp')
- in_weight_grad: float32 [1280, 1280], P(None, 'fsdp')
- down_weight_grad: float32 [1280, 1280], P('fsdp')
- qv_bias_grad: float32 [2, 1280], P(None, 'fsdp')
- in_bias_grad: float32 [1280], P('fsdp')
- out_bias_grad: float32 [2, 1280], replicated
- gains_grad: float32 [2, 1280], replicated
- scale_grad: float32 [80], replicated
Inputs may be any that keep to these rules, and one draw needn't show every extreme that they name: `block_table`: row r is a piece a and its mirror 16 - 1 - a; the first column is a permutation of 0 to 7. `block_marks`: along a row the marks never fall and start at 0; each mark covers 1 to 256 consecutive positions, one exactly 256.
All inputs are finite; a program needn't handle non-finite values.
Results may differ from a plain program's by a relative error of at most 0.015.
Values may be sent and summed in bfloat16 or wider, within the bound.
No kernel may reach another device: no remote copies, remote signals or barrier semaphores. Data moves between devices by JAX's collectives and lax.ppermute only.
A program may use at most 448 MiB of HBM per device.

v0:
```python
import math

import jax
import jax.numpy as jnp
from jax import lax
from jax.sharding import PartitionSpec as P

epsilon = 1e-06
negative = -1e30
base_rate = 1.442695041
tile_limit = 2048


def norm_rows(values, gain):
    factor = lax.rsqrt(jnp.mean(values * values, axis=-1, keepdims=True) + epsilon)
    return (factor, values * factor * gain)


def norm_back(values, factor, gain, gradient):
    weighted = gain * gradient
    inner = jnp.mean(weighted * values, axis=-1, keepdims=True)
    return factor * weighted - values * factor**3 * inner


def reorder(rows, piece_index, pieces):
    shaped = rows.reshape((pieces, -1) + rows.shape[1:])
    return shaped[piece_index].reshape((-1,) + rows.shape[1:])


def key_tile(kv_rows, marks, first_row, tile_rows, head_dim):
    block = lax.dynamic_slice_in_dim(kv_rows, first_row, tile_rows, 0)
    half_width = block.shape[1] // 2
    key_heads = block[:, :half_width].reshape(tile_rows, -1, head_dim)
    value_heads = block[:, half_width:].reshape(tile_rows, -1, head_dim)
    return (key_heads, value_heads, lax.dynamic_slice_in_dim(marks, first_row, tile_rows, 0))


def masked_scores(query_heads, key_heads, query_marks, key_marks):
    scores = jnp.einsum("qhd,khd->hqk", query_heads, key_heads, preferred_element_type=jnp.float32)
    return jnp.where(key_marks[None, None, :] <= query_marks[None, :, None], scores, negative)


def attend(query_heads, query_marks, kv_rows, marks, tile_rows):
    head_dim = query_heads.shape[2]
    seen = jnp.sum((marks <= jnp.max(query_marks)).astype(jnp.int32))
    needed = (seen + tile_rows - 1) // tile_rows
    stat_shape = (query_heads.shape[1], query_heads.shape[0])

    def gather_stats(tile_index, carry):
        running_top, running_total = carry
        key_heads, value_heads, key_marks = key_tile(
            kv_rows, marks, tile_index * tile_rows, tile_rows, head_dim
        )
        scores = masked_scores(query_heads, key_heads, query_marks, key_marks)
        new_top = jnp.maximum(running_top, jnp.max(scores, axis=-1))
        running_total = running_total * jnp.exp(running_top - new_top) + jnp.sum(
            jnp.exp(scores - new_top[..., None]), axis=-1
        )
        return (new_top, running_total)

    initial = (jnp.full(stat_shape, negative, jnp.float32), jnp.zeros(stat_shape, jnp.float32))
    running_top, running_total = lax.fori_loop(0, needed, gather_stats, initial)
    log_total = running_top + jnp.log(running_total)

    def add_values(tile_index, accumulated):
        key_heads, value_heads, key_marks = key_tile(
            kv_rows, marks, tile_index * tile_rows, tile_rows, head_dim
        )
        scores = masked_scores(query_heads, key_heads, query_marks, key_marks)
        weights = jnp.exp(scores - log_total[..., None]).astype(jnp.bfloat16)
        return accumulated + jnp.einsum(
            "hqk,khd->qhd", weights, value_heads, preferred_element_type=jnp.float32
        )

    accumulated = lax.fori_loop(0, needed, add_values, jnp.zeros(query_heads.shape, jnp.float32))
    return (accumulated, log_total, needed)


def query_inner(query_heads, query_marks, grad_heads, log_total, kv_rows, marks, needed, tile_rows):
    head_dim = query_heads.shape[2]

    def query_visit(tile_index, inner_sum):
        key_heads, value_heads, key_marks = key_tile(
            kv_rows, marks, tile_index * tile_rows, tile_rows, head_dim
        )
        scores = masked_scores(query_heads, key_heads, query_marks, key_marks)
        probability = jnp.exp(scores - log_total[..., None])
        grad_prob = jnp.einsum(
            "qhd,khd->hqk", grad_heads, value_heads, preferred_element_type=jnp.float32
        )
        return inner_sum + jnp.sum(probability * grad_prob, axis=-1)

    return lax.fori_loop(0, needed, query_visit, jnp.zeros(log_total.shape, jnp.float32))


def back_queries(
    query_heads,
    query_marks,
    grad_heads,
    log_total,
    inner_terms,
    kv_rows,
    marks,
    needed,
    tile_rows,
    key_buffer,
):
    head_dim = query_heads.shape[2]

    def back_visit(tile_index, carry):
        query_grad, buffer_rows = carry
        first_row = tile_index * tile_rows
        key_heads, value_heads, key_marks = key_tile(kv_rows, marks, first_row, tile_rows, head_dim)
        scores = masked_scores(query_heads, key_heads, query_marks, key_marks)
        probability = jnp.exp(scores - log_total[..., None])
        grad_prob = jnp.einsum(
            "qhd,khd->hqk", grad_heads, value_heads, preferred_element_type=jnp.float32
        )
        grad_score = (probability * (grad_prob - inner_terms[..., None])).astype(jnp.bfloat16)
        query_grad = query_grad + jnp.einsum(
            "hqk,khd->qhd", grad_score, key_heads, preferred_element_type=jnp.float32
        )
        grad_keys = jnp.einsum(
            "hqk,qhd->khd", grad_score, query_heads, preferred_element_type=jnp.float32
        )
        grad_values = jnp.einsum(
            "hqk,qhd->khd",
            probability.astype(jnp.bfloat16),
            grad_heads,
            preferred_element_type=jnp.float32,
        )
        update = jnp.concatenate(
            [grad_keys.reshape(tile_rows, -1), grad_values.reshape(tile_rows, -1)], axis=1
        )
        current = lax.dynamic_slice_in_dim(buffer_rows, first_row, tile_rows, 0)
        buffer_rows = lax.dynamic_update_slice_in_dim(buffer_rows, current + update, first_row, 0)
        return (query_grad, buffer_rows)

    return lax.fori_loop(
        0, needed, back_visit, (jnp.zeros(query_heads.shape, jnp.float32), key_buffer)
    )


def shards(
    layer_input,
    output_cotangent,
    qkv_weight,
    out_weight,
    in_weight,
    down_weight,
    qv_bias,
    in_bias,
    out_bias,
    norm_gains,
    query_scale,
    block_table,
    block_marks,
):
    batches, own_rows, model_width = layer_input.shape
    local_width = qkv_weight.shape[2]
    head_dim = query_scale.shape[0]
    pieces = block_table.shape[0] * 2
    seq_rows = block_marks.shape[1]
    piece_rows = seq_rows // pieces
    tile_rows = min(seq_rows, tile_limit)
    rank_index = lax.axis_index("context")
    flat_table = block_table.reshape(-1)
    inverse_order = (
        jnp.zeros((pieces,), jnp.int32).at[flat_table].set(jnp.arange(pieces, dtype=jnp.int32))
    )
    own_pieces = lax.dynamic_slice_in_dim(block_table, rank_index, 1, 0).reshape(-1)
    scale_factor = jnp.tile(
        base_rate / math.sqrt(head_dim) * jax.nn.softplus(query_scale), local_width // head_dim
    )
    contract_rows = (((0,), (0,)), ((), ()))
    contract_cols = (((1,), (1,)), ((), ()))
    qkv_total = jnp.zeros(qkv_weight.shape, jnp.float32)
    out_total = jnp.zeros(out_weight.shape, jnp.float32)
    in_total = jnp.zeros(in_weight.shape, jnp.float32)
    down_total = jnp.zeros(down_weight.shape, jnp.float32)
    qv_total = jnp.zeros(qv_bias.shape, jnp.float32)
    in_bias_total = jnp.zeros(in_bias.shape, jnp.float32)
    out_bias_total = jnp.zeros(out_bias.shape, jnp.float32)
    gains_total = jnp.zeros(norm_gains.shape, jnp.float32)
    scale_total = jnp.zeros(query_scale.shape, jnp.float32)
    outputs = []
    input_grads = []
    for batch_index in range(batches):
        marks = block_marks[batch_index]
        inputs = layer_input[batch_index].astype(jnp.float32)
        factor_one, normed_one = norm_rows(inputs, norm_gains[0])
        normed_all = lax.all_gather(normed_one.astype(jnp.bfloat16), "fsdp", axis=0, tiled=True)
        projected = jnp.einsum(
            "rd,kde->kre", normed_all, qkv_weight, preferred_element_type=jnp.float32
        )
        query = projected[0] + qv_bias[0]
        keys = projected[1].astype(jnp.bfloat16)
        values = (projected[2] + qv_bias[1]).astype(jnp.bfloat16)
        scaled = (query * scale_factor).astype(jnp.bfloat16)
        gathered = lax.all_gather(
            jnp.concatenate([keys, values], axis=1), "context", axis=0, tiled=True
        )
        kv_rows = reorder(gathered, inverse_order, pieces)
        query_marks = [
            lax.dynamic_slice_in_dim(marks, own_pieces[h] * piece_rows, piece_rows, 0)
            for h in range(2)
        ]
        query_heads = [
            scaled[h * piece_rows : (h + 1) * piece_rows].reshape(piece_rows, -1, head_dim)
            for h in range(2)
        ]
        results = [
            attend(query_heads[h], query_marks[h], kv_rows, marks, tile_rows) for h in range(2)
        ]
        attended = jnp.concatenate(
            [results[h][0].reshape(piece_rows, local_width) for h in range(2)], axis=0
        ).astype(jnp.bfloat16)
        branch = lax.psum_scatter(
            jnp.dot(attended, out_weight, preferred_element_type=jnp.float32),
            "fsdp",
            scatter_dimension=0,
            tiled=True,
        )
        hidden_one = inputs + branch + out_bias[0]
        factor_two, normed_two = norm_rows(hidden_one, norm_gains[1])
        normed_both = lax.all_gather(normed_two.astype(jnp.bfloat16), "fsdp", axis=0, tiled=True)
        hidden = jnp.dot(normed_both, in_weight, preferred_element_type=jnp.float32) + in_bias
        activated = jax.nn.silu(hidden).astype(jnp.bfloat16)
        feed_out = lax.psum_scatter(
            jnp.dot(activated, down_weight, preferred_element_type=jnp.float32).astype(
                jnp.bfloat16
            ),
            "fsdp",
            scatter_dimension=0,
            tiled=True,
        ).astype(jnp.float32)
        outputs.append((hidden_one + feed_out + out_bias[1]).astype(jnp.bfloat16))
        grad_out = output_cotangent[batch_index]
        grad_float = grad_out.astype(jnp.float32)
        grad_all = lax.all_gather(grad_out, "fsdp", axis=0, tiled=True)
        down_total = down_total + lax.dot_general(
            activated, grad_all, contract_rows, preferred_element_type=jnp.float32
        )
        grad_act = lax.dot_general(
            grad_all, down_weight, contract_cols, preferred_element_type=jnp.float32
        )
        gate_value = jax.nn.sigmoid(hidden)
        grad_hidden = (grad_act * gate_value * (1.0 + hidden * (1.0 - gate_value))).astype(
            jnp.bfloat16
        )
        in_total = in_total + lax.dot_general(
            normed_both, grad_hidden, contract_rows, preferred_element_type=jnp.float32
        )
        in_bias_total = in_bias_total + jnp.sum(grad_hidden.astype(jnp.float32), axis=0)
        grad_two = lax.psum_scatter(
            lax.dot_general(
                grad_hidden, in_weight, contract_cols, preferred_element_type=jnp.float32
            ),
            "fsdp",
            scatter_dimension=0,
            tiled=True,
        )
        grad_one = grad_float + norm_back(hidden_one, factor_two, norm_gains[1], grad_two)
        gains_second = jnp.sum(grad_two * hidden_one * factor_two, axis=0)
        bias_first = jnp.sum(grad_one, axis=0)
        bias_second = jnp.sum(grad_float, axis=0)
        grad_branch = lax.all_gather(grad_one.astype(jnp.bfloat16), "fsdp", axis=0, tiled=True)
        out_total = out_total + lax.dot_general(
            attended, grad_branch, contract_rows, preferred_element_type=jnp.float32
        )
        grad_attended = lax.dot_general(
            grad_branch, out_weight, contract_cols, preferred_element_type=jnp.float32
        ).astype(jnp.bfloat16)
        key_buffer = jnp.zeros((seq_rows, 2 * local_width), jnp.float32)
        query_parts = []
        inner_parts = []
        for half_index in range(2):
            lower = half_index * piece_rows
            grad_heads = grad_attended[lower : lower + piece_rows].reshape(piece_rows, -1, head_dim)
            inner_terms = query_inner(
                query_heads[half_index],
                query_marks[half_index],
                grad_heads,
                results[half_index][1],
                kv_rows,
                marks,
                results[half_index][2],
                tile_rows,
            )
            query_grad, key_buffer = back_queries(
                query_heads[half_index],
                query_marks[half_index],
                grad_heads,
                results[half_index][1],
                inner_terms,
                kv_rows,
                marks,
                results[half_index][2],
                tile_rows,
                key_buffer,
            )
            query_parts.append(query_grad.reshape(piece_rows, local_width))
            inner_parts.append(inner_terms)
        grad_scaled = jnp.concatenate(query_parts, axis=0)
        owned = lax.psum_scatter(
            reorder(key_buffer, flat_table, pieces), "context", scatter_dimension=0, tiled=True
        )
        grad_keys = owned[:, :local_width].astype(jnp.bfloat16)
        grad_values = owned[:, local_width:].astype(jnp.bfloat16)
        grad_query = (grad_scaled * scale_factor).astype(jnp.bfloat16)
        scale_total = scale_total + jnp.sum(
            (grad_scaled * query).reshape(grad_scaled.shape[0], -1, head_dim), axis=(0, 1)
        )
        stacked = jnp.stack([grad_query, grad_keys, grad_values], axis=1)
        qkv_total = qkv_total + jnp.einsum(
            "rd,rke->kde", normed_all, stacked, preferred_element_type=jnp.float32
        )
        qv_total = qv_total + jnp.stack(
            [
                jnp.sum(grad_query.astype(jnp.float32), axis=0),
                jnp.sum(grad_values.astype(jnp.float32), axis=0),
            ]
        )
        grad_normed = lax.psum_scatter(
            jnp.einsum(
                "rke,kde->rd", stacked, qkv_weight, preferred_element_type=jnp.float32
            ).astype(jnp.bfloat16),
            "fsdp",
            scatter_dimension=0,
            tiled=True,
        ).astype(jnp.float32)
        grad_input = grad_one + norm_back(inputs, factor_one, norm_gains[0], grad_normed)
        gains_first = jnp.sum(grad_normed * inputs * factor_one, axis=0)
        gains_total = gains_total + jnp.stack([gains_first, gains_second])
        out_bias_total = out_bias_total + jnp.stack([bias_first, bias_second])
        input_grads.append(grad_input.astype(jnp.bfloat16))
    scale_grad = scale_total * (base_rate / math.sqrt(head_dim)) * jax.nn.sigmoid(query_scale)
    qkv_total, out_total, in_total, down_total, qv_total, in_bias_total = lax.psum(
        (qkv_total, out_total, in_total, down_total, qv_total, in_bias_total), "context"
    )
    gains_total, out_bias_total, scale_grad = lax.psum(
        (gains_total, out_bias_total, scale_grad), ("context", "fsdp")
    )
    return (
        jnp.stack(outputs),
        jnp.stack(input_grads),
        qkv_total,
        out_total,
        in_total,
        down_total,
        qv_total,
        in_bias_total,
        out_bias_total,
        gains_total,
        scale_grad,
    )


def solution(mesh):
    in_specs = (
        P(None, ("context", "fsdp"), None),
        P(None, ("context", "fsdp"), None),
        P(None, None, "fsdp"),
        P("fsdp", None),
        P(None, "fsdp"),
        P("fsdp", None),
        P(None, "fsdp"),
        P("fsdp"),
        P(),
        P(),
        P(),
        P(),
        P(),
    )
    out_specs = (
        P(None, ("context", "fsdp"), None),
        P(None, ("context", "fsdp"), None),
        P(None, None, "fsdp"),
        P("fsdp", None),
        P(None, "fsdp"),
        P("fsdp", None),
        P(None, "fsdp"),
        P("fsdp"),
        P(),
        P(),
        P(),
    )
    return jax.shard_map(shards, mesh=mesh, in_specs=in_specs, out_specs=out_specs, check_vma=False)
```

profile of v0, /device:TPU:0, one launch (start us, length us, event | category | flops | bytes accessed | tf_op | source)
XLA Modules:
  0.0 1273.8 jit_solution(11988713011601497689)
XLA Ops:
  12.5 9.3 all_gather.51
  21.9 8.0 all_gather.48
  32.6 8.1 all_gather.45
  69.3 35.4 %all-gather.11.cloned.1.call-done = bf16[2048,640]{0,1:T(8,128)(2,1)} async-done(((bf16[256,640]{0,1:T(8,128)(2,1)}), bf16[2048,640]{0,1:T(8,128)(2,1)}) %all-gather.11.cloned.1.call-update) | async-done | bytes 2621456 | tf_op jit(solution)/shard_map/all_gather | solution.py:200
  104.6 4.4 copy.203
  113.2 4.4 copy.154
  140.8 21.6 %all-gather.9.cloned.1.call-done = bf16[2048,640]{0,1:T(8,128)(2,1)} async-done(((bf16[256,640]{0,1:T(8,128)(2,1)}), bf16[2048,640]{0,1:T(8,128)(2,1)}) %all-gather.9.cloned.1.call-update) | async-done | bytes 2621456 | tf_op jit(solution)/shard_map/all_gather | solution.py:200
  162.3 4.4 copy.202
  170.8 4.4 copy.145
  203.0 17.1 %all-gather.7.cloned.1.call-done = bf16[2048,640]{0,1:T(8,128)(2,1)} async-done(((bf16[256,640]{0,1:T(8,128)(2,1)}), bf16[2048,640]{0,1:T(8,128)(2,1)}) %all-gather.7.cloned.1.call-update) | async-done | bytes 2621456 | tf_op jit(solution)/shard_map/all_gather | solution.py:200
  220.1 4.4 copy.201
  224.4 4.3 gather_fusion
  228.7 4.4 copy.136
  237.4 4.6 while.314
  268.7 12.3 all-gather
  282.5 28.9 %reduce-scatter.16.cloned.1.call-done = f32[64,1280]{1,0:T(8,128)} async-done(((f32[256,1280]{1,0:T(8,128)}), f32[64,1280]{1,0:T(8,128)}) %reduce-scatter.16.cloned.1.call-update) | async-done | bytes 327696 | tf_op jit(solution)/shard_map/reduce_scatter | solution.py:218
  314.1 7.5 all_gather.47
  326.4 8.4 all-gather.1
  334.8 8.0 all_gather.50
  353.1 8.5 all-gather.2
  362.1 21.0 %reduce-scatter.34.cloned.1.call-done = f32[64,1280]{1,0:T(8,128)} async-done(((f32[256,1280]{1,0:T(8,128)}), f32[64,1280]{1,0:T(8,128)}) %reduce-scatter.34.cloned.1.call-update) | async-done | bytes 327696 | tf_op jit(solution)/shard_map/reduce_scatter | solution.py:255
  385.2 23.1 %reduce-scatter.18.cloned.1.call-done = bf16[64,1280]{1,0:T(8,128)(2,1)} async-done(((bf16[256,1280]{1,0:T(8,128)(2,1)}), bf16[64,1280]{1,0:T(8,128)(2,1)}) %reduce-scatter.18.cloned.1.call-update) | async-done | bytes 163856 | tf_op jit(solution)/shard_map/reduce_scatter | solution.py:229
  408.3 25.0 %reduce-scatter.22.cloned.1.call-done = bf16[64,1280]{1,0:T(8,128)(2,1)} async-done(((bf16[256,1280]{1,0:T(8,128)(2,1)}), bf16[64,1280]{1,0:T(8,128)(2,1)}) %reduce-scatter.22.cloned.1.call-update) | async-done | bytes 163856 | tf_op jit(solution)/shard_map/reduce_scatter | solution.py:229
  437.6 7.5 all_gather.57
  457.6 8.0 all_gather.53
  477.9 5.6 multiply_reduce_fusion.3
  494.3 4.2 fusion.21
  507.5 6.1 pad_maximum_fusion.2
  516.4 7.1 while.329
  516.4 7.0 add.1166
  523.6 6.1 pad_maximum_fusion.3
  529.8 7.3 while.331
  529.8 7.2 add.1171
  537.1 5.8 gather_fusion.4
  542.9 6.0 copy.205
  550.1 8.0 all_gather.55
  559.4 5.0 multiply_reduce_fusion.4
  576.4 4.3 fusion.25
  587.9 5.4 multiply_reduce_fusion.5
  615.5 6.3 pad_maximum_fusion.1
  627.7 7.5 while.325
  627.7 7.3 add.1156
  635.9 8.7 while.327
  635.9 6.9 add.1161
  644.6 5.8 gather_fusion.3
  650.3 6.0 copy.204
  662.0 8.2 all_gather.59
  686.0 4.2 fusion.9
  696.6 5.4 multiply_reduce_fusion.1
  712.9 4.3 fusion.13
  723.6 6.3 pad_maximum_fusion.5
  735.8 7.1 while.333
  735.8 6.9 add.1176
  742.9 7.1 while.335
  742.9 7.0 add.1181
  750.0 5.9 gather_fusion.5
  755.9 6.0 copy.206
  794.7 71.5 %reduce-scatter.42.cloned.1.call-done = f32[256,640]{0,1:T(8,128)} async-done(((f32[2048,640]{0,1:T(8,128)}), f32[256,640]{0,1:T(8,128)}) %reduce-scatter.42.cloned.1.call-update) | async-done | bytes 655376 | tf_op jit(solution)/shard_map/reduce_scatter | solution.py:305
  889.9 21.0 %all-reduce.1 = (f32[2,320]{1,0:T(2,128)}, f32[320]{0:T(512)}) all-reduce(f32[2,320]{1,0:T(2,128)S(1)} %fusion.123, f32[320]{0:T(512)S(1)} %copy-done.149), channel_id=1, replica_groups=mesh['context'=8,'fsdp'=4] {'context'}, use_global_device_ids=true, to_apply=%region_116.117 | all-reduce | flops 960 | bytes 7680 | tf_op jit(solution)/shard_map/psum | solution.py:338
  910.9 4.7 reduce-scatter.32.cloned.1.call-done
  915.6 24.9 %reduce-scatter.44.cloned.1.call-done = bf16[64,1280]{1,0:T(8,128)(2,1)} async-done(((bf16[256,1280]{1,0:T(8,128)(2,1)}), bf16[64,1280]{1,0:T(8,128)(2,1)}) %reduce-scatter.44.cloned.1.call-update) | async-done | bytes 163856 | tf_op jit(solution)/shard_map/reduce_scatter | solution.py:324
  942.1 45.5 %all-reduce = (f32[2,1280]{1,0:T(2,128)}, f32[2,1280]{1,0:T(2,128)}, f32[80]{0:T(128)}) all-reduce(f32[2,1280]{1,0:T(2,128)S(1)} %fusion.121, f32[2,1280]{1,0:T(2,128)S(1)} %fusion.122, f32[80]{0:T(128)} %divide_multiply_fusion), channel_id=1, replica_groups=mesh['context'=8,'fsdp'=4] {'context','fsdp'}, use_global_device_ids=true, to_apply=%region_127.128 | all-reduce | flops 5200 | bytes 41600 | tf_op jit(solution)/shard_map/psum | solution.py:341
  990.1 267.3 %all-reduce.5.cloned.1.call-done = (f32[3,1280,320]{1,2,0:T(8,128)}, f32[320,1280]{1,0:T(8,128)}, f32[1280,320]{0,1:T(8,128)}, f32[320,1280]{1,0:T(8,128)}) async-done(((f32[3,1280,320]{1,2,0:T(8,128)}, f32[320,1280]{1,0:T(8,128)}, f32[1280,320]{0,1:T(8,128)}, f32[320,1280]{1,0:T(8,128)}), (f32[3,1280,320]{1,2,0:T(8,128)}, f32[320,1280]{1,0:T(8,128)}, f32[1280,320]{0,1:T(8,128)}, ...) | async-done | bytes 9830416 | tf_op jit(solution)/shard_map/psum | solution.py:338
  1257.4 5.1 copy.395
  (711 shorter events, 388.2 us)
Async XLA Ops:
  7.2 22.7 %copy-start = (bf16[3,1280,320]{1,2,0:T(8,128)(2,1)S(1)}, bf16[3,1280,320]{1,2,0:T(8,128)(2,1)}, u32[]{:S(2)}) copy-start(bf16[3,1280,320]{1,2,0:T(8,128)(2,1)} %param.63) | copy-start | bytes 7372804
  7.2 97.5 %all-gather.11.cloned.1.call-start = ((), (), s32[]{:S(2)}) async-start(), calls=%async_computation.21 | async-start | bytes 2949120 | tf_op jit(solution)/shard_map/all_gather | solution.py:200
  9.3 12.6 copy-start.154
  10.7 11.2 copy-start.132
  11.3 10.6 copy-start.150
  11.3 10.6 copy-start.151
  21.9 10.7 copy-start.69
  30.7 12.9 %copy-start.90 = (f32[3,256,320]{1,2,0:T(8,128)}, f32[3,256,320]{1,2,0:T(8,128)S(1)}, u32[]{:S(2)}) copy-start(f32[3,256,320]{1,2,0:T(8,128)S(1)} %convolution_bitcast_fusion.3) | copy-start | bytes 2949124
  32.6 10.8 copy-start.157
  32.6 10.9 copy-start.156
  43.6 7.8 copy-start.155
  43.6 9.7 copy-start.144
  46.0 19.2 %copy-start.125 = (bf16[256,320]{0,1:T(8,128)(2,1)S(1)}, bf16[256,320]{0,1:T(8,128)(2,1)}, u32[]{:S(2)}) copy-start(bf16[256,320]{0,1:T(8,128)(2,1)} %get-tuple-element.3016) | copy-start | bytes 491524
  46.0 19.3 %copy-start.124 = (bf16[256,320]{0,1:T(8,128)(2,1)S(1)}, bf16[256,320]{0,1:T(8,128)(2,1)}, u32[]{:S(2)}) copy-start(bf16[256,320]{0,1:T(8,128)(2,1)} %get-tuple-element.3083) | copy-start | bytes 491524
  46.0 19.3 %copy-start.123 = (bf16[256,320]{0,1:T(8,128)(2,1)S(1)}, bf16[256,320]{0,1:T(8,128)(2,1)}, u32[]{:S(2)}) copy-start(bf16[256,320]{0,1:T(8,128)(2,1)} %get-tuple-element.3081) | copy-start | bytes 491524
  46.8 115.5 %all-gather.9.cloned.1.call-start = ((), (), s32[]{:S(2)}) async-start(), calls=%async_computation.18 | async-start | bytes 2949120 | tf_op jit(solution)/shard_map/all_gather | solution.py:200
  49.5 170.5 %all-gather.7.cloned.1.call-start = ((), (), s32[]{:S(2)}) async-start(), calls=%async_computation.15 | async-start | bytes 2949120 | tf_op jit(solution)/shard_map/all_gather | solution.py:200
  51.4 229.6 %reduce-scatter.24.cloned.1.call-start = ((), (), s32[]{:S(2)}) async-start(), calls=%async_computation.22 | async-start | bytes 1638400 | tf_op jit(solution)/shard_map/reduce_scatter | solution.py:218
  64.5 44.5 %copy-start.158 = (s32[16]{0:T(128)}, s32[16]{0:T(128)S(1)}, u32[]{:S(2)}) copy-start(s32[16]{0:T(128)S(1)} %fusion.125) | copy-start | bytes 196
  130.7 70.6 %copy-start.103 = (bf16[128,4,80]{0,2,1:T(8,128)(2,1)}, bf16[128,4,80]{0,2,1:T(8,128)(2,1)S(1)}, u32[]{:S(2)}) copy-start(bf16[128,4,80]{0,2,1:T(8,128)(2,1)S(1)} %copy.158) | copy-start | bytes 245764
  140.8 60.5 %copy-start.105 = (bf16[128,4,80]{0,2,1:T(8,128)(2,1)}, bf16[128,4,80]{0,2,1:T(8,128)(2,1)S(1)}, u32[]{:S(2)}) copy-start(bf16[128,4,80]{0,2,1:T(8,128)(2,1)S(1)} %copy.161) | copy-start | bytes 245764
  202.9 79.6 %reduce-scatter.20.cloned.1.call-start = ((), (), s32[]{:S(2)}) async-start(), calls=%async_computation.19 | async-start | bytes 1638400 | tf_op jit(solution)/shard_map/reduce_scatter | solution.py:218
  254.0 57.3 %reduce-scatter.16.cloned.1.call-start = ((), (), s32[]{:S(2)}) async-start(), calls=%async_computation.16 | async-start | bytes 1638400 | tf_op jit(solution)/shard_map/reduce_scatter | solution.py:218
  266.7 47.2 %copy-start.130 = (f32[1280]{0:T(1024)S(1)}, f32[1280]{0:T(1024)}, u32[]{:S(2)}) copy-start(f32[1280]{0:T(1024)} %get-tuple-element.2687) | copy-start | bytes 15364
  266.7 95.4 %reduce-scatter.28.cloned.1.call-start = ((), (), s32[]{:S(2)}) async-start(), calls=%async_computation.24 | async-start | bytes 1638400 | tf_op jit(solution)/shard_map/reduce_scatter | solution.py:255
  266.8 166.5 %copy-start.134 = (f32[1280]{0:T(1024)}, f32[1280]{0:T(1024)S(1)}, u32[]{:S(2)}) copy-start(f32[1280]{0:T(1024)S(1)} %get-tuple-element.2685) | copy-start | bytes 15364
  268.7 53.7 %copy-start.19 = (bf16[1280,320]{0,1:T(8,128)(2,1)S(1)}, bf16[1280,320]{0,1:T(8,128)(2,1)}, u32[]{:S(2)}) copy-start(bf16[1280,320]{0,1:T(8,128)(2,1)} %param.65) | copy-start | bytes 2457604
  268.7 53.7 %copy-start.147 = (f32[320]{0:T(512)S(1)}, f32[320]{0:T(512)}, u32[]{:S(2)}) copy-start(f32[320]{0:T(512)} %param.68) | copy-start | bytes 3844
  311.4 11.5 copy-start.75
  311.4 11.5 copy-start.160
  313.9 10.1 copy-start.52
  313.9 10.1 copy-start.53
  326.4 56.8 %reduce-scatter.34.cloned.1.call-start = ((), (), s32[]{:S(2)}) async-start(), calls=%async_computation.27 | async-start | bytes 1638400 | tf_op jit(solution)/shard_map/reduce_scatter | solution.py:255
  326.4 17.6 %copy-start.161 = (bf16[320,1280]{1,0:T(8,128)(2,1)S(1)}, bf16[320,1280]{1,0:T(8,128)(2,1)}, u32[]{:S(2)}) copy-start(bf16[320,1280]{1,0:T(8,128)(2,1)} %param.66) | copy-start | bytes 2457604
  334.8 10.4 copy-start.79
  347.5 60.8 %reduce-scatter.18.cloned.1.call-start = ((), (), s32[]{:S(2)}) async-start(), calls=%async_computation.17 | async-start | bytes 819200 | tf_op jit(solution)/shard_map/reduce_scatter | solution.py:229
  350.2 83.1 %reduce-scatter.22.cloned.1.call-start = ((), (), s32[]{:S(2)}) async-start(), calls=%async_computation.20 | async-start | bytes 819200 | tf_op jit(solution)/shard_map/reduce_scatter | solution.py:229
  353.0 303.4 %reduce-scatter.40.cloned.1.call-start = ((), (), s32[]{:S(2)}) async-start(), calls=%async_computation.30 | async-start | bytes 1638400 | tf_op jit(solution)/shard_map/reduce_scatter | solution.py:255
  353.1 291.5 %copy-start.152 = (s32[1024]{0:T(1024)}, s32[1024]{0:T(1024)S(1)}, u32[]{:S(2)}) copy-start(s32[1024]{0:T(1024)S(1)} %pad_clamp_fusion) | copy-start | bytes 12292
  362.1 75.5 %copy-start.153 = (f32[64]{0:T(128)}, f32[64]{0:T(128)S(1)}, u32[]{:S(2)}) copy-start(f32[64]{0:T(128)S(1)} %get-tuple-element.3100) | copy-start | bytes 772
  433.3 11.8 copy-start.21
  433.3 12.6 copy-start.8
  433.3 12.6 copy-start.15
  456.6 10.2 copy-start.77
  456.6 10.2 copy-start.162
  470.2 189.1 %reduce-scatter.26.cloned.1.call-start = ((), (), s32[]{:S(2)}) async-start(), calls=%async_computation.23 | async-start | bytes 819200 | tf_op jit(solution)/shard_map/reduce_scatter | solution.py:229
  523.5 250.8 %reduce-scatter.36.cloned.1.call-start = ((), (), s32[]{:S(2)}) async-start(), calls=%async_computation.28 | async-start | bytes 5898240 | tf_op jit(solution)/shard_map/reduce_scatter | solution.py:305
  548.9 10.0 copy-start.22
  548.9 235.5 %reduce-scatter.30.cloned.1.call-start = ((), (), s32[]{:S(2)}) async-start(), calls=%async_computation.25 | async-start | bytes 5898240 | tf_op jit(solution)/shard_map/reduce_scatter | solution.py:305
  549.0 10.4 copy-start.18
  627.7 7.3 copy-start.39
  656.3 209.8 %reduce-scatter.42.cloned.1.call-start = ((), (), s32[]{:S(2)}) async-start(), calls=%async_computation.31 | async-start | bytes 5898240 | tf_op jit(solution)/shard_map/reduce_scatter | solution.py:305
  659.3 11.7 copy-start.3
  662.0 9.0 copy-start.68
  761.9 149.0 %reduce-scatter.38.cloned.1.call-start = ((), (), s32[]{:S(2)}) async-start(), calls=%async_computation.29 | async-start | bytes 819200 | tf_op jit(solution)/shard_map/reduce_scatter | solution.py:324
  768.6 7.0 copy-start.81
  771.6 7.5 copy-start.83
  779.1 136.5 %reduce-scatter.32.cloned.1.call-start = ((), (), s32[]{:S(2)}) async-start(), calls=%async_computation.26 | async-start | bytes 819200 | tf_op jit(solution)/shard_map/reduce_scatter | solution.py:324
  789.2 151.3 %reduce-scatter.44.cloned.1.call-start = ((), (), s32[]{:S(2)}) async-start(), calls=%async_computation.32 | async-start | bytes 819200 | tf_op jit(solution)/shard_map/reduce_scatter | solution.py:324
  870.7 386.7 %all-reduce.5.cloned.1.call-start = ((), (), s32[]{:S(2)}) async-start(), calls=%async_computation.33 | async-start | bytes 19660800 | tf_op jit(solution)/shard_map/psum | solution.py:338
  878.1 62.4 %copy-start.37 = (bf16[3,64,1280]{2,1,0:T(8,128)(2,1)S(1)}, bf16[3,64,1280]{2,1,0:T(8,128)(2,1)}, u32[]{:S(2)}) copy-start(bf16[3,64,1280]{2,1,0:T(8,128)(2,1)} %param.61) | copy-start | bytes 1474564
  878.1 62.4 %copy-start.133 = (f32[1280]{0:T(1024)S(1)}, f32[1280]{0:T(1024)}, u32[]{:S(2)}) copy-start(f32[1280]{0:T(1024)} %copy-done.132) | copy-start | bytes 15364
  879.7 107.9 %copy-start.67 = (f32[64,1280]{1,0:T(8,128)S(1)}, f32[64,1280]{1,0:T(8,128)}, u32[]{:S(2)}) copy-start(f32[64,1280]{1,0:T(8,128)} %copy-done.66) | copy-start | bytes 983044
  881.6 8.3 copy-start.149
  (118 other events, 313.3 us)
Sparse Core Ops, SparseCore 0:
  46.9 57.6 all-gather.10
  107.3 55.0 all-gather.8
  165.0 55.0 all-gather.6
  222.4 24.6 reduce-scatter.23
  254.1 28.3 reduce-scatter.19
  285.5 25.8 reduce-scatter.15
  326.5 26.9 reduce-scatter.27
  356.6 26.5 reduce-scatter.33
  385.8 22.4 reduce-scatter.17
  410.8 22.4 reduce-scatter.21
  470.3 26.9 reduce-scatter.39
  523.6 22.9 reduce-scatter.25
  550.3 102.9 reduce-scatter.35
  656.7 103.1 reduce-scatter.29
  763.4 102.7 reduce-scatter.41
  868.5 22.2 reduce-scatter.37
  893.1 22.4 reduce-scatter.31
  918.0 22.4 reduce-scatter.43
  945.5 311.8 all-reduce.4
where the time goes:
time: 1290 us; the launch traced here: 1270 us
  waiting for transfers between devices  542 us (42%)
  local copies, waits for them, and re-layouts  209 us (16%)
  blocking collectives  168 us (13%)
  other arithmetic  166 us (13%)
  matrix products  164 us (13%)
  between operations  21.9 us (2%)
    psum x1, waiting for transfers between devices, shards(): lax.psum((qkv_total, out_total, in_total, down_total, qv_total, in_bias_t...  267 us
    all_gather x3, waiting for transfers between devices, shards(): lax.all_gather(jnp.concatenate([keys, values], axis=1), 'context', axis=0...  74 us
    reduce_scatter x3, waiting for transfers between devices, shards(): lax.psum_scatter(reorder(key_buffer, flat_table, pieces), 'context', scat...  71.5 us
    reduce_scatter x3, waiting for transfers between devices, shards(): lax.psum_scatter(jnp.dot(activated, down_weight, preferred_element_type=j...  48.2 us
    psum x1, blocking collectives, shards(): lax.psum((gains_total, out_bias_total, scale_grad), ('context', 'fsdp'))  45.5 us
    unnamed x327, local copies, waits for them, and re-layouts  42.8 us
    add x6, other arithmetic, back_visit(): current + update  42.3 us
    concatenate x6, other arithmetic, back_visit(): jnp.concatenate([grad_keys.reshape(tile_rows, -1), grad_values.reshape(ti...  31.3 us
  transfers between devices with their start and end apart: 19, of which 12 were waited for; matrix products, arithmetic and copies ran while one was open for 36% of the time, Pallas kernels for 0%

commit v1 on v0

v1 whole, which is shorter than its diff:
```python
import functools
import math

import jax
import jax.numpy as jnp
from jax import lax
from jax.experimental import pallas as pl
from jax.experimental.pallas import tpu as pltpu
from jax.sharding import PartitionSpec as P

epsilon = 1e-06
negative = -1e30
base_rate = 1.442695041
key_tile = 2048
vmem_bytes = 60 * 1024 * 1024
loop_tile = 1024
bf16 = jnp.bfloat16
f32 = jnp.float32

rows_cols = (((1,), (0,)), ((), ()))
cols_cols = (((1,), (1,)), ((), ()))
rows_rows = (((0,), (0,)), ((), ()))


def mm(left, right, dims=rows_cols):
    return lax.dot_general(left, right, dims, preferred_element_type=f32)


def call(kernel, out_shape, operands, scalars, scratch=(), flops=0, trans=0, tokens=()):
    moved = sum(o.size * o.dtype.itemsize for o in operands)
    moved += sum(o.size * o.dtype.itemsize for o in out_shape)
    specs = [pl.BlockSpec(memory_space=pltpu.SMEM)]
    specs += [pl.BlockSpec(memory_space=pltpu.VMEM)] * len(operands)
    specs += [pl.BlockSpec(memory_space=pl.ANY)] * len(tokens)
    used = 1 + len(operands)
    return pl.pallas_call(
        lambda *refs: kernel(*refs[:used], *refs[used + len(tokens) :]),
        out_shape=tuple(out_shape),
        in_specs=specs,
        out_specs=tuple(pl.BlockSpec(memory_space=pltpu.VMEM) for _ in out_shape),
        scratch_shapes=list(scratch),
        compiler_params=pltpu.CompilerParams(vmem_limit_bytes=vmem_bytes),
        cost_estimate=pl.CostEstimate(flops=flops, bytes_accessed=moved, transcendentals=trans),
    )(scalars, *operands, *tokens)


def loop(count, body):
    if count <= 16:
        for i in range(count):
            body(i)
    else:
        lax.fori_loop(0, count, lambda i, c: (body(i), c)[1], 0)


def shape(dims, kind):
    return jax.ShapeDtypeStruct(tuple(dims), kind)


def exchange(values, axis, size, bit):
    return lax.ppermute(values, axis, [(i, i ^ (1 << bit)) for i in range(size)])


def bits_of(size):
    return size.bit_length() - 1


def after(values, *tokens):
    leaves, tree = jax.tree.flatten(values)
    marks = jax.tree.leaves(tokens)
    anywhere = pl.BlockSpec(memory_space=pl.ANY)
    kept = pl.pallas_call(
        lambda *refs: None,
        out_shape=tuple(shape(v.shape, v.dtype) for v in leaves),
        in_specs=[anywhere] * (len(leaves) + len(marks)),
        out_specs=tuple(anywhere for _ in leaves),
        input_output_aliases={i: i for i in range(len(leaves))},
        cost_estimate=pl.CostEstimate(flops=0, bytes_accessed=0, transcendentals=0),
    )(*leaves, *marks)
    return jax.tree.unflatten(tree, kept)


def scatter_rows(parts, axis, size, tokens=()):
    held = dict(enumerate(parts))
    for bit in range(bits_of(size)):
        step = 1 << bit
        got = {k: exchange(held[k | step], axis, size, bit) for k in reversed(held) if not k & step}
        if bit < len(tokens):
            got = after(got, tokens[bit])
        held = {k: held[k].astype(f32) + got[k].astype(f32) for k in held if not k & step}
        held = {k: v.astype(bf16) if k else v for k, v in held.items()}
    return held[0]


def gather_rows(own, axis, size):
    held = {0: own}
    for bit in reversed(range(bits_of(size))):
        held.update({k | (1 << bit): exchange(v, axis, size, bit) for k, v in list(held.items())})
    return [held[k] for k in range(size)]


def swap_parts(parts, axis, size):
    return [parts[0]] + [lax.ppermute(parts[k], axis, [(i, i ^ k) for i in range(size)]) for k in range(1, size)]


def swap_all(parts, axis):
    return lax.all_to_all(parts, axis, 0, 0, tiled=True)


def summing(streams, axis, size):
    bits = bits_of(size)
    orders = []
    for index in range(len(streams)):
        order = list(range(bits))
        if index % 2 == 1 and bits > 1:
            order[0], order[1] = order[1], order[0]
        orders.append(order)
    held, sizes = list(streams), []
    for step in range(bits):
        sizes.append([h.shape[0] for h in held])
        keep, send = [], []
        for h, order in zip(held, orders):
            half = h.shape[0] // 2
            if h.shape[0] % 2:
                keep.append(h)
                send.append(h)
                continue
            mine = (lax.axis_index(axis) >> order[step]) & 1
            keep.append(lax.dynamic_slice_in_dim(h, mine * half, half, 0))
            send.append(lax.dynamic_slice_in_dim(h, (1 - mine) * half, half, 0))
        got = yield [exchange(v, axis, size, o[step]) for v, o in zip(send, orders)]
        held = [(k.astype(f32) + g.astype(f32)).astype(bf16) for k, g in zip(keep, got)]
    for step in reversed(range(bits)):
        wide = [h.shape[0] < r for h, r in zip(held, sizes[step])]
        got = yield [exchange(h, axis, size, o[step]) if w else h for h, o, w in zip(held, orders, wide)]
        for i, order in enumerate(orders):
            if wide[i]:
                low = ((lax.axis_index(axis) >> order[step]) & 1) == 0
                pair = (jnp.where(low, held[i], got[i]), jnp.where(low, got[i], held[i]))
                held[i] = jnp.concatenate(pair)
    return held


class Flow:
    def __init__(self, steps):
        self.steps, self.result = steps, None
        self.got = next(steps)

    def go(self, *tokens):
        if self.result is None:
            try:
                self.got = self.steps.send(after(self.got, *tokens) if tokens else self.got)
            except StopIteration as end:
                self.result = end.value
        return self.result

    def finish(self):
        while self.result is None:
            self.go()
        return self.result


def chunk(k, rows):
    return pl.ds(pl.multiple_of((k ^ lax.axis_index("fsdp")) * rows, rows), rows)


def first_parity(table):
    return lax.rem(table[0, lax.axis_index("context")], 2)


def invert(table, inverse_ref):
    def note(i):
        half = i % 2 if isinstance(i, int) else lax.rem(i, 2)
        inverse_ref[table[half, i // 2]] = i

    loop(2 * table.shape[1], note)


def store_parts(plan, parity, t, out_ref, b, kind):
    size, heads, group, members, dim, piece, batches = plan
    for h in range(heads):
        block = t[h * dim : (h + 1) * dim]
        cut = [block[:, s * piece : (s + 1) * piece] for s in range(2)]
        if b < batches - 1:
            for u in range(members):
                for s in range(2):
                    out_ref[h * group + b * members + u, 2 * kind + s] = cut[s]
        else:
            base = out_ref.shape[1] // 2 + 1
            for e in range(group):
                if kind == 0:
                    out_ref[h * group + e, base] = jnp.where(parity == e % 2, cut[0], cut[1])
                else:
                    for s in range(2):
                        out_ref[h * group + e, base + 2 * kind - 1 + s] = cut[s]


def project_kernel(plan, spread, sc, *refs):
    x_refs, (w_ref, gain_ref, bias_ref, factor_ref, n1_ref, send_ref) = refs[:spread], refs[spread:]
    batches = plan[6]
    rows = x_refs[0].shape[1]
    parity = first_parity(sc)
    for b in range(batches):
        for k in range(spread):
            x = x_refs[k][b].astype(f32)
            r = lax.rsqrt(jnp.mean(x * x, axis=-1, keepdims=True) + epsilon)
            n1_ref[b, chunk(k, rows), :] = (x * r * gain_ref[...]).astype(bf16)
    n1 = n1_ref[...].reshape(-1, n1_ref.shape[2])
    for i in range(3):
        y = mm(n1, w_ref[i], cols_cols)
        if i == 0:
            y = (y + bias_ref[0:1]) * factor_ref[...]
        elif i == 2:
            y = y + bias_ref[1:2]
        for b in range(batches):
            part = y[b * spread * rows : (b + 1) * spread * rows]
            store_parts(plan, parity, part.T.astype(bf16), send_ref, b, i)


def place(inverse_ref, index):
    slot = inverse_ref[index]
    return slot // 2, lax.rem(slot, 2)


def turned(block):
    filled = jnp.concatenate([block, jnp.zeros((128 - block.shape[0], block.shape[1]), block.dtype)], 0)
    return filled.T


def key_parts(block_index, stride, piece, seq):
    free = 2 * block_index * stride * piece
    last = min(((2 * block_index + 2) * stride + 2) * piece, seq)
    return free, last


def attend_kernel(plans, sc, got_ref, *refs):
    units = len(plans)
    ends, o_ref, outs, scratch = refs[:units], refs[units], refs[units + 1 : -4], refs[-4:]
    invert(sc, scratch[0])
    for i, plan in enumerate(plans):
        attend_unit(plan, got_ref, ends[i], o_ref, outs[2 * i], outs[2 * i + 1], *scratch)


def attend_unit(plan, got_ref, end_ref, o_ref, wide_ref, lse_ref, inverse_ref, k_ref, vt_ref, qt_ref):
    pieces, piece, dim, stride, q_parts, base, o_base = plan
    offset = lax.rem(lax.axis_index("context"), stride)
    seq = pieces * piece
    asked = pieces // stride

    def fill(p):
        at, which = place(inverse_ref, p)
        span = pl.ds(p * piece if isinstance(p, int) else pl.multiple_of(p * piece, piece), piece)
        k_ref[span, :] = turned(got_ref[at, base + q_parts + which])
        vt_ref[:, span] = got_ref[at, base + q_parts + 2 + which]

    loop(pieces, fill)
    for j in range(asked):
        at, which = place(inverse_ref, j * stride + offset)
        qt_ref[0:dim, j * piece : (j + 1) * piece] = got_ref[at, base + (which if q_parts == 2 else 0)]
    qt_ref[dim:, :] = jnp.zeros_like(qt_ref[dim:, :])
    if asked != o_ref.shape[0] * q_parts:
        for part in range(q_parts):
            o_ref[:, o_base + part] = jnp.zeros_like(o_ref[:, o_base + part])
    wide = 2 * piece
    for i in range(asked // 2):
        span = slice(i * wide, (i + 1) * wide)
        qt = qt_ref[:, span]
        end = end_ref[:, span]
        free, last = key_parts(i, stride, piece, seq)
        if last <= key_tile:
            masked = mm(k_ref[free:last, :], qt)
            at = lax.broadcasted_iota(jnp.int32, masked.shape, 0) + free
            masked = jnp.where(at < end, masked, negative)
            top = jnp.max(masked, axis=0, keepdims=True)
            if free:
                plain = mm(k_ref[0:free, :], qt)
                top = jnp.maximum(top, jnp.max(plain, axis=0, keepdims=True))
            weight = jnp.exp(masked - top)
            total = jnp.sum(weight, axis=0, keepdims=True)
            out = mm(vt_ref[:, free:last], weight.astype(bf16))
            if free:
                weight = jnp.exp(plain - top)
                total = total + jnp.sum(weight, axis=0, keepdims=True)
                out = out + mm(vt_ref[:, 0:free], weight.astype(bf16))
        else:

            def tile(t, carry):
                top, total, out = carry
                first = pl.multiple_of(t * loop_tile, loop_tile)
                scores = mm(k_ref[pl.ds(first, loop_tile), :], qt)
                at = lax.broadcasted_iota(jnp.int32, scores.shape, 0) + first
                scores = jnp.where(at < end, scores, negative)
                new = jnp.maximum(top, jnp.max(scores, axis=0, keepdims=True))
                weight = jnp.exp(scores - new)
                change = jnp.exp(top - new)
                total = total * change + jnp.sum(weight, axis=0, keepdims=True)
                out = out * change + mm(vt_ref[:, pl.ds(first, loop_tile)], weight.astype(bf16))
                return new, total, out

            start = (jnp.full((1, wide), negative, f32), jnp.zeros((1, wide), f32), jnp.zeros((dim, wide), f32))
            tiles = min(-(-last // loop_tile), seq // loop_tile)
            top, total, out = lax.fori_loop(0, tiles, tile, start)
        out = out / total
        wide_ref[:, span] = out
        lse_ref[:, span] = top + jnp.log(total)
        for s in range(2):
            at, which = place(inverse_ref, (2 * i + s) * stride + offset)
            o_ref[at, o_base + (which if q_parts == 2 else 0)] = out[:, s * piece : (s + 1) * piece].astype(bf16)


def attend_back_kernel(plans, sc, got_ref, do_ref, factor_ref, *refs):
    units = len(plans)
    saved, d_ref, scale_ref, scratch = refs[: 3 * units], refs[3 * units], refs[3 * units + 1], refs[3 * units + 2 :]
    scale = 0.0
    invert(sc, scratch[0])
    for i, plan in enumerate(plans):
        own = saved[3 * i : 3 * i + 3]
        scale = scale + attend_back_unit(plan, got_ref, do_ref, factor_ref, *own, d_ref, *scratch)
    scale_ref[...] = scale


def attend_back_unit(
    plan, got_ref, do_ref, factor_ref, end_ref, wide_ref, lse_ref, d_ref,
    inverse_ref, k_ref, kt_ref, v_ref, qt_ref, q_ref, dot_ref, dor_ref, dk_ref, dv_ref,
):
    pieces, piece, dim, stride, q_parts, base, o_base = plan
    offset = lax.rem(lax.axis_index("context"), stride)
    seq = pieces * piece
    asked = pieces // stride

    def fill(p):
        at, which = place(inverse_ref, p)
        span = pl.ds(p * piece if isinstance(p, int) else pl.multiple_of(p * piece, piece), piece)
        kt = got_ref[at, base + q_parts + which]
        if seq <= key_tile:
            kt_ref[:, span] = kt
        k_ref[span, :] = turned(kt)
        v_ref[span, :] = turned(got_ref[at, base + q_parts + 2 + which])

    loop(pieces, fill)
    for j in range(asked):
        at, which = place(inverse_ref, j * stride + offset)
        span = slice(j * piece, (j + 1) * piece)
        qt = got_ref[at, base + (which if q_parts == 2 else 0)]
        qt_ref[0:dim, span] = qt
        q_ref[span, :] = turned(qt)
        do = do_ref[at, o_base + (which if q_parts == 2 else 0)]
        dot_ref[0:dim, span] = do
        dor_ref[span, :] = turned(do)
    qt_ref[dim:, :] = jnp.zeros_like(qt_ref[dim:, :])
    dot_ref[dim:, :] = jnp.zeros_like(dot_ref[dim:, :])
    dk_ref[...] = jnp.zeros_like(dk_ref)
    dv_ref[...] = jnp.zeros_like(dv_ref)
    if asked != d_ref.shape[0] * q_parts:
        for part in range(q_parts):
            d_ref[:, base + part] = jnp.zeros_like(d_ref[:, base + part])
    wide = 2 * piece
    scale = jnp.zeros((dim, 1), f32)
    for i in range(asked // 2):
        span = slice(i * wide, (i + 1) * wide)
        qt, q, do, dor = qt_ref[:, span], q_ref[span, :], dot_ref[:, span], dor_ref[span, :]
        end, lse = end_ref[:, span], lse_ref[:, span]
        delta = jnp.sum(do[0:dim].astype(f32) * wide_ref[:, span], axis=0, keepdims=True)
        free, last = key_parts(i, stride, piece, seq)

        def visit(keys, masked_from):
            scores = mm(k_ref[keys, :], qt)
            if masked_from is not None:
                at = lax.broadcasted_iota(jnp.int32, scores.shape, 0) + masked_from
                scores = jnp.where(at < end, scores, negative)
            prob = jnp.exp(scores - lse)
            ds = (prob * (mm(v_ref[keys, :], do) - delta)).astype(bf16)
            dv_ref[keys, :] += mm(prob.astype(bf16), dor)
            dk_ref[keys, :] += mm(ds, q)
            return mm(kt_ref[:, keys] if seq <= key_tile else k_ref[keys, :].T[0:dim], ds)

        if last <= key_tile:
            dq = visit(pl.ds(free, last - free), free)
            if free:
                dq = dq + visit(pl.ds(0, free), None)
        else:

            def tile(t, dq):
                first = pl.multiple_of(t * loop_tile, loop_tile)
                return dq + visit(pl.ds(first, loop_tile), first)

            tiles = min(-(-last // loop_tile), seq // loop_tile)
            dq = lax.fori_loop(0, tiles, tile, jnp.zeros((dim, wide), f32))
        scale = scale + jnp.sum(dq * qt[0:dim].astype(f32), axis=1, keepdims=True)
        dq = (dq * factor_ref[...]).astype(bf16)
        for s in range(2):
            at, which = place(inverse_ref, (2 * i + s) * stride + offset)
            d_ref[at, base + (which if q_parts == 2 else 0)] = dq[:, s * piece : (s + 1) * piece]

    def give(p):
        at, which = place(inverse_ref, p)
        span = pl.ds(p * piece if isinstance(p, int) else pl.multiple_of(p * piece, piece), piece)
        d_ref[at, base + q_parts + which] = dk_ref[span, :].T[0:dim].astype(bf16)
        d_ref[at, base + q_parts + 2 + which] = dv_ref[span, :].T[0:dim].astype(bf16)

    loop(pieces, give)
    return scale


def total_of(blocks):
    if len(blocks) == 1:
        return blocks[0]
    return sum(b.astype(f32) for b in blocks[1:]) + blocks[0].astype(f32)


def collect(plan, even, got_ref, b, which, kind):
    size, heads, group, members, dim, piece, batches = plan
    base = got_ref.shape[1] // 2 + 1
    parts = []
    for h in range(heads):
        if b < batches - 1:
            blocks = [got_ref[h * group + b * members + u, 2 * kind + which] for u in range(members)]
        elif kind == 0:
            parity = even if which == 0 else 1 - even
            blocks = [got_ref[h * group + 2 * u + parity, base] for u in range(group // 2)]
        else:
            blocks = [got_ref[h * group + e, base + 2 * kind - 1 + which] for e in range(group)]
        parts.append(total_of(blocks).astype(bf16))
    return jnp.concatenate(parts, axis=0).T


def give_rows(value, held_ref, out_refs):
    batches, rows, _ = out_refs[0].shape
    held_ref[...] = value.astype(bf16).reshape(held_ref.shape)
    for k, out_ref in enumerate(out_refs):
        for b in range(batches):
            out_ref[b] = held_ref[b, chunk(k, rows), :]


def flat(ref):
    return ref[...].reshape(-1, ref.shape[-1])


def rows_kernel(plan, sc, got_ref, *refs):
    piece, batches = plan[5], plan[6]
    *out_refs, held_ref = refs
    rows = out_refs[0].shape[1]
    even = first_parity(sc)
    for b in range(batches):
        for s in range(2):
            held_ref[b, s * piece : (s + 1) * piece] = collect(plan, even, got_ref, b, s, 0)
        for k, out_ref in enumerate(out_refs):
            out_ref[b] = held_ref[b, chunk(k, rows), :]


def middle_kernel(spread, sc, *refs):
    o_refs, w_refs, bias_refs, refs = refs[:spread], refs[spread : 2 * spread], refs[2 * spread : 3 * spread], refs[3 * spread :]
    x_ref, g_ref, gain_ref, out_bias_ref, out_ref, grad_ref, n2_ref, dy_ref, sums_ref, du_sum_ref = refs[:10]
    a_refs, du_refs, do_refs = [refs[10 + i * spread : 10 + (i + 1) * spread] for i in range(3)]
    local = w_refs[0].shape[0] // 3
    kind = out_ref.shape
    wo = [w[0:local] for w in w_refs]
    wi = [w[local : 2 * local] for w in w_refs]
    wd = [w[2 * local :] for w in w_refs]
    h1 = flat(x_ref).astype(f32) + out_bias_ref[0:1]
    for k in range(spread):
        h1 = h1 + mm(flat(o_refs[k]), wo[k])
    r2 = lax.rsqrt(jnp.mean(h1 * h1, axis=-1, keepdims=True) + epsilon)
    n2 = (h1 * r2 * gain_ref[1:2]).astype(bf16)
    n2_ref[...] = n2.reshape(kind)
    g = flat(g_ref)
    out = h1 + out_bias_ref[1:2]
    dn2 = 0.0
    for k in range(spread):
        u = mm(n2, wi[k], cols_cols) + bias_refs[k][...]
        gate = 1.0 / (1.0 + jnp.exp(-u))
        a = (u * gate).astype(bf16)
        out = out + mm(a, wd[k])
        ga = mm(g, wd[k], cols_cols)
        du = (ga * gate * (1.0 + u * (1.0 - gate))).astype(bf16)
        dn2 = dn2 + mm(du, wi[k])
        a_refs[k][...] = a
        du_refs[k][...] = du
        du_sum_ref[pl.ds(k ^ lax.axis_index("fsdp"), 1), :] = jnp.sum(du.astype(f32), axis=0, keepdims=True)
    out_ref[...] = out.astype(bf16).reshape(kind)
    z2 = gain_ref[1:2] * dn2
    g = g.astype(f32)
    grad = g + r2 * z2 - h1 * (r2 * r2 * r2 * jnp.mean(z2 * h1, axis=-1, keepdims=True))
    grad_ref[...] = grad.reshape(kind)
    dy = grad.astype(bf16)
    dy_ref[...] = dy.reshape(kind)
    sums_ref[0:1] = jnp.sum(dn2 * h1 * r2, axis=0, keepdims=True)
    sums_ref[1:2] = jnp.sum(grad, axis=0, keepdims=True)
    sums_ref[2:3] = jnp.sum(g, axis=0, keepdims=True)
    for k in range(spread):
        do_refs[k][...] = mm(dy, wo[k], cols_cols).astype(bf16).reshape(do_refs[k].shape)


def grads_kernel(spread, sc, *refs):
    o_refs, du_refs, a_refs = [refs[i * spread : (i + 1) * spread] for i in range(3)]
    dy_ref, n2_ref, g_ref = refs[3 * spread : 3 * spread + 3]
    out_refs = refs[3 * spread + 3 :]
    for k in range(spread):
        local = du_refs[k].shape[1]
        out_refs[k][0:local] = mm(flat(o_refs[k]), flat(dy_ref), rows_rows).astype(bf16)
        out_refs[k][local : 2 * local] = mm(du_refs[k][...], flat(n2_ref), rows_rows).astype(bf16)
        out_refs[k][2 * local :] = mm(a_refs[k][...], flat(g_ref), rows_rows).astype(bf16)


def ahead_kernel(plan, spread, sc, *refs):
    do_refs, (send_ref, held_ref) = refs[:spread], refs[spread:]
    rows = do_refs[0].shape[1]
    parity = first_parity(sc)
    for b in range(plan[6]):
        for k in range(spread):
            held_ref[b, chunk(k, rows), :] = do_refs[k][b]
        store_parts(plan, parity, held_ref[b].T, send_ref, b, 0)


def back_kernel(plan, sc, got_ref, w_ref, n1_ref, gain_ref, d_ref, bias_ref, gain_sum_ref, *refs):
    *out_refs, held_ref = refs
    piece = plan[5]
    even = first_parity(sc)
    total = 0.0
    for kind in range(3):
        for b in range(plan[6]):
            for s in range(2):
                d_ref[kind, b, s * piece : (s + 1) * piece] = collect(plan, even, got_ref, b, s, kind)
        rows = d_ref[kind].reshape(-1, d_ref.shape[3])
        if kind != 1:
            bias_ref[kind // 2 : kind // 2 + 1] = jnp.sum(rows.astype(f32), axis=0, keepdims=True)
        total = total + mm(rows, w_ref[kind])
    give_rows(total, held_ref, out_refs)
    gain_sum_ref[...] = jnp.sum(total * flat(n1_ref).astype(f32), axis=0, keepdims=True) / gain_ref[...]


def shards(
    layer_input, output_cotangent, qkv_weight, out_weight, in_weight, down_weight, qv_bias, in_bias,
    out_bias, norm_gains, query_scale, block_table, block_marks,
):
    batches, own, width = layer_input.shape
    local = qkv_weight.shape[2]
    dim = query_scale.shape[0]
    heads = local // dim
    size = lax.axis_size("context")
    spread = lax.axis_size("fsdp")
    pieces = block_table.shape[0] * 2
    seq = block_marks.shape[1]
    piece = seq // pieces
    group = size // heads
    members = group // (batches - 1)
    plan = (size, heads, group, members, dim, piece, batches)
    rows = own * spread
    me = lax.axis_index("context")
    member = me % group
    scalars = block_table.T
    here = jnp.arange(1, seq + 1, dtype=jnp.int32)
    closing = jnp.concatenate([block_marks[:, 1:] != block_marks[:, :-1], jnp.ones((batches, 1), bool)], axis=1)
    ends = lax.cummin(jnp.where(closing, here, seq), axis=1, reverse=True)
    main_end = lax.dynamic_index_in_dim(ends, member // members, 0, keepdims=False)
    main_end = main_end.reshape(-1, members, piece)
    main_end = lax.dynamic_index_in_dim(main_end, member % members, 1, keepdims=False).reshape(1, -1)
    last_end = ends[batches - 1].reshape(-1, group, piece)
    last_end = lax.dynamic_index_in_dim(last_end, member, 1, keepdims=False).reshape(1, -1)
    factor = base_rate / math.sqrt(dim) * jax.nn.softplus(query_scale)
    factor_row = jnp.tile(factor, heads).reshape(1, local)
    factor_col = factor.reshape(dim, 1)
    gain_one, gain_two = norm_gains[0:1], norm_gains[1:2]

    tokens = batches * rows
    weight_flops = 2 * tokens * width * local
    qkv_turned = jnp.swapaxes(qkv_weight, 1, 2)
    in_turned = in_weight.T
    whole = shape((batches, rows, width), bf16)
    narrow = shape((batches, rows, local), bf16)
    parts = [shape((batches, own, width), bf16)] * spread
    thin_parts = [shape((batches, own, local), bf16)] * spread
    held = [pltpu.VMEM((batches, rows, width), bf16)]
    thin_held = [pltpu.VMEM((batches, rows, local), bf16)]
    asked = [pieces // members * piece, pieces // group * piece]
    mine = batches * own

    x_parts = gather_rows(layer_input, "fsdp", spread)
    n1, send = call(
        functools.partial(project_kernel, plan, spread),
        [whole, shape((size, 11, dim, piece), bf16)],
        [*x_parts, qkv_turned, gain_one, qv_bias, factor_row],
        scalars,
        flops=3 * weight_flops,
    )
    packed = jnp.concatenate([out_weight, in_turned, down_weight])
    w_parts = gather_rows(after(packed, x_parts[-1]), "fsdp", spread)
    bias_parts = gather_rows(after(in_bias.reshape(1, local), x_parts[-1]), "fsdp", spread)
    got = swap_all(send, "context")
    plans = [(pieces, piece, dim, members, 2, 0, 0), (pieces, piece, dim, group, 1, 6, 2)]
    o_send, main_wide, main_lse, last_wide, last_lse = call(
        functools.partial(attend_kernel, plans),
        [shape((size, 3, dim, piece), bf16)] + [shape((r, a), f32) for a in asked for r in (dim, 1)],
        [got, main_end, last_end],
        scalars,
        [
            pltpu.SMEM((pieces,), jnp.int32), pltpu.VMEM((seq, 128), bf16), pltpu.VMEM((dim, seq), bf16),
            pltpu.VMEM((128, asked[0]), bf16),
        ],
        flops=3 * sum(asked) * seq * dim,
        trans=sum(asked) * seq,
    )
    o_parts = call(
        functools.partial(rows_kernel, plan), thin_parts, [swap_all(o_send, "context")], scalars, thin_held
    )
    o_parts = swap_parts(o_parts, "fsdp", spread)
    own_kind = shape((batches, own, width), bf16)
    layer_output, grad_one, n2, dy, sums, du_sum, *rest = call(
        functools.partial(middle_kernel, spread),
        [own_kind, shape((batches, own, width), f32), own_kind, own_kind, shape((3, width), f32), shape((spread, local), f32)]
        + [shape((mine, local), bf16)] * (2 * spread)
        + thin_parts,
        [*o_parts, *w_parts, *bias_parts, layer_input, output_cotangent, norm_gains, out_bias],
        scalars,
        flops=12 * mine * width * width,
        trans=mine * local * spread,
    )
    a_parts, du_parts, do_parts = [rest[i * spread : (i + 1) * spread] for i in range(3)]
    w_grads = call(
        functools.partial(grads_kernel, spread),
        [shape((3 * local, width), bf16)] * spread,
        [*o_parts, *du_parts, *a_parts, dy, n2, output_cotangent],
        scalars,
        flops=6 * mine * width * width,
    )
    do_parts = swap_parts(do_parts, "fsdp", spread)
    (do_send,) = call(
        functools.partial(ahead_kernel, plan, spread),
        [shape((size, 3, dim, piece), bf16)],
        do_parts,
        scalars,
        thin_held,
        tokens=w_grads[:1],
    )
    do_got = swap_all(do_send, "context")
    early = scatter_rows([w[None] for w in w_grads], "fsdp", spread)[0].astype(bf16)
    d_send, scale_sum = call(
        functools.partial(attend_back_kernel, plans),
        [shape((size, 11, dim, piece), bf16), shape((dim, 1), f32)],
        [got, do_got, factor_col, main_end, main_wide, main_lse, last_end, last_wide, last_lse],
        scalars,
        [
            pltpu.SMEM((pieces,), jnp.int32),
            pltpu.VMEM((seq, 128), bf16), pltpu.VMEM((dim, min(seq, key_tile)), bf16), pltpu.VMEM((seq, 128), bf16),
            pltpu.VMEM((128, asked[0]), bf16), pltpu.VMEM((asked[0], 128), bf16),
            pltpu.VMEM((128, asked[0]), bf16), pltpu.VMEM((asked[0], 128), bf16),
            pltpu.VMEM((seq, 128), f32), pltpu.VMEM((seq, 128), f32),
        ],
        flops=8 * sum(asked) * seq * dim,
        trans=sum(asked) * seq,
    )
    d_got = swap_all(d_send, "context")
    half = early.shape[0] // 2
    early = after(early, d_got)
    early_flow = Flow(summing([early[:half], early[half:]], "context", size))

    d_rows, qv_sum, gain_one_sum, *part = call(
        functools.partial(back_kernel, plan),
        [shape((3, batches, rows, local), bf16), shape((2, local), f32), shape((1, width), f32)] + parts,
        [d_got, qkv_turned, n1, gain_one],
        scalars,
        held,
        flops=3 * weight_flops,
    )
    flat_rows = lambda v: v.reshape(tokens, -1)
    qkv = lax.dot_general(
        d_rows.reshape(3, tokens, local), flat_rows(n1), (((1,), (0,)), ((), ())), preferred_element_type=f32
    ).astype(bf16).reshape(3 * local, width)
    half = 3 * local // 2
    qkv_flow = Flow(summing([qkv[:half], qkv[half:]], "context", size))

    scale_part = scale_sum.reshape(-1) / factor
    small = jnp.concatenate([gain_one_sum.reshape(-1), sums.reshape(-1), du_sum.reshape(-1), scale_part])
    steps = [("fsdp", spread, bit) for bit in range(bits_of(spread))]
    steps += [("context", size, bit) for bit in range(bits_of(size))]
    early_flow.go()
    grad_normed = scatter_rows(part, "fsdp", spread)
    for index, (axis, count, bit) in enumerate(steps):
        small = after(small, qkv_flow.got)
        if index == bits_of(spread):
            small = jnp.concatenate([qv_sum.reshape(-1), small])
        got_small = exchange(small, axis, count, bit)
        qkv_flow.go()
        early_flow.go()
        small = small + got_small
    early = jnp.concatenate(early_flow.finish()).astype(f32)
    qkv = jnp.concatenate(qkv_flow.finish()).astype(f32).reshape(3, local, width)
    out_grad = early[:local]
    feed_grads = [early[local : 2 * local], early[2 * local :]]
    qv_grad = small[: 2 * local].reshape(2, local)
    rest = small[2 * local :]
    gains_grad = rest[: 2 * width].reshape(2, width)
    out_bias_grad = rest[2 * width : 4 * width].reshape(2, width)
    rest = rest[4 * width :]
    in_bias_grad = rest[: spread * local].reshape(spread, local)
    in_bias_grad = lax.dynamic_index_in_dim(in_bias_grad, lax.axis_index("fsdp"), 0, keepdims=False)
    scale_grad = rest[spread * local :] * (base_rate / math.sqrt(dim)) * jax.nn.sigmoid(query_scale)

    x_own = layer_input.astype(f32)
    factor_one = lax.rsqrt(jnp.mean(x_own * x_own, axis=-1, keepdims=True) + epsilon)
    weighted = norm_gains[0] * grad_normed
    inner = jnp.mean(weighted * x_own, axis=-1, keepdims=True)
    input_grad = (grad_one + factor_one * weighted - x_own * factor_one**3 * inner).astype(bf16)
    return (
        layer_output,
        input_grad,
        jnp.swapaxes(qkv, 1, 2),
        out_grad,
        feed_grads[0].T,
        feed_grads[1],
        qv_grad,
        in_bias_grad,
        out_bias_grad,
        gains_grad,
        scale_grad,
    )


def solution(mesh):
    in_specs = (
        P(None, ("context", "fsdp"), None),
        P(None, ("context", "fsdp"), None),
        P(None, None, "fsdp"),
        P("fsdp", None),
        P(None, "fsdp"),
        P("fsdp", None),
        P(None, "fsdp"),
        P("fsdp"),
        P(),
        P(),
        P(),
        P(),
        P(),
    )
    out_specs = (
        P(None, ("context", "fsdp"), None),
        P(None, ("context", "fsdp"), None),
        P(None, None, "fsdp"),
        P("fsdp", None),
        P(None, "fsdp"),
        P("fsdp", None),
        P(None, "fsdp"),
        P("fsdp"),
        P(),
        P(),
        P(),
    )
    return jax.shard_map(shards, mesh=mesh, in_specs=in_specs, out_specs=out_specs, check_vma=False)
```

time: 1290 us -> 412 us (0.32)
  waiting for transfers between devices: 542 us -> 191 us
  local copies, waits for them, and re-layouts: 209 us -> 24.2 us
  blocking collectives: 168 us -> 0 us
  matrix products: 164 us -> 4.2 us
  other arithmetic: 166 us -> 54.7 us
  Pallas kernels: 0 us -> 65.8 us
  starting transfers between devices: 1.45 us -> 66.5 us
  between operations: 21.9 us -> 1.6 us
    psum x1 -> x0, waiting for transfers between devices: 267 us -> none  [shards(): lax.psum((qkv_total, out_total, in_total, down_total, qv_total, in_bias_t...]
    reduce_scatter x15 -> x0, waiting for transfers between devices: 201 us -> none  [the longest x3 71.5 us: shards(): lax.psum_scatter(reorder(key_buffer, flat_table, pieces), 'context', scat...]
    dot_general x78 -> x1, matrix products: 164 us -> 4.2 us  [shards(): lax.dot_general(d_rows.reshape(3, tokens, local), flat_rows(n1), (((1,),...]
    ppermute x0 -> x50, waiting for transfers between devices: none -> 132 us  [the longest x44 124 us: exchange(): return lax.ppermute(values, axis, [(i, i ^ 1 << bit) for i in range(size)])]
    all_gather x12 -> x0, blocking collectives: 102 us -> none  [the longest x3 29.1 us: shards(): grad_all = lax.all_gather(grad_out, 'fsdp', axis=0, tiled=True)]
    reshape x22 -> x10, local copies, waits for them, and re-layouts: 86.3 us -> 4.01 us  [the longest x1 0.72 us: shards(): factor_col = factor.reshape(dim, 1)]
    all_gather x3 -> x0, waiting for transfers between devices: 74 us -> none  [shards(): lax.all_gather(jnp.concatenate([keys, values], axis=1), 'context', axis=0...]
    psum x2 -> x0, blocking collectives: 66.4 us -> none  [the longest x1 45.5 us: shards(): lax.psum((gains_total, out_bias_total, scale_grad), ('context', 'fsdp'))]
  transfers between devices with their start and end apart: 19 -> 54, of which waited for: 12 -> 25; matrix products, arithmetic and copies ran while one was open for 36% -> 18% of each run, Pallas kernels for 0% -> 12%
where the time goes in v1:
time: 412 us; the launch traced here: 408 us
  waiting for transfers between devices  191 us (46%)
  starting transfers between devices  66.5 us (16%)
  Pallas kernels  65.8 us (16%)
  other arithmetic  54.7 us (13%)
  local copies, waits for them, and re-layouts  24.2 us (6%)
  matrix products  4.2 us (1%)
    ppermute x44, waiting for transfers between devices, exchange(): return lax.ppermute(values, axis, [(i, i ^ 1 << bit) for i in range(size)])  124 us
    pallas_call x8, Pallas kernels, call(): pl.pallas_call(lambda *refs: kernel(*refs[:used], *refs[used + len(tokens...  65.8 us
    all_to_all x4, waiting for transfers between devices, swap_all(): return lax.all_to_all(parts, axis, 0, 0, tiled=True)  58.8 us
    ppermute x44, starting transfers between devices, exchange(): return lax.ppermute(values, axis, [(i, i ^ 1 << bit) for i in range(size)])  41.9 us
    all_to_all x4, starting transfers between devices, swap_all(): return lax.all_to_all(parts, axis, 0, 0, tiled=True)  20.8 us
    convert_element_type x12, other arithmetic, summing(): (k.astype(f32) + g.astype(f32)).astype(bf16)  9.72 us
  transfers between devices with their start and end apart: 54, of which 25 were waited for; matrix products, arithmetic and copies ran while one was open for 18% of the time, Pallas kernels for 12%

profile of v1, /device:TPU:0, one launch (start us, length us, event | category | flops | bytes accessed | tf_op | source)
XLA Modules:
  0.0 407.8 jit_solution(13281505667868689673)
XLA Ops:
  0.6 3.0 collective-permute-start.1
  3.6 11.4 %collective-permute-done.1.refs_3_ = bf16[3,64,1280]{2,1,0:T(8,128)(2,1)S(1)} collective-permute-done((bf16[3,64,1280]{2,1,0:T(8,128)(2,1)}, bf16[3,64,1280]{2,1,0:T(8,128)(2,1)S(1)}, u32[]{:S(2)}, u32[]{:S(2)}) %collective-permute-start.1) | collective-permute-done | bytes 491552 | tf_op jit(solution)/shard_map/ppermute | solution.py:60
  15.1 3.4 pad_maximum_fusion.refs_0_
  19.3 1.7 collective-permute-start.7
  23.7 7.6 %shard_map.212 = (bf16[3,256,1280]{2,1,0:T(8,128)(2,1)}, bf16[8,11,80,128]{3,2,1,0:T(8,128)(2,1)}) custom-call(s32[2,8]{1,0:T(2,128)} %bitcast.50, bf16[3,64,1280]{2,1,0:T(8,128)(2,1)} %refs_13_.1, bf16[3,64,1280]{2,1,0:T(8,128)(2,1)} %copy-done.36, bf16[3,64,1280]{2,1,0:T(8,128)(2,1)} %copy-done.35, bf16[3,64,1280]{2,1,0:T(8,128)(2,1)} %copy-done.9, ...), custom_call_target="tpu_custom_call" | custom-call | flops 1887436800 | bytes 8200960 | tf_op jit(solution)/shard_map/pallas_call | solution.py:36
  31.3 6.6 %all-to-all-start = ((bf16[8,11,80,128]{3,2,1,0:T(8,128)(2,1)}), bf16[8,11,80,128]{3,2,1,0:T(8,128)(2,1)}, u32[]{:S(2)}, u32[]{:S(2)}) async-start(bf16[8,11,80,128]{3,2,1,0:T(8,128)(2,1)} %get-tuple-element.53), calls=%async_computation | async-start | bytes 3604480 | tf_op jit(solution)/shard_map/all_to_all | solution.py:106
  37.9 37.3 %collective-permute-done.7.refs_7_ = bf16[960,1280]{1,0:T(8,128)(2,1)} collective-permute-done((bf16[960,1280]{1,0:T(8,128)(2,1)}, bf16[960,1280]{1,0:T(8,128)(2,1)}, u32[]{:S(2)}, u32[]{:S(2)}) %collective-permute-start.7) | collective-permute-done | bytes 2457632 | tf_op jit(solution)/shard_map/ppermute | solution.py:60
  75.4 7.0 %reduce-window.6 = s32[3,16,128]{2,1,0:T(8,128)S(1)} reduce-window(s32[3,16,128]{2,1,0:T(8,128)S(1)} %bitcast.47, s32[]{:T(128)} %constant.72.clone.1), window={size=1x1x128 pad=0_0x0_0x0_127}, to_apply=%region_0.1 | reduce-window | flops 780288 | bytes 49156 | tf_op jit(solution)/shard_map/reduce-window
  84.2 11.1 %shard_map.213 = (bf16[8,3,80,128]{3,2,1,0:T(8,128)(2,1)}, f32[80,2048]{1,0:T(8,128)}, f32[1,2048]{1,0:T(1,128)}, f32[80,1024]{1,0:T(8,128)}, f32[1,1024]{1,0:T(1,128)}) custom-call(s32[2,8]{1,0:T(2,128)} %bitcast.51, bf16[8,11,80,128]{3,2,1,0:T(8,128)(2,1)} %all-to-all-done.refs_1_, s32[1,2048]{1,0:T(1,128)} %constant_dynamic-slice_fusion.14.refs_2_.refs_4_, ...), custom_call_target="tpu_custom_call" | custom-call | flops 1509949440 | bytes 3301376 | tf_op jit(solution)/shard_map/pallas_call | solution.py:36
  95.3 6.3 %all-to-all-start.1 = ((bf16[8,3,80,128]{3,2,1,0:T(8,128)(2,1)}), bf16[8,3,80,128]{3,2,1,0:T(8,128)(2,1)S(1)}, u32[]{:S(2)}, u32[]{:S(2)}) async-start(bf16[8,3,80,128]{3,2,1,0:T(8,128)(2,1)} %get-tuple-element.54), calls=%async_computation.1 | async-start | bytes 983040 | tf_op jit(solution)/shard_map/all_to_all | solution.py:106
  102.2 1.5 collective-permute-start.10
  103.7 2.3 collective-permute-done.10.refs_11_
  106.0 10.0 %all-to-all-done.1.refs_1_ = bf16[8,3,80,128]{3,2,1,0:T(8,128)(2,1)S(1)} async-done(((bf16[8,3,80,128]{3,2,1,0:T(8,128)(2,1)}), bf16[8,3,80,128]{3,2,1,0:T(8,128)(2,1)S(1)}, u32[]{:S(2)}, u32[]{:S(2)}) %all-to-all-start.1) | async-done | bytes 491552 | tf_op jit(solution)/shard_map/all_to_all | solution.py:106
  116.8 2.1 shard_map.214
  118.9 1.6 collective-permute-start.4
  120.8 5.0 %collective-permute-done.4.refs_3_ = bf16[3,64,320]{2,1,0:T(8,128)(2,1)S(1)} collective-permute-done((bf16[3,64,320]{2,1,0:T(8,128)(2,1)}, bf16[3,64,320]{2,1,0:T(8,128)(2,1)S(1)}, u32[]{:S(2)}, u32[]{:S(2)}) %collective-permute-start.4) | collective-permute-done | bytes 122912 | tf_op jit(solution)/shard_map/ppermute | solution.py:102
  125.8 2.3 collective-permute-done.5.refs_4_
  128.7 13.8 %shard_map.217 = (bf16[3,64,1280]{2,1,0:T(8,128)(2,1)}, f32[3,64,1280]{2,1,0:T(8,128)}, bf16[3,64,1280]{2,1,0:T(8,128)(2,1)}, bf16[3,64,1280]{2,1,0:T(8,128)(2,1...) custom-call(s32[2,8]{1,0:T(2,128)} %bitcast.53, ...), custom_call_target="tpu_custom_call" | custom-call | flops 3774873600 | bytes 15283200 | tf_op jit(solution)/shard_map/pallas_call | solution.py:36
  142.9 1.5 collective-permute-start.13
  144.5 6.7 %shard_map.218 = (bf16[960,1280]{1,0:T(8,128)(2,1)}, bf16[960,1280]{1,0:T(8,128)(2,1)}, bf16[960,1280]{1,0:T(8,128)(2,1)}, bf16[960,1280]{1,0:T(8,128)(2,1)}) custom-call(s32[2,8]{1,0:T(2,128)} %bitcast.54, bf16[3,64,320]{2,1,0:T(8,128)(2,1)} %get-tuple-element.55.refs_1_, bf16[3,64,320]{2,1,0:T(8,128)(2,1)} %copy-done.37, bf16[3,64,320]{2,1,0:T(8,128)(2,1)} %copy-done.38, ...), custom_call_target="tpu_custom_call" | custom-call | flops 1887436800 | bytes 12779520 | tf_op jit(solution)/shard_map/pallas_call | solution.py:36
  152.2 2.2 shard_map.219
  154.4 3.8 all-to-all-start.2
  159.3 13.4 %all-to-all-done.2.refs_2_ = bf16[8,3,80,128]{3,2,1,0:T(8,128)(2,1)S(1)} async-done(((bf16[8,3,80,128]{3,2,1,0:T(8,128)(2,1)}), bf16[8,3,80,128]{3,2,1,0:T(8,128)(2,1)S(1)}, u32[]{:S(2)}, u32[]{:S(2)}) %all-to-all-start.2) | async-done | bytes 491552 | tf_op jit(solution)/shard_map/all_to_all | solution.py:106
  173.5 14.7 %shard_map.220 = (bf16[8,11,80,128]{3,2,1,0:T(8,128)(2,1)}, f32[80,1]{1,0:T(8,128)}) custom-call(s32[2,8]{1,0:T(2,128)} %bitcast.56, bf16[8,11,80,128]{3,2,1,0:T(8,128)(2,1)} %all-to-all-done.refs_1_, bf16[8,3,80,128]{3,2,1,0:T(8,128)(2,1)} %copy-done.20, f32[80,1]{1,0:T(8,128)} %copy.36.refs_3_, s32[1,2048]{1,0:T(1,128)} %constant_dynamic-slice_fusion.14.refs_2_.refs_4_, ...), custom_call_target="tpu_custom_call" | custom-call | flops 4026531840 | bytes 5104256 | tf_op jit(solution)/shard_map/pallas_call | solution.py:36
  188.2 4.1 %all-to-all-start.3 = ((bf16[8,11,80,128]{3,2,1,0:T(8,128)(2,1)}), bf16[8,11,80,128]{3,2,1,0:T(8,128)(2,1)S(1)}, u32[]{:S(2)}, u32[]{:S(2)}) async-start(bf16[8,11,80,128]{3,2,1,0:T(8,128)(2,1)} %get-tuple-element.80), calls=%async_computation.3 | async-start | bytes 3604480 | tf_op jit(solution)/shard_map/all_to_all | solution.py:106
  192.7 4.6 %fusion = bf16[1,960,1280]{2,1,0:T(8,128)(2,1)} fusion(bf16[1,960,1280]{2,1,0:T(8,128)(2,1)} %collective-permute-done.31, bf16[960,1280]{1,0:T(8,128)(2,1)} %get-tuple-element.88), kind=kLoop, calls=%fused_computation.1 | loop fusion | flops 4915200 | bytes 7372800 | tf_op jit(solution)/shard_map/convert_element_type | solution.py:90
  197.2 1.5 collective-permute-start.32
  198.7 35.4 %all-to-all-done.3.refs_1_ = bf16[8,11,80,128]{3,2,1,0:T(8,128)(2,1)S(1)} async-done(((bf16[8,11,80,128]{3,2,1,0:T(8,128)(2,1)}), bf16[8,11,80,128]{3,2,1,0:T(8,128)(2,1)S(1)}, u32[]{:S(2)}, u32[]{:S(2)}) %all-to-all-start.3) | async-done | bytes 1802272 | tf_op jit(solution)/shard_map/all_to_all | solution.py:106
  235.4 7.7 %shard_map.221 = (bf16[3,3,256,320]{3,2,1,0:T(8,128)(2,1)}, f32[2,320]{1,0:T(2,128)}, f32[1,1280]{1,0:T(1,128)}, bf16[3,64,1280]{2,1,0:T(8,128)(2,1)}, bf16[3,64...) custom-call(s32[2,8]{1,0:T(2,128)} %bitcast.57, ...), custom_call_target="tpu_custom_call" | custom-call | flops 1887436800 | bytes 9679360 | tf_op jit(solution)/shard_map/pallas_call | solution.py:36
  243.0 4.2 %bitcast_convert_fusion = bf16[3,320,1280]{2,1,0:T(8,128)(2,1)S(1)} fusion(bf16[3,3,256,320]{3,2,1,0:T(8,128)(2,1)} %get-tuple-element.86, bf16[3,256,1280]{2,1,0:T(8,128)(2,1)} %get-tuple-element.81.refs_3_), kind=kOutput, calls=%fused_computation.6 | convolution fusion | flops 1888665600 | bytes 5898240 | tf_op jit(solution)/shard_map/dot_general | solution.py:665
  248.6 1.5 collective-permute-start.18
  251.0 2.1 add_convert_fusion.4
  253.0 12.0 %collective-permute-done.24.refs_2_ = bf16[240,1280]{1,0:T(8,128)(2,1)S(1)} collective-permute-done((bf16[240,1280]{1,0:T(8,128)(2,1)}, bf16[240,1280]{1,0:T(8,128)(2,1)S(1)}, u32[]{:S(2)}, u32[]{:S(2)}) %collective-permute-start.24) | collective-permute-done | bytes 614432 | tf_op jit(solution)/shard_map/ppermute | solution.py:60
  265.0 1.4 collective-permute-start.17
  266.6 1.4 add_convert_fusion.2
  270.7 1.5 collective-permute-start.25
  273.2 4.9 %fusion.3.refs_0_ = bf16[960,1280]{1,0:T(8,128)(2,1)} fusion(bf16[1,960,1280]{2,1,0:T(8,128)(2,1)} %collective-permute-done.32, bf16[1,960,1280]{2,1,0:T(8,128)(2,1)} %collective-permute-done.30, bf16[960,1280]{1,0:T(8,128)(2,1)S(1)} %copy-done), kind=kLoop, calls=%fused_computation.7 | loop fusion | flops 7372800 | bytes 9830400 | tf_op jit(solution)/shard_map/convert_element_type | solution.py:635
  278.0 1.8 fusion.14
  280.7 1.7 collective-permute-start.39
  289.8 2.0 collective-permute-start.20
  291.8 1.6 fusion.5
  293.4 2.4 fusion.8
  295.8 4.6 %collective-permute-done.26.refs_2_ = bf16[60,1280]{1,0:T(8,128)(2,1)S(1)} collective-permute-done((bf16[60,1280]{1,0:T(8,128)(2,1)S(1)}, bf16[60,1280]{1,0:T(8,128)(2,1)S(1)}, u32[]{:S(2)}, u32[]{:S(2)}) %collective-permute-start.26) | collective-permute-done | bytes 153632 | tf_op jit(solution)/shard_map/ppermute | solution.py:60
  300.5 3.5 collective-permute-start.27
  306.9 3.2 collective-permute-start.21
  310.2 1.4 fusion.18.refs_0_
  311.5 2.0 collective-permute-done.27.refs_2_
  315.0 3.1 collective-permute-start.28
  320.4 2.1 collective-permute-start.22
  326.5 1.4 collective-permute-start.40
  327.9 1.4 add_convert_fusion.1
  332.0 2.0 collective-permute-start.29
  336.2 1.5 collective-permute-start.23
  337.7 12.0 %collective-permute-done.49 = f32[7120]{0:T(1024)S(1)} collective-permute-done((f32[7120]{0:T(1024)}, f32[7120]{0:T(1024)S(1)}, u32[]{:S(2)}, u32[]{:S(2)}) %collective-permute-start.49) | collective-permute-done | bytes 28512 | tf_op jit(solution)/shard_map/ppermute | solution.py:60
  353.0 3.5 collective-permute-start.41
  357.6 10.0 %collective-permute-done.41 = bf16[60,1280]{1,0:T(8,128)(2,1)S(1)} collective-permute-done((bf16[60,1280]{1,0:T(8,128)(2,1)S(1)}, bf16[60,1280]{1,0:T(8,128)(2,1)S(1)}, u32[]{:S(2)}, u32[]{:S(2)}) %collective-permute-start.41) | collective-permute-done | bytes 153632 | tf_op jit(solution)/shard_map/ppermute | solution.py:60
  367.7 8.6 %collective-permute-done.35 = bf16[60,1280]{1,0:T(8,128)(2,1)S(1)} collective-permute-done((bf16[60,1280]{1,0:T(8,128)(2,1)S(1)}, bf16[60,1280]{1,0:T(8,128)(2,1)S(1)}, u32[]{:S(2)}, u32[]{:S(2)}) %collective-permute-start.35) | collective-permute-done | bytes 153632 | tf_op jit(solution)/shard_map/ppermute | solution.py:60
  376.5 5.1 %collective-permute-done.42 = bf16[60,1280]{1,0:T(8,128)(2,1)S(1)} collective-permute-done((bf16[60,1280]{1,0:T(8,128)(2,1)S(1)}, bf16[60,1280]{1,0:T(8,128)(2,1)S(1)}, u32[]{:S(2)}, u32[]{:S(2)}) %collective-permute-start.42) | collective-permute-done | bytes 153632 | tf_op jit(solution)/shard_map/ppermute | solution.py:60
  381.8 1.6 collective-permute-done.36
  386.5 2.1 collective-permute-done.43
  388.9 4.9 %collective-permute-done.37 = bf16[120,1280]{1,0:T(8,128)(2,1)S(1)} collective-permute-done((bf16[120,1280]{1,0:T(8,128)(2,1)S(1)}, bf16[120,1280]{1,0:T(8,128)(2,1)S(1)}, u32[]{:S(2)}, u32[]{:S(2)}) %collective-permute-start.37) | collective-permute-done | bytes 307232 | tf_op jit(solution)/shard_map/ppermute | solution.py:60
  395.0 2.7 convert_bitcast_fusion
  397.7 6.7 %collective-permute-done.44 = bf16[240,1280]{1,0:T(8,128)(2,1)S(1)} collective-permute-done((bf16[240,1280]{1,0:T(8,128)(2,1)S(1)}, bf16[240,1280]{1,0:T(8,128)(2,1)S(1)}, u32[]{:S(2)}, u32[]{:S(2)}) %collective-permute-start.44) | collective-permute-done | bytes 614432 | tf_op jit(solution)/shard_map/ppermute | solution.py:60
  405.3 2.4 fusion.13
  (250 shorter events, 52.5 us)
Async XLA Ops:
  0.6 14.4 %collective-permute-start.1 = (bf16[3,64,1280]{2,1,0:T(8,128)(2,1)}, bf16[3,64,1280]{2,1,0:T(8,128)(2,1)S(1)}, u32[]{:S(2)}, u32[]{:S(2)}) collective-permute-start(bf16[3,64,1280]{2,1,0:T(8,128)(2,1)} %refs_13_.1), channel_id=1, source_target_pairs={{0,2},{1,3},{2,0},{3,1},{4,6},{5,7},{6,4},{7,5},{8,10},{9,11},{10,... | collective-permute-start | bytes 1474568 | tf_op jit(solution)/shard_map/ppermute | solution.py:60
  15.1 3.4 collective-permute-start.2
  19.3 55.9 %collective-permute-start.7 = (bf16[960,1280]{1,0:T(8,128)(2,1)}, bf16[960,1280]{1,0:T(8,128)(2,1)}, u32[]{:S(2)}, u32[]{:S(2)}) collective-permute-start(bf16[960,1280]{1,0:T(8,128)(2,1)} %shard_map.215.refs_5_), channel_id=1, source_target_pairs={{0,2},{1,3},{2,0},{3,1},{4,6},{5,7},{6,4},{7,5},{8,10},{9,11},{10,... | collective-permute-start | bytes 7372808 | tf_op jit(solution)/shard_map/ppermute | solution.py:60
  21.0 1.9 collective-permute-start
  31.3 43.9 %copy-start.27 = (s32[3,2048]{1,0:T(4,128)S(1)}, s32[3,2048]{1,0:T(4,128)}, u32[]{:S(2)}) copy-start(s32[3,2048]{1,0:T(4,128)} %param.25) | copy-start | bytes 73732
  31.3 52.9 %all-to-all-start = ((bf16[8,11,80,128]{3,2,1,0:T(8,128)(2,1)}), bf16[8,11,80,128]{3,2,1,0:T(8,128)(2,1)}, u32[]{:S(2)}, u32[]{:S(2)}) async-start(bf16[8,11,80,128]{3,2,1,0:T(8,128)(2,1)} %get-tuple-element.53), calls=%async_computation | async-start | bytes 3604480 | tf_op jit(solution)/shard_map/all_to_all | solution.py:106
  37.9 82.9 %collective-permute-start.6 = (bf16[960,1280]{1,0:T(8,128)(2,1)S(1)}, bf16[960,1280]{1,0:T(8,128)(2,1)}, u32[]{:S(2)}, u32[]{:S(2)}) collective-permute-start(bf16[960,1280]{1,0:T(8,128)(2,1)S(1)} %copy-done.1), channel_id=1, source_target_pairs={{0,1},{1,0},{2,3},{3,2},{4,5},{5,4},{6,7},{7,6},{8,9},{9,8},{10,11... | collective-permute-start | bytes 7372808 | tf_op jit(solution)/shard_map/ppermute | solution.py:60
  75.2 52.9 %collective-permute-start.8 = (bf16[960,1280]{1,0:T(8,128)(2,1)}, bf16[960,1280]{1,0:T(8,128)(2,1)}, u32[]{:S(2)}, u32[]{:S(2)}) collective-permute-start(bf16[960,1280]{1,0:T(8,128)(2,1)} %collective-permute-done.7.refs_7_), channel_id=1, source_target_pairs={{0,1},{1,0},{2,3},{3,2},{4,5},{5,4},{6,7},{7,6},{8,9},{9,8},{10,11... | collective-permute-start | bytes 7372808 | tf_op jit(solution)/shard_map/ppermute | solution.py:60
  84.2 17.4 %copy-start.34 = (f32[320]{0:T(512)S(1)}, f32[320]{0:T(512)}, u32[]{:S(2)}) copy-start(f32[320]{0:T(512)} %param.20) | copy-start | bytes 3844
  95.3 20.7 %all-to-all-start.1 = ((bf16[8,3,80,128]{3,2,1,0:T(8,128)(2,1)}), bf16[8,3,80,128]{3,2,1,0:T(8,128)(2,1)S(1)}, u32[]{:S(2)}, u32[]{:S(2)}) async-start(bf16[8,3,80,128]{3,2,1,0:T(8,128)(2,1)} %get-tuple-element.54), calls=%async_computation.1 | async-start | bytes 983040 | tf_op jit(solution)/shard_map/all_to_all | solution.py:106
  102.2 3.8 collective-permute-start.10
  103.7 15.2 %collective-permute-start.9 = (f32[1,320]{1,0:T(1,128)}, f32[1,320]{1,0:T(1,128)S(1)}, u32[]{:S(2)}, u32[]{:S(2)}) collective-permute-start(f32[1,320]{1,0:T(1,128)} %shard_map.216.refs_9_), channel_id=1, source_target_pairs={{0,1},{1,0},{2,3},{3,2},{4,5},{5,4},{6,7},{7,6},{8,9},{9,8},{10,11... | collective-permute-start | bytes 3848 | tf_op jit(solution)/shard_map/ppermute | solution.py:60
  106.0 22.1 %copy-start.40 = (f32[1,320]{1,0:T(1,128)}, f32[1,320]{1,0:T(1,128)S(1)}, u32[]{:S(2)}) copy-start(f32[1,320]{1,0:T(1,128)S(1)} %collective-permute-done.10.refs_11_) | copy-start | bytes 3844
  106.0 14.5 %collective-permute-start.11 = (f32[1,320]{1,0:T(1,128)S(1)}, f32[1,320]{1,0:T(1,128)S(1)}, u32[]{:S(2)}, u32[]{:S(2)}) collective-permute-start(f32[1,320]{1,0:T(1,128)S(1)} %collective-permute-done.10.refs_11_), channel_id=1, source_target_pairs={{0,1},{1,0},{2,3},{3,2},{4,5},{5,4},{6,7},{7,6},{8,9},{9,8},{10,11... | collective-permute-start | bytes 3848 | tf_op jit(solution)/shard_map/ppermute | solution.py:60
  118.9 1.9 collective-permute-start.3
  118.9 9.2 %copy-start.41 = (f32[1,320]{1,0:T(1,128)}, f32[1,320]{1,0:T(1,128)S(1)}, u32[]{:S(2)}) copy-start(f32[1,320]{1,0:T(1,128)S(1)} %collective-permute-done.9.refs_10_) | copy-start | bytes 3844
  118.9 6.9 %collective-permute-start.4 = (bf16[3,64,320]{2,1,0:T(8,128)(2,1)}, bf16[3,64,320]{2,1,0:T(8,128)(2,1)S(1)}, u32[]{:S(2)}, u32[]{:S(2)}) collective-permute-start(bf16[3,64,320]{2,1,0:T(8,128)(2,1)} %get-tuple-element.57), channel_id=1, source_target_pairs={{0,2},{1,3},{2,0},{3,1},{4,6},{5,7},{6,4},{7,5},{8,10},{9,11},{10,... | collective-permute-start | bytes 368648 | tf_op jit(solution)/shard_map/ppermute | solution.py:102
  120.5 7.6 %copy-start.42 = (f32[1,320]{1,0:T(1,128)}, f32[1,320]{1,0:T(1,128)S(1)}, u32[]{:S(2)}) copy-start(f32[1,320]{1,0:T(1,128)S(1)} %collective-permute-done.11.refs_12_) | copy-start | bytes 3844
  120.5 7.6 %collective-permute-start.5 = (bf16[3,64,320]{2,1,0:T(8,128)(2,1)}, bf16[3,64,320]{2,1,0:T(8,128)(2,1)S(1)}, u32[]{:S(2)}, u32[]{:S(2)}) collective-permute-start(bf16[3,64,320]{2,1,0:T(8,128)(2,1)} %get-tuple-element.58), channel_id=1, source_target_pairs={{0,3},{1,2},{2,1},{3,0},{4,7},{5,6},{6,5},{7,4},{8,11},{9,10},{10,... | collective-permute-start | bytes 368648 | tf_op jit(solution)/shard_map/ppermute | solution.py:102
  142.5 8.7 %collective-permute-start.12 = (bf16[3,64,320]{2,1,0:T(8,128)(2,1)}, bf16[3,64,320]{2,1,0:T(8,128)(2,1)S(1)}, u32[]{:S(2)}, u32[]{:S(2)}) collective-permute-start(bf16[3,64,320]{2,1,0:T(8,128)(2,1)} %get-tuple-element.62), channel_id=1, source_target_pairs={{0,1},{1,0},{2,3},{3,2},{4,5},{5,4},{6,7},{7,6},{8,9},{9,8},{10,11... | collective-permute-start | bytes 368648 | tf_op jit(solution)/shard_map/ppermute | solution.py:102
  142.9 8.4 %collective-permute-start.13 = (bf16[3,64,320]{2,1,0:T(8,128)(2,1)}, bf16[3,64,320]{2,1,0:T(8,128)(2,1)S(1)}, u32[]{:S(2)}, u32[]{:S(2)}) collective-permute-start(bf16[3,64,320]{2,1,0:T(8,128)(2,1)} %get-tuple-element.63), channel_id=1, source_target_pairs={{0,2},{1,3},{2,0},{3,1},{4,6},{5,7},{6,4},{7,5},{8,10},{9,11},{10,... | collective-permute-start | bytes 368648 | tf_op jit(solution)/shard_map/ppermute | solution.py:102
  144.4 7.2 %collective-permute-start.14 = (bf16[3,64,320]{2,1,0:T(8,128)(2,1)}, bf16[3,64,320]{2,1,0:T(8,128)(2,1)S(1)}, u32[]{:S(2)}, u32[]{:S(2)}) collective-permute-start(bf16[3,64,320]{2,1,0:T(8,128)(2,1)} %get-tuple-element.64), channel_id=1, source_target_pairs={{0,3},{1,2},{2,1},{3,0},{4,7},{5,6},{6,5},{7,4},{8,11},{9,10},{10,... | collective-permute-start | bytes 368648 | tf_op jit(solution)/shard_map/ppermute | solution.py:102
  154.4 18.3 %all-to-all-start.2 = ((bf16[8,3,80,128]{3,2,1,0:T(8,128)(2,1)}), bf16[8,3,80,128]{3,2,1,0:T(8,128)(2,1)S(1)}, u32[]{:S(2)}, u32[]{:S(2)}) async-start(bf16[8,3,80,128]{3,2,1,0:T(8,128)(2,1)} %shard_map.219), calls=%async_computation.2 | async-start | bytes 983040 | tf_op jit(solution)/shard_map/all_to_all | solution.py:106
  159.0 33.7 %collective-permute-start.31 = (bf16[1,960,1280]{2,1,0:T(8,128)(2,1)}, bf16[1,960,1280]{2,1,0:T(8,128)(2,1)}, u32[]{:S(2)}, u32[]{:S(2)}) collective-permute-start(bf16[1,960,1280]{2,1,0:T(8,128)(2,1)} %bitcast.15), channel_id=1, source_target_pairs={{0,1},{1,0},{2,3},{3,2},{4,5},{5,4},{6,7},{7,6},{8,9},{9,8},{10,11... | collective-permute-start | bytes 7372808 | tf_op jit(solution)/shard_map/ppermute | solution.py:60
  188.2 45.9 %all-to-all-start.3 = ((bf16[8,11,80,128]{3,2,1,0:T(8,128)(2,1)}), bf16[8,11,80,128]{3,2,1,0:T(8,128)(2,1)S(1)}, u32[]{:S(2)}, u32[]{:S(2)}) async-start(bf16[8,11,80,128]{3,2,1,0:T(8,128)(2,1)} %get-tuple-element.80), calls=%async_computation.3 | async-start | bytes 3604480 | tf_op jit(solution)/shard_map/all_to_all | solution.py:106
  192.4 80.4 %collective-permute-start.30 = (bf16[1,960,1280]{2,1,0:T(8,128)(2,1)}, bf16[1,960,1280]{2,1,0:T(8,128)(2,1)}, u32[]{:S(2)}, u32[]{:S(2)}) collective-permute-start(bf16[1,960,1280]{2,1,0:T(8,128)(2,1)} %bitcast.60), channel_id=1, source_target_pairs={{0,1},{1,0},{2,3},{3,2},{4,5},{5,4},{6,7},{7,6},{8,9},{9,8},{10,11... | collective-permute-start | bytes 7372808 | tf_op jit(solution)/shard_map/ppermute | solution.py:60
  197.2 75.9 %collective-permute-start.32 = (bf16[1,960,1280]{2,1,0:T(8,128)(2,1)}, bf16[1,960,1280]{2,1,0:T(8,128)(2,1)}, u32[]{:S(2)}, u32[]{:S(2)}) collective-permute-start(bf16[1,960,1280]{2,1,0:T(8,128)(2,1)} %fusion), channel_id=1, source_target_pairs={{0,2},{1,3},{2,0},{3,1},{4,6},{5,7},{6,4},{7,5},{8,10},{9,11},{10,... | collective-permute-start | bytes 7372808 | tf_op jit(solution)/shard_map/ppermute | solution.py:60
  247.4 3.3 collective-permute-start.16
  248.5 16.5 %collective-permute-start.24 = (bf16[240,1280]{1,0:T(8,128)(2,1)}, bf16[240,1280]{1,0:T(8,128)(2,1)S(1)}, u32[]{:S(2)}, u32[]{:S(2)}) collective-permute-start(bf16[240,1280]{1,0:T(8,128)(2,1)} %constant_dynamic-slice_fusion.9), channel_id=1, source_target_pairs={{0,8},{4,12},{8,0},{12,4},{16,24},{20,28},{24,16},{28,20},{1,9},{5... | collective-permute-start | bytes 1843208 | tf_op jit(solution)/shard_map/ppermute | solution.py:60
  248.6 17.8 %collective-permute-start.18 = (bf16[240,1280]{1,0:T(8,128)(2,1)S(1)}, bf16[240,1280]{1,0:T(8,128)(2,1)}, u32[]{:S(2)}, u32[]{:S(2)}) collective-permute-start(bf16[240,1280]{1,0:T(8,128)(2,1)S(1)} %constant_dynamic-slice_fusion.12), channel_id=1, source_target_pairs={{0,4},{4,0},{8,12},{12,8},{16,20},{20,16},{24,28},{28,24},{1,5},{5... | collective-permute-start | bytes 1843208 | tf_op jit(solution)/shard_map/ppermute | solution.py:60
  250.8 39.0 %collective-permute-start.15 = (bf16[3,64,1280]{2,1,0:T(8,128)(2,1)}, bf16[3,64,1280]{2,1,0:T(8,128)(2,1)}, u32[]{:S(2)}, u32[]{:S(2)}) collective-permute-start(bf16[3,64,1280]{2,1,0:T(8,128)(2,1)} %get-tuple-element.83), channel_id=1, source_target_pairs={{0,1},{1,0},{2,3},{3,2},{4,5},{5,4},{6,7},{7,6},{8,9},{9,8},{10,11... | collective-permute-start | bytes 1474568 | tf_op jit(solution)/shard_map/ppermute | solution.py:60
  265.0 26.7 %collective-permute-start.17 = (bf16[3,64,1280]{2,1,0:T(8,128)(2,1)}, bf16[3,64,1280]{2,1,0:T(8,128)(2,1)}, u32[]{:S(2)}, u32[]{:S(2)}) collective-permute-start(bf16[3,64,1280]{2,1,0:T(8,128)(2,1)} %add_convert_fusion.4), channel_id=1, source_target_pairs={{0,2},{1,3},{2,0},{3,1},{4,6},{5,7},{6,4},{7,5},{8,10},{9,11},{10,... | collective-permute-start | bytes 1474568 | tf_op jit(solution)/shard_map/ppermute | solution.py:60
  266.5 4.3 %collective-permute-start.45 = (f32[6480]{0:T(1024)}, f32[6480]{0:T(1024)S(1)}, u32[]{:S(2)}, u32[]{:S(2)}) collective-permute-start(f32[6480]{0:T(1024)} %shard_map.223), channel_id=1, source_target_pairs={{0,1},{1,0},{2,3},{3,2},{4,5},{5,4},{6,7},{7,6},{8,9},{9,8},{10,11... | collective-permute-start | bytes 77768 | tf_op jit(solution)/shard_map/ppermute | solution.py:60
  269.9 8.1 %copy-start.4 = (bf16[240,1280]{1,0:T(8,128)(2,1)}, bf16[240,1280]{1,0:T(8,128)(2,1)S(1)}, u32[]{:S(2)}) copy-start(bf16[240,1280]{1,0:T(8,128)(2,1)S(1)} %add_convert_fusion.3) | copy-start | bytes 1843204
  270.7 12.6 %collective-permute-start.25 = (bf16[120,1280]{1,0:T(8,128)(2,1)}, bf16[120,1280]{1,0:T(8,128)(2,1)S(1)}, u32[]{:S(2)}, u32[]{:S(2)}) collective-permute-start(bf16[120,1280]{1,0:T(8,128)(2,1)} %constant_dynamic-slice_fusion.8), channel_id=1, source_target_pairs={{0,4},{4,0},{8,12},{12,8},{16,20},{20,16},{24,28},{28,24},{1,5},{5... | collective-permute-start | bytes 921608 | tf_op jit(solution)/shard_map/ppermute | solution.py:60
  272.8 11.0 %collective-permute-start.19 = (bf16[120,1280]{1,0:T(8,128)(2,1)}, bf16[120,1280]{1,0:T(8,128)(2,1)}, u32[]{:S(2)}, u32[]{:S(2)}) collective-permute-start(bf16[120,1280]{1,0:T(8,128)(2,1)} %constant_dynamic-slice_fusion.11), channel_id=1, source_target_pairs={{0,8},{4,12},{8,0},{12,4},{16,24},{20,28},{24,16},{28,20},{1,9},{5... | collective-permute-start | bytes 921608 | tf_op jit(solution)/shard_map/ppermute | solution.py:60
  280.7 44.4 %collective-permute-start.39 = (bf16[240,1280]{1,0:T(8,128)(2,1)}, bf16[240,1280]{1,0:T(8,128)(2,1)}, u32[]{:S(2)}, u32[]{:S(2)}) collective-permute-start(bf16[240,1280]{1,0:T(8,128)(2,1)} %constant_dynamic-slice_fusion.3), channel_id=1, source_target_pairs={{0,8},{4,12},{8,0},{12,4},{16,24},{20,28},{24,16},{28,20},{1,9},{5... | collective-permute-start | bytes 1843208 | tf_op jit(solution)/shard_map/ppermute | solution.py:60
  283.3 44.6 %collective-permute-start.33 = (bf16[240,1280]{1,0:T(8,128)(2,1)}, bf16[240,1280]{1,0:T(8,128)(2,1)}, u32[]{:S(2)}, u32[]{:S(2)}) collective-permute-start(bf16[240,1280]{1,0:T(8,128)(2,1)} %constant_dynamic-slice_fusion.6), channel_id=1, source_target_pairs={{0,4},{4,0},{8,12},{12,8},{16,20},{20,16},{24,28},{28,24},{1,5},{5... | collective-permute-start | bytes 1843208 | tf_op jit(solution)/shard_map/ppermute | solution.py:60
  284.0 7.7 %copy-start.7 = (bf16[3,64,1280]{2,1,0:T(8,128)(2,1)S(1)}, bf16[3,64,1280]{2,1,0:T(8,128)(2,1)}, u32[]{:S(2)}) copy-start(bf16[3,64,1280]{2,1,0:T(8,128)(2,1)} %refs_13_.1) | copy-start | bytes 1474564
  284.0 7.7 %copy-start.8 = (bf16[3,64,1280]{2,1,0:T(8,128)(2,1)S(1)}, bf16[3,64,1280]{2,1,0:T(8,128)(2,1)}, u32[]{:S(2)}) copy-start(bf16[3,64,1280]{2,1,0:T(8,128)(2,1)} %get-tuple-element.82) | copy-start | bytes 1474564
  284.0 9.3 %copy-start.15 = (f32[3,64,1280]{2,1,0:T(8,128)S(1)}, f32[3,64,1280]{2,1,0:T(8,128)}, u32[]{:S(2)}) copy-start(f32[3,64,1280]{2,1,0:T(8,128)} %get-tuple-element.60) | copy-start | bytes 2949124
  284.1 4.1 %collective-permute-start.46 = (f32[6480]{0:T(1024)}, f32[6480]{0:T(1024)S(1)}, u32[]{:S(2)}, u32[]{:S(2)}) collective-permute-start(f32[6480]{0:T(1024)} %shard_map.224), channel_id=1, source_target_pairs={{0,2},{1,3},{2,0},{3,1},{4,6},{5,7},{6,4},{7,5},{8,10},{9,11},{10,... | collective-permute-start | bytes 77768 | tf_op jit(solution)/shard_map/ppermute | solution.py:60
  288.2 12.2 %collective-permute-start.26 = (bf16[60,1280]{1,0:T(8,128)(2,1)S(1)}, bf16[60,1280]{1,0:T(8,128)(2,1)S(1)}, u32[]{:S(2)}, u32[]{:S(2)}) collective-permute-start(bf16[60,1280]{1,0:T(8,128)(2,1)S(1)} %constant_dynamic-slice_fusion.7), channel_id=1, source_target_pairs={{0,16},{4,20},{8,24},{12,28},{16,0},{20,4},{24,8},{28,12},{1,17},{... | collective-permute-start | bytes 460808 | tf_op jit(solution)/shard_map/ppermute | solution.py:60
  289.8 14.3 %collective-permute-start.20 = (bf16[60,1280]{1,0:T(8,128)(2,1)S(1)}, bf16[60,1280]{1,0:T(8,128)(2,1)S(1)}, u32[]{:S(2)}, u32[]{:S(2)}) collective-permute-start(bf16[60,1280]{1,0:T(8,128)(2,1)S(1)} %constant_dynamic-slice_fusion.10), channel_id=1, source_target_pairs={{0,16},{4,20},{8,24},{12,28},{16,0},{20,4},{24,8},{28,12},{1,17},{... | collective-permute-start | bytes 460808 | tf_op jit(solution)/shard_map/ppermute | solution.py:60
  300.5 13.0 %collective-permute-start.27 = (bf16[60,1280]{1,0:T(8,128)(2,1)S(1)}, bf16[60,1280]{1,0:T(8,128)(2,1)S(1)}, u32[]{:S(2)}, u32[]{:S(2)}) collective-permute-start(bf16[60,1280]{1,0:T(8,128)(2,1)S(1)} %add_convert_fusion.11), channel_id=1, source_target_pairs={{0,16},{4,20},{8,24},{12,28},{16,0},{20,4},{24,8},{28,12},{1,17},{... | collective-permute-start | bytes 460808 | tf_op jit(solution)/shard_map/ppermute | solution.py:60
  305.5 4.7 %collective-permute-start.47 = (f32[7120]{0:T(1024)S(1)}, f32[7120]{0:T(1024)S(1)}, u32[]{:S(2)}, u32[]{:S(2)}) collective-permute-start(f32[7120]{0:T(1024)S(1)} %pad_maximum_fusion.11), channel_id=1, source_target_pairs={{0,4},{4,0},{8,12},{12,8},{16,20},{20,16},{24,28},{28,24},{1,5},{5... | collective-permute-start | bytes 85448 | tf_op jit(solution)/shard_map/ppermute | solution.py:60
  306.9 11.8 %collective-permute-start.21 = (bf16[60,1280]{1,0:T(8,128)(2,1)S(1)}, bf16[60,1280]{1,0:T(8,128)(2,1)S(1)}, u32[]{:S(2)}, u32[]{:S(2)}) collective-permute-start(bf16[60,1280]{1,0:T(8,128)(2,1)S(1)} %add_convert_fusion.12), channel_id=1, source_target_pairs={{0,16},{4,20},{8,24},{12,28},{16,0},{20,4},{24,8},{28,12},{1,17},{... | collective-permute-start | bytes 460808 | tf_op jit(solution)/shard_map/ppermute | solution.py:60
  315.0 15.0 %collective-permute-start.28 = (bf16[120,1280]{1,0:T(8,128)(2,1)}, bf16[120,1280]{1,0:T(8,128)(2,1)}, u32[]{:S(2)}, u32[]{:S(2)}) collective-permute-start(bf16[120,1280]{1,0:T(8,128)(2,1)} %pad_maximum_fusion.7), channel_id=1, source_target_pairs={{0,4},{4,0},{8,12},{12,8},{16,20},{20,16},{24,28},{28,24},{1,5},{5... | collective-permute-start | bytes 921608 | tf_op jit(solution)/shard_map/ppermute | solution.py:60
  319.4 4.4 %collective-permute-start.48 = (f32[7120]{0:T(1024)}, f32[7120]{0:T(1024)S(1)}, u32[]{:S(2)}, u32[]{:S(2)}) collective-permute-start(f32[7120]{0:T(1024)} %shard_map.226), channel_id=1, source_target_pairs={{0,8},{4,12},{8,0},{12,4},{16,24},{20,28},{24,16},{28,20},{1,9},{5... | collective-permute-start | bytes 85448 | tf_op jit(solution)/shard_map/ppermute | solution.py:60
  320.4 13.6 %collective-permute-start.22 = (bf16[120,1280]{1,0:T(8,128)(2,1)S(1)}, bf16[120,1280]{1,0:T(8,128)(2,1)}, u32[]{:S(2)}, u32[]{:S(2)}) collective-permute-start(bf16[120,1280]{1,0:T(8,128)(2,1)S(1)} %pad_maximum_fusion.6), channel_id=1, source_target_pairs={{0,8},{4,12},{8,0},{12,4},{16,24},{20,28},{24,16},{28,20},{1,9},{5... | collective-permute-start | bytes 921608 | tf_op jit(solution)/shard_map/ppermute | solution.py:60
  326.5 26.4 %collective-permute-start.40 = (bf16[120,1280]{1,0:T(8,128)(2,1)S(1)}, bf16[120,1280]{1,0:T(8,128)(2,1)S(1)}, u32[]{:S(2)}, u32[]{:S(2)}) collective-permute-start(bf16[120,1280]{1,0:T(8,128)(2,1)S(1)} %constant_dynamic-slice_fusion.2), channel_id=1, source_target_pairs={{0,4},{4,0},{8,12},{12,8},{16,20},{20,16},{24,28},{28,24},{1,5},{5... | collective-permute-start | bytes 921608 | tf_op jit(solution)/shard_map/ppermute | solution.py:60
  330.0 26.4 %collective-permute-start.34 = (bf16[120,1280]{1,0:T(8,128)(2,1)}, bf16[120,1280]{1,0:T(8,128)(2,1)}, u32[]{:S(2)}, u32[]{:S(2)}) collective-permute-start(bf16[120,1280]{1,0:T(8,128)(2,1)} %constant_dynamic-slice_fusion.5), channel_id=1, source_target_pairs={{0,8},{4,12},{8,0},{12,4},{16,24},{20,28},{24,16},{28,20},{1,9},{5... | collective-permute-start | bytes 921608 | tf_op jit(solution)/shard_map/ppermute | solution.py:60
  332.0 51.6 %collective-permute-start.29 = (bf16[240,1280]{1,0:T(8,128)(2,1)}, bf16[240,1280]{1,0:T(8,128)(2,1)}, u32[]{:S(2)}, u32[]{:S(2)}) collective-permute-start(bf16[240,1280]{1,0:T(8,128)(2,1)} %pad_maximum_fusion.3), channel_id=1, source_target_pairs={{0,8},{4,12},{8,0},{12,4},{16,24},{20,28},{24,16},{28,20},{1,9},{5... | collective-permute-start | bytes 1843208 | tf_op jit(solution)/shard_map/ppermute | solution.py:60
  334.0 15.7 %copy-start.22 = (f32[7120]{0:T(1024)S(1)}, f32[7120]{0:T(1024)}, u32[]{:S(2)}) copy-start(f32[7120]{0:T(1024)} %shard_map.227) | copy-start | bytes 85444
  334.0 15.7 %collective-permute-start.49 = (f32[7120]{0:T(1024)}, f32[7120]{0:T(1024)S(1)}, u32[]{:S(2)}, u32[]{:S(2)}) collective-permute-start(f32[7120]{0:T(1024)} %shard_map.227), channel_id=1, source_target_pairs={{0,16},{4,20},{8,24},{12,28},{16,0},{20,4},{24,8},{28,12},{1,17},{... | collective-permute-start | bytes 85448 | tf_op jit(solution)/shard_map/ppermute | solution.py:60
  336.2 48.7 %collective-permute-start.23 = (bf16[240,1280]{1,0:T(8,128)(2,1)}, bf16[240,1280]{1,0:T(8,128)(2,1)}, u32[]{:S(2)}, u32[]{:S(2)}) collective-permute-start(bf16[240,1280]{1,0:T(8,128)(2,1)} %pad_maximum_fusion.2), channel_id=1, source_target_pairs={{0,4},{4,0},{8,12},{12,8},{16,20},{20,16},{24,28},{28,24},{1,5},{5... | collective-permute-start | bytes 1843208 | tf_op jit(solution)/shard_map/ppermute | solution.py:60
  353.0 14.6 %collective-permute-start.41 = (bf16[60,1280]{1,0:T(8,128)(2,1)S(1)}, bf16[60,1280]{1,0:T(8,128)(2,1)S(1)}, u32[]{:S(2)}, u32[]{:S(2)}) collective-permute-start(bf16[60,1280]{1,0:T(8,128)(2,1)S(1)} %constant_dynamic-slice_fusion.1), channel_id=1, source_target_pairs={{0,16},{4,20},{8,24},{12,28},{16,0},{20,4},{24,8},{28,12},{1,17},{... | collective-permute-start | bytes 460808 | tf_op jit(solution)/shard_map/ppermute | solution.py:60
  357.5 18.8 %collective-permute-start.35 = (bf16[60,1280]{1,0:T(8,128)(2,1)S(1)}, bf16[60,1280]{1,0:T(8,128)(2,1)S(1)}, u32[]{:S(2)}, u32[]{:S(2)}) collective-permute-start(bf16[60,1280]{1,0:T(8,128)(2,1)S(1)} %constant_dynamic-slice_fusion.4), channel_id=1, source_target_pairs={{0,16},{4,20},{8,24},{12,28},{16,0},{20,4},{24,8},{28,12},{1,17},{... | collective-permute-start | bytes 460808 | tf_op jit(solution)/shard_map/ppermute | solution.py:60
  367.6 14.0 %collective-permute-start.42 = (bf16[60,1280]{1,0:T(8,128)(2,1)S(1)}, bf16[60,1280]{1,0:T(8,128)(2,1)S(1)}, u32[]{:S(2)}, u32[]{:S(2)}) collective-permute-start(bf16[60,1280]{1,0:T(8,128)(2,1)S(1)} %add_convert_fusion.9), channel_id=1, source_target_pairs={{0,16},{4,20},{8,24},{12,28},{16,0},{20,4},{24,8},{28,12},{1,17},{... | collective-permute-start | bytes 460808 | tf_op jit(solution)/shard_map/ppermute | solution.py:60
  376.4 7.0 %collective-permute-start.36 = (bf16[60,1280]{1,0:T(8,128)(2,1)S(1)}, bf16[60,1280]{1,0:T(8,128)(2,1)S(1)}, u32[]{:S(2)}, u32[]{:S(2)}) collective-permute-start(bf16[60,1280]{1,0:T(8,128)(2,1)S(1)} %add_convert_fusion.10), channel_id=1, source_target_pairs={{0,16},{4,20},{8,24},{12,28},{16,0},{20,4},{24,8},{28,12},{1,17},{... | collective-permute-start | bytes 460808 | tf_op jit(solution)/shard_map/ppermute | solution.py:60
  381.7 6.9 %collective-permute-start.43 = (bf16[120,1280]{1,0:T(8,128)(2,1)S(1)}, bf16[120,1280]{1,0:T(8,128)(2,1)S(1)}, u32[]{:S(2)}, u32[]{:S(2)}) collective-permute-start(bf16[120,1280]{1,0:T(8,128)(2,1)S(1)} %pad_maximum_fusion.9), channel_id=1, source_target_pairs={{0,4},{4,0},{8,12},{12,8},{16,20},{20,16},{24,28},{28,24},{1,5},{5... | collective-permute-start | bytes 921608 | tf_op jit(solution)/shard_map/ppermute | solution.py:60
  383.5 10.3 %collective-permute-start.37 = (bf16[120,1280]{1,0:T(8,128)(2,1)S(1)}, bf16[120,1280]{1,0:T(8,128)(2,1)S(1)}, u32[]{:S(2)}, u32[]{:S(2)}) collective-permute-start(bf16[120,1280]{1,0:T(8,128)(2,1)S(1)} %pad_maximum_fusion.8), channel_id=1, source_target_pairs={{0,8},{4,12},{8,0},{12,4},{16,24},{20,28},{24,16},{28,20},{1,9},{5... | collective-permute-start | bytes 921608 | tf_op jit(solution)/shard_map/ppermute | solution.py:60
  388.8 15.5 %collective-permute-start.44 = (bf16[240,1280]{1,0:T(8,128)(2,1)S(1)}, bf16[240,1280]{1,0:T(8,128)(2,1)S(1)}, u32[]{:S(2)}, u32[]{:S(2)}) collective-permute-start(bf16[240,1280]{1,0:T(8,128)(2,1)S(1)} %pad_maximum_fusion.5), channel_id=1, source_target_pairs={{0,8},{4,12},{8,0},{12,4},{16,24},{20,28},{24,16},{28,20},{1,9},{5... | collective-permute-start | bytes 1843208 | tf_op jit(solution)/shard_map/ppermute | solution.py:60
  394.0 10.7 %collective-permute-start.38 = (bf16[240,1280]{1,0:T(8,128)(2,1)S(1)}, bf16[240,1280]{1,0:T(8,128)(2,1)S(1)}, u32[]{:S(2)}, u32[]{:S(2)}) collective-permute-start(bf16[240,1280]{1,0:T(8,128)(2,1)S(1)} %pad_maximum_fusion.4), channel_id=1, source_target_pairs={{0,4},{4,0},{8,12},{12,8},{16,20},{20,16},{24,28},{28,24},{1,5},{5... | collective-permute-start | bytes 1843208 | tf_op jit(solution)/shard_map/ppermute | solution.py:60
  (34 other events, 92.1 us)

commit v2 on v1

--- a/solution.py
+++ b/solution.py
@@ -14,6 +14,11 @@
 key_tile = 2048
 vmem_bytes = 60 * 1024 * 1024
 loop_tile = 1024
+kernel_us = {
+    "project_kernel": 7, "attend_kernel": 11, "middle_kernel": 14, "attend_back_kernel": 15, "grads_kernel": 7, "back_kernel": 11,
+}
+ahead_rounds = 1
+flops_per_us = 1153500000
 bf16 = jnp.bfloat16
 f32 = jnp.float32
 
@@ -26,13 +31,12 @@
     return lax.dot_general(left, right, dims, preferred_element_type=f32)
 
 
-def call(kernel, out_shape, operands, scalars, scratch=(), flops=0, trans=0, tokens=()):
-    moved = sum(o.size * o.dtype.itemsize for o in operands)
-    moved += sum(o.size * o.dtype.itemsize for o in out_shape)
+def call(kernel, out_shape, operands, scalars, scratch=(), tokens=(), weight=1):
     specs = [pl.BlockSpec(memory_space=pltpu.SMEM)]
     specs += [pl.BlockSpec(memory_space=pltpu.VMEM)] * len(operands)
     specs += [pl.BlockSpec(memory_space=pl.ANY)] * len(tokens)
     used = 1 + len(operands)
+    weight = kernel_us.get(getattr(kernel, "func", kernel).__name__, weight)
     return pl.pallas_call(
         lambda *refs: kernel(*refs[:used], *refs[used + len(tokens) :]),
         out_shape=tuple(out_shape),
@@ -40,7 +44,7 @@
         out_specs=tuple(pl.BlockSpec(memory_space=pltpu.VMEM) for _ in out_shape),
         scratch_shapes=list(scratch),
         compiler_params=pltpu.CompilerParams(vmem_limit_bytes=vmem_bytes),
-        cost_estimate=pl.CostEstimate(flops=flops, bytes_accessed=moved, transcendentals=trans),
+        cost_estimate=pl.CostEstimate(flops=int(weight * flops_per_us), bytes_accessed=0, transcendentals=0),
     )(scalars, *operands, *tokens)
 
 
@@ -79,23 +83,39 @@
     return jax.tree.unflatten(tree, kept)
 
 
-def scatter_rows(parts, axis, size, tokens=()):
-    held = dict(enumerate(parts))
+def gather_rows(own, axis, size, token=None):
+    held = {0: own}
+    for bit in reversed(range(bits_of(size))):
+        if token is not None:
+            held = {k: after(v, token) if k else v for k, v in held.items()}
+        held.update({k | (1 << bit): exchange(v, axis, size, bit) for k, v in list(held.items())})
+    return [held[k] for k in range(size)]
+
+
+def spread_rows(own, first, axis, size, token):
+    top = bits_of(size) - 1
+    held = {0: own}
+    for bit in reversed(range(top)):
+        held.update({k | (1 << bit): exchange(v, axis, size, bit) for k, v in list(held.items())})
+    held[1 << top] = after(first, token)
+    for bit in reversed(range(top)):
+        more = [k for k in held if k >> top and not k & ((1 << (bit + 1)) - 1)]
+        held.update({k | (1 << bit): exchange(held[k], axis, size, bit) for k in more})
+    return [held[k] for k in range(size)]
+
+
+def scatter_parts(parts, axis, size):
+    held = {k: [v] for k, v in enumerate(parts)}
+    sent = parts[0]
     for bit in range(bits_of(size)):
         step = 1 << bit
-        got = {k: exchange(held[k | step], axis, size, bit) for k in reversed(held) if not k & step}
-        if bit < len(tokens):
-            got = after(got, tokens[bit])
-        held = {k: held[k].astype(f32) + got[k].astype(f32) for k in held if not k & step}
-        held = {k: v.astype(bf16) if k else v for k, v in held.items()}
-    return held[0]
-
-
-def gather_rows(own, axis, size):
-    held = {0: own}
-    for bit in reversed(range(bits_of(size))):
-        held.update({k | (1 << bit): exchange(v, axis, size, bit) for k, v in list(held.items())})
-    return [held[k] for k in range(size)]
+        for k in reversed([k for k in held if k & step]):
+            terms = held.pop(k)
+            if len(terms) > 1:
+                terms = [sum(t.astype(f32) for t in terms).astype(bf16)]
+            sent = terms[0]
+            held[k ^ step].append(exchange(sent, axis, size, bit))
+    return held[0], sent
 
 
 def swap_parts(parts, axis, size):
@@ -106,57 +126,109 @@
     return lax.all_to_all(parts, axis, 0, 0, tiled=True)
 
 
-def summing(streams, axis, size):
-    bits = bits_of(size)
-    orders = []
-    for index in range(len(streams)):
-        order = list(range(bits))
-        if index % 2 == 1 and bits > 1:
-            order[0], order[1] = order[1], order[0]
-        orders.append(order)
-    held, sizes = list(streams), []
-    for step in range(bits):
-        sizes.append([h.shape[0] for h in held])
-        keep, send = [], []
-        for h, order in zip(held, orders):
-            half = h.shape[0] // 2
-            if h.shape[0] % 2:
-                keep.append(h)
-                send.append(h)
-                continue
-            mine = (lax.axis_index(axis) >> order[step]) & 1
-            keep.append(lax.dynamic_slice_in_dim(h, mine * half, half, 0))
-            send.append(lax.dynamic_slice_in_dim(h, (1 - mine) * half, half, 0))
-        got = yield [exchange(v, axis, size, o[step]) for v, o in zip(send, orders)]
-        held = [(k.astype(f32) + g.astype(f32)).astype(bf16) for k, g in zip(keep, got)]
-    for step in reversed(range(bits)):
-        wide = [h.shape[0] < r for h, r in zip(held, sizes[step])]
-        got = yield [exchange(h, axis, size, o[step]) if w else h for h, o, w in zip(held, orders, wide)]
-        for i, order in enumerate(orders):
-            if wide[i]:
-                low = ((lax.axis_index(axis) >> order[step]) & 1) == 0
-                pair = (jnp.where(low, held[i], got[i]), jnp.where(low, got[i], held[i]))
-                held[i] = jnp.concatenate(pair)
-    return held
-
-
-class Flow:
-    def __init__(self, steps):
-        self.steps, self.result = steps, None
-        self.got = next(steps)
-
-    def go(self, *tokens):
-        if self.result is None:
-            try:
-                self.got = self.steps.send(after(self.got, *tokens) if tokens else self.got)
-            except StopIteration as end:
-                self.result = end.value
-        return self.result
-
-    def finish(self):
-        while self.result is None:
-            self.go()
-        return self.result
+def with_bit(index, place, bit):
+    low = index & ((1 << place) - 1)
+    return low | (bit << place) | ((index >> place) << (place + 1))
+
+
+class Sums:
+    def __init__(self, size, kinds, rows, lanes):
+        self.size, self.bits = size, bits_of(size)
+        self.block = (kinds, rows, lanes)
+        first = list(range(self.bits))
+        second = first[:]
+        if self.bits > 1:
+            second[0], second[1] = 1, 0
+        self.orders = [first, second]
+        self.step, self.result = 0, None
+
+    def bit(self, stream, step):
+        return self.orders[stream][step if step < self.bits else 2 * self.bits - 1 - step]
+
+    def left(self, stream, step):
+        order = self.orders[stream]
+        return sorted(order[step + 1 :] if step < self.bits else order[2 * self.bits - step :])
+
+    def groups(self, step):
+        found = {}
+        for stream in range(2):
+            found.setdefault(self.bit(stream, step), []).append(stream)
+        return [(bit, streams, 1 << len(self.left(streams[0], step))) for bit, streams in found.items()]
+
+    def shapes(self, step):
+        return [shape((len(streams) * count,) + self.block, bf16) for _, streams, count in self.groups(step)]
+
+    def at(self, refs, stream, step, index):
+        for ref, (_, streams, count) in zip(refs, self.groups(step)):
+            if stream in streams:
+                return ref.at[streams.index(stream) * count + index]
+
+    def deal(self, read, send_refs, keep_refs, step):
+        me = lax.axis_index("context")
+        for stream in range(2):
+            bit, left = self.bit(stream, step), self.left(stream, step)
+            place = sorted(left + [bit]).index(bit)
+            mine = (me >> bit) & 1
+            for j in range(1 << len(left)):
+                self.at(send_refs, stream, step, j)[...] = read(stream, with_bit(j, place, 1 - mine)).astype(bf16)
+                self.at(keep_refs, stream, step, j)[...] = read(stream, with_bit(j, place, mine)).astype(bf16)
+
+    def start(self, send, keep):
+        self.keep = keep
+        self.got = [exchange(v, "context", self.size, bit) for v, (bit, _, _) in zip(send, self.groups(self.step))]
+
+    def fold(self, scalars, finals=(), extra=(), tokens=()):
+        step, last = self.step, self.step == 2 * self.bits - 1
+        halving = step + 1 < self.bits
+        outs = list(finals) if last else self.shapes(step + 1) * (2 if halving else 1)
+        count, width = len(self.keep), len(outs)
+
+        def kernel(sc, *refs):
+            keep, got = refs[:count], refs[count : 2 * count]
+            pairs, out = refs[2 * count : 2 * count + 2 * len(extra)], refs[2 * count + 2 * len(extra) :]
+            for i in range(len(extra)):
+                out[width + i][...] = pairs[2 * i][...] + pairs[2 * i + 1][...]
+
+            def total(stream, index):
+                return self.at(keep, stream, step, index)[...].astype(f32) + self.at(got, stream, step, index)[...].astype(f32)
+
+            if halving:
+                half = len(outs) // 2
+                self.deal(total, out[:half], out[half:width], step + 1)
+                return
+            me = lax.axis_index("context")
+            for stream in range(2):
+                if step < self.bits:
+                    self.at(out, stream, step + 1, 0)[...] = total(stream, 0).astype(bf16)
+                    continue
+                bit, left = self.bit(stream, step), self.left(stream, step)
+                place = sorted(left + [bit]).index(bit)
+                mine = (me >> bit) & 1
+                for j in range(1 << len(left)):
+                    for refs_in, side in ((keep, mine), (got, 1 - mine)):
+                        value = self.at(refs_in, stream, step, j)[...]
+                        index = with_bit(j, place, side)
+                        if not last:
+                            self.at(out, stream, step + 1, index)[...] = value
+                            continue
+                        kinds, rows, lanes = self.block
+                        span = pl.ds(pl.multiple_of(index * rows, rows), rows)
+                        for kind in range(kinds):
+                            to = out[kind] if width > 1 else out[0].at[kind]
+                            to[span, stream * lanes : (stream + 1) * lanes] = value[kind].astype(f32)
+
+        outs = outs + [shape(a.shape, a.dtype) for a, _ in extra]
+        operands = [*self.keep, *self.got] + [v for pair in extra for v in pair]
+        made = list(call(kernel, outs, operands, scalars, tokens=tokens, weight=8))
+        self.step += 1
+        self.token = made[0]
+        if last:
+            self.result = made[:width]
+        elif halving:
+            self.start(made[: width // 2], made[width // 2 : width])
+        else:
+            self.start(made[:width], made[:width])
+        return made[width:]
 
 
 def chunk(k, rows):
@@ -420,7 +492,7 @@
         else:
             blocks = [got_ref[h * group + e, base + 2 * kind - 1 + which] for e in range(group)]
         parts.append(total_of(blocks).astype(bf16))
-    return jnp.concatenate(parts, axis=0).T
+    return jnp.concatenate(parts, axis=0)
 
 
 def give_rows(value, held_ref, out_refs):
@@ -442,23 +514,26 @@
     even = first_parity(sc)
     for b in range(batches):
         for s in range(2):
-            held_ref[b, s * piece : (s + 1) * piece] = collect(plan, even, got_ref, b, s, 0)
+            held_ref[b, s * piece : (s + 1) * piece] = collect(plan, even, got_ref, b, s, 0).T
         for k, out_ref in enumerate(out_refs):
             out_ref[b] = held_ref[b, chunk(k, rows), :]
 
 
+def copy_kernel(sc, *refs):
+    count = len(refs) // 2
+    for source, target in zip(refs[:count], refs[count:]):
+        target[...] = source[...]
+
+
 def middle_kernel(spread, sc, *refs):
-    o_refs, w_refs, bias_refs, refs = refs[:spread], refs[spread : 2 * spread], refs[2 * spread : 3 * spread], refs[3 * spread :]
+    o_refs, wo, wi, wd, bias_refs = [refs[i * spread : (i + 1) * spread] for i in range(5)]
+    refs = refs[5 * spread :]
     x_ref, g_ref, gain_ref, out_bias_ref, out_ref, grad_ref, n2_ref, dy_ref, sums_ref, du_sum_ref = refs[:10]
-    a_refs, du_refs, do_refs = [refs[10 + i * spread : 10 + (i + 1) * spread] for i in range(3)]
-    local = w_refs[0].shape[0] // 3
+    hidden_refs, do_refs = [refs[10 + i * spread : 10 + (i + 1) * spread] for i in range(2)]
     kind = out_ref.shape
-    wo = [w[0:local] for w in w_refs]
-    wi = [w[local : 2 * local] for w in w_refs]
-    wd = [w[2 * local :] for w in w_refs]
     h1 = flat(x_ref).astype(f32) + out_bias_ref[0:1]
     for k in range(spread):
-        h1 = h1 + mm(flat(o_refs[k]), wo[k])
+        h1 = h1 + mm(flat(o_refs[k]), wo[k][...])
     r2 = lax.rsqrt(jnp.mean(h1 * h1, axis=-1, keepdims=True) + epsilon)
     n2 = (h1 * r2 * gain_ref[1:2]).astype(bf16)
     n2_ref[...] = n2.reshape(kind)
@@ -466,15 +541,15 @@
     out = h1 + out_bias_ref[1:2]
     dn2 = 0.0
     for k in range(spread):
-        u = mm(n2, wi[k], cols_cols) + bias_refs[k][...]
+        u = mm(n2, wi[k][...], cols_cols) + bias_refs[k][...]
         gate = 1.0 / (1.0 + jnp.exp(-u))
         a = (u * gate).astype(bf16)
-        out = out + mm(a, wd[k])
-        ga = mm(g, wd[k], cols_cols)
+        out = out + mm(a, wd[k][...])
+        ga = mm(g, wd[k][...], cols_cols)
         du = (ga * gate * (1.0 + u * (1.0 - gate))).astype(bf16)
-        dn2 = dn2 + mm(du, wi[k])
-        a_refs[k][...] = a
-        du_refs[k][...] = du
+        dn2 = dn2 + mm(du, wi[k][...])
+        hidden_refs[k][0] = a
+        hidden_refs[k][1] = du
         du_sum_ref[pl.ds(k ^ lax.axis_index("fsdp"), 1), :] = jnp.sum(du.astype(f32), axis=0, keepdims=True)
     out_ref[...] = out.astype(bf16).reshape(kind)
     z2 = gain_ref[1:2] * dn2
@@ -487,18 +562,42 @@
     sums_ref[1:2] = jnp.sum(grad, axis=0, keepdims=True)
     sums_ref[2:3] = jnp.sum(g, axis=0, keepdims=True)
     for k in range(spread):
-        do_refs[k][...] = mm(dy, wo[k], cols_cols).astype(bf16).reshape(do_refs[k].shape)
-
-
-def grads_kernel(spread, sc, *refs):
-    o_refs, du_refs, a_refs = [refs[i * spread : (i + 1) * spread] for i in range(3)]
-    dy_ref, n2_ref, g_ref = refs[3 * spread : 3 * spread + 3]
-    out_refs = refs[3 * spread + 3 :]
-    for k in range(spread):
-        local = du_refs[k].shape[1]
-        out_refs[k][0:local] = mm(flat(o_refs[k]), flat(dy_ref), rows_rows).astype(bf16)
-        out_refs[k][local : 2 * local] = mm(du_refs[k][...], flat(n2_ref), rows_rows).astype(bf16)
-        out_refs[k][2 * local :] = mm(a_refs[k][...], flat(g_ref), rows_rows).astype(bf16)
+        do_refs[k][...] = mm(dy, wo[k][...], cols_cols).astype(bf16).reshape(do_refs[k].shape)
+
+
+def cut_rows(value, out_ref, kind):
+    chunks, _, rows, _ = out_ref.shape
+    for c in range(chunks):
+        out_ref[c, kind] = value[c * rows : (c + 1) * rows].astype(bf16)
+
+
+def grads_kernel(spread, sums, sc, *refs):
+    o_refs, hidden_refs, dy_refs, n2_refs, g_refs = [refs[i * spread : (i + 1) * spread] for i in range(5)]
+    *out_refs, cut_ref = refs[5 * spread :]
+    stack = lambda parts: jnp.concatenate([p[...].reshape(-1, p.shape[-1]) for p in parts])
+    target = cut_ref if sums else out_refs[0]
+    cut_rows(mm(stack([h.at[0] for h in hidden_refs]), stack(g_refs), rows_rows), target, 2)
+    cut_rows(mm(stack([h.at[1] for h in hidden_refs]), stack(n2_refs), rows_rows), target, 1)
+    cut_rows(mm(stack(o_refs), stack(dy_refs), rows_rows), target, 0)
+    if sums:
+        deal_cuts(sums, cut_ref, out_refs)
+
+
+def deal_cuts(sums, cut_ref, out_refs):
+    half = len(out_refs) // 2
+    lanes = sums.block[2]
+    read = lambda stream, index: cut_ref[index, :, :, stream * lanes : (stream + 1) * lanes]
+    sums.deal(read, out_refs[:half], out_refs[half:], 0)
+
+
+def close_kernel(terms, sc, *refs):
+    part_refs, (x_ref, grad_ref, gain_ref, out_ref) = refs[:terms], refs[terms:]
+    dn1 = sum(flat(p).astype(f32) for p in part_refs)
+    x = flat(x_ref).astype(f32)
+    r1 = lax.rsqrt(jnp.mean(x * x, axis=-1, keepdims=True) + epsilon)
+    z1 = gain_ref[0:1] * dn1
+    out = flat(grad_ref) + r1 * z1 - x * (r1 * r1 * r1 * jnp.mean(z1 * x, axis=-1, keepdims=True))
+    out_ref[...] = out.astype(bf16).reshape(out_ref.shape)
 
 
 def ahead_kernel(plan, spread, sc, *refs):
@@ -511,21 +610,41 @@
         store_parts(plan, parity, held_ref[b].T, send_ref, b, 0)
 
 
-def back_kernel(plan, sc, got_ref, w_ref, n1_ref, gain_ref, d_ref, bias_ref, gain_sum_ref, *refs):
-    *out_refs, held_ref = refs
-    piece = plan[5]
+def back_kernel(plan, spread, sums, sc, got_ref, w_ref, n1_ref, gain_ref, small_ref, out_small_ref, *refs):
+    size, heads, group, members, dim, piece, batches = plan
+    part_refs, refs = refs[:spread], refs[spread:]
+    *out_refs, held_ref, turned_ref, cut_ref = refs
+    local = heads * dim
     even = first_parity(sc)
+    out_small_ref[...] = small_ref[...]
     total = 0.0
+    bias = []
+    n1 = flat(n1_ref)
+    target = cut_ref if sums else out_refs[0]
     for kind in range(3):
-        for b in range(plan[6]):
+        for b in range(batches):
             for s in range(2):
-                d_ref[kind, b, s * piece : (s + 1) * piece] = collect(plan, even, got_ref, b, s, kind)
-        rows = d_ref[kind].reshape(-1, d_ref.shape[3])
+                at = (2 * b + s) * piece
+                turned_ref[:, at : at + piece] = collect(plan, even, got_ref, b, s, kind)
+        turned_rows = turned_ref[...]
+        rows = turned_rows.T
         if kind != 1:
-            bias_ref[kind // 2 : kind // 2 + 1] = jnp.sum(rows.astype(f32), axis=0, keepdims=True)
+            bias.append(jnp.sum(rows.astype(f32), axis=0, keepdims=True))
         total = total + mm(rows, w_ref[kind])
-    give_rows(total, held_ref, out_refs)
-    gain_sum_ref[...] = jnp.sum(total * flat(n1_ref).astype(f32), axis=0, keepdims=True) / gain_ref[...]
+        cut_rows(mm(turned_rows, n1), target, kind)
+    give_rows(total, held_ref, part_refs)
+    out_small_ref[0:1] = jnp.sum(total * n1.astype(f32), axis=0, keepdims=True) / gain_ref[...]
+    slots = spread // 2
+    for f in range(spread):
+
+        @pl.when(lax.axis_index("fsdp") == f)
+        def _():
+            for i in range(2):
+                first = (f % slots) * 2 * local + i * local
+                out_small_ref[5 + f // slots : 6 + f // slots, first : first + local] = bias[i]
+
+    if sums:
+        deal_cuts(sums, cut_ref, out_refs)
 
 
 def shards(
@@ -580,11 +699,8 @@
         [whole, shape((size, 11, dim, piece), bf16)],
         [*x_parts, qkv_turned, gain_one, qv_bias, factor_row],
         scalars,
-        flops=3 * weight_flops,
-    )
-    packed = jnp.concatenate([out_weight, in_turned, down_weight])
-    w_parts = gather_rows(after(packed, x_parts[-1]), "fsdp", spread)
-    bias_parts = gather_rows(after(in_bias.reshape(1, local), x_parts[-1]), "fsdp", spread)
+        tokens=[main_end, last_end],
+    )
     got = swap_all(send, "context")
     plans = [(pieces, piece, dim, members, 2, 0, 0), (pieces, piece, dim, group, 1, 6, 2)]
     o_send, main_wide, main_lse, last_wide, last_lse = call(
@@ -596,43 +712,42 @@
             pltpu.SMEM((pieces,), jnp.int32), pltpu.VMEM((seq, 128), bf16), pltpu.VMEM((dim, seq), bf16),
             pltpu.VMEM((128, asked[0]), bf16),
         ],
-        flops=3 * sum(asked) * seq * dim,
-        trans=sum(asked) * seq,
-    )
+    )
+    others = [out_weight, in_turned, down_weight, in_bias.reshape(1, local), output_cotangent]
+    others = call(copy_kernel, [shape(v.shape, v.dtype) for v in others], others, scalars, tokens=[send])
+    *others, g_copy = others
+    others = [gather_rows(v, "fsdp", spread, o_send) for v in others]
+    g_first = exchange(g_copy, "fsdp", spread, bits_of(spread) - 1)
     o_parts = call(
-        functools.partial(rows_kernel, plan), thin_parts, [swap_all(o_send, "context")], scalars, thin_held
-    )
-    o_parts = swap_parts(o_parts, "fsdp", spread)
+        functools.partial(rows_kernel, plan), thin_parts, [swap_all(o_send, "context")], scalars, thin_held,
+        tokens=[g_first],
+    )
+    g_parts = spread_rows(g_copy, g_first, "fsdp", spread, o_parts[0])
+    o_local, o_parts = o_parts, swap_parts(o_parts, "fsdp", spread)
+    even_cuts = local % (8 * size) == 0
+    cuts = size if even_cuts else 1
+    cut_shape = shape((cuts, 3, local // cuts, width), bf16)
     own_kind = shape((batches, own, width), bf16)
     layer_output, grad_one, n2, dy, sums, du_sum, *rest = call(
         functools.partial(middle_kernel, spread),
         [own_kind, shape((batches, own, width), f32), own_kind, own_kind, shape((3, width), f32), shape((spread, local), f32)]
-        + [shape((mine, local), bf16)] * (2 * spread)
+        + [shape((2, mine, local), bf16)] * spread
         + thin_parts,
-        [*o_parts, *w_parts, *bias_parts, layer_input, output_cotangent, norm_gains, out_bias],
+        [*o_parts, *others[0], *others[1], *others[2], *others[3], layer_input, output_cotangent, norm_gains, out_bias],
         scalars,
-        flops=12 * mine * width * width,
-        trans=mine * local * spread,
-    )
-    a_parts, du_parts, do_parts = [rest[i * spread : (i + 1) * spread] for i in range(3)]
-    w_grads = call(
-        functools.partial(grads_kernel, spread),
-        [shape((3 * local, width), bf16)] * spread,
-        [*o_parts, *du_parts, *a_parts, dy, n2, output_cotangent],
-        scalars,
-        flops=6 * mine * width * width,
-    )
-    do_parts = swap_parts(do_parts, "fsdp", spread)
+    )
+    hidden_parts, do_parts = rest[:spread], swap_parts(rest[spread:], "fsdp", spread)
     (do_send,) = call(
         functools.partial(ahead_kernel, plan, spread),
         [shape((size, 3, dim, piece), bf16)],
         do_parts,
         scalars,
         thin_held,
-        tokens=w_grads[:1],
     )
     do_got = swap_all(do_send, "context")
-    early = scatter_rows([w[None] for w in w_grads], "fsdp", spread)[0].astype(bf16)
+    hidden_parts = swap_parts(hidden_parts, "fsdp", spread)
+    n2_first = exchange(n2, "fsdp", spread, bits_of(spread) - 1)
+    dy_first = exchange(dy, "fsdp", spread, bits_of(spread) - 1)
     d_send, scale_sum = call(
         functools.partial(attend_back_kernel, plans),
         [shape((size, 11, dim, piece), bf16), shape((dim, 1), f32)],
@@ -645,61 +760,91 @@
             pltpu.VMEM((128, asked[0]), bf16), pltpu.VMEM((asked[0], 128), bf16),
             pltpu.VMEM((seq, 128), f32), pltpu.VMEM((seq, 128), f32),
         ],
-        flops=8 * sum(asked) * seq * dim,
-        trans=sum(asked) * seq,
-    )
-    d_got = swap_all(d_send, "context")
-    half = early.shape[0] // 2
-    early = after(early, d_got)
-    early_flow = Flow(summing([early[:half], early[half:]], "context", size))
-
-    d_rows, qv_sum, gain_one_sum, *part = call(
-        functools.partial(back_kernel, plan),
-        [shape((3, batches, rows, local), bf16), shape((2, local), f32), shape((1, width), f32)] + parts,
-        [d_got, qkv_turned, n1, gain_one],
+    )
+    n2_parts = spread_rows(n2, n2_first, "fsdp", spread, scale_sum)
+    dy_parts = spread_rows(dy, dy_first, "fsdp", spread, scale_sum)
+    new_sums = lambda: Sums(size, 3, local // size, width // 2) if even_cuts else None
+    early, last = new_sums(), new_sums()
+    dealt = early.shapes(0) * 2 if even_cuts else [cut_shape]
+    cut_scratch = [pltpu.VMEM(cut_shape.shape, bf16)]
+    early_made = call(
+        functools.partial(grads_kernel, spread, early),
+        dealt,
+        [*o_local, *hidden_parts, *dy_parts, *n2_parts, *g_parts],
         scalars,
-        held,
-        flops=3 * weight_flops,
-    )
-    flat_rows = lambda v: v.reshape(tokens, -1)
-    qkv = lax.dot_general(
-        d_rows.reshape(3, tokens, local), flat_rows(n1), (((1,), (0,)), ((), ())), preferred_element_type=f32
-    ).astype(bf16).reshape(3 * local, width)
-    half = 3 * local // 2
-    qkv_flow = Flow(summing([qkv[:half], qkv[half:]], "context", size))
-
-    scale_part = scale_sum.reshape(-1) / factor
-    small = jnp.concatenate([gain_one_sum.reshape(-1), sums.reshape(-1), du_sum.reshape(-1), scale_part])
+        cut_scratch,
+        tokens=[scale_sum],
+    )
+    d_got = swap_all(after(d_send, hidden_parts[1:], n2_first), "context")
+    small = [jnp.zeros((1, width), f32), sums, du_sum.reshape(1, width), jnp.zeros((2, width), f32)]
+    small.append(jnp.pad(scale_sum.reshape(1, dim) / factor, ((0, 0), (0, width - dim))))
+    small = jnp.concatenate(small)
+    if even_cuts:
+        early.start(early_made[: len(early_made) // 2], early_made[len(early_made) // 2 :])
+        for _ in range(ahead_rounds):
+            early.fold(scalars)
+    small, *made = call(
+        functools.partial(back_kernel, plan, spread, last),
+        [shape(small.shape, f32)] + parts + dealt,
+        [d_got, qkv_turned, n1, gain_one, small],
+        scalars,
+        held + [pltpu.VMEM((local, tokens), bf16)] + cut_scratch,
+        tokens=[early.token] if even_cuts and ahead_rounds else [],
+    )
+    part, made = made[:spread], made[spread:]
     steps = [("fsdp", spread, bit) for bit in range(bits_of(spread))]
     steps += [("context", size, bit) for bit in range(bits_of(size))]
-    early_flow.go()
-    grad_normed = scatter_rows(part, "fsdp", spread)
-    for index, (axis, count, bit) in enumerate(steps):
-        small = after(small, qkv_flow.got)
-        if index == bits_of(spread):
-            small = jnp.concatenate([qv_sum.reshape(-1), small])
-        got_small = exchange(small, axis, count, bit)
-        qkv_flow.go()
-        early_flow.go()
-        small = small + got_small
-    early = jnp.concatenate(early_flow.finish()).astype(f32)
-    qkv = jnp.concatenate(qkv_flow.finish()).astype(f32).reshape(3, local, width)
-    out_grad = early[:local]
-    feed_grads = [early[local : 2 * local], early[2 * local :]]
-    qv_grad = small[: 2 * local].reshape(2, local)
-    rest = small[2 * local :]
-    gains_grad = rest[: 2 * width].reshape(2, width)
-    out_bias_grad = rest[2 * width : 4 * width].reshape(2, width)
-    rest = rest[4 * width :]
-    in_bias_grad = rest[: spread * local].reshape(spread, local)
-    in_bias_grad = lax.dynamic_index_in_dim(in_bias_grad, lax.axis_index("fsdp"), 0, keepdims=False)
-    scale_grad = rest[spread * local :] * (base_rate / math.sqrt(dim)) * jax.nn.sigmoid(query_scale)
-
-    x_own = layer_input.astype(f32)
-    factor_one = lax.rsqrt(jnp.mean(x_own * x_own, axis=-1, keepdims=True) + epsilon)
-    weighted = norm_gains[0] * grad_normed
-    inner = jnp.mean(weighted * x_own, axis=-1, keepdims=True)
-    input_grad = (grad_one + factor_one * weighted - x_own * factor_one**3 * inner).astype(bf16)
+    dn1_terms, _ = scatter_parts(part, "fsdp", spread)
+
+    def close(*tokens):
+        return call(
+            functools.partial(close_kernel, len(dn1_terms)),
+            [own_kind],
+            [*dn1_terms, layer_input, grad_one, norm_gains],
+            scalars,
+            tokens=tokens,
+        )[0]
+
+    qkv_kind = shape((3, local, width), f32)
+    if even_cuts:
+        last.start(made[: len(made) // 2], made[len(made) // 2 :])
+        order = ["early"] * (2 - ahead_rounds) + ["last", "early"] * (2 * early.bits - 2) + ["last"] * 2
+        order = [early if name == "early" else last for name in order]
+        ends = {early: [shape((local, width), f32)] * 3, last: [qkv_kind]}
+        adds = (1, 2, 4, 6, 8)
+        seen, pending, done = small, None, 0
+        for index, flow in enumerate(order):
+            if pending is None and done < len(steps):
+                pending = exchange(small, *steps[done])
+            extra = [(small, pending)] if pending is not None and index in adds else []
+            finals = ends[flow] if flow.step == 2 * flow.bits - 1 else []
+            added = flow.fold(scalars, finals, extra, [seen])
+            seen = flow.token
+            if extra:
+                small, pending, done = added[0], None, done + 1
+            if index == 4:
+                input_grad = close(seen)
+                seen = input_grad
+        if pending is not None:
+            small, done = small + pending, done + 1
+        steps = steps[done:]
+        for axis, count, bit in steps:
+            small = small + exchange(small, axis, count, bit)
+        (qkv,) = last.result
+        out_grad, *feed_grads = early.result
+    else:
+        for axis, count, bit in steps:
+            small = small + exchange(small, axis, count, bit)
+        input_grad = close()
+        whole_sum = lambda v: lax.psum(v, "context").astype(f32).reshape(3, local, width)
+        qkv = whole_sum(made[0])
+        out_grad, *feed_grads = whole_sum(early_made[0])
+    gains_grad = small[0:2]
+    out_bias_grad = small[2:4]
+    own_slot = lambda v: lax.dynamic_index_in_dim(v.reshape(spread, -1), lax.axis_index("fsdp"), 0, keepdims=False)
+    in_bias_grad = own_slot(small[4])
+    qv_grad = own_slot(small[5:7]).reshape(2, local)
+    scale_grad = small[7, :dim] * (base_rate / math.sqrt(dim)) * jax.nn.sigmoid(query_scale)
     return (
         layer_output,
         input_grad,

time: 412 us -> 372 us (0.903)
  other arithmetic: 54.7 us -> 9.74 us
  Pallas kernels: 65.8 us -> 107 us
  waiting for transfers between devices: 191 us -> 154 us
  matrix products: 4.2 us -> 0 us
    pallas_call x8 -> x22, Pallas kernels: 65.8 us -> 107 us  [call(): pl.pallas_call(lambda *refs: kernel(*refs[:used], *refs[used + len(tokens...]
    ppermute x44 -> x52, waiting for transfers between devices: 124 us -> 97.2 us  [exchange(): return lax.ppermute(values, axis, [(i, i ^ 1 << bit) for i in range(size)])]
    convert_element_type x17 -> x1, other arithmetic: 24 us -> 0.11 us  [scatter_parts(): terms = [sum((t.astype(f32) for t in terms)).astype(bf16)]]
    all_to_all x4, waiting for transfers between devices: 58.8 us -> 42.4 us  [swap_all(): return lax.all_to_all(parts, axis, 0, 0, tiled=True)]
    unnamed x90 -> x138, local copies, waits for them, and re-layouts: 7.99 us -> 19.6 us
    concatenate x12 -> x0, other arithmetic: 7.78 us -> none  [the longest x1 3.41 us: shards(): packed = jnp.concatenate([out_weight, in_turned, down_weight])]
    select_n x12 -> x0, other arithmetic: 6.55 us -> none  [summing(): pair = (jnp.where(low, held[i], got[i]), jnp.where(low, got[i], held[i]))]
    ppermute x6 -> x9, waiting for transfers between devices: 7.64 us -> 13.9 us  [swap_parts(): lax.ppermute(parts[k], axis, [(i, i ^ k) for i in range(size)])]
  transfers between devices with their start and end apart: 54 -> 65, of which waited for: 25 -> 24; matrix products, arithmetic and copies ran while one was open for 18% -> 5% of each run, Pallas kernels for 12% -> 21%
where the time goes in v2:
time: 372 us; the launch traced here: 366 us
  waiting for transfers between devices  154 us (41%)
  Pallas kernels  107 us (29%)
  starting transfers between devices  67.1 us (18%)
  local copies, waits for them, and re-layouts  27.1 us (7%)
  other arithmetic  9.74 us (3%)
    pallas_call x22, Pallas kernels, call(): pl.pallas_call(lambda *refs: kernel(*refs[:used], *refs[used + len(tokens...  107 us
    ppermute x52, waiting for transfers between devices, exchange(): return lax.ppermute(values, axis, [(i, i ^ 1 << bit) for i in range(size)])  97.2 us
    all_to_all x4, waiting for transfers between devices, swap_all(): return lax.all_to_all(parts, axis, 0, 0, tiled=True)  42.4 us
    ppermute x52, starting transfers between devices, exchange(): return lax.ppermute(values, axis, [(i, i ^ 1 << bit) for i in range(size)])  40.3 us
    all_to_all x4, starting transfers between devices, swap_all(): return lax.all_to_all(parts, axis, 0, 0, tiled=True)  20.8 us
    unnamed x138, local copies, waits for them, and re-layouts  19.6 us
    ppermute x9, waiting for transfers between devices, swap_parts(): lax.ppermute(parts[k], axis, [(i, i ^ k) for i in range(size)])  13.9 us
  transfers between devices with their start and end apart: 65, of which 24 were waited for; matrix products, arithmetic and copies ran while one was open for 5% of the time, Pallas kernels for 21%

profile of v2, /device:TPU:0, one launch (start us, length us, event | category | flops | bytes accessed | tf_op | source)
XLA Modules:
  0.0 365.8 jit_solution(800205991586521724)
XLA Ops:
  0.6 3.0 collective-permute-start.1
  4.6 7.0 %reduce-window.6 = s32[3,16,128]{2,1,0:T(8,128)S(1)} reduce-window(s32[3,16,128]{2,1,0:T(8,128)S(1)} %bitcast.27, s32[]{:T(128)} %constant.70.clone.1), window={size=1x1x128 pad=0_0x0_0x0_127}, to_apply=%region_0.1 | reduce-window | flops 780288 | bytes 49156 | tf_op jit(solution)/shard_map/reduce-window
  13.6 1.5 collective-permute-done.1.refs_3_
  18.5 7.6 %shard_map.212 = (bf16[3,256,1280]{2,1,0:T(8,128)(2,1)}, bf16[8,11,80,128]{3,2,1,0:T(8,128)(2,1)}) custom-call(s32[2,8]{1,0:T(2,128)} %bitcast.30, bf16[3,64,1280]{2,1,0:T(8,128)(2,1)} %refs_4_.1, bf16[3,64,1280]{2,1,0:T(8,128)(2,1)} %copy-done.34, bf16[3,64,1280]{2,1,0:T(8,128)(2,1)} %copy-done.33, bf16[3,64,1280]{2,1,0:T(8,128)(2,1)} %copy-done.38, ...), custom_call_target="tpu_custom_call" | custom-call | flops 8074500096 | tf_op jit(solution)/shard_map/pallas_call | solution.py:40
  26.1 6.5 %all-to-all-start = ((bf16[8,11,80,128]{3,2,1,0:T(8,128)(2,1)}), bf16[8,11,80,128]{3,2,1,0:T(8,128)(2,1)S(1)}, u32[]{:S(2)}, u32[]{:S(2)}) async-start(bf16[8,11,80,128]{3,2,1,0:T(8,128)(2,1)} %get-tuple-element.85.refs_6_), calls=%async_computation | async-start | bytes 3604480 | tf_op jit(solution)/shard_map/all_to_all | solution.py:126
  33.1 3.5 shard_map.214
  36.6 1.5 collective-permute-start.17
  38.9 1.5 collective-permute-start.14
  40.4 1.5 collective-permute-start.8
  42.5 32.7 %all-to-all-done.refs_1_ = bf16[8,11,80,128]{3,2,1,0:T(8,128)(2,1)S(1)} async-done(((bf16[8,11,80,128]{3,2,1,0:T(8,128)(2,1)}), bf16[8,11,80,128]{3,2,1,0:T(8,128)(2,1)S(1)}, u32[]{:S(2)}, u32[]{:S(2)}) %all-to-all-start) | async-done | bytes 1802272 | tf_op jit(solution)/shard_map/all_to_all | solution.py:126
  76.3 11.1 %shard_map.213 = (bf16[8,3,80,128]{3,2,1,0:T(8,128)(2,1)}, f32[80,2048]{1,0:T(8,128)}, f32[1,2048]{1,0:T(1,128)}, f32[80,1024]{1,0:T(8,128)}, f32[1,1024]{1,0:T(1,128)}) custom-call(s32[2,8]{1,0:T(2,128)} %bitcast.32, bf16[8,11,80,128]{3,2,1,0:T(8,128)(2,1)} %copy-done.1, s32[1,2048]{1,0:T(1,128)} %constant_dynamic-slice_fusion.refs_9_.refs_2_.refs_4_, ...), custom_call_target="tpu_custom_call" | custom-call | flops 12688499712 | tf_op jit(solution)/shard_map/pallas_call | solution.py:40
  87.4 3.9 %all-to-all-start.1 = ((bf16[8,3,80,128]{3,2,1,0:T(8,128)(2,1)}), bf16[8,3,80,128]{3,2,1,0:T(8,128)(2,1)S(1)}, u32[]{:S(2)}, u32[]{:S(2)}) async-start(bf16[8,3,80,128]{3,2,1,0:T(8,128)(2,1)} %get-tuple-element.86.refs_1_), calls=%async_computation.1 | async-start | bytes 983040 | tf_op jit(solution)/shard_map/all_to_all | solution.py:126
  92.0 2.6 collective-permute-done.8.refs_0_
  94.6 10.1 %collective-permute-done.3.refs_2_.refs_0_ = bf16[3,64,1280]{2,1,0:T(8,128)(2,1)} collective-permute-done((bf16[3,64,1280]{2,1,0:T(8,128)(2,1)}, bf16[3,64,1280]{2,1,0:T(8,128)(2,1)}, u32[]{:S(2)}, u32[]{:S(2)}) %collective-permute-start.3) | collective-permute-done | bytes 491552 | tf_op jit(solution)/shard_map/ppermute | solution.py:64
  106.3 2.1 shard_map.215
  110.3 5.3 %collective-permute-done.5.refs_3_ = bf16[3,64,320]{2,1,0:T(8,128)(2,1)S(1)} collective-permute-done((bf16[3,64,320]{2,1,0:T(8,128)(2,1)}, bf16[3,64,320]{2,1,0:T(8,128)(2,1)S(1)}, u32[]{:S(2)}, u32[]{:S(2)}) %collective-permute-start.5) | collective-permute-done | bytes 122912 | tf_op jit(solution)/shard_map/ppermute | solution.py:122
  115.6 1.7 collective-permute-done.6.refs_4_
  118.0 13.8 %shard_map.220 = (bf16[3,64,1280]{2,1,0:T(8,128)(2,1)}, f32[3,64,1280]{2,1,0:T(8,128)}, bf16[3,64,1280]{2,1,0:T(8,128)(2,1)}, bf16[3,64,1280]{2,1,0:T(8,128)(2,1...) custom-call(s32[2,8]{1,0:T(2,128)} %bitcast.34, ...), custom_call_target="tpu_custom_call" | custom-call | flops 16149000192 | tf_op jit(solution)/shard_map/pallas_call | solution.py:40
  133.8 5.5 %collective-permute-done.20.refs_3_ = bf16[3,64,320]{2,1,0:T(8,128)(2,1)S(1)} collective-permute-done((bf16[3,64,320]{2,1,0:T(8,128)(2,1)}, bf16[3,64,320]{2,1,0:T(8,128)(2,1)S(1)}, u32[]{:S(2)}, u32[]{:S(2)}) %collective-permute-start.20) | collective-permute-done | bytes 122912 | tf_op jit(solution)/shard_map/ppermute | solution.py:122
  139.3 1.4 collective-permute-done.21.refs_4_
  141.4 2.3 shard_map.221
  143.7 6.5 %all-to-all-start.2 = ((bf16[8,3,80,128]{3,2,1,0:T(8,128)(2,1)}), bf16[8,3,80,128]{3,2,1,0:T(8,128)(2,1)S(1)}, u32[]{:S(2)}, u32[]{:S(2)}) async-start(bf16[8,3,80,128]{3,2,1,0:T(8,128)(2,1)} %shard_map.221), calls=%async_computation.2 | async-start | bytes 983040 | tf_op jit(solution)/shard_map/all_to_all | solution.py:126
  152.0 1.5 collective-permute-start.23
  153.6 1.5 collective-permute-start.27
  155.0 9.7 %all-to-all-done.2.refs_2_ = bf16[8,3,80,128]{3,2,1,0:T(8,128)(2,1)S(1)} async-done(((bf16[8,3,80,128]{3,2,1,0:T(8,128)(2,1)}), bf16[8,3,80,128]{3,2,1,0:T(8,128)(2,1)S(1)}, u32[]{:S(2)}, u32[]{:S(2)}) %all-to-all-start.2) | async-done | bytes 491552 | tf_op jit(solution)/shard_map/all_to_all | solution.py:126
  165.6 14.7 %shard_map.222 = (bf16[8,11,80,128]{3,2,1,0:T(8,128)(2,1)}, f32[80,1]{1,0:T(8,128)}) custom-call(s32[2,8]{1,0:T(2,128)} %bitcast.36, bf16[8,11,80,128]{3,2,1,0:T(8,128)(2,1)} %copy-done.1, bf16[8,3,80,128]{3,2,1,0:T(8,128)(2,1)} %copy-done.8, f32[80,1]{1,0:T(8,128)} %copy.35.refs_3_, s32[1,2048]{1,0:T(1,128)} %constant_dynamic-slice_fusion.refs_9_.refs_2_.refs_4_, ...), custom_call_target="tpu_custom_call" | custom-call | flops 17302499328 | tf_op jit(solution)/shard_map/pallas_call | solution.py:40
  181.3 4.0 %all-to-all-start.3 = ((bf16[8,11,80,128]{3,2,1,0:T(8,128)(2,1)}), bf16[8,11,80,128]{3,2,1,0:T(8,128)(2,1)S(1)}, u32[]{:S(2)}, u32[]{:S(2)}) async-start(bf16[8,11,80,128]{3,2,1,0:T(8,128)(2,1)} %shard_map.223), calls=%async_computation.3 | async-start | bytes 3604480 | tf_op jit(solution)/shard_map/all_to_all | solution.py:126
  185.9 2.3 collective-permute-done.27.refs_0_
  191.9 6.9 %shard_map.227 = (bf16[4,3,40,640]{3,2,1,0:T(8,128)(2,1)}, bf16[4,3,40,640]{3,2,1,0:T(8,128)(2,1)}, bf16[4,3,40,640]{3,2,1,0:T(8,128)(2,1)}, bf16[4,3,40,640]{3,2,1,0:T(8,128)(2,1)}) custom-call(s32[2,8]{1,0:T(2,128)} %bitcast.37, bf16[3,64,320]{2,1,0:T(8,128)(2,1)} %get-tuple-element.88.refs_1_, bf16[3,64,320]{2,1,0:T(8,128)(2,1)} %get-tuple-element.89.refs_2_, ...), custom_call_target="tpu_custom_call" | custom-call | flops 8074500096 | tf_op jit(solution)/shard_map/pallas_call | solution.py:40
  198.8 1.8 collective-permute-start.33
  200.6 1.5 collective-permute-start.34
  203.0 19.7 %collective-permute-done.33.refs_3_ = bf16[4,3,40,640]{3,2,1,0:T(8,128)(2,1)S(1)} collective-permute-done((bf16[4,3,40,640]{3,2,1,0:T(8,128)(2,1)}, bf16[4,3,40,640]{3,2,1,0:T(8,128)(2,1)S(1)}, u32[]{:S(2)}, u32[]{:S(2)}) %collective-permute-start.33) | collective-permute-done | bytes 614432 | tf_op jit(solution)/shard_map/ppermute | solution.py:64
  222.7 7.6 %collective-permute-done.34.refs_4_ = bf16[4,3,40,640]{3,2,1,0:T(8,128)(2,1)S(1)} collective-permute-done((bf16[4,3,40,640]{3,2,1,0:T(8,128)(2,1)}, bf16[4,3,40,640]{3,2,1,0:T(8,128)(2,1)S(1)}, u32[]{:S(2)}, u32[]{:S(2)}) %collective-permute-start.34) | collective-permute-done | bytes 614432 | tf_op jit(solution)/shard_map/ppermute | solution.py:64
  231.1 2.8 shard_map.228
  237.3 10.8 %shard_map.229 = (f32[8,1280]{1,0:T(8,128)}, bf16[3,64,1280]{2,1,0:T(8,128)(2,1)}, bf16[3,64,1280]{2,1,0:T(8,128)(2,1)}, bf16[3,64,1280]{2,1,0:T(8,128)(2,1)}, b...) custom-call(s32[2,8]{1,0:T(2,128)} %bitcast.39, ...), custom_call_target="tpu_custom_call" | custom-call | flops 12688499712 | tf_op jit(solution)/shard_map/pallas_call | solution.py:40
  250.8 2.3 shard_map.230
  253.1 2.2 collective-permute-start.40
  255.9 6.5 %collective-permute-done.41.refs_3_ = bf16[4,3,40,640]{3,2,1,0:T(8,128)(2,1)S(1)} collective-permute-done((bf16[4,3,40,640]{3,2,1,0:T(8,128)(2,1)}, bf16[4,3,40,640]{3,2,1,0:T(8,128)(2,1)S(1)}, u32[]{:S(2)}, u32[]{:S(2)}) %collective-permute-start.41) | collective-permute-done | bytes 614432 | tf_op jit(solution)/shard_map/ppermute | solution.py:64
  262.4 7.6 %collective-permute-done.42.refs_4_ = bf16[4,3,40,640]{3,2,1,0:T(8,128)(2,1)S(1)} collective-permute-done((bf16[4,3,40,640]{3,2,1,0:T(8,128)(2,1)}, bf16[4,3,40,640]{3,2,1,0:T(8,128)(2,1)S(1)}, u32[]{:S(2)}, u32[]{:S(2)}) %collective-permute-start.42) | collective-permute-done | bytes 614432 | tf_op jit(solution)/shard_map/ppermute | solution.py:64
  270.9 2.9 shard_map.231
  274.5 1.5 collective-permute-start.37
  276.8 1.7 collective-permute-done.44.refs_4_
  279.1 1.9 shard_map.232
  280.9 1.5 collective-permute-start.45
  282.5 3.1 collective-permute-done.47.refs_3_
  285.6 1.7 collective-permute-start.46
  288.0 2.2 shard_map.233
  290.4 12.3 %collective-permute-done.45.refs_2_ = bf16[2,3,40,640]{3,2,1,0:T(8,128)(2,1)S(1)} collective-permute-done((bf16[2,3,40,640]{3,2,1,0:T(8,128)(2,1)}, bf16[2,3,40,640]{3,2,1,0:T(8,128)(2,1)S(1)}, u32[]{:S(2)}, u32[]{:S(2)}) %collective-permute-start.45) | collective-permute-done | bytes 307232 | tf_op jit(solution)/shard_map/ppermute | solution.py:64
  303.5 2.0 shard_map.234
  306.6 2.0 collective-permute-start.53
  309.4 3.1 shard_map.235.refs_3_
  313.2 1.9 shard_map.236.refs_7_.refs_1_
  316.8 2.4 shard_map.237
  320.5 1.9 collective-permute-start.57
  322.9 3.5 collective-permute-done.50.refs_2_
  327.2 1.9 shard_map.238
  330.1 7.0 %collective-permute-done.58.refs_6_ = f32[8,1280]{1,0:T(8,128)S(1)} collective-permute-done((f32[8,1280]{1,0:T(8,128)}, f32[8,1280]{1,0:T(8,128)S(1)}, u32[]{:S(2)}, u32[]{:S(2)}) %collective-permute-start.58) | collective-permute-done | bytes 40992 | tf_op jit(solution)/shard_map/ppermute | solution.py:64
  337.1 2.1 collective-permute-done.57.refs_4_
  340.1 4.2 %shard_map.239 = (f32[320,1280]{1,0:T(8,128)}, f32[320,1280]{1,0:T(8,128)}, f32[320,1280]{1,0:T(8,128)}, f32[8,1280]{1,0:T(8,128)}) custom-call(s32[2,8]{1,0:T(2,128)} %bitcast.49, bf16[4,3,40,640]{3,2,1,0:T(8,128)(2,1)} %get-tuple-element.148.refs_3_.refs_1_, bf16[4,3,40,640]{3,2,1,0:T(8,128)(2,1)} %get-tuple-element.151.refs_2_, ...), custom_call_target="tpu_custom_call" | custom-call | flops 9228000256 | tf_op jit(solution)/shard_map/pallas_call | solution.py:40
  345.1 2.4 shard_map.240
  348.5 2.0 collective-permute-start.60
  353.1 5.9 %collective-permute-done.59.refs_3_ = bf16[4,3,40,640]{3,2,1,0:T(8,128)(2,1)S(1)} collective-permute-done((bf16[4,3,40,640]{3,2,1,0:T(8,128)(2,1)}, bf16[4,3,40,640]{3,2,1,0:T(8,128)(2,1)S(1)}, u32[]{:S(2)}, u32[]{:S(2)}) %collective-permute-start.59) | collective-permute-done | bytes 614432 | tf_op jit(solution)/shard_map/ppermute | solution.py:64
  359.0 1.5 collective-permute-done.60.refs_4_
  361.3 4.2 %shard_map.241 = f32[3,320,1280]{2,1,0:T(8,128)} custom-call(s32[2,8]{1,0:T(2,128)} %bitcast.51, bf16[4,3,40,640]{3,2,1,0:T(8,128)(2,1)} %get-tuple-element.154.refs_1_.refs_5_, bf16[4,3,40,640]{3,2,1,0:T(8,128)(2,1)} %get-tuple-element.155.refs_2_, bf16[4,3,40,640]{3,2,1,0:T(8,128)(2,1)} %copy-done.26, bf16[4,3,40,640]{3,2,1,0:T(8,128)(2,1)} %copy-done.27, ...), custom_call_target="tpu_custom_call" | custom-call | flops 9228000256 | tf_op jit(solution)/shard_map/pallas_call | solution.py:40
  (269 shorter events, 51.6 us)
Async XLA Ops:
  0.6 14.4 %collective-permute-start.1 = (bf16[3,64,1280]{2,1,0:T(8,128)(2,1)}, bf16[3,64,1280]{2,1,0:T(8,128)(2,1)S(1)}, u32[]{:S(2)}, u32[]{:S(2)}) collective-permute-start(bf16[3,64,1280]{2,1,0:T(8,128)(2,1)} %refs_4_.1), channel_id=1, source_target_pairs={{0,2},{1,3},{2,0},{3,1},{4,6},{5,7},{6,4},{7,5},{8,10},{9,11},{10,... | collective-permute-start | bytes 1474568 | tf_op jit(solution)/shard_map/ppermute | solution.py:64
  3.6 14.0 %collective-permute-start = (bf16[3,64,1280]{2,1,0:T(8,128)(2,1)}, bf16[3,64,1280]{2,1,0:T(8,128)(2,1)S(1)}, u32[]{:S(2)}, u32[]{:S(2)}) collective-permute-start(bf16[3,64,1280]{2,1,0:T(8,128)(2,1)} %refs_4_.1), channel_id=1, source_target_pairs={{0,1},{1,0},{2,3},{3,2},{4,5},{5,4},{6,7},{7,6},{8,9},{9,8},{10,11... | collective-permute-start | bytes 1474568 | tf_op jit(solution)/shard_map/ppermute | solution.py:64
  15.1 2.5 collective-permute-start.2
  26.1 49.0 %all-to-all-start = ((bf16[8,11,80,128]{3,2,1,0:T(8,128)(2,1)}), bf16[8,11,80,128]{3,2,1,0:T(8,128)(2,1)S(1)}, u32[]{:S(2)}, u32[]{:S(2)}) async-start(bf16[8,11,80,128]{3,2,1,0:T(8,128)(2,1)} %get-tuple-element.85.refs_6_), calls=%async_computation | async-start | bytes 3604480 | tf_op jit(solution)/shard_map/all_to_all | solution.py:126
  36.6 3.8 %collective-permute-start.17 = (f32[1,320]{1,0:T(1,128)}, f32[1,320]{1,0:T(1,128)S(1)}, u32[]{:S(2)}, u32[]{:S(2)}) collective-permute-start(f32[1,320]{1,0:T(1,128)} %get-tuple-element.95.refs_17_), channel_id=1, source_target_pairs={{0,2},{1,3},{2,0},{3,1},{4,6},{5,7},{6,4},{7,5},{8,10},{9,11},{10,... | collective-permute-start | bytes 3848 | tf_op jit(solution)/shard_map/ppermute | solution.py:64
  38.1 3.8 %collective-permute-start.16 = (f32[1,320]{1,0:T(1,128)}, f32[1,320]{1,0:T(1,128)S(1)}, u32[]{:S(2)}, u32[]{:S(2)}) collective-permute-start(f32[1,320]{1,0:T(1,128)} %get-tuple-element.95.refs_17_), channel_id=1, source_target_pairs={{0,1},{1,0},{2,3},{3,2},{4,5},{5,4},{6,7},{7,6},{8,9},{9,8},{10,11... | collective-permute-start | bytes 3848 | tf_op jit(solution)/shard_map/ppermute | solution.py:64
  38.1 53.2 %collective-permute-start.11 = (bf16[320,1280]{1,0:T(8,128)(2,1)}, bf16[320,1280]{1,0:T(8,128)(2,1)}, u32[]{:S(2)}, u32[]{:S(2)}) collective-permute-start(bf16[320,1280]{1,0:T(8,128)(2,1)} %get-tuple-element.93.refs_9_), channel_id=1, source_target_pairs={{0,2},{1,3},{2,0},{3,1},{4,6},{5,7},{6,4},{7,5},{8,10},{9,11},{10,... | collective-permute-start | bytes 2457608 | tf_op jit(solution)/shard_map/ppermute | solution.py:64
  38.7 66.1 %collective-permute-start.10 = (bf16[320,1280]{1,0:T(8,128)(2,1)}, bf16[320,1280]{1,0:T(8,128)(2,1)}, u32[]{:S(2)}, u32[]{:S(2)}) collective-permute-start(bf16[320,1280]{1,0:T(8,128)(2,1)} %get-tuple-element.93.refs_9_), channel_id=1, source_target_pairs={{0,1},{1,0},{2,3},{3,2},{4,5},{5,4},{6,7},{7,6},{8,9},{9,8},{10,11... | collective-permute-start | bytes 2457608 | tf_op jit(solution)/shard_map/ppermute | solution.py:64
  38.9 52.6 %collective-permute-start.14 = (bf16[320,1280]{1,0:T(8,128)(2,1)}, bf16[320,1280]{1,0:T(8,128)(2,1)S(1)}, u32[]{:S(2)}, u32[]{:S(2)}) collective-permute-start(bf16[320,1280]{1,0:T(8,128)(2,1)} %get-tuple-element.94.refs_13_), channel_id=1, source_target_pairs={{0,2},{1,3},{2,0},{3,1},{4,6},{5,7},{6,4},{7,5},{8,10},{9,11},{10,... | collective-permute-start | bytes 2457608 | tf_op jit(solution)/shard_map/ppermute | solution.py:64
  40.4 54.2 %collective-permute-start.8 = (bf16[320,1280]{1,0:T(8,128)(2,1)}, bf16[320,1280]{1,0:T(8,128)(2,1)}, u32[]{:S(2)}, u32[]{:S(2)}) collective-permute-start(bf16[320,1280]{1,0:T(8,128)(2,1)} %get-tuple-element.92.refs_5_), channel_id=1, source_target_pairs={{0,2},{1,3},{2,0},{3,1},{4,6},{5,7},{6,4},{7,5},{8,10},{9,11},{10,... | collective-permute-start | bytes 2457608 | tf_op jit(solution)/shard_map/ppermute | solution.py:64
  41.9 62.8 %collective-permute-start.3 = (bf16[3,64,1280]{2,1,0:T(8,128)(2,1)}, bf16[3,64,1280]{2,1,0:T(8,128)(2,1)}, u32[]{:S(2)}, u32[]{:S(2)}) collective-permute-start(bf16[3,64,1280]{2,1,0:T(8,128)(2,1)} %get-tuple-element.87.refs_17_), channel_id=1, source_target_pairs={{0,2},{1,3},{2,0},{3,1},{4,6},{5,7},{6,4},{7,5},{8,10},{9,11},{10,... | collective-permute-start | bytes 1474568 | tf_op jit(solution)/shard_map/ppermute | solution.py:64
  87.4 18.0 %all-to-all-start.1 = ((bf16[8,3,80,128]{3,2,1,0:T(8,128)(2,1)}), bf16[8,3,80,128]{3,2,1,0:T(8,128)(2,1)S(1)}, u32[]{:S(2)}, u32[]{:S(2)}) async-start(bf16[8,3,80,128]{3,2,1,0:T(8,128)(2,1)} %get-tuple-element.86.refs_1_), calls=%async_computation.1 | async-start | bytes 983040 | tf_op jit(solution)/shard_map/all_to_all | solution.py:126
  91.4 13.9 %collective-permute-start.13 = (bf16[320,1280]{1,0:T(8,128)(2,1)}, bf16[320,1280]{1,0:T(8,128)(2,1)S(1)}, u32[]{:S(2)}, u32[]{:S(2)}) collective-permute-start(bf16[320,1280]{1,0:T(8,128)(2,1)} %get-tuple-element.94.refs_13_), channel_id=1, source_target_pairs={{0,1},{1,0},{2,3},{3,2},{4,5},{5,4},{6,7},{7,6},{8,9},{9,8},{10,11... | collective-permute-start | bytes 2457608 | tf_op jit(solution)/shard_map/ppermute | solution.py:64
  91.5 16.9 %collective-permute-start.7 = (bf16[320,1280]{1,0:T(8,128)(2,1)S(1)}, bf16[320,1280]{1,0:T(8,128)(2,1)}, u32[]{:S(2)}, u32[]{:S(2)}) collective-permute-start(bf16[320,1280]{1,0:T(8,128)(2,1)S(1)} %copy-done.18), channel_id=1, source_target_pairs={{0,1},{1,0},{2,3},{3,2},{4,5},{5,4},{6,7},{7,6},{8,9},{9,8},{10,11... | collective-permute-start | bytes 2457608 | tf_op jit(solution)/shard_map/ppermute | solution.py:64
  94.6 15.2 %collective-permute-start.12 = (bf16[320,1280]{1,0:T(8,128)(2,1)}, bf16[320,1280]{1,0:T(8,128)(2,1)}, u32[]{:S(2)}, u32[]{:S(2)}) collective-permute-start(bf16[320,1280]{1,0:T(8,128)(2,1)} %shard_map.217.refs_11_), channel_id=1, source_target_pairs={{0,1},{1,0},{2,3},{3,2},{4,5},{5,4},{6,7},{7,6},{8,9},{9,8},{10,11... | collective-permute-start | bytes 2457608 | tf_op jit(solution)/shard_map/ppermute | solution.py:64
  104.7 5.5 %collective-permute-start.15 = (bf16[320,1280]{1,0:T(8,128)(2,1)S(1)}, bf16[320,1280]{1,0:T(8,128)(2,1)}, u32[]{:S(2)}, u32[]{:S(2)}) collective-permute-start(bf16[320,1280]{1,0:T(8,128)(2,1)S(1)} %copy-done.4), channel_id=1, source_target_pairs={{0,1},{1,0},{2,3},{3,2},{4,5},{5,4},{6,7},{7,6},{8,9},{9,8},{10,11... | collective-permute-start | bytes 2457608 | tf_op jit(solution)/shard_map/ppermute | solution.py:64
  104.8 5.5 %collective-permute-start.9 = (bf16[320,1280]{1,0:T(8,128)(2,1)}, bf16[320,1280]{1,0:T(8,128)(2,1)}, u32[]{:S(2)}, u32[]{:S(2)}) collective-permute-start(bf16[320,1280]{1,0:T(8,128)(2,1)} %shard_map.216.refs_7_), channel_id=1, source_target_pairs={{0,1},{1,0},{2,3},{3,2},{4,5},{5,4},{6,7},{7,6},{8,9},{9,8},{10,11... | collective-permute-start | bytes 2457608 | tf_op jit(solution)/shard_map/ppermute | solution.py:64
  105.3 3.4 collective-permute-start.18
  108.7 6.9 %collective-permute-start.5 = (bf16[3,64,320]{2,1,0:T(8,128)(2,1)}, bf16[3,64,320]{2,1,0:T(8,128)(2,1)S(1)}, u32[]{:S(2)}, u32[]{:S(2)}) collective-permute-start(bf16[3,64,320]{2,1,0:T(8,128)(2,1)} %get-tuple-element.90.refs_3_), channel_id=1, source_target_pairs={{0,2},{1,3},{2,0},{3,1},{4,6},{5,7},{6,4},{7,5},{8,10},{9,11},{10,... | collective-permute-start | bytes 368648 | tf_op jit(solution)/shard_map/ppermute | solution.py:122
  109.8 7.6 %collective-permute-start.6 = (bf16[3,64,320]{2,1,0:T(8,128)(2,1)}, bf16[3,64,320]{2,1,0:T(8,128)(2,1)S(1)}, u32[]{:S(2)}, u32[]{:S(2)}) collective-permute-start(bf16[3,64,320]{2,1,0:T(8,128)(2,1)} %get-tuple-element.91.refs_4_), channel_id=1, source_target_pairs={{0,3},{1,2},{2,1},{3,0},{4,7},{5,6},{6,5},{7,4},{8,11},{9,10},{10,... | collective-permute-start | bytes 368648 | tf_op jit(solution)/shard_map/ppermute | solution.py:122
  131.8 2.0 collective-permute-start.19
  132.4 6.9 %collective-permute-start.20 = (bf16[3,64,320]{2,1,0:T(8,128)(2,1)}, bf16[3,64,320]{2,1,0:T(8,128)(2,1)S(1)}, u32[]{:S(2)}, u32[]{:S(2)}) collective-permute-start(bf16[3,64,320]{2,1,0:T(8,128)(2,1)} %get-tuple-element.99), channel_id=1, source_target_pairs={{0,2},{1,3},{2,0},{3,1},{4,6},{5,7},{6,4},{7,5},{8,10},{9,11},{10,... | collective-permute-start | bytes 368648 | tf_op jit(solution)/shard_map/ppermute | solution.py:122
  133.7 7.0 %collective-permute-start.21 = (bf16[3,64,320]{2,1,0:T(8,128)(2,1)}, bf16[3,64,320]{2,1,0:T(8,128)(2,1)S(1)}, u32[]{:S(2)}, u32[]{:S(2)}) collective-permute-start(bf16[3,64,320]{2,1,0:T(8,128)(2,1)} %get-tuple-element.100), channel_id=1, source_target_pairs={{0,3},{1,2},{2,1},{3,0},{4,7},{5,6},{6,5},{7,4},{8,11},{9,10},{10,... | collective-permute-start | bytes 368648 | tf_op jit(solution)/shard_map/ppermute | solution.py:122
  143.7 21.1 %all-to-all-start.2 = ((bf16[8,3,80,128]{3,2,1,0:T(8,128)(2,1)}), bf16[8,3,80,128]{3,2,1,0:T(8,128)(2,1)S(1)}, u32[]{:S(2)}, u32[]{:S(2)}) async-start(bf16[8,3,80,128]{3,2,1,0:T(8,128)(2,1)} %shard_map.221), calls=%async_computation.2 | async-start | bytes 983040 | tf_op jit(solution)/shard_map/all_to_all | solution.py:126
  150.2 3.4 collective-permute-start.22
  151.4 37.7 %collective-permute-start.31 = (bf16[3,64,1280]{2,1,0:T(8,128)(2,1)}, bf16[3,64,1280]{2,1,0:T(8,128)(2,1)}, u32[]{:S(2)}, u32[]{:S(2)}) collective-permute-start(bf16[3,64,1280]{2,1,0:T(8,128)(2,1)} %get-tuple-element.87.refs_17_), channel_id=1, source_target_pairs={{0,1},{1,0},{2,3},{3,2},{4,5},{5,4},{6,7},{7,6},{8,9},{9,8},{10,11... | collective-permute-start | bytes 1474568 | tf_op jit(solution)/shard_map/ppermute | solution.py:64
  151.5 28.8 %collective-permute-start.25 = (bf16[3,64,1280]{2,1,0:T(8,128)(2,1)S(1)}, bf16[3,64,1280]{2,1,0:T(8,128)(2,1)S(1)}, u32[]{:S(2)}, u32[]{:S(2)}) collective-permute-start(bf16[3,64,1280]{2,1,0:T(8,128)(2,1)S(1)} %copy-done.28), channel_id=1, source_target_pairs={{0,2},{1,3},{2,0},{3,1},{4,6},{5,7},{6,4},{7,5},{8,10},{9,11},{10,... | collective-permute-start | bytes 1474568 | tf_op jit(solution)/shard_map/ppermute | solution.py:64
  152.0 28.2 %collective-permute-start.23 = (bf16[2,192,320]{2,1,0:T(8,128)(2,1)S(1)}, bf16[2,192,320]{2,1,0:T(8,128)(2,1)S(1)}, u32[]{:S(2)}, u32[]{:S(2)}) collective-permute-start(bf16[2,192,320]{2,1,0:T(8,128)(2,1)S(1)} %copy-done.52), channel_id=1, source_target_pairs={{0,2},{1,3},{2,0},{3,1},{4,6},{5,7},{6,4},{7,5},{8,10},{9,11},{10,... | collective-permute-start | bytes 737288 | tf_op jit(solution)/shard_map/ppermute | solution.py:122
  153.5 26.7 %collective-permute-start.24 = (bf16[2,192,320]{2,1,0:T(8,128)(2,1)S(1)}, bf16[2,192,320]{2,1,0:T(8,128)(2,1)S(1)}, u32[]{:S(2)}, u32[]{:S(2)}) collective-permute-start(bf16[2,192,320]{2,1,0:T(8,128)(2,1)S(1)} %copy-done.51), channel_id=1, source_target_pairs={{0,3},{1,2},{2,1},{3,0},{4,7},{5,6},{6,5},{7,4},{8,11},{9,10},{10,... | collective-permute-start | bytes 737288 | tf_op jit(solution)/shard_map/ppermute | solution.py:122
  153.6 34.7 %collective-permute-start.27 = (bf16[3,64,1280]{2,1,0:T(8,128)(2,1)}, bf16[3,64,1280]{2,1,0:T(8,128)(2,1)S(1)}, u32[]{:S(2)}, u32[]{:S(2)}) collective-permute-start(bf16[3,64,1280]{2,1,0:T(8,128)(2,1)} %get-tuple-element.115.refs_9_), channel_id=1, source_target_pairs={{0,2},{1,3},{2,0},{3,1},{4,6},{5,7},{6,4},{7,5},{8,10},{9,11},{10,... | collective-permute-start | bytes 1474568 | tf_op jit(solution)/shard_map/ppermute | solution.py:64
  181.3 54.8 %all-to-all-start.3 = ((bf16[8,11,80,128]{3,2,1,0:T(8,128)(2,1)}), bf16[8,11,80,128]{3,2,1,0:T(8,128)(2,1)S(1)}, u32[]{:S(2)}, u32[]{:S(2)}) async-start(bf16[8,11,80,128]{3,2,1,0:T(8,128)(2,1)} %shard_map.223), calls=%async_computation.3 | async-start | bytes 3604480 | tf_op jit(solution)/shard_map/all_to_all | solution.py:126
  185.3 3.8 %collective-permute-start.32 = (bf16[3,64,1280]{2,1,0:T(8,128)(2,1)}, bf16[3,64,1280]{2,1,0:T(8,128)(2,1)}, u32[]{:S(2)}, u32[]{:S(2)}) collective-permute-start(bf16[3,64,1280]{2,1,0:T(8,128)(2,1)} %shard_map.226.refs_19_), channel_id=1, source_target_pairs={{0,1},{1,0},{2,3},{3,2},{4,5},{5,4},{6,7},{7,6},{8,9},{9,8},{10,11... | collective-permute-start | bytes 1474568 | tf_op jit(solution)/shard_map/ppermute | solution.py:64
  185.4 3.7 %collective-permute-start.26 = (bf16[3,64,1280]{2,1,0:T(8,128)(2,1)S(1)}, bf16[3,64,1280]{2,1,0:T(8,128)(2,1)}, u32[]{:S(2)}, u32[]{:S(2)}) collective-permute-start(bf16[3,64,1280]{2,1,0:T(8,128)(2,1)S(1)} %copy-done.30), channel_id=1, source_target_pairs={{0,1},{1,0},{2,3},{3,2},{4,5},{5,4},{6,7},{7,6},{8,9},{9,8},{10,11... | collective-permute-start | bytes 1474568 | tf_op jit(solution)/shard_map/ppermute | solution.py:64
  185.9 3.2 collective-permute-start.29
  188.2 2.2 collective-permute-start.30
  189.1 2.1 collective-permute-start.28
  198.8 23.8 %collective-permute-start.33 = (bf16[4,3,40,640]{3,2,1,0:T(8,128)(2,1)}, bf16[4,3,40,640]{3,2,1,0:T(8,128)(2,1)S(1)}, u32[]{:S(2)}, u32[]{:S(2)}) collective-permute-start(bf16[4,3,40,640]{3,2,1,0:T(8,128)(2,1)} %get-tuple-element.118), channel_id=1, source_target_pairs={{0,4},{4,0},{8,12},{12,8},{16,20},{20,16},{24,28},{28,24},{1,5},{5... | collective-permute-start | bytes 1843208 | tf_op jit(solution)/shard_map/ppermute | solution.py:64
  200.6 29.7 %collective-permute-start.34 = (bf16[4,3,40,640]{3,2,1,0:T(8,128)(2,1)}, bf16[4,3,40,640]{3,2,1,0:T(8,128)(2,1)S(1)}, u32[]{:S(2)}, u32[]{:S(2)}) collective-permute-start(bf16[4,3,40,640]{3,2,1,0:T(8,128)(2,1)} %get-tuple-element.119), channel_id=1, source_target_pairs={{0,8},{4,12},{8,0},{12,4},{16,24},{20,28},{24,16},{28,20},{1,9},{5... | collective-permute-start | bytes 1843208 | tf_op jit(solution)/shard_map/ppermute | solution.py:64
  233.9 16.1 %collective-permute-start.38 = (bf16[2,3,40,640]{3,2,1,0:T(8,128)(2,1)}, bf16[2,3,40,640]{3,2,1,0:T(8,128)(2,1)S(1)}, u32[]{:S(2)}, u32[]{:S(2)}) collective-permute-start(bf16[2,3,40,640]{3,2,1,0:T(8,128)(2,1)} %get-tuple-element.120.refs_6_), channel_id=1, source_target_pairs={{0,8},{4,12},{8,0},{12,4},{16,24},{20,28},{24,16},{28,20},{1,9},{5... | collective-permute-start | bytes 921608 | tf_op jit(solution)/shard_map/ppermute | solution.py:64
  235.1 14.9 %collective-permute-start.39 = (bf16[2,3,40,640]{3,2,1,0:T(8,128)(2,1)}, bf16[2,3,40,640]{3,2,1,0:T(8,128)(2,1)S(1)}, u32[]{:S(2)}, u32[]{:S(2)}) collective-permute-start(bf16[2,3,40,640]{3,2,1,0:T(8,128)(2,1)} %get-tuple-element.128), channel_id=1, source_target_pairs={{0,4},{4,0},{8,12},{12,8},{16,20},{20,16},{24,28},{28,24},{1,5},{5... | collective-permute-start | bytes 921608 | tf_op jit(solution)/shard_map/ppermute | solution.py:64
  248.1 14.3 %collective-permute-start.41 = (bf16[4,3,40,640]{3,2,1,0:T(8,128)(2,1)}, bf16[4,3,40,640]{3,2,1,0:T(8,128)(2,1)S(1)}, u32[]{:S(2)}, u32[]{:S(2)}) collective-permute-start(bf16[4,3,40,640]{3,2,1,0:T(8,128)(2,1)} %get-tuple-element.134), channel_id=1, source_target_pairs={{0,4},{4,0},{8,12},{12,8},{16,20},{20,16},{24,28},{28,24},{1,5},{5... | collective-permute-start | bytes 1843208 | tf_op jit(solution)/shard_map/ppermute | solution.py:64
  249.1 21.0 %collective-permute-start.42 = (bf16[4,3,40,640]{3,2,1,0:T(8,128)(2,1)}, bf16[4,3,40,640]{3,2,1,0:T(8,128)(2,1)S(1)}, u32[]{:S(2)}, u32[]{:S(2)}) collective-permute-start(bf16[4,3,40,640]{3,2,1,0:T(8,128)(2,1)} %get-tuple-element.135), channel_id=1, source_target_pairs={{0,8},{4,12},{8,0},{12,4},{16,24},{20,28},{24,16},{28,20},{1,9},{5... | collective-permute-start | bytes 1843208 | tf_op jit(solution)/shard_map/ppermute | solution.py:64
  249.9 5.6 %collective-permute-start.43 = (f32[8,1280]{1,0:T(8,128)}, f32[8,1280]{1,0:T(8,128)S(1)}, u32[]{:S(2)}, u32[]{:S(2)}) collective-permute-start(f32[8,1280]{1,0:T(8,128)} %get-tuple-element.129.refs_5_), channel_id=1, source_target_pairs={{0,1},{1,0},{2,3},{3,2},{4,5},{5,4},{6,7},{7,6},{8,9},{9,8},{10,11... | collective-permute-start | bytes 122888 | tf_op jit(solution)/shard_map/ppermute | solution.py:64
  253.1 22.9 %collective-permute-start.40 = (bf16[2,3,40,640]{3,2,1,0:T(8,128)(2,1)}, bf16[2,3,40,640]{3,2,1,0:T(8,128)(2,1)S(1)}, u32[]{:S(2)}, u32[]{:S(2)}) collective-permute-start(bf16[2,3,40,640]{3,2,1,0:T(8,128)(2,1)} %get-tuple-element.131.refs_7_), channel_id=1, source_target_pairs={{0,16},{4,20},{8,24},{12,28},{16,0},{20,4},{24,8},{28,12},{1,17},{... | collective-permute-start | bytes 921608 | tf_op jit(solution)/shard_map/ppermute | solution.py:64
  255.3 19.0 %collective-permute-start.36 = (bf16[3,64,1280]{2,1,0:T(8,128)(2,1)S(1)}, bf16[3,64,1280]{2,1,0:T(8,128)(2,1)S(1)}, u32[]{:S(2)}, u32[]{:S(2)}) collective-permute-start(bf16[3,64,1280]{2,1,0:T(8,128)(2,1)S(1)} %copy-done.36), channel_id=1, source_target_pairs={{0,1},{1,0},{2,3},{3,2},{4,5},{5,4},{6,7},{7,6},{8,9},{9,8},{10,11... | collective-permute-start | bytes 1474568 | tf_op jit(solution)/shard_map/ppermute | solution.py:64
  255.6 51.0 %collective-permute-start.35 = (bf16[3,64,1280]{2,1,0:T(8,128)(2,1)S(1)}, bf16[3,64,1280]{2,1,0:T(8,128)(2,1)S(1)}, u32[]{:S(2)}, u32[]{:S(2)}) collective-permute-start(bf16[3,64,1280]{2,1,0:T(8,128)(2,1)S(1)} %copy-done.31), channel_id=1, source_target_pairs={{0,1},{1,0},{2,3},{3,2},{4,5},{5,4},{6,7},{7,6},{8,9},{9,8},{10,11... | collective-permute-start | bytes 1474568 | tf_op jit(solution)/shard_map/ppermute | solution.py:64
  273.7 4.7 %collective-permute-start.44 = (f32[8,1280]{1,0:T(8,128)}, f32[8,1280]{1,0:T(8,128)S(1)}, u32[]{:S(2)}, u32[]{:S(2)}) collective-permute-start(f32[8,1280]{1,0:T(8,128)} %get-tuple-element.136.refs_3_), channel_id=1, source_target_pairs={{0,2},{1,3},{2,0},{3,1},{4,6},{5,7},{6,4},{7,5},{8,10},{9,11},{10,... | collective-permute-start | bytes 122888 | tf_op jit(solution)/shard_map/ppermute | solution.py:64
  274.5 34.1 %collective-permute-start.37 = (bf16[3,64,1280]{2,1,0:T(8,128)(2,1)S(1)}, bf16[3,64,1280]{2,1,0:T(8,128)(2,1)S(1)}, u32[]{:S(2)}, u32[]{:S(2)}) collective-permute-start(bf16[3,64,1280]{2,1,0:T(8,128)(2,1)S(1)} %add_convert_fusion), channel_id=1, source_target_pairs={{0,2},{1,3},{2,0},{3,1},{4,6},{5,7},{6,4},{7,5},{8,10},{9,11},{10,... | collective-permute-start | bytes 1474568 | tf_op jit(solution)/shard_map/ppermute | solution.py:64
  276.0 9.6 %collective-permute-start.47 = (bf16[2,3,40,640]{3,2,1,0:T(8,128)(2,1)}, bf16[2,3,40,640]{3,2,1,0:T(8,128)(2,1)S(1)}, u32[]{:S(2)}, u32[]{:S(2)}) collective-permute-start(bf16[2,3,40,640]{3,2,1,0:T(8,128)(2,1)} %get-tuple-element.137.refs_5_), channel_id=1, source_target_pairs={{0,8},{4,12},{8,0},{12,4},{16,24},{20,28},{24,16},{28,20},{1,9},{5... | collective-permute-start | bytes 921608 | tf_op jit(solution)/shard_map/ppermute | solution.py:64
  276.0 11.3 %collective-permute-start.48 = (bf16[2,3,40,640]{3,2,1,0:T(8,128)(2,1)}, bf16[2,3,40,640]{3,2,1,0:T(8,128)(2,1)S(1)}, u32[]{:S(2)}, u32[]{:S(2)}) collective-permute-start(bf16[2,3,40,640]{3,2,1,0:T(8,128)(2,1)} %get-tuple-element.142), channel_id=1, source_target_pairs={{0,4},{4,0},{8,12},{12,8},{16,20},{20,16},{24,28},{28,24},{1,5},{5... | collective-permute-start | bytes 921608 | tf_op jit(solution)/shard_map/ppermute | solution.py:64
  280.9 21.8 %collective-permute-start.45 = (bf16[2,3,40,640]{3,2,1,0:T(8,128)(2,1)}, bf16[2,3,40,640]{3,2,1,0:T(8,128)(2,1)S(1)}, u32[]{:S(2)}, u32[]{:S(2)}) collective-permute-start(bf16[2,3,40,640]{3,2,1,0:T(8,128)(2,1)} %get-tuple-element.138.refs_5_.refs_1_), channel_id=1, source_target_pairs={{0,16},{4,20},{8,24},{12,28},{16,0},{20,4},{24,8},{28,12},{1,17},{... | collective-permute-start | bytes 921608 | tf_op jit(solution)/shard_map/ppermute | solution.py:64
  285.6 4.8 %collective-permute-start.46 = (f32[8,1280]{1,0:T(8,128)}, f32[8,1280]{1,0:T(8,128)S(1)}, u32[]{:S(2)}, u32[]{:S(2)}) collective-permute-start(f32[8,1280]{1,0:T(8,128)} %get-tuple-element.139.refs_3_), channel_id=1, source_target_pairs={{0,4},{4,0},{8,12},{12,8},{16,20},{20,16},{24,28},{28,24},{1,5},{5... | collective-permute-start | bytes 122888 | tf_op jit(solution)/shard_map/ppermute | solution.py:64
  290.2 22.3 %collective-permute-start.49 = (bf16[2,3,40,640]{3,2,1,0:T(8,128)(2,1)}, bf16[2,3,40,640]{3,2,1,0:T(8,128)(2,1)S(1)}, u32[]{:S(2)}, u32[]{:S(2)}) collective-permute-start(bf16[2,3,40,640]{3,2,1,0:T(8,128)(2,1)} %get-tuple-element.143.refs_5_), channel_id=1, source_target_pairs={{0,16},{4,20},{8,24},{12,28},{16,0},{20,4},{24,8},{28,12},{1,17},{... | collective-permute-start | bytes 921608 | tf_op jit(solution)/shard_map/ppermute | solution.py:64
  305.5 9.9 %collective-permute-start.51 = (bf16[2,3,40,640]{3,2,1,0:T(8,128)(2,1)}, bf16[2,3,40,640]{3,2,1,0:T(8,128)(2,1)S(1)}, u32[]{:S(2)}, u32[]{:S(2)}) collective-permute-start(bf16[2,3,40,640]{3,2,1,0:T(8,128)(2,1)} %get-tuple-element.144.refs_7_.refs_1_), channel_id=1, source_target_pairs={{0,8},{4,12},{8,0},{12,4},{16,24},{20,28},{24,16},{28,20},{1,9},{5... | collective-permute-start | bytes 921608 | tf_op jit(solution)/shard_map/ppermute | solution.py:64
  305.5 9.9 %collective-permute-start.52 = (bf16[2,3,40,640]{3,2,1,0:T(8,128)(2,1)}, bf16[2,3,40,640]{3,2,1,0:T(8,128)(2,1)S(1)}, u32[]{:S(2)}, u32[]{:S(2)}) collective-permute-start(bf16[2,3,40,640]{3,2,1,0:T(8,128)(2,1)} %get-tuple-element.146.refs_2_), channel_id=1, source_target_pairs={{0,4},{4,0},{8,12},{12,8},{16,20},{20,16},{24,28},{28,24},{1,5},{5... | collective-permute-start | bytes 921608 | tf_op jit(solution)/shard_map/ppermute | solution.py:64
  306.6 8.8 %collective-permute-start.53 = (f32[8,1280]{1,0:T(8,128)}, f32[8,1280]{1,0:T(8,128)S(1)}, u32[]{:S(2)}, u32[]{:S(2)}) collective-permute-start(f32[8,1280]{1,0:T(8,128)} %get-tuple-element.147.refs_5_), channel_id=1, source_target_pairs={{0,8},{4,12},{8,0},{12,4},{16,24},{20,28},{24,16},{28,20},{1,9},{5... | collective-permute-start | bytes 122888 | tf_op jit(solution)/shard_map/ppermute | solution.py:64
  315.1 11.4 %collective-permute-start.50 = (bf16[2,3,40,640]{3,2,1,0:T(8,128)(2,1)}, bf16[2,3,40,640]{3,2,1,0:T(8,128)(2,1)S(1)}, u32[]{:S(2)}, u32[]{:S(2)}) collective-permute-start(bf16[2,3,40,640]{3,2,1,0:T(8,128)(2,1)} %shard_map.236.refs_7_.refs_1_), channel_id=1, source_target_pairs={{0,16},{4,20},{8,24},{12,28},{16,0},{20,4},{24,8},{28,12},{1,17},{... | collective-permute-start | bytes 921608 | tf_op jit(solution)/shard_map/ppermute | solution.py:64
  319.2 17.9 %collective-permute-start.56 = (bf16[4,3,40,640]{3,2,1,0:T(8,128)(2,1)}, bf16[4,3,40,640]{3,2,1,0:T(8,128)(2,1)S(1)}, u32[]{:S(2)}, u32[]{:S(2)}) collective-permute-start(bf16[4,3,40,640]{3,2,1,0:T(8,128)(2,1)} %get-tuple-element.148.refs_3_.refs_1_), channel_id=1, source_target_pairs={{0,4},{4,0},{8,12},{12,8},{16,20},{20,16},{24,28},{28,24},{1,5},{5... | collective-permute-start | bytes 1843208 | tf_op jit(solution)/shard_map/ppermute | solution.py:64
  320.5 18.7 %collective-permute-start.57 = (bf16[4,3,40,640]{3,2,1,0:T(8,128)(2,1)}, bf16[4,3,40,640]{3,2,1,0:T(8,128)(2,1)S(1)}, u32[]{:S(2)}, u32[]{:S(2)}) collective-permute-start(bf16[4,3,40,640]{3,2,1,0:T(8,128)(2,1)} %get-tuple-element.151.refs_2_), channel_id=1, source_target_pairs={{0,8},{4,12},{8,0},{12,4},{16,24},{20,28},{24,16},{28,20},{1,9},{5... | collective-permute-start | bytes 1843208 | tf_op jit(solution)/shard_map/ppermute | solution.py:64
  322.4 14.7 %collective-permute-start.58 = (f32[8,1280]{1,0:T(8,128)}, f32[8,1280]{1,0:T(8,128)S(1)}, u32[]{:S(2)}, u32[]{:S(2)}) collective-permute-start(f32[8,1280]{1,0:T(8,128)} %get-tuple-element.152.refs_5_), channel_id=1, source_target_pairs={{0,16},{4,20},{8,24},{12,28},{16,0},{20,4},{24,8},{28,12},{1,17},{... | collective-permute-start | bytes 122888 | tf_op jit(solution)/shard_map/ppermute | solution.py:64
  329.1 15.2 %collective-permute-start.54 = (bf16[2,3,40,640]{3,2,1,0:T(8,128)(2,1)}, bf16[2,3,40,640]{3,2,1,0:T(8,128)(2,1)S(1)}, u32[]{:S(2)}, u32[]{:S(2)}) collective-permute-start(bf16[2,3,40,640]{3,2,1,0:T(8,128)(2,1)} %get-tuple-element.149.refs_7_.refs_1_), channel_id=1, source_target_pairs={{0,8},{4,12},{8,0},{12,4},{16,24},{20,28},{24,16},{28,20},{1,9},{5... | collective-permute-start | bytes 921608 | tf_op jit(solution)/shard_map/ppermute | solution.py:64
  329.1 15.2 %collective-permute-start.55 = (bf16[2,3,40,640]{3,2,1,0:T(8,128)(2,1)}, bf16[2,3,40,640]{3,2,1,0:T(8,128)(2,1)S(1)}, u32[]{:S(2)}, u32[]{:S(2)}) collective-permute-start(bf16[2,3,40,640]{3,2,1,0:T(8,128)(2,1)} %get-tuple-element.150.refs_2_), channel_id=1, source_target_pairs={{0,4},{4,0},{8,12},{12,8},{16,20},{20,16},{24,28},{28,24},{1,5},{5... | collective-permute-start | bytes 921608 | tf_op jit(solution)/shard_map/ppermute | solution.py:64
  347.5 11.5 %collective-permute-start.59 = (bf16[4,3,40,640]{3,2,1,0:T(8,128)(2,1)}, bf16[4,3,40,640]{3,2,1,0:T(8,128)(2,1)S(1)}, u32[]{:S(2)}, u32[]{:S(2)}) collective-permute-start(bf16[4,3,40,640]{3,2,1,0:T(8,128)(2,1)} %get-tuple-element.154.refs_1_.refs_5_), channel_id=1, source_target_pairs={{0,4},{4,0},{8,12},{12,8},{16,20},{20,16},{24,28},{28,24},{1,5},{5... | collective-permute-start | bytes 1843208 | tf_op jit(solution)/shard_map/ppermute | solution.py:64
  348.5 12.0 %collective-permute-start.60 = (bf16[4,3,40,640]{3,2,1,0:T(8,128)(2,1)}, bf16[4,3,40,640]{3,2,1,0:T(8,128)(2,1)S(1)}, u32[]{:S(2)}, u32[]{:S(2)}) collective-permute-start(bf16[4,3,40,640]{3,2,1,0:T(8,128)(2,1)} %get-tuple-element.155.refs_2_), channel_id=1, source_target_pairs={{0,8},{4,12},{8,0},{12,4},{16,24},{20,28},{24,16},{28,20},{1,9},{5... | collective-permute-start | bytes 1843208 | tf_op jit(solution)/shard_map/ppermute | solution.py:64
  (69 other events, 417.2 us)

commit v3 on v2

--- a/solution.py
+++ b/solution.py
@@ -14,9 +14,11 @@
 key_tile = 2048
 vmem_bytes = 60 * 1024 * 1024
 loop_tile = 1024
+spare_bytes = 36 * 1024 * 1024
 kernel_us = {
     "project_kernel": 7, "attend_kernel": 11, "middle_kernel": 14, "attend_back_kernel": 15, "grads_kernel": 7, "back_kernel": 11,
 }
+lead = 3
 ahead_rounds = 1
 flops_per_us = 1153500000
 bf16 = jnp.bfloat16
@@ -29,6 +31,11 @@
 
 def mm(left, right, dims=rows_cols):
     return lax.dot_general(left, right, dims, preferred_element_type=f32)
+
+
+def padded_bytes(value):
+    *rest, last = value.shape
+    return math.prod(rest) * -(-last // 128) * 128 * jnp.dtype(value.dtype).itemsize
 
 
 def call(kernel, out_shape, operands, scalars, scratch=(), tokens=(), weight=1):
@@ -36,6 +43,7 @@
     specs += [pl.BlockSpec(memory_space=pltpu.VMEM)] * len(operands)
     specs += [pl.BlockSpec(memory_space=pl.ANY)] * len(tokens)
     used = 1 + len(operands)
+    room = spare_bytes + 2 * sum(padded_bytes(v) for v in [*operands, *out_shape, *scratch])
     weight = kernel_us.get(getattr(kernel, "func", kernel).__name__, weight)
     return pl.pallas_call(
         lambda *refs: kernel(*refs[:used], *refs[used + len(tokens) :]),
@@ -43,7 +51,7 @@
         in_specs=specs,
         out_specs=tuple(pl.BlockSpec(memory_space=pltpu.VMEM) for _ in out_shape),
         scratch_shapes=list(scratch),
-        compiler_params=pltpu.CompilerParams(vmem_limit_bytes=vmem_bytes),
+        compiler_params=pltpu.CompilerParams(vmem_limit_bytes=min(vmem_bytes, room)),
         cost_estimate=pl.CostEstimate(flops=int(weight * flops_per_us), bytes_accessed=0, transcendentals=0),
     )(scalars, *operands, *tokens)
 
@@ -132,9 +140,10 @@
 
 
 class Sums:
-    def __init__(self, size, kinds, rows, lanes):
+    def __init__(self, size, kinds, rows, lanes, tail=0):
         self.size, self.bits = size, bits_of(size)
-        self.block = (kinds, rows, lanes)
+        self.kinds, self.rows, self.tail = kinds, rows, tail
+        self.block = (1, kinds * rows + tail, lanes) if tail else (kinds, rows, lanes)
         first = list(range(self.bits))
         second = first[:]
         if self.bits > 1:
@@ -177,17 +186,17 @@
         self.keep = keep
         self.got = [exchange(v, "context", self.size, bit) for v, (bit, _, _) in zip(send, self.groups(self.step))]
 
-    def fold(self, scalars, finals=(), extra=(), tokens=()):
+    def fold(self, scalars, finals=(), tokens=(), group=None):
         step, last = self.step, self.step == 2 * self.bits - 1
         halving = step + 1 < self.bits
+        summed = self.tail and step + 1 == self.bits
         outs = list(finals) if last else self.shapes(step + 1) * (2 if halving else 1)
         count, width = len(self.keep), len(outs)
+        lanes = self.block[2]
 
         def kernel(sc, *refs):
             keep, got = refs[:count], refs[count : 2 * count]
-            pairs, out = refs[2 * count : 2 * count + 2 * len(extra)], refs[2 * count + 2 * len(extra) :]
-            for i in range(len(extra)):
-                out[width + i][...] = pairs[2 * i][...] + pairs[2 * i + 1][...]
+            out = refs[2 * count :]
 
             def total(stream, index):
                 return self.at(keep, stream, step, index)[...].astype(f32) + self.at(got, stream, step, index)[...].astype(f32)
@@ -199,7 +208,10 @@
             me = lax.axis_index("context")
             for stream in range(2):
                 if step < self.bits:
-                    self.at(out, stream, step + 1, 0)[...] = total(stream, 0).astype(bf16)
+                    value = total(stream, 0)
+                    self.at(out, stream, step + 1, 0)[...] = value.astype(bf16)
+                    if summed:
+                        out[width][:, stream * lanes : (stream + 1) * lanes] = value[0, -self.tail :]
                     continue
                 bit, left = self.bit(stream, step), self.left(stream, step)
                 place = sorted(left + [bit]).index(bit)
@@ -211,14 +223,17 @@
                         if not last:
                             self.at(out, stream, step + 1, index)[...] = value
                             continue
-                        kinds, rows, lanes = self.block
+                        kinds, rows = self.kinds, self.rows
                         span = pl.ds(pl.multiple_of(index * rows, rows), rows)
+                        value = value.astype(f32)
                         for kind in range(kinds):
                             to = out[kind] if width > 1 else out[0].at[kind]
-                            to[span, stream * lanes : (stream + 1) * lanes] = value[kind].astype(f32)
-
-        outs = outs + [shape(a.shape, a.dtype) for a, _ in extra]
-        operands = [*self.keep, *self.got] + [v for pair in extra for v in pair]
+                            part = value[0, kind * rows : (kind + 1) * rows] if self.tail else value[kind]
+                            to[span, stream * lanes : (stream + 1) * lanes] = part
+
+        if summed:
+            outs = outs + [shape((self.tail, 2 * lanes), f32)]
+        operands = [*self.keep, *self.got]
         made = list(call(kernel, outs, operands, scalars, tokens=tokens, weight=8))
         self.step += 1
         self.token = made[0]
@@ -228,7 +243,7 @@
             self.start(made[: width // 2], made[width // 2 : width])
         else:
             self.start(made[:width], made[:width])
-        return made[width:]
+        return made[width] if summed else None
 
 
 def chunk(k, rows):
@@ -278,14 +293,14 @@
             n1_ref[b, chunk(k, rows), :] = (x * r * gain_ref[...]).astype(bf16)
     n1 = n1_ref[...].reshape(-1, n1_ref.shape[2])
     for i in range(3):
-        y = mm(n1, w_ref[i], cols_cols)
+        y = mm(w_ref[i], n1, cols_cols)
         if i == 0:
-            y = (y + bias_ref[0:1]) * factor_ref[...]
+            y = (y + bias_ref[:, 0:1]) * factor_ref[...]
         elif i == 2:
-            y = y + bias_ref[1:2]
+            y = y + bias_ref[:, 1:2]
+        y = y.astype(bf16)
         for b in range(batches):
-            part = y[b * spread * rows : (b + 1) * spread * rows]
-            store_parts(plan, parity, part.T.astype(bf16), send_ref, b, i)
+            store_parts(plan, parity, y[:, b * spread * rows : (b + 1) * spread * rows], send_ref, b, i)
 
 
 def place(inverse_ref, index):
@@ -517,12 +532,6 @@
             held_ref[b, s * piece : (s + 1) * piece] = collect(plan, even, got_ref, b, s, 0).T
         for k, out_ref in enumerate(out_refs):
             out_ref[b] = held_ref[b, chunk(k, rows), :]
-
-
-def copy_kernel(sc, *refs):
-    count = len(refs) // 2
-    for source, target in zip(refs[:count], refs[count:]):
-        target[...] = source[...]
 
 
 def middle_kernel(spread, sc, *refs):
@@ -566,9 +575,14 @@
 
 
 def cut_rows(value, out_ref, kind):
-    chunks, _, rows, _ = out_ref.shape
+    chunks = out_ref.shape[0]
+    rows = value.shape[0] // chunks
     for c in range(chunks):
-        out_ref[c, kind] = value[c * rows : (c + 1) * rows].astype(bf16)
+        part = value[c * rows : (c + 1) * rows]
+        if out_ref.shape[1] == 1:
+            out_ref[c, 0, kind * rows : (kind + 1) * rows] = part.astype(out_ref.dtype)
+        else:
+            out_ref[c, kind] = part.astype(out_ref.dtype)
 
 
 def grads_kernel(spread, sums, sc, *refs):
@@ -634,15 +648,11 @@
         cut_rows(mm(turned_rows, n1), target, kind)
     give_rows(total, held_ref, part_refs)
     out_small_ref[0:1] = jnp.sum(total * n1.astype(f32), axis=0, keepdims=True) / gain_ref[...]
-    slots = spread // 2
-    for f in range(spread):
-
-        @pl.when(lax.axis_index("fsdp") == f)
-        def _():
-            for i in range(2):
-                first = (f % slots) * 2 * local + i * local
-                out_small_ref[5 + f // slots : 6 + f // slots, first : first + local] = bias[i]
-
+    for i in range(2):
+        out_small_ref[5:6, i * local : (i + 1) * local] = bias[i]
+    if sums:
+        for c in range(cut_ref.shape[0]):
+            cut_ref[c, 0, sums.kinds * sums.rows :] = out_small_ref[...]
     if sums:
         deal_cuts(sums, cut_ref, out_refs)
 
@@ -676,7 +686,7 @@
     last_end = ends[batches - 1].reshape(-1, group, piece)
     last_end = lax.dynamic_index_in_dim(last_end, member, 1, keepdims=False).reshape(1, -1)
     factor = base_rate / math.sqrt(dim) * jax.nn.softplus(query_scale)
-    factor_row = jnp.tile(factor, heads).reshape(1, local)
+    factor_rows = jnp.tile(factor, heads).reshape(local, 1)
     factor_col = factor.reshape(dim, 1)
     gain_one, gain_two = norm_gains[0:1], norm_gains[1:2]
 
@@ -697,7 +707,7 @@
     n1, send = call(
         functools.partial(project_kernel, plan, spread),
         [whole, shape((size, 11, dim, piece), bf16)],
-        [*x_parts, qkv_turned, gain_one, qv_bias, factor_row],
+        [*x_parts, qkv_turned, gain_one, qv_bias.T, factor_rows],
         scalars,
         tokens=[main_end, last_end],
     )
@@ -714,7 +724,6 @@
         ],
     )
     others = [out_weight, in_turned, down_weight, in_bias.reshape(1, local), output_cotangent]
-    others = call(copy_kernel, [shape(v.shape, v.dtype) for v in others], others, scalars, tokens=[send])
     *others, g_copy = others
     others = [gather_rows(v, "fsdp", spread, o_send) for v in others]
     g_first = exchange(g_copy, "fsdp", spread, bits_of(spread) - 1)
@@ -764,7 +773,9 @@
     n2_parts = spread_rows(n2, n2_first, "fsdp", spread, scale_sum)
     dy_parts = spread_rows(dy, dy_first, "fsdp", spread, scale_sum)
     new_sums = lambda: Sums(size, 3, local // size, width // 2) if even_cuts else None
-    early, last = new_sums(), new_sums()
+    early = new_sums()
+    last = Sums(size, 3, local // size, width // 2, 8) if even_cuts else None
+    last_cut = (size, 1, 3 * local // size + 8, width) if even_cuts else (8, 128)
     dealt = early.shapes(0) * 2 if even_cuts else [cut_shape]
     cut_scratch = [pltpu.VMEM(cut_shape.shape, bf16)]
     early_made = call(
@@ -779,21 +790,21 @@
     small = [jnp.zeros((1, width), f32), sums, du_sum.reshape(1, width), jnp.zeros((2, width), f32)]
     small.append(jnp.pad(scale_sum.reshape(1, dim) / factor, ((0, 0), (0, width - dim))))
     small = jnp.concatenate(small)
+    for bit in range(bits_of(spread)):
+        small = small + exchange(small, "fsdp", spread, bit)
     if even_cuts:
         early.start(early_made[: len(early_made) // 2], early_made[len(early_made) // 2 :])
         for _ in range(ahead_rounds):
             early.fold(scalars)
     small, *made = call(
         functools.partial(back_kernel, plan, spread, last),
-        [shape(small.shape, f32)] + parts + dealt,
+        [shape(small.shape, f32)] + parts + (last.shapes(0) * 2 if even_cuts else [cut_shape]),
         [d_got, qkv_turned, n1, gain_one, small],
         scalars,
-        held + [pltpu.VMEM((local, tokens), bf16)] + cut_scratch,
+        held + [pltpu.VMEM((local, tokens), bf16), pltpu.VMEM(last_cut, f32)],
         tokens=[early.token] if even_cuts and ahead_rounds else [],
     )
     part, made = made[:spread], made[spread:]
-    steps = [("fsdp", spread, bit) for bit in range(bits_of(spread))]
-    steps += [("context", size, bit) for bit in range(bits_of(size))]
     dn1_terms, _ = scatter_parts(part, "fsdp", spread)
 
     def close(*tokens):
@@ -808,42 +819,35 @@
     qkv_kind = shape((3, local, width), f32)
     if even_cuts:
         last.start(made[: len(made) // 2], made[len(made) // 2 :])
-        order = ["early"] * (2 - ahead_rounds) + ["last", "early"] * (2 * early.bits - 2) + ["last"] * 2
+        order = ["early"] * (lead - ahead_rounds) + ["last", "early"] * (2 * early.bits - lead) + ["last"] * lead
         order = [early if name == "early" else last for name in order]
         ends = {early: [shape((local, width), f32)] * 3, last: [qkv_kind]}
-        adds = (1, 2, 4, 6, 8)
-        seen, pending, done = small, None, 0
+        seen = small
         for index, flow in enumerate(order):
-            if pending is None and done < len(steps):
-                pending = exchange(small, *steps[done])
-            extra = [(small, pending)] if pending is not None and index in adds else []
             finals = ends[flow] if flow.step == 2 * flow.bits - 1 else []
-            added = flow.fold(scalars, finals, extra, [seen])
+            added = flow.fold(scalars, finals, [seen])
             seen = flow.token
-            if extra:
-                small, pending, done = added[0], None, done + 1
-            if index == 4:
+            if added is not None:
+                small = added
+            if index == 5:
                 input_grad = close(seen)
                 seen = input_grad
-        if pending is not None:
-            small, done = small + pending, done + 1
-        steps = steps[done:]
-        for axis, count, bit in steps:
-            small = small + exchange(small, axis, count, bit)
         (qkv,) = last.result
         out_grad, *feed_grads = early.result
     else:
-        for axis, count, bit in steps:
-            small = small + exchange(small, axis, count, bit)
+        small = lax.psum(small, "context")
         input_grad = close()
         whole_sum = lambda v: lax.psum(v, "context").astype(f32).reshape(3, local, width)
         qkv = whole_sum(made[0])
         out_grad, *feed_grads = whole_sum(early_made[0])
-    gains_grad = small[0:2]
+    first_gain = small[0:1]
+    for bit in range(bits_of(spread)):
+        first_gain = first_gain + exchange(first_gain, "fsdp", spread, bit)
+    gains_grad = jnp.concatenate([first_gain, small[1:2]])
     out_bias_grad = small[2:4]
-    own_slot = lambda v: lax.dynamic_index_in_dim(v.reshape(spread, -1), lax.axis_index("fsdp"), 0, keepdims=False)
-    in_bias_grad = own_slot(small[4])
-    qv_grad = own_slot(small[5:7]).reshape(2, local)
+    in_bias_grad = small[4].reshape(spread, local)
+    in_bias_grad = lax.dynamic_index_in_dim(in_bias_grad, lax.axis_index("fsdp"), 0, keepdims=False)
+    qv_grad = small[5, : 2 * local].reshape(2, local)
     scale_grad = small[7, :dim] * (base_rate / math.sqrt(dim)) * jax.nn.sigmoid(query_scale)
     return (
         layer_output,

time: 372 us -> 350 us (0.941)
  Pallas kernels: 107 us -> 80 us
  waiting for transfers between devices: 154 us -> 168 us
  local copies, waits for them, and re-layouts: 27.1 us -> 20.6 us
    pallas_call x22 -> x21, Pallas kernels: 107 us -> 80 us  [call(): pl.pallas_call(lambda *refs: kernel(*refs[:used], *refs[used + len(tokens...]
    all_to_all x4, waiting for transfers between devices: 42.4 us -> 49.9 us  [swap_all(): return lax.all_to_all(parts, axis, 0, 0, tiled=True)]
    ppermute x52 -> x51, waiting for transfers between devices: 97.2 us -> 104 us  [exchange(): return lax.ppermute(values, axis, [(i, i ^ 1 << bit) for i in range(size)])]
    unnamed x138 -> x139, local copies, waits for them, and re-layouts: 19.6 us -> 16.6 us
    ppermute x52 -> x51, starting transfers between devices: 40.3 us -> 38.8 us  [exchange(): return lax.ppermute(values, axis, [(i, i ^ 1 << bit) for i in range(size)])]
  transfers between devices with their start and end apart: 65 -> 64, of which waited for: 24 -> 33; matrix products, arithmetic and copies ran while one was open for 5% -> 5% of each run, Pallas kernels for 21% -> 16%
where the time goes in v3:
time: 350 us; the launch traced here: 345 us
  waiting for transfers between devices  168 us (48%)
  Pallas kernels  80 us (23%)
  starting transfers between devices  63.7 us (18%)
  local copies, waits for them, and re-layouts  20.6 us (6%)
  other arithmetic  11 us (3%)
    ppermute x51, waiting for transfers between devices, exchange(): return lax.ppermute(values, axis, [(i, i ^ 1 << bit) for i in range(size)])  104 us
    pallas_call x21, Pallas kernels, call(): pl.pallas_call(lambda *refs: kernel(*refs[:used], *refs[used + len(tokens...  80 us
    all_to_all x4, waiting for transfers between devices, swap_all(): return lax.all_to_all(parts, axis, 0, 0, tiled=True)  49.9 us
    ppermute x51, starting transfers between devices, exchange(): return lax.ppermute(values, axis, [(i, i ^ 1 << bit) for i in range(size)])  38.8 us
    all_to_all x4, starting transfers between devices, swap_all(): return lax.all_to_all(parts, axis, 0, 0, tiled=True)  19.1 us
    unnamed x139, local copies, waits for them, and re-layouts  16.6 us
    ppermute x9, waiting for transfers between devices, swap_parts(): lax.ppermute(parts[k], axis, [(i, i ^ k) for i in range(size)])  14.1 us
    another operation x2, other arithmetic  7.21 us
  transfers between devices with their start and end apart: 64, of which 33 were waited for; matrix products, arithmetic and copies ran while one was open for 5% of the time, Pallas kernels for 16%

profile of v3, /device:TPU:0, one launch (start us, length us, event | category | flops | bytes accessed | tf_op | source)
XLA Modules:
  0.0 345.0 jit_solution(126729205341684701)
XLA Ops:
  0.6 3.0 collective-permute-start.1
  4.6 7.0 %reduce-window.6 = s32[3,16,128]{2,1,0:T(8,128)S(1)} reduce-window(s32[3,16,128]{2,1,0:T(8,128)S(1)} %bitcast.49, s32[]{:T(128)} %constant.66.clone.1), window={size=1x1x128 pad=0_0x0_0x0_127}, to_apply=%region_0.1 | reduce-window | flops 780288 | bytes 49156 | tf_op jit(solution)/shard_map/reduce-window
  13.0 2.1 collective-permute-done.1.refs_3_
  19.4 6.2 %shard_map.212 = (bf16[3,256,1280]{2,1,0:T(8,128)(2,1)}, bf16[8,11,80,128]{3,2,1,0:T(8,128)(2,1)}) custom-call(s32[2,8]{1,0:T(2,128)S(1)} %bitcast.32, bf16[3,64,1280]{2,1,0:T(8,128)(2,1)S(1)} %copy-done.7, bf16[3,64,1280]{2,1,0:T(8,128)(2,1)S(1)} %collective-permute-done.refs_2_, bf16[3,64,1280]{2,1,0:T(8,128)(2,1)} %copy-done.55, ...), custom_call_target="tpu_custom_call" | custom-call | flops 8074500096 | tf_op jit(solution)/shard_map/pallas_call | solution.py:48
  25.7 6.5 %all-to-all-start = ((bf16[8,11,80,128]{3,2,1,0:T(8,128)(2,1)}), bf16[8,11,80,128]{3,2,1,0:T(8,128)(2,1)S(1)}, u32[]{:S(2)}, u32[]{:S(2)}) async-start(bf16[8,11,80,128]{3,2,1,0:T(8,128)(2,1)} %get-tuple-element.76), calls=%async_computation | async-start | bytes 3604480 | tf_op jit(solution)/shard_map/all_to_all | solution.py:134
  32.2 1.6 collective-permute-start.17
  34.5 1.5 collective-permute-start.14
  36.0 1.3 collective-permute-start.8
  38.0 36.6 %all-to-all-done.refs_1_ = bf16[8,11,80,128]{3,2,1,0:T(8,128)(2,1)S(1)} async-done(((bf16[8,11,80,128]{3,2,1,0:T(8,128)(2,1)}), bf16[8,11,80,128]{3,2,1,0:T(8,128)(2,1)S(1)}, u32[]{:S(2)}, u32[]{:S(2)}) %all-to-all-start) | async-done | bytes 1802272 | tf_op jit(solution)/shard_map/all_to_all | solution.py:134
  74.6 10.6 %shard_map.213 = (bf16[8,3,80,128]{3,2,1,0:T(8,128)(2,1)}, f32[80,2048]{1,0:T(8,128)S(1)}, f32[1,2048]{1,0:T(1,128)S(1)}, f32[80,1024]{1,0:T(8,128)S(1)}, f32[1,1024]{1,0:T(1,128)S(1)}) custom-call(s32[2,8]{1,0:T(2,128)S(1)} %bitcast.33, bf16[8,11,80,128]{3,2,1,0:T(8,128)(2,1)S(1)} %all-to-all-done.refs_1_, ...), custom_call_target="tpu_custom_call" | custom-call | flops 12688499712 | tf_op jit(solution)/shard_map/pallas_call | solution.py:48
  86.8 3.9 %all-to-all-start.1 = ((bf16[8,3,80,128]{3,2,1,0:T(8,128)(2,1)}), bf16[8,3,80,128]{3,2,1,0:T(8,128)(2,1)S(1)}, u32[]{:S(2)}, u32[]{:S(2)}) async-start(bf16[8,3,80,128]{3,2,1,0:T(8,128)(2,1)} %get-tuple-element.77.refs_1_), calls=%async_computation.1 | async-start | bytes 983040 | tf_op jit(solution)/shard_map/all_to_all | solution.py:134
  91.8 8.5 %collective-permute-done.3.refs_2_.refs_0_ = bf16[3,64,1280]{2,1,0:T(8,128)(2,1)S(1)} collective-permute-done((bf16[3,64,1280]{2,1,0:T(8,128)(2,1)}, bf16[3,64,1280]{2,1,0:T(8,128)(2,1)S(1)}, u32[]{:S(2)}, u32[]{:S(2)}) %collective-permute-start.3) | collective-permute-done | bytes 491552 | tf_op jit(solution)/shard_map/ppermute | solution.py:72
  100.9 3.8 %all-to-all-done.1.refs_1_ = bf16[8,3,80,128]{3,2,1,0:T(8,128)(2,1)S(1)} async-done(((bf16[8,3,80,128]{3,2,1,0:T(8,128)(2,1)}), bf16[8,3,80,128]{3,2,1,0:T(8,128)(2,1)S(1)}, u32[]{:S(2)}, u32[]{:S(2)}) %all-to-all-start.1) | async-done | bytes 491552 | tf_op jit(solution)/shard_map/all_to_all | solution.py:134
  106.3 1.6 collective-permute-start.5
  108.2 4.8 %collective-permute-done.5.refs_3_ = bf16[3,64,320]{2,1,0:T(8,128)(2,1)S(1)} collective-permute-done((bf16[3,64,320]{2,1,0:T(8,128)(2,1)S(1)}, bf16[3,64,320]{2,1,0:T(8,128)(2,1)S(1)}, u32[]{:S(2)}, u32[]{:S(2)}) %collective-permute-start.5) | collective-permute-done | bytes 122912 | tf_op jit(solution)/shard_map/ppermute | solution.py:130
  113.0 2.2 collective-permute-done.6.refs_4_
  115.9 13.8 %shard_map.219 = (bf16[3,64,1280]{2,1,0:T(8,128)(2,1)}, f32[3,64,1280]{2,1,0:T(8,128)}, bf16[3,64,1280]{2,1,0:T(8,128)(2,1)}, bf16[3,64,1280]{2,1,0:T(8,128)(2,1...) custom-call(s32[2,8]{1,0:T(2,128)} %bitcast.28, ...), custom_call_target="tpu_custom_call" | custom-call | flops 16149000192 | tf_op jit(solution)/shard_map/pallas_call | solution.py:48
  130.1 1.5 collective-permute-start.20
  131.7 5.3 %collective-permute-done.20.refs_3_ = bf16[3,64,320]{2,1,0:T(8,128)(2,1)S(1)} collective-permute-done((bf16[3,64,320]{2,1,0:T(8,128)(2,1)}, bf16[3,64,320]{2,1,0:T(8,128)(2,1)S(1)}, u32[]{:S(2)}, u32[]{:S(2)}) %collective-permute-start.20) | collective-permute-done | bytes 122912 | tf_op jit(solution)/shard_map/ppermute | solution.py:130
  137.0 1.7 collective-permute-done.21.refs_4_
  139.7 1.6 shard_map.220
  141.2 4.1 %all-to-all-start.2 = ((bf16[8,3,80,128]{3,2,1,0:T(8,128)(2,1)}), bf16[8,3,80,128]{3,2,1,0:T(8,128)(2,1)S(1)}, u32[]{:S(2)}, u32[]{:S(2)}) async-start(bf16[8,3,80,128]{3,2,1,0:T(8,128)(2,1)} %shard_map.220), calls=%async_computation.2 | async-start | bytes 983040 | tf_op jit(solution)/shard_map/all_to_all | solution.py:134
  146.7 1.5 collective-permute-start.25
  150.3 9.6 %all-to-all-done.2.refs_2_ = bf16[8,3,80,128]{3,2,1,0:T(8,128)(2,1)S(1)} async-done(((bf16[8,3,80,128]{3,2,1,0:T(8,128)(2,1)}), bf16[8,3,80,128]{3,2,1,0:T(8,128)(2,1)S(1)}, u32[]{:S(2)}, u32[]{:S(2)}) %all-to-all-start.2) | async-done | bytes 491552 | tf_op jit(solution)/shard_map/all_to_all | solution.py:134
  160.6 14.7 %shard_map.221 = (bf16[8,11,80,128]{3,2,1,0:T(8,128)(2,1)}, f32[80,1]{1,0:T(8,128)}) custom-call(s32[2,8]{1,0:T(2,128)} %bitcast.29, bf16[8,11,80,128]{3,2,1,0:T(8,128)(2,1)} %copy-done, bf16[8,3,80,128]{3,2,1,0:T(8,128)(2,1)} %copy-done.37, f32[80,1]{1,0:T(8,128)} %copy.38.refs_3_, s32[1,2048]{1,0:T(1,128)} %copy-done.3, f32[80,2048]{1,0:T(8,128)} %copy-done.27, ...), custom_call_target="tpu_custom_call" | custom-call | flops 17302499328 | tf_op jit(solution)/shard_map/pallas_call | solution.py:48
  176.3 4.6 %all-to-all-start.3 = ((bf16[8,11,80,128]{3,2,1,0:T(8,128)(2,1)}), bf16[8,11,80,128]{3,2,1,0:T(8,128)(2,1)}, u32[]{:S(2)}, u32[]{:S(2)}) async-start(bf16[8,11,80,128]{3,2,1,0:T(8,128)(2,1)} %shard_map.222), calls=%async_computation.3 | async-start | bytes 3604480 | tf_op jit(solution)/shard_map/all_to_all | solution.py:134
  181.6 1.7 collective-permute-done.29.refs_0_
  184.4 1.1 collective-permute-done.32.refs_16_
  187.1 6.9 %shard_map.226 = (bf16[4,3,40,640]{3,2,1,0:T(8,128)(2,1)}, bf16[4,3,40,640]{3,2,1,0:T(8,128)(2,1)}, bf16[4,3,40,640]{3,2,1,0:T(8,128)(2,1)}, bf16[4,3,40,640]{3,2,1,0:T(8,128)(2,1)}) custom-call(s32[2,8]{1,0:T(2,128)} %bitcast.30, bf16[3,64,320]{2,1,0:T(8,128)(2,1)} %copy-done.2, bf16[3,64,320]{2,1,0:T(8,128)(2,1)} %copy-done.10, ...), custom_call_target="tpu_custom_call" | custom-call | flops 8074500096 | tf_op jit(solution)/shard_map/pallas_call | solution.py:48
  194.0 1.7 collective-permute-start.35
  195.7 1.5 collective-permute-start.36
  197.6 1.2 collective-permute-done.26
  198.8 1.5 collective-permute-start.27
  200.3 2.5 collective-permute-done.27
  203.4 14.4 %collective-permute-done.35.refs_3_ = bf16[4,3,40,640]{3,2,1,0:T(8,128)(2,1)S(1)} collective-permute-done((bf16[4,3,40,640]{3,2,1,0:T(8,128)(2,1)}, bf16[4,3,40,640]{3,2,1,0:T(8,128)(2,1)S(1)}, u32[]{:S(2)}, u32[]{:S(2)}) %collective-permute-start.35) | collective-permute-done | bytes 614432 | tf_op jit(solution)/shard_map/ppermute | solution.py:72
  217.8 7.4 %collective-permute-done.36.refs_4_ = bf16[4,3,40,640]{3,2,1,0:T(8,128)(2,1)S(1)} collective-permute-done((bf16[4,3,40,640]{3,2,1,0:T(8,128)(2,1)}, bf16[4,3,40,640]{3,2,1,0:T(8,128)(2,1)S(1)}, u32[]{:S(2)}, u32[]{:S(2)}) %collective-permute-start.36) | collective-permute-done | bytes 614432 | tf_op jit(solution)/shard_map/ppermute | solution.py:72
  225.2 1.1 copy-done.23
  226.3 1.1 copy-done.24
  228.2 1.2 collective-permute-start.40
  229.4 1.1 collective-permute-start.41
  230.5 10.2 %shard_map.228 = (f32[8,1280]{1,0:T(8,128)}, bf16[3,64,1280]{2,1,0:T(8,128)(2,1)}, bf16[3,64,1280]{2,1,0:T(8,128)(2,1)}, bf16[3,64,1280]{2,1,0:T(8,128)(2,1)}, b...) custom-call(s32[2,8]{1,0:T(2,128)} %bitcast.31, ...), custom_call_target="tpu_custom_call" | custom-call | flops 12688499712 | tf_op jit(solution)/shard_map/pallas_call | solution.py:48
  242.3 2.2 collective-permute-start.42
  244.8 1.9 collective-permute-start.45
  247.2 10.2 %collective-permute-done.42.refs_2_ = bf16[2,3,40,640]{3,2,1,0:T(8,128)(2,1)S(1)} collective-permute-done((bf16[2,3,40,640]{3,2,1,0:T(8,128)(2,1)S(1)}, bf16[2,3,40,640]{3,2,1,0:T(8,128)(2,1)S(1)}, u32[]{:S(2)}, u32[]{:S(2)}) %collective-permute-start.42) | collective-permute-done | bytes 307232 | tf_op jit(solution)/shard_map/ppermute | solution.py:72
  258.6 1.6 collective-permute-start.39
  260.1 11.6 %collective-permute-done.45.refs_4_ = bf16[4,1,128,640]{3,2,1,0:T(8,128)(2,1)S(1)} collective-permute-done((bf16[4,1,128,640]{3,2,1,0:T(8,128)(2,1)S(1)}, bf16[4,1,128,640]{3,2,1,0:T(8,128)(2,1)S(1)}, u32[]{:S(2)}, u32[]{:S(2)}) %collective-permute-start.45) | collective-permute-done | bytes 655392 | tf_op jit(solution)/shard_map/ppermute | solution.py:72
  274.0 1.8 collective-permute-start.46
  275.9 11.0 %collective-permute-done.48.refs_3_ = bf16[2,1,128,640]{3,2,1,0:T(8,128)(2,1)S(1)} collective-permute-done((bf16[2,1,128,640]{3,2,1,0:T(8,128)(2,1)S(1)}, bf16[2,1,128,640]{3,2,1,0:T(8,128)(2,1)S(1)}, u32[]{:S(2)}, u32[]{:S(2)}) %collective-permute-start.48) | collective-permute-done | bytes 327712 | tf_op jit(solution)/shard_map/ppermute | solution.py:72
  287.7 2.4 collective-permute-done.46.refs_3_
  290.1 6.9 %collective-permute-done.47.refs_4_ = bf16[2,3,40,640]{3,2,1,0:T(8,128)(2,1)S(1)} collective-permute-done((bf16[2,3,40,640]{3,2,1,0:T(8,128)(2,1)S(1)}, bf16[2,3,40,640]{3,2,1,0:T(8,128)(2,1)S(1)}, u32[]{:S(2)}, u32[]{:S(2)}) %collective-permute-start.47) | collective-permute-done | bytes 307232 | tf_op jit(solution)/shard_map/ppermute | solution.py:72
  297.8 1.9 shard_map.235.refs_3_
  301.5 6.4 %collective-permute-done.52.refs_3_ = bf16[4,3,40,640]{3,2,1,0:T(8,128)(2,1)S(1)} collective-permute-done((bf16[4,3,40,640]{3,2,1,0:T(8,128)(2,1)S(1)}, bf16[4,3,40,640]{3,2,1,0:T(8,128)(2,1)S(1)}, u32[]{:S(2)}, u32[]{:S(2)}) %collective-permute-start.52) | collective-permute-done | bytes 614432 | tf_op jit(solution)/shard_map/ppermute | solution.py:72
  307.8 4.8 %collective-permute-done.53.refs_4_ = bf16[4,3,40,640]{3,2,1,0:T(8,128)(2,1)S(1)} collective-permute-done((bf16[4,3,40,640]{3,2,1,0:T(8,128)(2,1)S(1)}, bf16[4,3,40,640]{3,2,1,0:T(8,128)(2,1)S(1)}, u32[]{:S(2)}, u32[]{:S(2)}) %collective-permute-start.53) | collective-permute-done | bytes 614432 | tf_op jit(solution)/shard_map/ppermute | solution.py:72
  312.6 3.1 shard_map.237
  316.2 1.4 copy-done.18
  318.4 2.0 collective-permute-start.55
  320.4 5.0 %collective-permute-done.54.refs_3_ = bf16[2,1,128,640]{3,2,1,0:T(8,128)(2,1)S(1)} collective-permute-done((bf16[2,1,128,640]{3,2,1,0:T(8,128)(2,1)S(1)}, bf16[2,1,128,640]{3,2,1,0:T(8,128)(2,1)S(1)}, u32[]{:S(2)}, u32[]{:S(2)}) %collective-permute-start.54) | collective-permute-done | bytes 327712 | tf_op jit(solution)/shard_map/ppermute | solution.py:72
  325.4 1.2 collective-permute-done.55.refs_4_
  327.3 2.4 collective-permute-start.56
  329.7 3.5 %collective-permute-start.57 = (bf16[4,1,128,640]{3,2,1,0:T(8,128)(2,1)S(1)}, bf16[4,1,128,640]{3,2,1,0:T(8,128)(2,1)S(1)}, u32[]{:S(2)}, u32[]{:S(2)}) collective-permute-start(bf16[4,1,128,640]{3,2,1,0:T(8,128)(2,1)S(1)} %get-tuple-element.137.refs_2_), channel_id=1, source_target_pairs={{0,8},{4,12},{8,0},{12,4},{16,24},{20,28},{24,16},{28,20},{1,9},{5... | collective-permute-start | bytes 1966088 | tf_op jit(solution)/shard_map/ppermute | solution.py:72
  333.7 1.5 collective-permute-start.59
  338.0 1.6 collective-permute-done.56.refs_3_
  339.6 2.1 collective-permute-done.57.refs_4_
  341.7 3.1 shard_map.240
  (271 shorter events, 39.5 us)
Async XLA Ops:
  0.6 14.4 %collective-permute-start.1 = (bf16[3,64,1280]{2,1,0:T(8,128)(2,1)}, bf16[3,64,1280]{2,1,0:T(8,128)(2,1)S(1)}, u32[]{:S(2)}, u32[]{:S(2)}) collective-permute-start(bf16[3,64,1280]{2,1,0:T(8,128)(2,1)} %refs_4_.1), channel_id=1, source_target_pairs={{0,2},{1,3},{2,0},{3,1},{4,6},{5,7},{6,4},{7,5},{8,10},{9,11},{10,... | collective-permute-start | bytes 1474568 | tf_op jit(solution)/shard_map/ppermute | solution.py:72
  3.6 13.2 %collective-permute-start = (bf16[3,64,1280]{2,1,0:T(8,128)(2,1)}, bf16[3,64,1280]{2,1,0:T(8,128)(2,1)S(1)}, u32[]{:S(2)}, u32[]{:S(2)}) collective-permute-start(bf16[3,64,1280]{2,1,0:T(8,128)(2,1)} %refs_4_.1), channel_id=1, source_target_pairs={{0,1},{1,0},{2,3},{3,2},{4,5},{5,4},{6,7},{7,6},{8,9},{9,8},{10,11... | collective-permute-start | bytes 1474568 | tf_op jit(solution)/shard_map/ppermute | solution.py:72
  15.1 1.9 collective-permute-start.2
  25.7 48.9 %all-to-all-start = ((bf16[8,11,80,128]{3,2,1,0:T(8,128)(2,1)}), bf16[8,11,80,128]{3,2,1,0:T(8,128)(2,1)S(1)}, u32[]{:S(2)}, u32[]{:S(2)}) async-start(bf16[8,11,80,128]{3,2,1,0:T(8,128)(2,1)} %get-tuple-element.76), calls=%async_computation | async-start | bytes 3604480 | tf_op jit(solution)/shard_map/all_to_all | solution.py:134
  32.2 3.8 %collective-permute-start.17 = (f32[1,320]{1,0:T(1,128)S(1)}, f32[1,320]{1,0:T(1,128)S(1)}, u32[]{:S(2)}, u32[]{:S(2)}) collective-permute-start(f32[1,320]{1,0:T(1,128)S(1)} %reshape.63.refs_17_), channel_id=1, source_target_pairs={{0,2},{1,3},{2,0},{3,1},{4,6},{5,7},{6,4},{7,5},{8,10},{9,11},{10,... | collective-permute-start | bytes 3848 | tf_op jit(solution)/shard_map/ppermute | solution.py:72
  33.8 3.6 %collective-permute-start.16 = (f32[1,320]{1,0:T(1,128)S(1)}, f32[1,320]{1,0:T(1,128)S(1)}, u32[]{:S(2)}, u32[]{:S(2)}) collective-permute-start(f32[1,320]{1,0:T(1,128)S(1)} %reshape.63.refs_17_), channel_id=1, source_target_pairs={{0,1},{1,0},{2,3},{3,2},{4,5},{5,4},{6,7},{7,6},{8,9},{9,8},{10,11... | collective-permute-start | bytes 3848 | tf_op jit(solution)/shard_map/ppermute | solution.py:72
  33.8 57.0 %collective-permute-start.11 = (bf16[320,1280]{1,0:T(8,128)(2,1)}, bf16[320,1280]{1,0:T(8,128)(2,1)}, u32[]{:S(2)}, u32[]{:S(2)}) collective-permute-start(bf16[320,1280]{1,0:T(8,128)(2,1)} %bitcast.5.refs_9_), channel_id=1, source_target_pairs={{0,2},{1,3},{2,0},{3,1},{4,6},{5,7},{6,4},{7,5},{8,10},{9,11},{10,... | collective-permute-start | bytes 2457608 | tf_op jit(solution)/shard_map/ppermute | solution.py:72
  34.3 66.0 %collective-permute-start.10 = (bf16[320,1280]{1,0:T(8,128)(2,1)}, bf16[320,1280]{1,0:T(8,128)(2,1)}, u32[]{:S(2)}, u32[]{:S(2)}) collective-permute-start(bf16[320,1280]{1,0:T(8,128)(2,1)} %bitcast.5.refs_9_), channel_id=1, source_target_pairs={{0,1},{1,0},{2,3},{3,2},{4,5},{5,4},{6,7},{7,6},{8,9},{9,8},{10,11... | collective-permute-start | bytes 2457608 | tf_op jit(solution)/shard_map/ppermute | solution.py:72
  34.5 56.3 %collective-permute-start.14 = (bf16[320,1280]{1,0:T(8,128)(2,1)}, bf16[320,1280]{1,0:T(8,128)(2,1)S(1)}, u32[]{:S(2)}, u32[]{:S(2)}) collective-permute-start(bf16[320,1280]{1,0:T(8,128)(2,1)} %refs_13_.1), channel_id=1, source_target_pairs={{0,2},{1,3},{2,0},{3,1},{4,6},{5,7},{6,4},{7,5},{8,10},{9,11},{10,... | collective-permute-start | bytes 2457608 | tf_op jit(solution)/shard_map/ppermute | solution.py:72
  36.0 55.3 %collective-permute-start.8 = (bf16[320,1280]{1,0:T(8,128)(2,1)}, bf16[320,1280]{1,0:T(8,128)(2,1)}, u32[]{:S(2)}, u32[]{:S(2)}) collective-permute-start(bf16[320,1280]{1,0:T(8,128)(2,1)} %refs_5_.1), channel_id=1, source_target_pairs={{0,2},{1,3},{2,0},{3,1},{4,6},{5,7},{6,4},{7,5},{8,10},{9,11},{10,... | collective-permute-start | bytes 2457608 | tf_op jit(solution)/shard_map/ppermute | solution.py:72
  37.3 62.9 %collective-permute-start.3 = (bf16[3,64,1280]{2,1,0:T(8,128)(2,1)}, bf16[3,64,1280]{2,1,0:T(8,128)(2,1)S(1)}, u32[]{:S(2)}, u32[]{:S(2)}) collective-permute-start(bf16[3,64,1280]{2,1,0:T(8,128)(2,1)} %refs_17_.1), channel_id=1, source_target_pairs={{0,2},{1,3},{2,0},{3,1},{4,6},{5,7},{6,4},{7,5},{8,10},{9,11},{10,... | collective-permute-start | bytes 1474568 | tf_op jit(solution)/shard_map/ppermute | solution.py:72
  86.8 17.9 %all-to-all-start.1 = ((bf16[8,3,80,128]{3,2,1,0:T(8,128)(2,1)}), bf16[8,3,80,128]{3,2,1,0:T(8,128)(2,1)S(1)}, u32[]{:S(2)}, u32[]{:S(2)}) async-start(bf16[8,3,80,128]{3,2,1,0:T(8,128)(2,1)} %get-tuple-element.77.refs_1_), calls=%async_computation.1 | async-start | bytes 983040 | tf_op jit(solution)/shard_map/all_to_all | solution.py:134
  90.8 10.0 %collective-permute-start.13 = (bf16[320,1280]{1,0:T(8,128)(2,1)}, bf16[320,1280]{1,0:T(8,128)(2,1)S(1)}, u32[]{:S(2)}, u32[]{:S(2)}) collective-permute-start(bf16[320,1280]{1,0:T(8,128)(2,1)} %refs_13_.1), channel_id=1, source_target_pairs={{0,1},{1,0},{2,3},{3,2},{4,5},{5,4},{6,7},{7,6},{8,9},{9,8},{10,11... | collective-permute-start | bytes 2457608 | tf_op jit(solution)/shard_map/ppermute | solution.py:72
  90.9 15.3 %collective-permute-start.7 = (bf16[320,1280]{1,0:T(8,128)(2,1)}, bf16[320,1280]{1,0:T(8,128)(2,1)}, u32[]{:S(2)}, u32[]{:S(2)}) collective-permute-start(bf16[320,1280]{1,0:T(8,128)(2,1)} %refs_5_.1), channel_id=1, source_target_pairs={{0,1},{1,0},{2,3},{3,2},{4,5},{5,4},{6,7},{7,6},{8,9},{9,8},{10,11... | collective-permute-start | bytes 2457608 | tf_op jit(solution)/shard_map/ppermute | solution.py:72
  91.4 16.5 %collective-permute-start.12 = (bf16[320,1280]{1,0:T(8,128)(2,1)}, bf16[320,1280]{1,0:T(8,128)(2,1)}, u32[]{:S(2)}, u32[]{:S(2)}) collective-permute-start(bf16[320,1280]{1,0:T(8,128)(2,1)} %shard_map.216.refs_11_), channel_id=1, source_target_pairs={{0,1},{1,0},{2,3},{3,2},{4,5},{5,4},{6,7},{7,6},{8,9},{9,8},{10,11... | collective-permute-start | bytes 2457608 | tf_op jit(solution)/shard_map/ppermute | solution.py:72
  100.3 7.9 %collective-permute-start.15 = (bf16[320,1280]{1,0:T(8,128)(2,1)S(1)}, bf16[320,1280]{1,0:T(8,128)(2,1)S(1)}, u32[]{:S(2)}, u32[]{:S(2)}) collective-permute-start(bf16[320,1280]{1,0:T(8,128)(2,1)S(1)} %copy-done.34), channel_id=1, source_target_pairs={{0,1},{1,0},{2,3},{3,2},{4,5},{5,4},{6,7},{7,6},{8,9},{9,8},{10,11... | collective-permute-start | bytes 2457608 | tf_op jit(solution)/shard_map/ppermute | solution.py:72
  100.3 7.9 %collective-permute-start.9 = (bf16[320,1280]{1,0:T(8,128)(2,1)}, bf16[320,1280]{1,0:T(8,128)(2,1)}, u32[]{:S(2)}, u32[]{:S(2)}) collective-permute-start(bf16[320,1280]{1,0:T(8,128)(2,1)} %shard_map.215.refs_7_), channel_id=1, source_target_pairs={{0,1},{1,0},{2,3},{3,2},{4,5},{5,4},{6,7},{7,6},{8,9},{9,8},{10,11... | collective-permute-start | bytes 2457608 | tf_op jit(solution)/shard_map/ppermute | solution.py:72
  100.8 5.5 %collective-permute-start.18 = (f32[1,320]{1,0:T(1,128)}, f32[1,320]{1,0:T(1,128)S(1)}, u32[]{:S(2)}, u32[]{:S(2)}) collective-permute-start(f32[1,320]{1,0:T(1,128)} %shard_map.218.refs_19_), channel_id=1, source_target_pairs={{0,1},{1,0},{2,3},{3,2},{4,5},{5,4},{6,7},{7,6},{8,9},{9,8},{10,11... | collective-permute-start | bytes 3848 | tf_op jit(solution)/shard_map/ppermute | solution.py:72
  106.2 2.0 collective-permute-start.4
  106.3 6.7 %collective-permute-start.5 = (bf16[3,64,320]{2,1,0:T(8,128)(2,1)S(1)}, bf16[3,64,320]{2,1,0:T(8,128)(2,1)S(1)}, u32[]{:S(2)}, u32[]{:S(2)}) collective-permute-start(bf16[3,64,320]{2,1,0:T(8,128)(2,1)S(1)} %get-tuple-element.80.refs_3_), channel_id=1, source_target_pairs={{0,2},{1,3},{2,0},{3,1},{4,6},{5,7},{6,4},{7,5},{8,10},{9,11},{10,... | collective-permute-start | bytes 368648 | tf_op jit(solution)/shard_map/ppermute | solution.py:130
  107.9 7.4 %collective-permute-start.6 = (bf16[3,64,320]{2,1,0:T(8,128)(2,1)S(1)}, bf16[3,64,320]{2,1,0:T(8,128)(2,1)S(1)}, u32[]{:S(2)}, u32[]{:S(2)}) collective-permute-start(bf16[3,64,320]{2,1,0:T(8,128)(2,1)S(1)} %get-tuple-element.81.refs_4_), channel_id=1, source_target_pairs={{0,3},{1,2},{2,1},{3,0},{4,7},{5,6},{6,5},{7,4},{8,11},{9,10},{10,... | collective-permute-start | bytes 368648 | tf_op jit(solution)/shard_map/ppermute | solution.py:130
  129.7 1.9 collective-permute-start.19
  130.1 6.9 %collective-permute-start.20 = (bf16[3,64,320]{2,1,0:T(8,128)(2,1)}, bf16[3,64,320]{2,1,0:T(8,128)(2,1)S(1)}, u32[]{:S(2)}, u32[]{:S(2)}) collective-permute-start(bf16[3,64,320]{2,1,0:T(8,128)(2,1)} %get-tuple-element.85), channel_id=1, source_target_pairs={{0,2},{1,3},{2,0},{3,1},{4,6},{5,7},{6,4},{7,5},{8,10},{9,11},{10,... | collective-permute-start | bytes 368648 | tf_op jit(solution)/shard_map/ppermute | solution.py:130
  131.6 7.1 %collective-permute-start.21 = (bf16[3,64,320]{2,1,0:T(8,128)(2,1)}, bf16[3,64,320]{2,1,0:T(8,128)(2,1)S(1)}, u32[]{:S(2)}, u32[]{:S(2)}) collective-permute-start(bf16[3,64,320]{2,1,0:T(8,128)(2,1)} %get-tuple-element.86), channel_id=1, source_target_pairs={{0,3},{1,2},{2,1},{3,0},{4,7},{5,6},{6,5},{7,4},{8,11},{9,10},{10,... | collective-permute-start | bytes 368648 | tf_op jit(solution)/shard_map/ppermute | solution.py:130
  141.2 18.6 %all-to-all-start.2 = ((bf16[8,3,80,128]{3,2,1,0:T(8,128)(2,1)}), bf16[8,3,80,128]{3,2,1,0:T(8,128)(2,1)S(1)}, u32[]{:S(2)}, u32[]{:S(2)}) async-start(bf16[8,3,80,128]{3,2,1,0:T(8,128)(2,1)} %shard_map.220), calls=%async_computation.2 | async-start | bytes 983040 | tf_op jit(solution)/shard_map/all_to_all | solution.py:134
  145.4 4.3 %collective-permute-start.22 = (bf16[2,192,320]{2,1,0:T(8,128)(2,1)S(1)}, bf16[2,192,320]{2,1,0:T(8,128)(2,1)S(1)}, u32[]{:S(2)}, u32[]{:S(2)}) collective-permute-start(bf16[2,192,320]{2,1,0:T(8,128)(2,1)S(1)} %copy-done.61), channel_id=1, source_target_pairs={{0,1},{1,0},{2,3},{3,2},{4,5},{5,4},{6,7},{7,6},{8,9},{9,8},{10,11... | collective-permute-start | bytes 737288 | tf_op jit(solution)/shard_map/ppermute | solution.py:130
  145.8 38.4 %collective-permute-start.33 = (bf16[3,64,1280]{2,1,0:T(8,128)(2,1)S(1)}, bf16[3,64,1280]{2,1,0:T(8,128)(2,1)}, u32[]{:S(2)}, u32[]{:S(2)}) collective-permute-start(bf16[3,64,1280]{2,1,0:T(8,128)(2,1)S(1)} %copy-done.51), channel_id=1, source_target_pairs={{0,1},{1,0},{2,3},{3,2},{4,5},{5,4},{6,7},{7,6},{8,9},{9,8},{10,11... | collective-permute-start | bytes 1474568 | tf_op jit(solution)/shard_map/ppermute | solution.py:72
  146.7 28.7 %collective-permute-start.25 = (bf16[3,64,1280]{2,1,0:T(8,128)(2,1)S(1)}, bf16[3,64,1280]{2,1,0:T(8,128)(2,1)S(1)}, u32[]{:S(2)}, u32[]{:S(2)}) collective-permute-start(bf16[3,64,1280]{2,1,0:T(8,128)(2,1)S(1)} %copy-done.52), channel_id=1, source_target_pairs={{0,2},{1,3},{2,0},{3,1},{4,6},{5,7},{6,4},{7,5},{8,10},{9,11},{10,... | collective-permute-start | bytes 1474568 | tf_op jit(solution)/shard_map/ppermute | solution.py:72
  148.2 27.1 %collective-permute-start.23 = (bf16[2,192,320]{2,1,0:T(8,128)(2,1)}, bf16[2,192,320]{2,1,0:T(8,128)(2,1)S(1)}, u32[]{:S(2)}, u32[]{:S(2)}) collective-permute-start(bf16[2,192,320]{2,1,0:T(8,128)(2,1)} %get-tuple-element.93), channel_id=1, source_target_pairs={{0,2},{1,3},{2,0},{3,1},{4,6},{5,7},{6,4},{7,5},{8,10},{9,11},{10,... | collective-permute-start | bytes 737288 | tf_op jit(solution)/shard_map/ppermute | solution.py:130
  148.7 26.6 %collective-permute-start.24 = (bf16[2,192,320]{2,1,0:T(8,128)(2,1)}, bf16[2,192,320]{2,1,0:T(8,128)(2,1)S(1)}, u32[]{:S(2)}, u32[]{:S(2)}) collective-permute-start(bf16[2,192,320]{2,1,0:T(8,128)(2,1)} %get-tuple-element.94), channel_id=1, source_target_pairs={{0,3},{1,2},{2,1},{3,0},{4,7},{5,6},{6,5},{7,4},{8,11},{9,10},{10,... | collective-permute-start | bytes 737288 | tf_op jit(solution)/shard_map/ppermute | solution.py:130
  149.6 33.7 %collective-permute-start.29 = (bf16[3,64,1280]{2,1,0:T(8,128)(2,1)}, bf16[3,64,1280]{2,1,0:T(8,128)(2,1)S(1)}, u32[]{:S(2)}, u32[]{:S(2)}) collective-permute-start(bf16[3,64,1280]{2,1,0:T(8,128)(2,1)} %get-tuple-element.101.refs_9_), channel_id=1, source_target_pairs={{0,2},{1,3},{2,0},{3,1},{4,6},{5,7},{6,4},{7,5},{8,10},{9,11},{10,... | collective-permute-start | bytes 1474568 | tf_op jit(solution)/shard_map/ppermute | solution.py:72
  176.3 54.2 %all-to-all-start.3 = ((bf16[8,11,80,128]{3,2,1,0:T(8,128)(2,1)}), bf16[8,11,80,128]{3,2,1,0:T(8,128)(2,1)}, u32[]{:S(2)}, u32[]{:S(2)}) async-start(bf16[8,11,80,128]{3,2,1,0:T(8,128)(2,1)} %shard_map.222), calls=%async_computation.3 | async-start | bytes 3604480 | tf_op jit(solution)/shard_map/all_to_all | solution.py:134
  181.0 3.2 collective-permute-start.34
  181.1 3.2 collective-permute-start.28
  181.5 2.9 collective-permute-start.31
  183.4 2.2 collective-permute-start.32
  184.2 2.1 collective-permute-start.30
  194.0 23.8 %collective-permute-start.35 = (bf16[4,3,40,640]{3,2,1,0:T(8,128)(2,1)}, bf16[4,3,40,640]{3,2,1,0:T(8,128)(2,1)S(1)}, u32[]{:S(2)}, u32[]{:S(2)}) collective-permute-start(bf16[4,3,40,640]{3,2,1,0:T(8,128)(2,1)} %get-tuple-element.104), channel_id=1, source_target_pairs={{0,4},{4,0},{8,12},{12,8},{16,20},{20,16},{24,28},{28,24},{1,5},{5... | collective-permute-start | bytes 1843208 | tf_op jit(solution)/shard_map/ppermute | solution.py:72
  195.7 29.5 %collective-permute-start.36 = (bf16[4,3,40,640]{3,2,1,0:T(8,128)(2,1)}, bf16[4,3,40,640]{3,2,1,0:T(8,128)(2,1)S(1)}, u32[]{:S(2)}, u32[]{:S(2)}) collective-permute-start(bf16[4,3,40,640]{3,2,1,0:T(8,128)(2,1)} %get-tuple-element.105), channel_id=1, source_target_pairs={{0,8},{4,12},{8,0},{12,4},{16,24},{20,28},{24,16},{28,20},{1,9},{5... | collective-permute-start | bytes 1843208 | tf_op jit(solution)/shard_map/ppermute | solution.py:72
  197.5 1.3 collective-permute-start.26
  198.8 4.0 %collective-permute-start.27 = (f32[8,1280]{1,0:T(8,128)S(1)}, f32[8,1280]{1,0:T(8,128)S(1)}, u32[]{:S(2)}, u32[]{:S(2)}) collective-permute-start(f32[8,1280]{1,0:T(8,128)S(1)} %add.56), channel_id=1, source_target_pairs={{0,2},{1,3},{2,0},{3,1},{4,6},{5,7},{6,4},{7,5},{8,10},{9,11},{10,... | collective-permute-start | bytes 122888 | tf_op jit(solution)/shard_map/ppermute | solution.py:72
  228.2 12.5 %collective-permute-start.40 = (bf16[2,3,40,640]{3,2,1,0:T(8,128)(2,1)S(1)}, bf16[2,3,40,640]{3,2,1,0:T(8,128)(2,1)S(1)}, u32[]{:S(2)}, u32[]{:S(2)}) collective-permute-start(bf16[2,3,40,640]{3,2,1,0:T(8,128)(2,1)S(1)} %get-tuple-element.106.refs_6_), channel_id=1, source_target_pairs={{0,8},{4,12},{8,0},{12,4},{16,24},{20,28},{24,16},{28,20},{1,9},{5... | collective-permute-start | bytes 921608 | tf_op jit(solution)/shard_map/ppermute | solution.py:72
  229.4 11.4 %collective-permute-start.41 = (bf16[2,3,40,640]{3,2,1,0:T(8,128)(2,1)S(1)}, bf16[2,3,40,640]{3,2,1,0:T(8,128)(2,1)S(1)}, u32[]{:S(2)}, u32[]{:S(2)}) collective-permute-start(bf16[2,3,40,640]{3,2,1,0:T(8,128)(2,1)S(1)} %get-tuple-element.114), channel_id=1, source_target_pairs={{0,4},{4,0},{8,12},{12,8},{16,20},{20,16},{24,28},{28,24},{1,5},{5... | collective-permute-start | bytes 921608 | tf_op jit(solution)/shard_map/ppermute | solution.py:72
  242.3 15.1 %collective-permute-start.42 = (bf16[2,3,40,640]{3,2,1,0:T(8,128)(2,1)S(1)}, bf16[2,3,40,640]{3,2,1,0:T(8,128)(2,1)S(1)}, u32[]{:S(2)}, u32[]{:S(2)}) collective-permute-start(bf16[2,3,40,640]{3,2,1,0:T(8,128)(2,1)S(1)} %get-tuple-element.117.refs_3_), channel_id=1, source_target_pairs={{0,16},{4,20},{8,24},{12,28},{16,0},{20,4},{24,8},{28,12},{1,17},{... | collective-permute-start | bytes 921608 | tf_op jit(solution)/shard_map/ppermute | solution.py:72
  244.5 15.6 %collective-permute-start.44 = (bf16[4,1,128,640]{3,2,1,0:T(8,128)(2,1)S(1)}, bf16[4,1,128,640]{3,2,1,0:T(8,128)(2,1)S(1)}, u32[]{:S(2)}, u32[]{:S(2)}) collective-permute-start(bf16[4,1,128,640]{3,2,1,0:T(8,128)(2,1)S(1)} %copy-done.50), channel_id=1, source_target_pairs={{0,4},{4,0},{8,12},{12,8},{16,20},{20,16},{24,28},{28,24},{1,5},{5... | collective-permute-start | bytes 1966088 | tf_op jit(solution)/shard_map/ppermute | solution.py:72
  244.8 26.9 %collective-permute-start.45 = (bf16[4,1,128,640]{3,2,1,0:T(8,128)(2,1)S(1)}, bf16[4,1,128,640]{3,2,1,0:T(8,128)(2,1)S(1)}, u32[]{:S(2)}, u32[]{:S(2)}) collective-permute-start(bf16[4,1,128,640]{3,2,1,0:T(8,128)(2,1)S(1)} %copy-done.49), channel_id=1, source_target_pairs={{0,8},{4,12},{8,0},{12,4},{16,24},{20,28},{24,16},{28,20},{1,9},{5... | collective-permute-start | bytes 1966088 | tf_op jit(solution)/shard_map/ppermute | solution.py:72
  246.7 11.4 %collective-permute-start.38 = (bf16[3,64,1280]{2,1,0:T(8,128)(2,1)S(1)}, bf16[3,64,1280]{2,1,0:T(8,128)(2,1)S(1)}, u32[]{:S(2)}, u32[]{:S(2)}) collective-permute-start(bf16[3,64,1280]{2,1,0:T(8,128)(2,1)S(1)} %copy-done.56), channel_id=1, source_target_pairs={{0,1},{1,0},{2,3},{3,2},{4,5},{5,4},{6,7},{7,6},{8,9},{9,8},{10,11... | collective-permute-start | bytes 1474568 | tf_op jit(solution)/shard_map/ppermute | solution.py:72
  246.7 51.1 %collective-permute-start.37 = (bf16[3,64,1280]{2,1,0:T(8,128)(2,1)S(1)}, bf16[3,64,1280]{2,1,0:T(8,128)(2,1)S(1)}, u32[]{:S(2)}, u32[]{:S(2)}) collective-permute-start(bf16[3,64,1280]{2,1,0:T(8,128)(2,1)S(1)} %copy-done.54), channel_id=1, source_target_pairs={{0,1},{1,0},{2,3},{3,2},{4,5},{5,4},{6,7},{7,6},{8,9},{9,8},{10,11... | collective-permute-start | bytes 1474568 | tf_op jit(solution)/shard_map/ppermute | solution.py:72
  258.0 15.4 %collective-permute-start.43 = (bf16[2,3,40,640]{3,2,1,0:T(8,128)(2,1)S(1)}, bf16[2,3,40,640]{3,2,1,0:T(8,128)(2,1)S(1)}, u32[]{:S(2)}, u32[]{:S(2)}) collective-permute-start(bf16[2,3,40,640]{3,2,1,0:T(8,128)(2,1)S(1)} %shard_map.230.refs_5_.refs_1_), channel_id=1, source_target_pairs={{0,16},{4,20},{8,24},{12,28},{16,0},{20,4},{24,8},{28,12},{1,17},{... | collective-permute-start | bytes 921608 | tf_op jit(solution)/shard_map/ppermute | solution.py:72
  258.6 39.2 %collective-permute-start.39 = (bf16[3,64,1280]{2,1,0:T(8,128)(2,1)S(1)}, bf16[3,64,1280]{2,1,0:T(8,128)(2,1)S(1)}, u32[]{:S(2)}, u32[]{:S(2)}) collective-permute-start(bf16[3,64,1280]{2,1,0:T(8,128)(2,1)S(1)} %add_convert_fusion), channel_id=1, source_target_pairs={{0,2},{1,3},{2,0},{3,1},{4,6},{5,7},{6,4},{7,5},{8,10},{9,11},{10,... | collective-permute-start | bytes 1474568 | tf_op jit(solution)/shard_map/ppermute | solution.py:72
  272.7 14.2 %collective-permute-start.48 = (bf16[2,1,128,640]{3,2,1,0:T(8,128)(2,1)S(1)}, bf16[2,1,128,640]{3,2,1,0:T(8,128)(2,1)S(1)}, u32[]{:S(2)}, u32[]{:S(2)}) collective-permute-start(bf16[2,1,128,640]{3,2,1,0:T(8,128)(2,1)S(1)} %get-tuple-element.122.refs_3_), channel_id=1, source_target_pairs={{0,8},{4,12},{8,0},{12,4},{16,24},{20,28},{24,16},{28,20},{1,9},{5... | collective-permute-start | bytes 983048 | tf_op jit(solution)/shard_map/ppermute | solution.py:72
  272.7 14.1 %collective-permute-start.49 = (bf16[2,1,128,640]{3,2,1,0:T(8,128)(2,1)S(1)}, bf16[2,1,128,640]{3,2,1,0:T(8,128)(2,1)S(1)}, u32[]{:S(2)}, u32[]{:S(2)}) collective-permute-start(bf16[2,1,128,640]{3,2,1,0:T(8,128)(2,1)S(1)} %get-tuple-element.127), channel_id=1, source_target_pairs={{0,4},{4,0},{8,12},{12,8},{16,20},{20,16},{24,28},{28,24},{1,5},{5... | collective-permute-start | bytes 983048 | tf_op jit(solution)/shard_map/ppermute | solution.py:72
  274.0 16.1 %collective-permute-start.46 = (bf16[2,3,40,640]{3,2,1,0:T(8,128)(2,1)S(1)}, bf16[2,3,40,640]{3,2,1,0:T(8,128)(2,1)S(1)}, u32[]{:S(2)}, u32[]{:S(2)}) collective-permute-start(bf16[2,3,40,640]{3,2,1,0:T(8,128)(2,1)S(1)} %get-tuple-element.123.refs_5_.refs_1_), channel_id=1, source_target_pairs={{0,8},{4,12},{8,0},{12,4},{16,24},{20,28},{24,16},{28,20},{1,9},{5... | collective-permute-start | bytes 921608 | tf_op jit(solution)/shard_map/ppermute | solution.py:72
  286.8 10.1 %collective-permute-start.47 = (bf16[2,3,40,640]{3,2,1,0:T(8,128)(2,1)S(1)}, bf16[2,3,40,640]{3,2,1,0:T(8,128)(2,1)S(1)}, u32[]{:S(2)}, u32[]{:S(2)}) collective-permute-start(bf16[2,3,40,640]{3,2,1,0:T(8,128)(2,1)S(1)} %get-tuple-element.124.refs_2_), channel_id=1, source_target_pairs={{0,4},{4,0},{8,12},{12,8},{16,20},{20,16},{24,28},{28,24},{1,5},{5... | collective-permute-start | bytes 921608 | tf_op jit(solution)/shard_map/ppermute | solution.py:72
  287.6 12.1 %collective-permute-start.50 = (bf16[2,1,128,640]{3,2,1,0:T(8,128)(2,1)S(1)}, bf16[2,1,128,640]{3,2,1,0:T(8,128)(2,1)S(1)}, u32[]{:S(2)}, u32[]{:S(2)}) collective-permute-start(bf16[2,1,128,640]{3,2,1,0:T(8,128)(2,1)S(1)} %get-tuple-element.128.refs_5_), channel_id=1, source_target_pairs={{0,16},{4,20},{8,24},{12,28},{16,0},{20,4},{24,8},{28,12},{1,17},{... | collective-permute-start | bytes 983048 | tf_op jit(solution)/shard_map/ppermute | solution.py:72
  297.6 10.2 %collective-permute-start.52 = (bf16[4,3,40,640]{3,2,1,0:T(8,128)(2,1)S(1)}, bf16[4,3,40,640]{3,2,1,0:T(8,128)(2,1)S(1)}, u32[]{:S(2)}, u32[]{:S(2)}) collective-permute-start(bf16[4,3,40,640]{3,2,1,0:T(8,128)(2,1)S(1)} %get-tuple-element.129.refs_7_.refs_1_), channel_id=1, source_target_pairs={{0,4},{4,0},{8,12},{12,8},{16,20},{20,16},{24,28},{28,24},{1,5},{5... | collective-permute-start | bytes 1843208 | tf_op jit(solution)/shard_map/ppermute | solution.py:72
  297.7 14.9 %collective-permute-start.53 = (bf16[4,3,40,640]{3,2,1,0:T(8,128)(2,1)S(1)}, bf16[4,3,40,640]{3,2,1,0:T(8,128)(2,1)S(1)}, u32[]{:S(2)}, u32[]{:S(2)}) collective-permute-start(bf16[4,3,40,640]{3,2,1,0:T(8,128)(2,1)S(1)} %get-tuple-element.132.refs_2_), channel_id=1, source_target_pairs={{0,8},{4,12},{8,0},{12,4},{16,24},{20,28},{24,16},{28,20},{1,9},{5... | collective-permute-start | bytes 1843208 | tf_op jit(solution)/shard_map/ppermute | solution.py:72
  301.4 14.8 %collective-permute-start.51 = (bf16[2,1,128,640]{3,2,1,0:T(8,128)(2,1)S(1)}, bf16[2,1,128,640]{3,2,1,0:T(8,128)(2,1)S(1)}, u32[]{:S(2)}, u32[]{:S(2)}) collective-permute-start(bf16[2,1,128,640]{3,2,1,0:T(8,128)(2,1)S(1)} %get-tuple-element.131.refs_5_.refs_1_), channel_id=1, source_target_pairs={{0,16},{4,20},{8,24},{12,28},{16,0},{20,4},{24,8},{28,12},{1,17},{... | collective-permute-start | bytes 983048 | tf_op jit(solution)/shard_map/ppermute | solution.py:72
  318.3 7.1 %collective-permute-start.54 = (bf16[2,1,128,640]{3,2,1,0:T(8,128)(2,1)S(1)}, bf16[2,1,128,640]{3,2,1,0:T(8,128)(2,1)S(1)}, u32[]{:S(2)}, u32[]{:S(2)}) collective-permute-start(bf16[2,1,128,640]{3,2,1,0:T(8,128)(2,1)S(1)} %get-tuple-element.134.refs_1_.refs_5_), channel_id=1, source_target_pairs={{0,8},{4,12},{8,0},{12,4},{16,24},{20,28},{24,16},{28,20},{1,9},{5... | collective-permute-start | bytes 983048 | tf_op jit(solution)/shard_map/ppermute | solution.py:72
  318.4 8.3 %collective-permute-start.55 = (bf16[2,1,128,640]{3,2,1,0:T(8,128)(2,1)S(1)}, bf16[2,1,128,640]{3,2,1,0:T(8,128)(2,1)S(1)}, u32[]{:S(2)}, u32[]{:S(2)}) collective-permute-start(bf16[2,1,128,640]{3,2,1,0:T(8,128)(2,1)S(1)} %get-tuple-element.135.refs_2_), channel_id=1, source_target_pairs={{0,4},{4,0},{8,12},{12,8},{16,20},{20,16},{24,28},{28,24},{1,5},{5... | collective-permute-start | bytes 983048 | tf_op jit(solution)/shard_map/ppermute | solution.py:72
  320.4 13.3 %collective-permute-start.58 = (f32[1,1280]{1,0:T(1,128)S(1)}, f32[1,1280]{1,0:T(1,128)S(1)}, u32[]{:S(2)}, u32[]{:S(2)}) collective-permute-start(f32[1,1280]{1,0:T(1,128)S(1)} %slice.46), channel_id=1, source_target_pairs={{0,1},{1,0},{2,3},{3,2},{4,5},{5,4},{6,7},{7,6},{8,9},{9,8},{10,11... | collective-permute-start | bytes 15368 | tf_op jit(solution)/shard_map/ppermute | solution.py:72
  327.3 12.2 %collective-permute-start.56 = (bf16[4,1,128,640]{3,2,1,0:T(8,128)(2,1)S(1)}, bf16[4,1,128,640]{3,2,1,0:T(8,128)(2,1)S(1)}, u32[]{:S(2)}, u32[]{:S(2)}) collective-permute-start(bf16[4,1,128,640]{3,2,1,0:T(8,128)(2,1)S(1)} %get-tuple-element.136.refs_1_.refs_5_), channel_id=1, source_target_pairs={{0,4},{4,0},{8,12},{12,8},{16,20},{20,16},{24,28},{28,24},{1,5},{5... | collective-permute-start | bytes 1966088 | tf_op jit(solution)/shard_map/ppermute | solution.py:72
  329.7 12.0 %collective-permute-start.57 = (bf16[4,1,128,640]{3,2,1,0:T(8,128)(2,1)S(1)}, bf16[4,1,128,640]{3,2,1,0:T(8,128)(2,1)S(1)}, u32[]{:S(2)}, u32[]{:S(2)}) collective-permute-start(bf16[4,1,128,640]{3,2,1,0:T(8,128)(2,1)S(1)} %get-tuple-element.137.refs_2_), channel_id=1, source_target_pairs={{0,8},{4,12},{8,0},{12,4},{16,24},{20,28},{24,16},{28,20},{1,9},{5... | collective-permute-start | bytes 1966088 | tf_op jit(solution)/shard_map/ppermute | solution.py:72
  333.7 3.7 %collective-permute-start.59 = (f32[1,1280]{1,0:T(1,128)S(1)}, f32[1,1280]{1,0:T(1,128)S(1)}, u32[]{:S(2)}, u32[]{:S(2)}) collective-permute-start(f32[1,1280]{1,0:T(1,128)S(1)} %get-tuple-element.141), channel_id=1, source_target_pairs={{0,2},{1,3},{2,0},{3,1},{4,6},{5,7},{6,4},{7,5},{8,10},{9,11},{10,... | collective-permute-start | bytes 15368 | tf_op jit(solution)/shard_map/ppermute | solution.py:72
  (68 other events, 739.3 us)

commit v4 on v3

--- a/solution.py
+++ b/solution.py
@@ -13,12 +13,14 @@
 base_rate = 1.442695041
 key_tile = 2048
 vmem_bytes = 60 * 1024 * 1024
-loop_tile = 1024
+loop_tile = 512
+full_bytes = 62 * 1024 * 1024
 spare_bytes = 36 * 1024 * 1024
 kernel_us = {
     "project_kernel": 7, "attend_kernel": 11, "middle_kernel": 14, "attend_back_kernel": 15, "grads_kernel": 7, "back_kernel": 11,
 }
-lead = 3
+round_order = "EEQEQEQQEQQ"
+first_share = 768
 ahead_rounds = 1
 flops_per_us = 1153500000
 bf16 = jnp.bfloat16
@@ -38,7 +40,7 @@
     return math.prod(rest) * -(-last // 128) * 128 * jnp.dtype(value.dtype).itemsize
 
 
-def call(kernel, out_shape, operands, scalars, scratch=(), tokens=(), weight=1):
+def call(kernel, out_shape, operands, scalars, scratch=(), tokens=(), weight=1, most=vmem_bytes):
     specs = [pl.BlockSpec(memory_space=pltpu.SMEM)]
     specs += [pl.BlockSpec(memory_space=pltpu.VMEM)] * len(operands)
     specs += [pl.BlockSpec(memory_space=pl.ANY)] * len(tokens)
@@ -51,7 +53,7 @@
         in_specs=specs,
         out_specs=tuple(pl.BlockSpec(memory_space=pltpu.VMEM) for _ in out_shape),
         scratch_shapes=list(scratch),
-        compiler_params=pltpu.CompilerParams(vmem_limit_bytes=min(vmem_bytes, room)),
+        compiler_params=pltpu.CompilerParams(vmem_limit_bytes=min(most, room)),
         cost_estimate=pl.CostEstimate(flops=int(weight * flops_per_us), bytes_accessed=0, transcendentals=0),
     )(scalars, *operands, *tokens)
 
@@ -140,10 +142,11 @@
 
 
 class Sums:
-    def __init__(self, size, kinds, rows, lanes, tail=0):
+    def __init__(self, size, kinds, rows, lanes, cut, tail=0):
         self.size, self.bits = size, bits_of(size)
         self.kinds, self.rows, self.tail = kinds, rows, tail
-        self.block = (1, kinds * rows + tail, lanes) if tail else (kinds, rows, lanes)
+        self.block = (1, kinds * rows + tail) if tail else (kinds, rows)
+        self.spans = [slice(0, cut), slice(cut, lanes)]
         first = list(range(self.bits))
         second = first[:]
         if self.bits > 1:
@@ -165,12 +168,18 @@
         return [(bit, streams, 1 << len(self.left(streams[0], step))) for bit, streams in found.items()]
 
     def shapes(self, step):
-        return [shape((len(streams) * count,) + self.block, bf16) for _, streams, count in self.groups(step)]
+        width = [span.stop - span.start for span in self.spans]
+        return [
+            shape((count,) + self.block + (sum(width[v] for v in streams),), bf16)
+            for _, streams, count in self.groups(step)
+        ]
 
     def at(self, refs, stream, step, index):
-        for ref, (_, streams, count) in zip(refs, self.groups(step)):
+        span = self.spans[stream]
+        for ref, (_, streams, _) in zip(refs, self.groups(step)):
             if stream in streams:
-                return ref.at[streams.index(stream) * count + index]
+                first = span.start if len(streams) > 1 else 0
+                return ref.at[index, :, :, first : first + span.stop - span.start]
 
     def deal(self, read, send_refs, keep_refs, step):
         me = lax.axis_index("context")
@@ -192,7 +201,7 @@
         summed = self.tail and step + 1 == self.bits
         outs = list(finals) if last else self.shapes(step + 1) * (2 if halving else 1)
         count, width = len(self.keep), len(outs)
-        lanes = self.block[2]
+        lanes = self.spans[1].stop
 
         def kernel(sc, *refs):
             keep, got = refs[:count], refs[count : 2 * count]
@@ -211,7 +220,7 @@
                     value = total(stream, 0)
                     self.at(out, stream, step + 1, 0)[...] = value.astype(bf16)
                     if summed:
-                        out[width][:, stream * lanes : (stream + 1) * lanes] = value[0, -self.tail :]
+                        out[width][:, self.spans[stream]] = value[0, -self.tail :]
                     continue
                 bit, left = self.bit(stream, step), self.left(stream, step)
                 place = sorted(left + [bit]).index(bit)
@@ -229,10 +238,10 @@
                         for kind in range(kinds):
                             to = out[kind] if width > 1 else out[0].at[kind]
                             part = value[0, kind * rows : (kind + 1) * rows] if self.tail else value[kind]
-                            to[span, stream * lanes : (stream + 1) * lanes] = part
+                            to[span, self.spans[stream]] = part
 
         if summed:
-            outs = outs + [shape((self.tail, 2 * lanes), f32)]
+            outs = outs + [shape((self.tail, lanes), f32)]
         operands = [*self.keep, *self.got]
         made = list(call(kernel, outs, operands, scalars, tokens=tokens, weight=8))
         self.step += 1
@@ -324,10 +333,10 @@
     ends, o_ref, outs, scratch = refs[:units], refs[units], refs[units + 1 : -4], refs[-4:]
     invert(sc, scratch[0])
     for i, plan in enumerate(plans):
-        attend_unit(plan, got_ref, ends[i], o_ref, outs[2 * i], outs[2 * i + 1], *scratch)
-
-
-def attend_unit(plan, got_ref, end_ref, o_ref, wide_ref, lse_ref, inverse_ref, k_ref, vt_ref, qt_ref):
+        attend_unit(plan, got_ref, ends[i], o_ref, outs[i], *scratch)
+
+
+def attend_unit(plan, got_ref, end_ref, o_ref, lse_ref, inverse_ref, k_ref, vt_ref, qt_ref):
     pieces, piece, dim, stride, q_parts, base, o_base = plan
     offset = lax.rem(lax.axis_index("context"), stride)
     seq = pieces * piece
@@ -387,7 +396,6 @@
             tiles = min(-(-last // loop_tile), seq // loop_tile)
             top, total, out = lax.fori_loop(0, tiles, tile, start)
         out = out / total
-        wide_ref[:, span] = out
         lse_ref[:, span] = top + jnp.log(total)
         for s in range(2):
             at, which = place(inverse_ref, (2 * i + s) * stride + offset)
@@ -396,17 +404,17 @@
 
 def attend_back_kernel(plans, sc, got_ref, do_ref, factor_ref, *refs):
     units = len(plans)
-    saved, d_ref, scale_ref, scratch = refs[: 3 * units], refs[3 * units], refs[3 * units + 1], refs[3 * units + 2 :]
+    o_ref, saved, (d_ref, scale_ref), scratch = refs[0], refs[1 : 1 + 2 * units], refs[1 + 2 * units : 3 + 2 * units], refs[3 + 2 * units :]
     scale = 0.0
     invert(sc, scratch[0])
     for i, plan in enumerate(plans):
-        own = saved[3 * i : 3 * i + 3]
-        scale = scale + attend_back_unit(plan, got_ref, do_ref, factor_ref, *own, d_ref, *scratch)
+        own = saved[2 * i : 2 * i + 2]
+        scale = scale + attend_back_unit(plan, got_ref, do_ref, factor_ref, o_ref, *own, d_ref, *scratch)
     scale_ref[...] = scale
 
 
 def attend_back_unit(
-    plan, got_ref, do_ref, factor_ref, end_ref, wide_ref, lse_ref, d_ref,
+    plan, got_ref, do_ref, factor_ref, o_ref, end_ref, lse_ref, d_ref,
     inverse_ref, k_ref, kt_ref, v_ref, qt_ref, q_ref, dot_ref, dor_ref, dk_ref, dv_ref,
 ):
     pieces, piece, dim, stride, q_parts, base, o_base = plan
@@ -446,7 +454,9 @@
         span = slice(i * wide, (i + 1) * wide)
         qt, q, do, dor = qt_ref[:, span], q_ref[span, :], dot_ref[:, span], dor_ref[span, :]
         end, lse = end_ref[:, span], lse_ref[:, span]
-        delta = jnp.sum(do[0:dim].astype(f32) * wide_ref[:, span], axis=0, keepdims=True)
+        owners = [place(inverse_ref, (2 * i + s) * stride + offset) for s in range(2)]
+        o = jnp.concatenate([o_ref[at, o_base + (which if q_parts == 2 else 0)] for at, which in owners], axis=1)
+        delta = jnp.sum(do[0:dim].astype(f32) * o.astype(f32), axis=0, keepdims=True)
         free, last = key_parts(i, stride, piece, seq)
 
         def visit(keys, masked_from):
@@ -599,8 +609,7 @@
 
 def deal_cuts(sums, cut_ref, out_refs):
     half = len(out_refs) // 2
-    lanes = sums.block[2]
-    read = lambda stream, index: cut_ref[index, :, :, stream * lanes : (stream + 1) * lanes]
+    read = lambda stream, index: cut_ref[index, :, :, sums.spans[stream]]
     sums.deal(read, out_refs[:half], out_refs[half:], 0)
 
 
@@ -713,9 +722,9 @@
     )
     got = swap_all(send, "context")
     plans = [(pieces, piece, dim, members, 2, 0, 0), (pieces, piece, dim, group, 1, 6, 2)]
-    o_send, main_wide, main_lse, last_wide, last_lse = call(
+    o_send, main_lse, last_lse = call(
         functools.partial(attend_kernel, plans),
-        [shape((size, 3, dim, piece), bf16)] + [shape((r, a), f32) for a in asked for r in (dim, 1)],
+        [shape((size, 3, dim, piece), bf16)] + [shape((1, a), f32) for a in asked],
         [got, main_end, last_end],
         scalars,
         [
@@ -760,9 +769,10 @@
     d_send, scale_sum = call(
         functools.partial(attend_back_kernel, plans),
         [shape((size, 11, dim, piece), bf16), shape((dim, 1), f32)],
-        [got, do_got, factor_col, main_end, main_wide, main_lse, last_end, last_wide, last_lse],
+        [got, do_got, factor_col, o_send, main_end, main_lse, last_end, last_lse],
         scalars,
-        [
+        most=vmem_bytes if seq <= key_tile else full_bytes,
+        scratch=[
             pltpu.SMEM((pieces,), jnp.int32),
             pltpu.VMEM((seq, 128), bf16), pltpu.VMEM((dim, min(seq, key_tile)), bf16), pltpu.VMEM((seq, 128), bf16),
             pltpu.VMEM((128, asked[0]), bf16), pltpu.VMEM((asked[0], 128), bf16),
@@ -772,9 +782,9 @@
     )
     n2_parts = spread_rows(n2, n2_first, "fsdp", spread, scale_sum)
     dy_parts = spread_rows(dy, dy_first, "fsdp", spread, scale_sum)
-    new_sums = lambda: Sums(size, 3, local // size, width // 2) if even_cuts else None
-    early = new_sums()
-    last = Sums(size, 3, local // size, width // 2, 8) if even_cuts else None
+    cut = width * first_share // 1280 // 128 * 128
+    new_sums = lambda tail: Sums(size, 3, local // size, width, cut, tail) if even_cuts else None
+    early, last = new_sums(0), new_sums(8)
     last_cut = (size, 1, 3 * local // size + 8, width) if even_cuts else (8, 128)
     dealt = early.shapes(0) * 2 if even_cuts else [cut_shape]
     cut_scratch = [pltpu.VMEM(cut_shape.shape, bf16)]
@@ -819,8 +829,8 @@
     qkv_kind = shape((3, local, width), f32)
     if even_cuts:
         last.start(made[: len(made) // 2], made[len(made) // 2 :])
-        order = ["early"] * (lead - ahead_rounds) + ["last", "early"] * (2 * early.bits - lead) + ["last"] * lead
-        order = [early if name == "early" else last for name in order]
+        order = round_order
+        order = [early if name == "E" else last for name in order]
         ends = {early: [shape((local, width), f32)] * 3, last: [qkv_kind]}
         seen = small
         for index, flow in enumerate(order):

time: 350 us -> 349 us (level)
  waiting for transfers between devices: 168 us -> 175 us
  starting transfers between devices: 63.7 us -> 56.8 us
    ppermute x51, waiting for transfers between devices: 104 us -> 112 us  [exchange(): return lax.ppermute(values, axis, [(i, i ^ 1 << bit) for i in range(size)])]
    ppermute x51, starting transfers between devices: 38.8 us -> 31.9 us  [exchange(): return lax.ppermute(values, axis, [(i, i ^ 1 << bit) for i in range(size)])]
    unnamed x139 -> x135, local copies, waits for them, and re-layouts: 16.6 us -> 14.7 us
  transfers between devices with their start and end apart: 64 -> 64, of which waited for: 33 -> 31; matrix products, arithmetic and copies ran while one was open for 5% -> 5% of each run, Pallas kernels for 16% -> 16%
where the time goes in v4:
time: 349 us; the launch traced here: 343 us
  waiting for transfers between devices  175 us (50%)
  Pallas kernels  79.9 us (23%)
  starting transfers between devices  56.8 us (16%)
  local copies, waits for them, and re-layouts  18.7 us (5%)
  other arithmetic  11 us (3%)
    ppermute x51, waiting for transfers between devices, exchange(): return lax.ppermute(values, axis, [(i, i ^ 1 << bit) for i in range(size)])  112 us
    pallas_call x21, Pallas kernels, call(): pl.pallas_call(lambda *refs: kernel(*refs[:used], *refs[used + len(tokens...  79.9 us
    all_to_all x4, waiting for transfers between devices, swap_all(): return lax.all_to_all(parts, axis, 0, 0, tiled=True)  48.6 us
    ppermute x51, starting transfers between devices, exchange(): return lax.ppermute(values, axis, [(i, i ^ 1 << bit) for i in range(size)])  31.9 us
    all_to_all x4, starting transfers between devices, swap_all(): return lax.all_to_all(parts, axis, 0, 0, tiled=True)  19.2 us
    unnamed x135, local copies, waits for them, and re-layouts  14.7 us
    ppermute x9, waiting for transfers between devices, swap_parts(): lax.ppermute(parts[k], axis, [(i, i ^ k) for i in range(size)])  14.1 us
    another operation x2, other arithmetic  7.21 us
  transfers between devices with their start and end apart: 64, of which 31 were waited for; matrix products, arithmetic and copies ran while one was open for 5% of the time, Pallas kernels for 16%

profile of v4, /device:TPU:0, one launch (start us, length us, event | category | flops | bytes accessed | tf_op | source)
XLA Modules:
  0.0 343.3 jit_solution(13789474425189026488)
XLA Ops:
  0.6 3.0 collective-permute-start.1
  4.6 7.0 %reduce-window.6 = s32[3,16,128]{2,1,0:T(8,128)S(1)} reduce-window(s32[3,16,128]{2,1,0:T(8,128)S(1)} %bitcast.49, s32[]{:T(128)} %constant.66.clone.1), window={size=1x1x128 pad=0_0x0_0x0_127}, to_apply=%region_0.1 | reduce-window | flops 780288 | bytes 49156 | tf_op jit(solution)/shard_map/reduce-window
  13.0 2.1 collective-permute-done.1.refs_3_
  17.7 1.0 copy-done.7
  19.4 6.3 %shard_map.212 = (bf16[3,256,1280]{2,1,0:T(8,128)(2,1)}, bf16[8,11,80,128]{3,2,1,0:T(8,128)(2,1)}) custom-call(s32[2,8]{1,0:T(2,128)S(1)} %bitcast.32, bf16[3,64,1280]{2,1,0:T(8,128)(2,1)S(1)} %copy-done.7, bf16[3,64,1280]{2,1,0:T(8,128)(2,1)S(1)} %collective-permute-done.refs_2_, bf16[3,64,1280]{2,1,0:T(8,128)(2,1)} %copy-done.53, ...), custom_call_target="tpu_custom_call" | custom-call | flops 8074500096 | tf_op jit(solution)/shard_map/pallas_call | solution.py:50
  25.7 6.4 %all-to-all-start = ((bf16[8,11,80,128]{3,2,1,0:T(8,128)(2,1)}), bf16[8,11,80,128]{3,2,1,0:T(8,128)(2,1)S(1)}, u32[]{:S(2)}, u32[]{:S(2)}) async-start(bf16[8,11,80,128]{3,2,1,0:T(8,128)(2,1)} %get-tuple-element.74), calls=%async_computation | async-start | bytes 3604480 | tf_op jit(solution)/shard_map/all_to_all | solution.py:136
  32.2 1.6 collective-permute-start.17
  34.5 1.5 collective-permute-start.14
  36.0 1.3 collective-permute-start.8
  38.0 36.6 %all-to-all-done.refs_1_ = bf16[8,11,80,128]{3,2,1,0:T(8,128)(2,1)S(1)} async-done(((bf16[8,11,80,128]{3,2,1,0:T(8,128)(2,1)}), bf16[8,11,80,128]{3,2,1,0:T(8,128)(2,1)S(1)}, u32[]{:S(2)}, u32[]{:S(2)}) %all-to-all-start) | async-done | bytes 1802272 | tf_op jit(solution)/shard_map/all_to_all | solution.py:136
  74.6 10.6 %shard_map.213 = (bf16[8,3,80,128]{3,2,1,0:T(8,128)(2,1)}, f32[1,2048]{1,0:T(1,128)S(1)}, f32[1,1024]{1,0:T(1,128)S(1)}) custom-call(s32[2,8]{1,0:T(2,128)S(1)} %bitcast.33, bf16[8,11,80,128]{3,2,1,0:T(8,128)(2,1)S(1)} %all-to-all-done.refs_1_, s32[1,2048]{1,0:T(1,128)S(1)} %constant_dynamic-slice_fusion.refs_9_.refs_2_.refs_5_, ...), custom_call_target="tpu_custom_call" | custom-call | flops 12688499712 | tf_op jit(solution)/shard_map/pallas_call | solution.py:50
  85.3 3.9 %all-to-all-start.1 = ((bf16[8,3,80,128]{3,2,1,0:T(8,128)(2,1)}), bf16[8,3,80,128]{3,2,1,0:T(8,128)(2,1)S(1)}, u32[]{:S(2)}, u32[]{:S(2)}) async-start(bf16[8,3,80,128]{3,2,1,0:T(8,128)(2,1)} %get-tuple-element.75.refs_1_.refs_4_), calls=%async_computation.1 | async-start | bytes 983040 | tf_op jit(solution)/shard_map/all_to_all | solution.py:136
  90.2 10.0 %collective-permute-done.3.refs_2_.refs_0_ = bf16[3,64,1280]{2,1,0:T(8,128)(2,1)S(1)} collective-permute-done((bf16[3,64,1280]{2,1,0:T(8,128)(2,1)}, bf16[3,64,1280]{2,1,0:T(8,128)(2,1)S(1)}, u32[]{:S(2)}, u32[]{:S(2)}) %collective-permute-start.3) | collective-permute-done | bytes 491552 | tf_op jit(solution)/shard_map/ppermute | solution.py:74
  100.9 2.2 all-to-all-done.1.refs_1_
  104.7 1.6 collective-permute-start.5
  106.6 4.8 %collective-permute-done.5.refs_3_ = bf16[3,64,320]{2,1,0:T(8,128)(2,1)S(1)} collective-permute-done((bf16[3,64,320]{2,1,0:T(8,128)(2,1)S(1)}, bf16[3,64,320]{2,1,0:T(8,128)(2,1)S(1)}, u32[]{:S(2)}, u32[]{:S(2)}) %collective-permute-start.5) | collective-permute-done | bytes 122912 | tf_op jit(solution)/shard_map/ppermute | solution.py:132
  111.4 2.2 collective-permute-done.6.refs_4_
  114.3 13.8 %shard_map.219 = (bf16[3,64,1280]{2,1,0:T(8,128)(2,1)}, f32[3,64,1280]{2,1,0:T(8,128)}, bf16[3,64,1280]{2,1,0:T(8,128)(2,1)}, bf16[3,64,1280]{2,1,0:T(8,128)(2,1...) custom-call(s32[2,8]{1,0:T(2,128)} %bitcast.28, ...), custom_call_target="tpu_custom_call" | custom-call | flops 16149000192 | tf_op jit(solution)/shard_map/pallas_call | solution.py:50
  128.5 1.5 collective-permute-start.20
  130.1 5.3 %collective-permute-done.20.refs_3_ = bf16[3,64,320]{2,1,0:T(8,128)(2,1)S(1)} collective-permute-done((bf16[3,64,320]{2,1,0:T(8,128)(2,1)}, bf16[3,64,320]{2,1,0:T(8,128)(2,1)S(1)}, u32[]{:S(2)}, u32[]{:S(2)}) %collective-permute-start.20) | collective-permute-done | bytes 122912 | tf_op jit(solution)/shard_map/ppermute | solution.py:132
  135.4 1.7 collective-permute-done.21.refs_4_
  138.0 1.6 shard_map.220
  139.6 4.2 %all-to-all-start.2 = ((bf16[8,3,80,128]{3,2,1,0:T(8,128)(2,1)}), bf16[8,3,80,128]{3,2,1,0:T(8,128)(2,1)S(1)}, u32[]{:S(2)}, u32[]{:S(2)}) async-start(bf16[8,3,80,128]{3,2,1,0:T(8,128)(2,1)} %shard_map.220), calls=%async_computation.2 | async-start | bytes 983040 | tf_op jit(solution)/shard_map/all_to_all | solution.py:136
  145.2 1.3 collective-permute-start.25
  148.7 9.7 %all-to-all-done.2.refs_2_ = bf16[8,3,80,128]{3,2,1,0:T(8,128)(2,1)S(1)} async-done(((bf16[8,3,80,128]{3,2,1,0:T(8,128)(2,1)}), bf16[8,3,80,128]{3,2,1,0:T(8,128)(2,1)S(1)}, u32[]{:S(2)}, u32[]{:S(2)}) %all-to-all-start.2) | async-done | bytes 491552 | tf_op jit(solution)/shard_map/all_to_all | solution.py:136
  159.2 14.6 %shard_map.221 = (bf16[8,11,80,128]{3,2,1,0:T(8,128)(2,1)}, f32[80,1]{1,0:T(8,128)}) custom-call(s32[2,8]{1,0:T(2,128)} %bitcast.29, bf16[8,11,80,128]{3,2,1,0:T(8,128)(2,1)} %copy-done, bf16[8,3,80,128]{3,2,1,0:T(8,128)(2,1)} %copy-done.35, f32[80,1]{1,0:T(8,128)} %copy.38.refs_3_, bf16[8,3,80,128]{3,2,1,0:T(8,128)(2,1)} %get-tuple-element.75.refs_1_.refs_4_, ...), custom_call_target="tpu_custom_call" | custom-call | flops 17302499328 | tf_op jit(solution)/shard_map/pallas_call | solution.py:50
  174.8 4.6 %all-to-all-start.3 = ((bf16[8,11,80,128]{3,2,1,0:T(8,128)(2,1)}), bf16[8,11,80,128]{3,2,1,0:T(8,128)(2,1)}, u32[]{:S(2)}, u32[]{:S(2)}) async-start(bf16[8,11,80,128]{3,2,1,0:T(8,128)(2,1)} %shard_map.222), calls=%async_computation.3 | async-start | bytes 3604480 | tf_op jit(solution)/shard_map/all_to_all | solution.py:136
  180.1 1.8 collective-permute-done.29.refs_0_
  182.9 1.2 collective-permute-done.32.refs_16_
  185.6 6.9 %shard_map.226 = (bf16[4,3,40,768]{3,2,1,0:T(8,128)(2,1)}, bf16[4,3,40,512]{3,2,1,0:T(8,128)(2,1)}, bf16[4,3,40,768]{3,2,1,0:T(8,128)(2,1)}, bf16[4,3,40,512]{3,2,1,0:T(8,128)(2,1)}) custom-call(s32[2,8]{1,0:T(2,128)} %bitcast.30, bf16[3,64,320]{2,1,0:T(8,128)(2,1)} %copy-done.2, bf16[3,64,320]{2,1,0:T(8,128)(2,1)} %copy-done.10, ...), custom_call_target="tpu_custom_call" | custom-call | flops 8074500096 | tf_op jit(solution)/shard_map/pallas_call | solution.py:50
  192.5 1.8 collective-permute-start.35
  194.3 1.5 collective-permute-start.36
  196.2 1.2 collective-permute-done.26
  197.4 1.3 collective-permute-start.27
  198.6 2.7 collective-permute-done.27
  202.0 18.2 %collective-permute-done.36.refs_4_ = bf16[4,3,40,512]{3,2,1,0:T(8,128)(2,1)S(1)} collective-permute-done((bf16[4,3,40,512]{3,2,1,0:T(8,128)(2,1)}, bf16[4,3,40,512]{3,2,1,0:T(8,128)(2,1)S(1)}, u32[]{:S(2)}, u32[]{:S(2)}) %collective-permute-start.36) | collective-permute-done | bytes 491552 | tf_op jit(solution)/shard_map/ppermute | solution.py:74
  220.2 1.1 copy-done.23
  221.3 1.0 copy-done.24
  223.3 2.6 collective-permute-start.40
  226.7 10.3 %shard_map.228 = (f32[8,1280]{1,0:T(8,128)}, bf16[3,64,1280]{2,1,0:T(8,128)(2,1)}, bf16[3,64,1280]{2,1,0:T(8,128)(2,1)}, bf16[3,64,1280]{2,1,0:T(8,128)(2,1)}, b...) custom-call(s32[2,8]{1,0:T(2,128)} %bitcast.31, ...), custom_call_target="tpu_custom_call" | custom-call | flops 12688499712 | tf_op jit(solution)/shard_map/pallas_call | solution.py:50
  238.5 2.1 collective-permute-start.42
  240.6 1.3 collective-permute-start.44
  241.8 0.9 collective-permute-start.45
  243.3 10.4 %collective-permute-done.42.refs_2_ = bf16[1,3,40,1280]{3,2,1,0:T(8,128)(2,1)S(1)} collective-permute-done((bf16[1,3,40,1280]{3,2,1,0:T(8,128)(2,1)S(1)}, bf16[1,3,40,1280]{3,2,1,0:T(8,128)(2,1)S(1)}, u32[]{:S(2)}, u32[]{:S(2)}) %collective-permute-start.42) | collective-permute-done | bytes 307232 | tf_op jit(solution)/shard_map/ppermute | solution.py:74
  254.8 1.1 collective-permute-start.39
  256.0 6.1 %collective-permute-done.45.refs_4_ = bf16[4,1,128,512]{3,2,1,0:T(8,128)(2,1)S(1)} collective-permute-done((bf16[4,1,128,512]{3,2,1,0:T(8,128)(2,1)S(1)}, bf16[4,1,128,512]{3,2,1,0:T(8,128)(2,1)S(1)}, u32[]{:S(2)}, u32[]{:S(2)}) %collective-permute-start.45) | collective-permute-done | bytes 524320 | tf_op jit(solution)/shard_map/ppermute | solution.py:74
  263.0 1.2 collective-permute-start.49
  264.2 6.5 %collective-permute-done.43.refs_2_ = bf16[1,3,40,1280]{3,2,1,0:T(8,128)(2,1)S(1)} collective-permute-done((bf16[1,3,40,1280]{3,2,1,0:T(8,128)(2,1)S(1)}, bf16[1,3,40,1280]{3,2,1,0:T(8,128)(2,1)S(1)}, u32[]{:S(2)}, u32[]{:S(2)}) %collective-permute-start.43) | collective-permute-done | bytes 307232 | tf_op jit(solution)/shard_map/ppermute | solution.py:74
  271.4 1.7 collective-permute-start.47
  273.0 6.1 %collective-permute-done.48.refs_3_ = bf16[2,1,128,768]{3,2,1,0:T(8,128)(2,1)S(1)} collective-permute-done((bf16[2,1,128,768]{3,2,1,0:T(8,128)(2,1)S(1)}, bf16[2,1,128,768]{3,2,1,0:T(8,128)(2,1)S(1)}, u32[]{:S(2)}, u32[]{:S(2)}) %collective-permute-start.48) | collective-permute-done | bytes 393248 | tf_op jit(solution)/shard_map/ppermute | solution.py:74
  280.0 7.3 %collective-permute-done.46.refs_3_ = bf16[2,3,40,768]{3,2,1,0:T(8,128)(2,1)S(1)} collective-permute-done((bf16[2,3,40,768]{3,2,1,0:T(8,128)(2,1)S(1)}, bf16[2,3,40,768]{3,2,1,0:T(8,128)(2,1)S(1)}, u32[]{:S(2)}, u32[]{:S(2)}) %collective-permute-start.46) | collective-permute-done | bytes 368672 | tf_op jit(solution)/shard_map/ppermute | solution.py:74
  288.0 1.9 shard_map.235.refs_3_
  289.9 9.4 %collective-permute-done.50.refs_2_ = bf16[1,1,128,1280]{3,2,1,0:T(8,128)(2,1)S(1)} collective-permute-done((bf16[1,1,128,1280]{3,2,1,0:T(8,128)(2,1)S(1)}, bf16[1,1,128,1280]{3,2,1,0:T(8,128)(2,1)S(1)}, u32[]{:S(2)}, u32[]{:S(2)}) %collective-permute-start.50) | collective-permute-done | bytes 327712 | tf_op jit(solution)/shard_map/ppermute | solution.py:74
  299.3 1.0 copy-done.19
  301.3 7.8 %collective-permute-done.51.refs_2_ = bf16[1,1,128,1280]{3,2,1,0:T(8,128)(2,1)S(1)} collective-permute-done((bf16[1,1,128,1280]{3,2,1,0:T(8,128)(2,1)S(1)}, bf16[1,1,128,1280]{3,2,1,0:T(8,128)(2,1)S(1)}, u32[]{:S(2)}, u32[]{:S(2)}) %collective-permute-start.51) | collective-permute-done | bytes 327712 | tf_op jit(solution)/shard_map/ppermute | solution.py:74
  309.9 8.6 %collective-permute-done.55.refs_4_ = bf16[4,3,40,512]{3,2,1,0:T(8,128)(2,1)S(1)} collective-permute-done((bf16[4,3,40,512]{3,2,1,0:T(8,128)(2,1)S(1)}, bf16[4,3,40,512]{3,2,1,0:T(8,128)(2,1)S(1)}, u32[]{:S(2)}, u32[]{:S(2)}) %collective-permute-start.55) | collective-permute-done | bytes 491552 | tf_op jit(solution)/shard_map/ppermute | solution.py:74
  318.5 3.1 shard_map.238
  321.7 1.1 collective-permute-done.52.refs_3_
  322.7 1.4 copy-done.18
  324.8 1.0 collective-permute-start.56
  328.9 1.2 collective-permute-done.59
  330.7 5.6 %collective-permute-done.57.refs_4_ = bf16[4,1,128,512]{3,2,1,0:T(8,128)(2,1)S(1)} collective-permute-done((bf16[4,1,128,512]{3,2,1,0:T(8,128)(2,1)S(1)}, bf16[4,1,128,512]{3,2,1,0:T(8,128)(2,1)S(1)}, u32[]{:S(2)}, u32[]{:S(2)}) %collective-permute-start.57) | collective-permute-done | bytes 524320 | tf_op jit(solution)/shard_map/ppermute | solution.py:74
  336.4 3.6 %collective-permute-done.56.refs_3_ = bf16[4,1,128,768]{3,2,1,0:T(8,128)(2,1)S(1)} collective-permute-done((bf16[4,1,128,768]{3,2,1,0:T(8,128)(2,1)S(1)}, bf16[4,1,128,768]{3,2,1,0:T(8,128)(2,1)S(1)}, u32[]{:S(2)}, u32[]{:S(2)}) %collective-permute-start.56) | collective-permute-done | bytes 786464 | tf_op jit(solution)/shard_map/ppermute | solution.py:74
  340.0 3.1 shard_map.240
  (267 shorter events, 35.8 us)
Async XLA Ops:
  0.6 14.4 %collective-permute-start.1 = (bf16[3,64,1280]{2,1,0:T(8,128)(2,1)}, bf16[3,64,1280]{2,1,0:T(8,128)(2,1)S(1)}, u32[]{:S(2)}, u32[]{:S(2)}) collective-permute-start(bf16[3,64,1280]{2,1,0:T(8,128)(2,1)} %refs_4_.1), channel_id=1, source_target_pairs={{0,2},{1,3},{2,0},{3,1},{4,6},{5,7},{6,4},{7,5},{8,10},{9,11},{10,... | collective-permute-start | bytes 1474568 | tf_op jit(solution)/shard_map/ppermute | solution.py:74
  3.6 13.2 %collective-permute-start = (bf16[3,64,1280]{2,1,0:T(8,128)(2,1)}, bf16[3,64,1280]{2,1,0:T(8,128)(2,1)S(1)}, u32[]{:S(2)}, u32[]{:S(2)}) collective-permute-start(bf16[3,64,1280]{2,1,0:T(8,128)(2,1)} %refs_4_.1), channel_id=1, source_target_pairs={{0,1},{1,0},{2,3},{3,2},{4,5},{5,4},{6,7},{7,6},{8,9},{9,8},{10,11... | collective-permute-start | bytes 1474568 | tf_op jit(solution)/shard_map/ppermute | solution.py:74
  15.1 1.9 collective-permute-start.2
  25.7 48.9 %all-to-all-start = ((bf16[8,11,80,128]{3,2,1,0:T(8,128)(2,1)}), bf16[8,11,80,128]{3,2,1,0:T(8,128)(2,1)S(1)}, u32[]{:S(2)}, u32[]{:S(2)}) async-start(bf16[8,11,80,128]{3,2,1,0:T(8,128)(2,1)} %get-tuple-element.74), calls=%async_computation | async-start | bytes 3604480 | tf_op jit(solution)/shard_map/all_to_all | solution.py:136
  32.2 3.8 %collective-permute-start.17 = (f32[1,320]{1,0:T(1,128)S(1)}, f32[1,320]{1,0:T(1,128)S(1)}, u32[]{:S(2)}, u32[]{:S(2)}) collective-permute-start(f32[1,320]{1,0:T(1,128)S(1)} %reshape.63.refs_17_), channel_id=1, source_target_pairs={{0,2},{1,3},{2,0},{3,1},{4,6},{5,7},{6,4},{7,5},{8,10},{9,11},{10,... | collective-permute-start | bytes 3848 | tf_op jit(solution)/shard_map/ppermute | solution.py:74
  33.7 3.6 %collective-permute-start.16 = (f32[1,320]{1,0:T(1,128)S(1)}, f32[1,320]{1,0:T(1,128)S(1)}, u32[]{:S(2)}, u32[]{:S(2)}) collective-permute-start(f32[1,320]{1,0:T(1,128)S(1)} %reshape.63.refs_17_), channel_id=1, source_target_pairs={{0,1},{1,0},{2,3},{3,2},{4,5},{5,4},{6,7},{7,6},{8,9},{9,8},{10,11... | collective-permute-start | bytes 3848 | tf_op jit(solution)/shard_map/ppermute | solution.py:74
  33.7 55.4 %collective-permute-start.11 = (bf16[320,1280]{1,0:T(8,128)(2,1)}, bf16[320,1280]{1,0:T(8,128)(2,1)}, u32[]{:S(2)}, u32[]{:S(2)}) collective-permute-start(bf16[320,1280]{1,0:T(8,128)(2,1)} %bitcast.5.refs_9_), channel_id=1, source_target_pairs={{0,2},{1,3},{2,0},{3,1},{4,6},{5,7},{6,4},{7,5},{8,10},{9,11},{10,... | collective-permute-start | bytes 2457608 | tf_op jit(solution)/shard_map/ppermute | solution.py:74
  34.3 66.0 %collective-permute-start.10 = (bf16[320,1280]{1,0:T(8,128)(2,1)}, bf16[320,1280]{1,0:T(8,128)(2,1)}, u32[]{:S(2)}, u32[]{:S(2)}) collective-permute-start(bf16[320,1280]{1,0:T(8,128)(2,1)} %bitcast.5.refs_9_), channel_id=1, source_target_pairs={{0,1},{1,0},{2,3},{3,2},{4,5},{5,4},{6,7},{7,6},{8,9},{9,8},{10,11... | collective-permute-start | bytes 2457608 | tf_op jit(solution)/shard_map/ppermute | solution.py:74
  34.5 54.8 %collective-permute-start.14 = (bf16[320,1280]{1,0:T(8,128)(2,1)}, bf16[320,1280]{1,0:T(8,128)(2,1)S(1)}, u32[]{:S(2)}, u32[]{:S(2)}) collective-permute-start(bf16[320,1280]{1,0:T(8,128)(2,1)} %refs_13_.1), channel_id=1, source_target_pairs={{0,2},{1,3},{2,0},{3,1},{4,6},{5,7},{6,4},{7,5},{8,10},{9,11},{10,... | collective-permute-start | bytes 2457608 | tf_op jit(solution)/shard_map/ppermute | solution.py:74
  36.0 54.2 %collective-permute-start.8 = (bf16[320,1280]{1,0:T(8,128)(2,1)}, bf16[320,1280]{1,0:T(8,128)(2,1)}, u32[]{:S(2)}, u32[]{:S(2)}) collective-permute-start(bf16[320,1280]{1,0:T(8,128)(2,1)} %refs_5_.1), channel_id=1, source_target_pairs={{0,2},{1,3},{2,0},{3,1},{4,6},{5,7},{6,4},{7,5},{8,10},{9,11},{10,... | collective-permute-start | bytes 2457608 | tf_op jit(solution)/shard_map/ppermute | solution.py:74
  37.3 62.9 %collective-permute-start.3 = (bf16[3,64,1280]{2,1,0:T(8,128)(2,1)}, bf16[3,64,1280]{2,1,0:T(8,128)(2,1)S(1)}, u32[]{:S(2)}, u32[]{:S(2)}) collective-permute-start(bf16[3,64,1280]{2,1,0:T(8,128)(2,1)} %refs_17_.1), channel_id=1, source_target_pairs={{0,2},{1,3},{2,0},{3,1},{4,6},{5,7},{6,4},{7,5},{8,10},{9,11},{10,... | collective-permute-start | bytes 1474568 | tf_op jit(solution)/shard_map/ppermute | solution.py:74
  85.3 17.8 %all-to-all-start.1 = ((bf16[8,3,80,128]{3,2,1,0:T(8,128)(2,1)}), bf16[8,3,80,128]{3,2,1,0:T(8,128)(2,1)S(1)}, u32[]{:S(2)}, u32[]{:S(2)}) async-start(bf16[8,3,80,128]{3,2,1,0:T(8,128)(2,1)} %get-tuple-element.75.refs_1_.refs_4_), calls=%async_computation.1 | async-start | bytes 983040 | tf_op jit(solution)/shard_map/all_to_all | solution.py:136
  89.2 11.6 %collective-permute-start.13 = (bf16[320,1280]{1,0:T(8,128)(2,1)}, bf16[320,1280]{1,0:T(8,128)(2,1)S(1)}, u32[]{:S(2)}, u32[]{:S(2)}) collective-permute-start(bf16[320,1280]{1,0:T(8,128)(2,1)} %refs_13_.1), channel_id=1, source_target_pairs={{0,1},{1,0},{2,3},{3,2},{4,5},{5,4},{6,7},{7,6},{8,9},{9,8},{10,11... | collective-permute-start | bytes 2457608 | tf_op jit(solution)/shard_map/ppermute | solution.py:74
  89.3 15.3 %collective-permute-start.7 = (bf16[320,1280]{1,0:T(8,128)(2,1)}, bf16[320,1280]{1,0:T(8,128)(2,1)}, u32[]{:S(2)}, u32[]{:S(2)}) collective-permute-start(bf16[320,1280]{1,0:T(8,128)(2,1)} %refs_5_.1), channel_id=1, source_target_pairs={{0,1},{1,0},{2,3},{3,2},{4,5},{5,4},{6,7},{7,6},{8,9},{9,8},{10,11... | collective-permute-start | bytes 2457608 | tf_op jit(solution)/shard_map/ppermute | solution.py:74
  90.2 16.1 %collective-permute-start.12 = (bf16[320,1280]{1,0:T(8,128)(2,1)}, bf16[320,1280]{1,0:T(8,128)(2,1)}, u32[]{:S(2)}, u32[]{:S(2)}) collective-permute-start(bf16[320,1280]{1,0:T(8,128)(2,1)} %shard_map.216.refs_11_), channel_id=1, source_target_pairs={{0,1},{1,0},{2,3},{3,2},{4,5},{5,4},{6,7},{7,6},{8,9},{9,8},{10,11... | collective-permute-start | bytes 2457608 | tf_op jit(solution)/shard_map/ppermute | solution.py:74
  100.2 6.3 %collective-permute-start.15 = (bf16[320,1280]{1,0:T(8,128)(2,1)S(1)}, bf16[320,1280]{1,0:T(8,128)(2,1)S(1)}, u32[]{:S(2)}, u32[]{:S(2)}) collective-permute-start(bf16[320,1280]{1,0:T(8,128)(2,1)S(1)} %copy-done.32), channel_id=1, source_target_pairs={{0,1},{1,0},{2,3},{3,2},{4,5},{5,4},{6,7},{7,6},{8,9},{9,8},{10,11... | collective-permute-start | bytes 2457608 | tf_op jit(solution)/shard_map/ppermute | solution.py:74
  100.3 6.3 %collective-permute-start.9 = (bf16[320,1280]{1,0:T(8,128)(2,1)}, bf16[320,1280]{1,0:T(8,128)(2,1)}, u32[]{:S(2)}, u32[]{:S(2)}) collective-permute-start(bf16[320,1280]{1,0:T(8,128)(2,1)} %shard_map.215.refs_7_), channel_id=1, source_target_pairs={{0,1},{1,0},{2,3},{3,2},{4,5},{5,4},{6,7},{7,6},{8,9},{9,8},{10,11... | collective-permute-start | bytes 2457608 | tf_op jit(solution)/shard_map/ppermute | solution.py:74
  100.8 3.9 %collective-permute-start.18 = (f32[1,320]{1,0:T(1,128)}, f32[1,320]{1,0:T(1,128)S(1)}, u32[]{:S(2)}, u32[]{:S(2)}) collective-permute-start(f32[1,320]{1,0:T(1,128)} %shard_map.218.refs_19_), channel_id=1, source_target_pairs={{0,1},{1,0},{2,3},{3,2},{4,5},{5,4},{6,7},{7,6},{8,9},{9,8},{10,11... | collective-permute-start | bytes 3848 | tf_op jit(solution)/shard_map/ppermute | solution.py:74
  104.6 2.0 collective-permute-start.4
  104.7 6.7 %collective-permute-start.5 = (bf16[3,64,320]{2,1,0:T(8,128)(2,1)S(1)}, bf16[3,64,320]{2,1,0:T(8,128)(2,1)S(1)}, u32[]{:S(2)}, u32[]{:S(2)}) collective-permute-start(bf16[3,64,320]{2,1,0:T(8,128)(2,1)S(1)} %get-tuple-element.78.refs_3_), channel_id=1, source_target_pairs={{0,2},{1,3},{2,0},{3,1},{4,6},{5,7},{6,4},{7,5},{8,10},{9,11},{10,... | collective-permute-start | bytes 368648 | tf_op jit(solution)/shard_map/ppermute | solution.py:132
  106.2 7.4 %collective-permute-start.6 = (bf16[3,64,320]{2,1,0:T(8,128)(2,1)S(1)}, bf16[3,64,320]{2,1,0:T(8,128)(2,1)S(1)}, u32[]{:S(2)}, u32[]{:S(2)}) collective-permute-start(bf16[3,64,320]{2,1,0:T(8,128)(2,1)S(1)} %get-tuple-element.79.refs_4_), channel_id=1, source_target_pairs={{0,3},{1,2},{2,1},{3,0},{4,7},{5,6},{6,5},{7,4},{8,11},{9,10},{10,... | collective-permute-start | bytes 368648 | tf_op jit(solution)/shard_map/ppermute | solution.py:132
  128.1 1.9 collective-permute-start.19
  128.5 6.9 %collective-permute-start.20 = (bf16[3,64,320]{2,1,0:T(8,128)(2,1)}, bf16[3,64,320]{2,1,0:T(8,128)(2,1)S(1)}, u32[]{:S(2)}, u32[]{:S(2)}) collective-permute-start(bf16[3,64,320]{2,1,0:T(8,128)(2,1)} %get-tuple-element.83), channel_id=1, source_target_pairs={{0,2},{1,3},{2,0},{3,1},{4,6},{5,7},{6,4},{7,5},{8,10},{9,11},{10,... | collective-permute-start | bytes 368648 | tf_op jit(solution)/shard_map/ppermute | solution.py:132
  130.0 7.1 %collective-permute-start.21 = (bf16[3,64,320]{2,1,0:T(8,128)(2,1)}, bf16[3,64,320]{2,1,0:T(8,128)(2,1)S(1)}, u32[]{:S(2)}, u32[]{:S(2)}) collective-permute-start(bf16[3,64,320]{2,1,0:T(8,128)(2,1)} %get-tuple-element.84), channel_id=1, source_target_pairs={{0,3},{1,2},{2,1},{3,0},{4,7},{5,6},{6,5},{7,4},{8,11},{9,10},{10,... | collective-permute-start | bytes 368648 | tf_op jit(solution)/shard_map/ppermute | solution.py:132
  139.6 18.8 %all-to-all-start.2 = ((bf16[8,3,80,128]{3,2,1,0:T(8,128)(2,1)}), bf16[8,3,80,128]{3,2,1,0:T(8,128)(2,1)S(1)}, u32[]{:S(2)}, u32[]{:S(2)}) async-start(bf16[8,3,80,128]{3,2,1,0:T(8,128)(2,1)} %shard_map.220), calls=%async_computation.2 | async-start | bytes 983040 | tf_op jit(solution)/shard_map/all_to_all | solution.py:136
  143.8 4.1 %collective-permute-start.22 = (bf16[2,192,320]{2,1,0:T(8,128)(2,1)S(1)}, bf16[2,192,320]{2,1,0:T(8,128)(2,1)S(1)}, u32[]{:S(2)}, u32[]{:S(2)}) collective-permute-start(bf16[2,192,320]{2,1,0:T(8,128)(2,1)S(1)} %copy-done.59), channel_id=1, source_target_pairs={{0,1},{1,0},{2,3},{3,2},{4,5},{5,4},{6,7},{7,6},{8,9},{9,8},{10,11... | collective-permute-start | bytes 737288 | tf_op jit(solution)/shard_map/ppermute | solution.py:132
  144.3 38.4 %collective-permute-start.33 = (bf16[3,64,1280]{2,1,0:T(8,128)(2,1)S(1)}, bf16[3,64,1280]{2,1,0:T(8,128)(2,1)}, u32[]{:S(2)}, u32[]{:S(2)}) collective-permute-start(bf16[3,64,1280]{2,1,0:T(8,128)(2,1)S(1)} %copy-done.49), channel_id=1, source_target_pairs={{0,1},{1,0},{2,3},{3,2},{4,5},{5,4},{6,7},{7,6},{8,9},{9,8},{10,11... | collective-permute-start | bytes 1474568 | tf_op jit(solution)/shard_map/ppermute | solution.py:74
  145.2 28.7 %collective-permute-start.25 = (bf16[3,64,1280]{2,1,0:T(8,128)(2,1)S(1)}, bf16[3,64,1280]{2,1,0:T(8,128)(2,1)S(1)}, u32[]{:S(2)}, u32[]{:S(2)}) collective-permute-start(bf16[3,64,1280]{2,1,0:T(8,128)(2,1)S(1)} %copy-done.50), channel_id=1, source_target_pairs={{0,2},{1,3},{2,0},{3,1},{4,6},{5,7},{6,4},{7,5},{8,10},{9,11},{10,... | collective-permute-start | bytes 1474568 | tf_op jit(solution)/shard_map/ppermute | solution.py:74
  146.5 27.3 %collective-permute-start.23 = (bf16[2,192,320]{2,1,0:T(8,128)(2,1)}, bf16[2,192,320]{2,1,0:T(8,128)(2,1)S(1)}, u32[]{:S(2)}, u32[]{:S(2)}) collective-permute-start(bf16[2,192,320]{2,1,0:T(8,128)(2,1)} %get-tuple-element.89), channel_id=1, source_target_pairs={{0,2},{1,3},{2,0},{3,1},{4,6},{5,7},{6,4},{7,5},{8,10},{9,11},{10,... | collective-permute-start | bytes 737288 | tf_op jit(solution)/shard_map/ppermute | solution.py:132
  147.2 26.7 %collective-permute-start.24 = (bf16[2,192,320]{2,1,0:T(8,128)(2,1)}, bf16[2,192,320]{2,1,0:T(8,128)(2,1)S(1)}, u32[]{:S(2)}, u32[]{:S(2)}) collective-permute-start(bf16[2,192,320]{2,1,0:T(8,128)(2,1)} %get-tuple-element.90), channel_id=1, source_target_pairs={{0,3},{1,2},{2,1},{3,0},{4,7},{5,6},{6,5},{7,4},{8,11},{9,10},{10,... | collective-permute-start | bytes 737288 | tf_op jit(solution)/shard_map/ppermute | solution.py:132
  147.9 34.0 %collective-permute-start.29 = (bf16[3,64,1280]{2,1,0:T(8,128)(2,1)}, bf16[3,64,1280]{2,1,0:T(8,128)(2,1)S(1)}, u32[]{:S(2)}, u32[]{:S(2)}) collective-permute-start(bf16[3,64,1280]{2,1,0:T(8,128)(2,1)} %get-tuple-element.97.refs_9_), channel_id=1, source_target_pairs={{0,2},{1,3},{2,0},{3,1},{4,6},{5,7},{6,4},{7,5},{8,10},{9,11},{10,... | collective-permute-start | bytes 1474568 | tf_op jit(solution)/shard_map/ppermute | solution.py:74
  174.8 51.9 %all-to-all-start.3 = ((bf16[8,11,80,128]{3,2,1,0:T(8,128)(2,1)}), bf16[8,11,80,128]{3,2,1,0:T(8,128)(2,1)}, u32[]{:S(2)}, u32[]{:S(2)}) async-start(bf16[8,11,80,128]{3,2,1,0:T(8,128)(2,1)} %shard_map.222), calls=%async_computation.3 | async-start | bytes 3604480 | tf_op jit(solution)/shard_map/all_to_all | solution.py:136
  179.5 3.2 collective-permute-start.34
  179.6 3.2 collective-permute-start.28
  180.1 2.9 collective-permute-start.31
  181.9 2.2 collective-permute-start.32
  182.7 2.1 collective-permute-start.30
  192.5 27.7 %collective-permute-start.35 = (bf16[4,3,40,768]{3,2,1,0:T(8,128)(2,1)}, bf16[4,3,40,768]{3,2,1,0:T(8,128)(2,1)S(1)}, u32[]{:S(2)}, u32[]{:S(2)}) collective-permute-start(bf16[4,3,40,768]{3,2,1,0:T(8,128)(2,1)} %get-tuple-element.100), channel_id=1, source_target_pairs={{0,4},{4,0},{8,12},{12,8},{16,20},{20,16},{24,28},{28,24},{1,5},{5... | collective-permute-start | bytes 2211848 | tf_op jit(solution)/shard_map/ppermute | solution.py:74
  194.3 25.9 %collective-permute-start.36 = (bf16[4,3,40,512]{3,2,1,0:T(8,128)(2,1)}, bf16[4,3,40,512]{3,2,1,0:T(8,128)(2,1)S(1)}, u32[]{:S(2)}, u32[]{:S(2)}) collective-permute-start(bf16[4,3,40,512]{3,2,1,0:T(8,128)(2,1)} %get-tuple-element.101), channel_id=1, source_target_pairs={{0,8},{4,12},{8,0},{12,4},{16,24},{20,28},{24,16},{28,20},{1,9},{5... | collective-permute-start | bytes 1474568 | tf_op jit(solution)/shard_map/ppermute | solution.py:74
  196.1 1.3 collective-permute-start.26
  197.4 4.0 %collective-permute-start.27 = (f32[8,1280]{1,0:T(8,128)S(1)}, f32[8,1280]{1,0:T(8,128)S(1)}, u32[]{:S(2)}, u32[]{:S(2)}) collective-permute-start(f32[8,1280]{1,0:T(8,128)S(1)} %add.56), channel_id=1, source_target_pairs={{0,2},{1,3},{2,0},{3,1},{4,6},{5,7},{6,4},{7,5},{8,10},{9,11},{10,... | collective-permute-start | bytes 122888 | tf_op jit(solution)/shard_map/ppermute | solution.py:74
  223.3 13.7 %collective-permute-start.40 = (bf16[2,3,40,768]{3,2,1,0:T(8,128)(2,1)S(1)}, bf16[2,3,40,768]{3,2,1,0:T(8,128)(2,1)S(1)}, u32[]{:S(2)}, u32[]{:S(2)}) collective-permute-start(bf16[2,3,40,768]{3,2,1,0:T(8,128)(2,1)S(1)} %get-tuple-element.102.refs_6_), channel_id=1, source_target_pairs={{0,8},{4,12},{8,0},{12,4},{16,24},{20,28},{24,16},{28,20},{1,9},{5... | collective-permute-start | bytes 1105928 | tf_op jit(solution)/shard_map/ppermute | solution.py:74
  225.8 11.2 %collective-permute-start.41 = (bf16[2,3,40,512]{3,2,1,0:T(8,128)(2,1)S(1)}, bf16[2,3,40,512]{3,2,1,0:T(8,128)(2,1)S(1)}, u32[]{:S(2)}, u32[]{:S(2)}) collective-permute-start(bf16[2,3,40,512]{3,2,1,0:T(8,128)(2,1)S(1)} %get-tuple-element.110), channel_id=1, source_target_pairs={{0,4},{4,0},{8,12},{12,8},{16,20},{20,16},{24,28},{28,24},{1,5},{5... | collective-permute-start | bytes 737288 | tf_op jit(solution)/shard_map/ppermute | solution.py:74
  238.5 15.2 %collective-permute-start.42 = (bf16[1,3,40,1280]{3,2,1,0:T(8,128)(2,1)S(1)}, bf16[1,3,40,1280]{3,2,1,0:T(8,128)(2,1)S(1)}, u32[]{:S(2)}, u32[]{:S(2)}) collective-permute-start(bf16[1,3,40,1280]{3,2,1,0:T(8,128)(2,1)S(1)} %get-tuple-element.113.refs_3_), channel_id=1, source_target_pairs={{0,16},{4,20},{8,24},{12,28},{16,0},{20,4},{24,8},{28,12},{1,17},{... | collective-permute-start | bytes 921608 | tf_op jit(solution)/shard_map/ppermute | solution.py:74
  240.6 21.5 %collective-permute-start.44 = (bf16[4,1,128,768]{3,2,1,0:T(8,128)(2,1)S(1)}, bf16[4,1,128,768]{3,2,1,0:T(8,128)(2,1)S(1)}, u32[]{:S(2)}, u32[]{:S(2)}) collective-permute-start(bf16[4,1,128,768]{3,2,1,0:T(8,128)(2,1)S(1)} %copy-done.47), channel_id=1, source_target_pairs={{0,4},{4,0},{8,12},{12,8},{16,20},{20,16},{24,28},{28,24},{1,5},{5... | collective-permute-start | bytes 2359304 | tf_op jit(solution)/shard_map/ppermute | solution.py:74
  241.8 20.2 %collective-permute-start.45 = (bf16[4,1,128,512]{3,2,1,0:T(8,128)(2,1)S(1)}, bf16[4,1,128,512]{3,2,1,0:T(8,128)(2,1)S(1)}, u32[]{:S(2)}, u32[]{:S(2)}) collective-permute-start(bf16[4,1,128,512]{3,2,1,0:T(8,128)(2,1)S(1)} %copy-done.48), channel_id=1, source_target_pairs={{0,8},{4,12},{8,0},{12,4},{16,24},{20,28},{24,16},{28,20},{1,9},{5... | collective-permute-start | bytes 1572872 | tf_op jit(solution)/shard_map/ppermute | solution.py:74
  242.8 11.6 %collective-permute-start.38 = (bf16[3,64,1280]{2,1,0:T(8,128)(2,1)S(1)}, bf16[3,64,1280]{2,1,0:T(8,128)(2,1)S(1)}, u32[]{:S(2)}, u32[]{:S(2)}) collective-permute-start(bf16[3,64,1280]{2,1,0:T(8,128)(2,1)S(1)} %copy-done.54), channel_id=1, source_target_pairs={{0,1},{1,0},{2,3},{3,2},{4,5},{5,4},{6,7},{7,6},{8,9},{9,8},{10,11... | collective-permute-start | bytes 1474568 | tf_op jit(solution)/shard_map/ppermute | solution.py:74
  242.8 45.2 %collective-permute-start.37 = (bf16[3,64,1280]{2,1,0:T(8,128)(2,1)S(1)}, bf16[3,64,1280]{2,1,0:T(8,128)(2,1)S(1)}, u32[]{:S(2)}, u32[]{:S(2)}) collective-permute-start(bf16[3,64,1280]{2,1,0:T(8,128)(2,1)S(1)} %copy-done.52), channel_id=1, source_target_pairs={{0,1},{1,0},{2,3},{3,2},{4,5},{5,4},{6,7},{7,6},{8,9},{9,8},{10,11... | collective-permute-start | bytes 1474568 | tf_op jit(solution)/shard_map/ppermute | solution.py:74
  254.3 16.4 %collective-permute-start.43 = (bf16[1,3,40,1280]{3,2,1,0:T(8,128)(2,1)S(1)}, bf16[1,3,40,1280]{3,2,1,0:T(8,128)(2,1)S(1)}, u32[]{:S(2)}, u32[]{:S(2)}) collective-permute-start(bf16[1,3,40,1280]{3,2,1,0:T(8,128)(2,1)S(1)} %shard_map.230.refs_5_.refs_1_), channel_id=1, source_target_pairs={{0,16},{4,20},{8,24},{12,28},{16,0},{20,4},{24,8},{28,12},{1,17},{... | collective-permute-start | bytes 921608 | tf_op jit(solution)/shard_map/ppermute | solution.py:74
  254.8 33.1 %collective-permute-start.39 = (bf16[3,64,1280]{2,1,0:T(8,128)(2,1)S(1)}, bf16[3,64,1280]{2,1,0:T(8,128)(2,1)S(1)}, u32[]{:S(2)}, u32[]{:S(2)}) collective-permute-start(bf16[3,64,1280]{2,1,0:T(8,128)(2,1)S(1)} %add_convert_fusion), channel_id=1, source_target_pairs={{0,2},{1,3},{2,0},{3,1},{4,6},{5,7},{6,4},{7,5},{8,10},{9,11},{10,... | collective-permute-start | bytes 1474568 | tf_op jit(solution)/shard_map/ppermute | solution.py:74
  262.9 16.2 %collective-permute-start.48 = (bf16[2,1,128,768]{3,2,1,0:T(8,128)(2,1)S(1)}, bf16[2,1,128,768]{3,2,1,0:T(8,128)(2,1)S(1)}, u32[]{:S(2)}, u32[]{:S(2)}) collective-permute-start(bf16[2,1,128,768]{3,2,1,0:T(8,128)(2,1)S(1)} %get-tuple-element.118.refs_3_), channel_id=1, source_target_pairs={{0,8},{4,12},{8,0},{12,4},{16,24},{20,28},{24,16},{28,20},{1,9},{5... | collective-permute-start | bytes 1179656 | tf_op jit(solution)/shard_map/ppermute | solution.py:74
  263.0 8.4 %collective-permute-start.49 = (bf16[2,1,128,512]{3,2,1,0:T(8,128)(2,1)S(1)}, bf16[2,1,128,512]{3,2,1,0:T(8,128)(2,1)S(1)}, u32[]{:S(2)}, u32[]{:S(2)}) collective-permute-start(bf16[2,1,128,512]{3,2,1,0:T(8,128)(2,1)S(1)} %get-tuple-element.123), channel_id=1, source_target_pairs={{0,4},{4,0},{8,12},{12,8},{16,20},{20,16},{24,28},{28,24},{1,5},{5... | collective-permute-start | bytes 786440 | tf_op jit(solution)/shard_map/ppermute | solution.py:74
  271.3 16.0 %collective-permute-start.46 = (bf16[2,3,40,768]{3,2,1,0:T(8,128)(2,1)S(1)}, bf16[2,3,40,768]{3,2,1,0:T(8,128)(2,1)S(1)}, u32[]{:S(2)}, u32[]{:S(2)}) collective-permute-start(bf16[2,3,40,768]{3,2,1,0:T(8,128)(2,1)S(1)} %get-tuple-element.119.refs_5_.refs_1_), channel_id=1, source_target_pairs={{0,8},{4,12},{8,0},{12,4},{16,24},{20,28},{24,16},{28,20},{1,9},{5... | collective-permute-start | bytes 1105928 | tf_op jit(solution)/shard_map/ppermute | solution.py:74
  271.4 8.6 %collective-permute-start.47 = (bf16[2,3,40,512]{3,2,1,0:T(8,128)(2,1)S(1)}, bf16[2,3,40,512]{3,2,1,0:T(8,128)(2,1)S(1)}, u32[]{:S(2)}, u32[]{:S(2)}) collective-permute-start(bf16[2,3,40,512]{3,2,1,0:T(8,128)(2,1)S(1)} %get-tuple-element.120.refs_2_), channel_id=1, source_target_pairs={{0,4},{4,0},{8,12},{12,8},{16,20},{20,16},{24,28},{28,24},{1,5},{5... | collective-permute-start | bytes 737288 | tf_op jit(solution)/shard_map/ppermute | solution.py:74
  279.9 19.4 %collective-permute-start.50 = (bf16[1,1,128,1280]{3,2,1,0:T(8,128)(2,1)S(1)}, bf16[1,1,128,1280]{3,2,1,0:T(8,128)(2,1)S(1)}, u32[]{:S(2)}, u32[]{:S(2)}) collective-permute-start(bf16[1,1,128,1280]{3,2,1,0:T(8,128)(2,1)S(1)} %get-tuple-element.124.refs_5_), channel_id=1, source_target_pairs={{0,16},{4,20},{8,24},{12,28},{16,0},{20,4},{24,8},{28,12},{1,17},{... | collective-permute-start | bytes 983048 | tf_op jit(solution)/shard_map/ppermute | solution.py:74
  301.0 8.1 %collective-permute-start.51 = (bf16[1,1,128,1280]{3,2,1,0:T(8,128)(2,1)S(1)}, bf16[1,1,128,1280]{3,2,1,0:T(8,128)(2,1)S(1)}, u32[]{:S(2)}, u32[]{:S(2)}) collective-permute-start(bf16[1,1,128,1280]{3,2,1,0:T(8,128)(2,1)S(1)} %get-tuple-element.127.refs_1_.refs_3_), channel_id=1, source_target_pairs={{0,16},{4,20},{8,24},{12,28},{16,0},{20,4},{24,8},{28,12},{1,17},{... | collective-permute-start | bytes 983048 | tf_op jit(solution)/shard_map/ppermute | solution.py:74
  301.0 17.5 %collective-permute-start.54 = (bf16[4,3,40,768]{3,2,1,0:T(8,128)(2,1)S(1)}, bf16[4,3,40,768]{3,2,1,0:T(8,128)(2,1)S(1)}, u32[]{:S(2)}, u32[]{:S(2)}) collective-permute-start(bf16[4,3,40,768]{3,2,1,0:T(8,128)(2,1)S(1)} %get-tuple-element.125.refs_7_.refs_1_), channel_id=1, source_target_pairs={{0,4},{4,0},{8,12},{12,8},{16,20},{20,16},{24,28},{28,24},{1,5},{5... | collective-permute-start | bytes 2211848 | tf_op jit(solution)/shard_map/ppermute | solution.py:74
  301.1 17.4 %collective-permute-start.55 = (bf16[4,3,40,512]{3,2,1,0:T(8,128)(2,1)S(1)}, bf16[4,3,40,512]{3,2,1,0:T(8,128)(2,1)S(1)}, u32[]{:S(2)}, u32[]{:S(2)}) collective-permute-start(bf16[4,3,40,512]{3,2,1,0:T(8,128)(2,1)S(1)} %get-tuple-element.130.refs_2_), channel_id=1, source_target_pairs={{0,8},{4,12},{8,0},{12,4},{16,24},{20,28},{24,16},{28,20},{1,9},{5... | collective-permute-start | bytes 1474568 | tf_op jit(solution)/shard_map/ppermute | solution.py:74
  301.2 25.2 %collective-permute-start.58 = (f32[1,1280]{1,0:T(1,128)S(1)}, f32[1,1280]{1,0:T(1,128)S(1)}, u32[]{:S(2)}, u32[]{:S(2)}) collective-permute-start(f32[1,1280]{1,0:T(1,128)S(1)} %slice.46), channel_id=1, source_target_pairs={{0,1},{1,0},{2,3},{3,2},{4,5},{5,4},{6,7},{7,6},{8,9},{9,8},{10,11... | collective-permute-start | bytes 15368 | tf_op jit(solution)/shard_map/ppermute | solution.py:74
  309.7 13.0 %collective-permute-start.52 = (bf16[2,1,128,768]{3,2,1,0:T(8,128)(2,1)S(1)}, bf16[2,1,128,768]{3,2,1,0:T(8,128)(2,1)S(1)}, u32[]{:S(2)}, u32[]{:S(2)}) collective-permute-start(bf16[2,1,128,768]{3,2,1,0:T(8,128)(2,1)S(1)} %get-tuple-element.128.refs_5_.refs_1_), channel_id=1, source_target_pairs={{0,8},{4,12},{8,0},{12,4},{16,24},{20,28},{24,16},{28,20},{1,9},{5... | collective-permute-start | bytes 1179656 | tf_op jit(solution)/shard_map/ppermute | solution.py:74
  309.8 11.8 %collective-permute-start.53 = (bf16[2,1,128,512]{3,2,1,0:T(8,128)(2,1)S(1)}, bf16[2,1,128,512]{3,2,1,0:T(8,128)(2,1)S(1)}, u32[]{:S(2)}, u32[]{:S(2)}) collective-permute-start(bf16[2,1,128,512]{3,2,1,0:T(8,128)(2,1)S(1)} %get-tuple-element.129.refs_2_), channel_id=1, source_target_pairs={{0,4},{4,0},{8,12},{12,8},{16,20},{20,16},{24,28},{28,24},{1,5},{5... | collective-permute-start | bytes 786440 | tf_op jit(solution)/shard_map/ppermute | solution.py:74
  324.8 15.2 %collective-permute-start.56 = (bf16[4,1,128,768]{3,2,1,0:T(8,128)(2,1)S(1)}, bf16[4,1,128,768]{3,2,1,0:T(8,128)(2,1)S(1)}, u32[]{:S(2)}, u32[]{:S(2)}) collective-permute-start(bf16[4,1,128,768]{3,2,1,0:T(8,128)(2,1)S(1)} %get-tuple-element.132.refs_1_.refs_5_), channel_id=1, source_target_pairs={{0,4},{4,0},{8,12},{12,8},{16,20},{20,16},{24,28},{28,24},{1,5},{5... | collective-permute-start | bytes 2359304 | tf_op jit(solution)/shard_map/ppermute | solution.py:74
  326.4 10.0 %collective-permute-start.57 = (bf16[4,1,128,512]{3,2,1,0:T(8,128)(2,1)S(1)}, bf16[4,1,128,512]{3,2,1,0:T(8,128)(2,1)S(1)}, u32[]{:S(2)}, u32[]{:S(2)}) collective-permute-start(bf16[4,1,128,512]{3,2,1,0:T(8,128)(2,1)S(1)} %get-tuple-element.133.refs_2_), channel_id=1, source_target_pairs={{0,8},{4,12},{8,0},{12,4},{16,24},{20,28},{24,16},{28,20},{1,9},{5... | collective-permute-start | bytes 1572872 | tf_op jit(solution)/shard_map/ppermute | solution.py:74
  326.4 3.7 %collective-permute-start.59 = (f32[1,1280]{1,0:T(1,128)S(1)}, f32[1,1280]{1,0:T(1,128)S(1)}, u32[]{:S(2)}, u32[]{:S(2)}) collective-permute-start(f32[1,1280]{1,0:T(1,128)S(1)} %get-tuple-element.137), channel_id=1, source_target_pairs={{0,2},{1,3},{2,0},{3,1},{4,6},{5,7},{6,4},{7,5},{8,10},{9,11},{10,... | collective-permute-start | bytes 15368 | tf_op jit(solution)/shard_map/ppermute | solution.py:74
  (66 other events, 714.0 us)

commit v5 on v4

--- a/solution.py
+++ b/solution.py
@@ -19,7 +19,7 @@
 kernel_us = {
     "project_kernel": 7, "attend_kernel": 11, "middle_kernel": 14, "attend_back_kernel": 15, "grads_kernel": 7, "back_kernel": 11,
 }
-round_order = "EEQEQEQQEQQ"
+round_order = "EEQEQEQQQEQ"
 first_share = 768
 ahead_rounds = 1
 flops_per_us = 1153500000
@@ -40,12 +40,12 @@
     return math.prod(rest) * -(-last // 128) * 128 * jnp.dtype(value.dtype).itemsize
 
 
-def call(kernel, out_shape, operands, scalars, scratch=(), tokens=(), weight=1, most=vmem_bytes):
+def call(kernel, out_shape, operands, scalars, scratch=(), tokens=(), weight=1, most=vmem_bytes, loose=()):
     specs = [pl.BlockSpec(memory_space=pltpu.SMEM)]
-    specs += [pl.BlockSpec(memory_space=pltpu.VMEM)] * len(operands)
+    specs += [pl.BlockSpec(memory_space=pl.ANY if i in loose else pltpu.VMEM) for i in range(len(operands))]
     specs += [pl.BlockSpec(memory_space=pl.ANY)] * len(tokens)
     used = 1 + len(operands)
-    room = spare_bytes + 2 * sum(padded_bytes(v) for v in [*operands, *out_shape, *scratch])
+    room = spare_bytes + 2 * sum(padded_bytes(v) for v in [*operands, *out_shape, *scratch] if "sem" not in str(v.dtype))
     weight = kernel_us.get(getattr(kernel, "func", kernel).__name__, weight)
     return pl.pallas_call(
         lambda *refs: kernel(*refs[:used], *refs[used + len(tokens) :]),
@@ -545,13 +545,20 @@
 
 
 def middle_kernel(spread, sc, *refs):
-    o_refs, wo, wi, wd, bias_refs = [refs[i * spread : (i + 1) * spread] for i in range(5)]
-    refs = refs[5 * spread :]
+    o_refs, *far, bias_refs = [refs[i * spread : (i + 1) * spread] for i in range(5)]
+    *refs, near_ref, arrived = refs[5 * spread :]
+    copies = [
+        [pltpu.make_async_copy(far[i][k], near_ref.at[i, k], arrived.at[i, k]) for k in range(spread)] for i in range(3)
+    ]
+    for copy in copies[0] + [copies[i][k] for k in range(spread) for i in (1, 2)]:
+        copy.start()
+    wo, wi, wd = [[near_ref.at[i, k] for k in range(spread)] for i in range(3)]
     x_ref, g_ref, gain_ref, out_bias_ref, out_ref, grad_ref, n2_ref, dy_ref, sums_ref, du_sum_ref = refs[:10]
     hidden_refs, do_refs = [refs[10 + i * spread : 10 + (i + 1) * spread] for i in range(2)]
     kind = out_ref.shape
     h1 = flat(x_ref).astype(f32) + out_bias_ref[0:1]
     for k in range(spread):
+        copies[0][k].wait()
         h1 = h1 + mm(flat(o_refs[k]), wo[k][...])
     r2 = lax.rsqrt(jnp.mean(h1 * h1, axis=-1, keepdims=True) + epsilon)
     n2 = (h1 * r2 * gain_ref[1:2]).astype(bf16)
@@ -560,6 +567,8 @@
     out = h1 + out_bias_ref[1:2]
     dn2 = 0.0
     for k in range(spread):
+        copies[1][k].wait()
+        copies[2][k].wait()
         u = mm(n2, wi[k][...], cols_cols) + bias_refs[k][...]
         gate = 1.0 / (1.0 + jnp.exp(-u))
         a = (u * gate).astype(bf16)
@@ -753,6 +762,8 @@
         + thin_parts,
         [*o_parts, *others[0], *others[1], *others[2], *others[3], layer_input, output_cotangent, norm_gains, out_bias],
         scalars,
+        scratch=[pltpu.VMEM((3, spread, local, width), bf16), pltpu.SemaphoreType.DMA((3, spread))],
+        loose=range(spread, 4 * spread),
     )
     hidden_parts, do_parts = rest[:spread], swap_parts(rest[spread:], "fsdp", spread)
     (do_send,) = call(

time: 349 us -> 347 us (level)
    unnamed x135 -> x133, local copies, waits for them, and re-layouts: 14.7 us -> 13.3 us
  transfers between devices with their start and end apart: 64 -> 64, of which waited for: 31 -> 31; matrix products, arithmetic and copies ran while one was open for 5% -> 6% of each run, Pallas kernels for 16% -> 16%
where the time goes in v5:
time: 347 us; the launch traced here: 342 us
  waiting for transfers between devices  172 us (50%)
  Pallas kernels  80.2 us (23%)
  starting transfers between devices  56.3 us (16%)
  local copies, waits for them, and re-layouts  17.9 us (5%)
  other arithmetic  13.6 us (4%)
    ppermute x51, waiting for transfers between devices, exchange(): return lax.ppermute(values, axis, [(i, i ^ 1 << bit) for i in range(size)])  109 us
    pallas_call x21, Pallas kernels, call(): pl.pallas_call(lambda *refs: kernel(*refs[:used], *refs[used + len(tokens...  80.2 us
    all_to_all x4, waiting for transfers between devices, swap_all(): return lax.all_to_all(parts, axis, 0, 0, tiled=True)  48.6 us
    ppermute x51, starting transfers between devices, exchange(): return lax.ppermute(values, axis, [(i, i ^ 1 << bit) for i in range(size)])  31.2 us
    all_to_all x4, starting transfers between devices, swap_all(): return lax.all_to_all(parts, axis, 0, 0, tiled=True)  19.3 us
    ppermute x9, waiting for transfers between devices, swap_parts(): lax.ppermute(parts[k], axis, [(i, i ^ k) for i in range(size)])  14.1 us
    unnamed x133, local copies, waits for them, and re-layouts  13.3 us
    another operation x2, other arithmetic  7.21 us
  transfers between devices with their start and end apart: 64, of which 31 were waited for; matrix products, arithmetic and copies ran while one was open for 6% of the time, Pallas kernels for 16%

profile of v5, /device:TPU:0, one launch (start us, length us, event | category | flops | bytes accessed | tf_op | source)
XLA Modules:
  0.0 341.7 jit_solution(6821701213197226943)
XLA Ops:
  0.6 3.0 collective-permute-start.1
  4.6 7.0 %reduce-window.6 = s32[3,16,128]{2,1,0:T(8,128)S(1)} reduce-window(s32[3,16,128]{2,1,0:T(8,128)S(1)} %bitcast.49, s32[]{:T(128)} %constant.66.clone.1), window={size=1x1x128 pad=0_0x0_0x0_127}, to_apply=%region_0.1 | reduce-window | flops 780288 | bytes 49156 | tf_op jit(solution)/shard_map/reduce-window
  13.0 2.1 collective-permute-done.1.refs_3_
  17.7 1.0 copy-done.7
  19.4 6.3 %shard_map.212 = (bf16[3,256,1280]{2,1,0:T(8,128)(2,1)}, bf16[8,11,80,128]{3,2,1,0:T(8,128)(2,1)}) custom-call(s32[2,8]{1,0:T(2,128)S(1)} %bitcast.32, bf16[3,64,1280]{2,1,0:T(8,128)(2,1)S(1)} %copy-done.7, bf16[3,64,1280]{2,1,0:T(8,128)(2,1)S(1)} %collective-permute-done.refs_2_, bf16[3,64,1280]{2,1,0:T(8,128)(2,1)} %copy-done.52, ...), custom_call_target="tpu_custom_call" | custom-call | flops 8074500096 | tf_op jit(solution)/shard_map/pallas_call | solution.py:50
  25.7 6.5 %all-to-all-start = ((bf16[8,11,80,128]{3,2,1,0:T(8,128)(2,1)}), bf16[8,11,80,128]{3,2,1,0:T(8,128)(2,1)S(1)}, u32[]{:S(2)}, u32[]{:S(2)}) async-start(bf16[8,11,80,128]{3,2,1,0:T(8,128)(2,1)} %get-tuple-element.74), calls=%async_computation | async-start | bytes 3604480 | tf_op jit(solution)/shard_map/all_to_all | solution.py:136
  32.2 1.6 collective-permute-start.17
  34.5 1.5 collective-permute-start.14
  36.0 1.3 collective-permute-start.8
  38.1 36.6 %all-to-all-done.refs_1_ = bf16[8,11,80,128]{3,2,1,0:T(8,128)(2,1)S(1)} async-done(((bf16[8,11,80,128]{3,2,1,0:T(8,128)(2,1)}), bf16[8,11,80,128]{3,2,1,0:T(8,128)(2,1)S(1)}, u32[]{:S(2)}, u32[]{:S(2)}) %all-to-all-start) | async-done | bytes 1802272 | tf_op jit(solution)/shard_map/all_to_all | solution.py:136
  74.7 10.6 %shard_map.213 = (bf16[8,3,80,128]{3,2,1,0:T(8,128)(2,1)}, f32[1,2048]{1,0:T(1,128)S(1)}, f32[1,1024]{1,0:T(1,128)S(1)}) custom-call(s32[2,8]{1,0:T(2,128)S(1)} %bitcast.33, bf16[8,11,80,128]{3,2,1,0:T(8,128)(2,1)S(1)} %all-to-all-done.refs_1_, s32[1,2048]{1,0:T(1,128)S(1)} %constant_dynamic-slice_fusion.refs_9_.refs_2_.refs_5_, ...), custom_call_target="tpu_custom_call" | custom-call | flops 12688499712 | tf_op jit(solution)/shard_map/pallas_call | solution.py:50
  85.3 3.9 %all-to-all-start.1 = ((bf16[8,3,80,128]{3,2,1,0:T(8,128)(2,1)}), bf16[8,3,80,128]{3,2,1,0:T(8,128)(2,1)S(1)}, u32[]{:S(2)}, u32[]{:S(2)}) async-start(bf16[8,3,80,128]{3,2,1,0:T(8,128)(2,1)} %get-tuple-element.75.refs_1_.refs_4_), calls=%async_computation.1 | async-start | bytes 983040 | tf_op jit(solution)/shard_map/all_to_all | solution.py:136
  90.3 10.0 %collective-permute-done.3.refs_2_.refs_0_ = bf16[3,64,1280]{2,1,0:T(8,128)(2,1)S(1)} collective-permute-done((bf16[3,64,1280]{2,1,0:T(8,128)(2,1)}, bf16[3,64,1280]{2,1,0:T(8,128)(2,1)S(1)}, u32[]{:S(2)}, u32[]{:S(2)}) %collective-permute-start.3) | collective-permute-done | bytes 491552 | tf_op jit(solution)/shard_map/ppermute | solution.py:74
  100.9 2.3 all-to-all-done.1.refs_1_
  104.8 1.6 collective-permute-start.5
  106.7 4.8 %collective-permute-done.5.refs_3_ = bf16[3,64,320]{2,1,0:T(8,128)(2,1)S(1)} collective-permute-done((bf16[3,64,320]{2,1,0:T(8,128)(2,1)S(1)}, bf16[3,64,320]{2,1,0:T(8,128)(2,1)S(1)}, u32[]{:S(2)}, u32[]{:S(2)}) %collective-permute-start.5) | collective-permute-done | bytes 122912 | tf_op jit(solution)/shard_map/ppermute | solution.py:132
  111.5 2.2 collective-permute-done.6.refs_4_
  114.4 13.0 %shard_map.219 = (bf16[3,64,1280]{2,1,0:T(8,128)(2,1)}, f32[3,64,1280]{2,1,0:T(8,128)}, bf16[3,64,1280]{2,1,0:T(8,128)(2,1)}, bf16[3,64,1280]{2,1,0:T(8,128)(2,1...) custom-call(s32[2,8]{1,0:T(2,128)} %bitcast.28, ...), custom_call_target="tpu_custom_call" | custom-call | flops 16149000192 | tf_op jit(solution)/shard_map/pallas_call | solution.py:50
  127.8 1.5 collective-permute-start.20
  129.3 5.3 %collective-permute-done.20.refs_3_ = bf16[3,64,320]{2,1,0:T(8,128)(2,1)S(1)} collective-permute-done((bf16[3,64,320]{2,1,0:T(8,128)(2,1)}, bf16[3,64,320]{2,1,0:T(8,128)(2,1)S(1)}, u32[]{:S(2)}, u32[]{:S(2)}) %collective-permute-start.20) | collective-permute-done | bytes 122912 | tf_op jit(solution)/shard_map/ppermute | solution.py:132
  134.7 1.7 collective-permute-done.21.refs_4_
  137.3 1.6 shard_map.220
  138.9 4.3 %all-to-all-start.2 = ((bf16[8,3,80,128]{3,2,1,0:T(8,128)(2,1)}), bf16[8,3,80,128]{3,2,1,0:T(8,128)(2,1)S(1)}, u32[]{:S(2)}, u32[]{:S(2)}) async-start(bf16[8,3,80,128]{3,2,1,0:T(8,128)(2,1)} %shard_map.220), calls=%async_computation.2 | async-start | bytes 983040 | tf_op jit(solution)/shard_map/all_to_all | solution.py:136
  144.5 1.4 collective-permute-start.25
  148.0 9.7 %all-to-all-done.2.refs_2_ = bf16[8,3,80,128]{3,2,1,0:T(8,128)(2,1)S(1)} async-done(((bf16[8,3,80,128]{3,2,1,0:T(8,128)(2,1)}), bf16[8,3,80,128]{3,2,1,0:T(8,128)(2,1)S(1)}, u32[]{:S(2)}, u32[]{:S(2)}) %all-to-all-start.2) | async-done | bytes 491552 | tf_op jit(solution)/shard_map/all_to_all | solution.py:136
  158.5 14.6 %shard_map.221 = (bf16[8,11,80,128]{3,2,1,0:T(8,128)(2,1)}, f32[80,1]{1,0:T(8,128)}) custom-call(s32[2,8]{1,0:T(2,128)} %bitcast.29, bf16[8,11,80,128]{3,2,1,0:T(8,128)(2,1)} %copy-done, bf16[8,3,80,128]{3,2,1,0:T(8,128)(2,1)} %copy-done.34, f32[80,1]{1,0:T(8,128)} %copy.38.refs_3_, bf16[8,3,80,128]{3,2,1,0:T(8,128)(2,1)} %get-tuple-element.75.refs_1_.refs_4_, ...), custom_call_target="tpu_custom_call" | custom-call | flops 17302499328 | tf_op jit(solution)/shard_map/pallas_call | solution.py:50
  174.1 4.7 %all-to-all-start.3 = ((bf16[8,11,80,128]{3,2,1,0:T(8,128)(2,1)}), bf16[8,11,80,128]{3,2,1,0:T(8,128)(2,1)}, u32[]{:S(2)}, u32[]{:S(2)}) async-start(bf16[8,11,80,128]{3,2,1,0:T(8,128)(2,1)} %shard_map.222), calls=%async_computation.3 | async-start | bytes 3604480 | tf_op jit(solution)/shard_map/all_to_all | solution.py:136
  179.5 1.7 collective-permute-done.29.refs_0_
  182.3 1.1 collective-permute-done.32.refs_16_
  184.9 6.9 %shard_map.226 = (bf16[4,3,40,768]{3,2,1,0:T(8,128)(2,1)}, bf16[4,3,40,512]{3,2,1,0:T(8,128)(2,1)}, bf16[4,3,40,768]{3,2,1,0:T(8,128)(2,1)}, bf16[4,3,40,512]{3,2,1,0:T(8,128)(2,1)}) custom-call(s32[2,8]{1,0:T(2,128)} %bitcast.30, bf16[3,64,320]{2,1,0:T(8,128)(2,1)} %copy-done.2, bf16[3,64,320]{2,1,0:T(8,128)(2,1)} %copy-done.10, ...), custom_call_target="tpu_custom_call" | custom-call | flops 8074500096 | tf_op jit(solution)/shard_map/pallas_call | solution.py:50
  191.8 1.8 collective-permute-start.35
  193.6 1.5 collective-permute-start.36
  195.5 1.2 collective-permute-done.26
  196.7 1.3 collective-permute-start.27
  198.0 2.7 collective-permute-done.27
  201.3 18.2 %collective-permute-done.36.refs_4_ = bf16[4,3,40,512]{3,2,1,0:T(8,128)(2,1)S(1)} collective-permute-done((bf16[4,3,40,512]{3,2,1,0:T(8,128)(2,1)}, bf16[4,3,40,512]{3,2,1,0:T(8,128)(2,1)S(1)}, u32[]{:S(2)}, u32[]{:S(2)}) %collective-permute-start.36) | collective-permute-done | bytes 491552 | tf_op jit(solution)/shard_map/ppermute | solution.py:74
  219.5 1.1 copy-done.22
  220.6 1.0 copy-done.23
  222.6 2.5 collective-permute-start.40
  226.0 10.3 %shard_map.228 = (f32[8,1280]{1,0:T(8,128)}, bf16[3,64,1280]{2,1,0:T(8,128)(2,1)}, bf16[3,64,1280]{2,1,0:T(8,128)(2,1)}, bf16[3,64,1280]{2,1,0:T(8,128)(2,1)}, b...) custom-call(s32[2,8]{1,0:T(2,128)} %bitcast.31, ...), custom_call_target="tpu_custom_call" | custom-call | flops 12688499712 | tf_op jit(solution)/shard_map/pallas_call | solution.py:50
  237.8 2.1 collective-permute-start.42
  239.9 1.3 collective-permute-start.44
  242.6 10.4 %collective-permute-done.42.refs_2_ = bf16[1,3,40,1280]{3,2,1,0:T(8,128)(2,1)S(1)} collective-permute-done((bf16[1,3,40,1280]{3,2,1,0:T(8,128)(2,1)S(1)}, bf16[1,3,40,1280]{3,2,1,0:T(8,128)(2,1)S(1)}, u32[]{:S(2)}, u32[]{:S(2)}) %collective-permute-start.42) | collective-permute-done | bytes 307232 | tf_op jit(solution)/shard_map/ppermute | solution.py:74
  254.2 1.2 collective-permute-start.39
  255.3 6.0 %collective-permute-done.45.refs_4_ = bf16[4,1,128,512]{3,2,1,0:T(8,128)(2,1)S(1)} collective-permute-done((bf16[4,1,128,512]{3,2,1,0:T(8,128)(2,1)S(1)}, bf16[4,1,128,512]{3,2,1,0:T(8,128)(2,1)S(1)}, u32[]{:S(2)}, u32[]{:S(2)}) %collective-permute-start.45) | collective-permute-done | bytes 524320 | tf_op jit(solution)/shard_map/ppermute | solution.py:74
  262.3 1.2 collective-permute-start.49
  263.6 6.5 %collective-permute-done.43.refs_2_ = bf16[1,3,40,1280]{3,2,1,0:T(8,128)(2,1)S(1)} collective-permute-done((bf16[1,3,40,1280]{3,2,1,0:T(8,128)(2,1)S(1)}, bf16[1,3,40,1280]{3,2,1,0:T(8,128)(2,1)S(1)}, u32[]{:S(2)}, u32[]{:S(2)}) %collective-permute-start.43) | collective-permute-done | bytes 307232 | tf_op jit(solution)/shard_map/ppermute | solution.py:74
  270.7 1.6 collective-permute-start.47
  272.3 6.2 %collective-permute-done.48.refs_3_ = bf16[2,1,128,768]{3,2,1,0:T(8,128)(2,1)S(1)} collective-permute-done((bf16[2,1,128,768]{3,2,1,0:T(8,128)(2,1)S(1)}, bf16[2,1,128,768]{3,2,1,0:T(8,128)(2,1)S(1)}, u32[]{:S(2)}, u32[]{:S(2)}) %collective-permute-start.48) | collective-permute-done | bytes 393248 | tf_op jit(solution)/shard_map/ppermute | solution.py:74
  279.4 7.2 %collective-permute-done.46.refs_3_ = bf16[2,3,40,768]{3,2,1,0:T(8,128)(2,1)S(1)} collective-permute-done((bf16[2,3,40,768]{3,2,1,0:T(8,128)(2,1)S(1)}, bf16[2,3,40,768]{3,2,1,0:T(8,128)(2,1)S(1)}, u32[]{:S(2)}, u32[]{:S(2)}) %collective-permute-start.46) | collective-permute-done | bytes 368672 | tf_op jit(solution)/shard_map/ppermute | solution.py:74
  287.3 1.9 shard_map.235.refs_3_
  289.2 10.2 %collective-permute-done.50.refs_2_ = bf16[1,1,128,1280]{3,2,1,0:T(8,128)(2,1)S(1)} collective-permute-done((bf16[1,1,128,1280]{3,2,1,0:T(8,128)(2,1)S(1)}, bf16[1,1,128,1280]{3,2,1,0:T(8,128)(2,1)S(1)}, u32[]{:S(2)}, u32[]{:S(2)}) %collective-permute-start.50) | collective-permute-done | bytes 327712 | tf_op jit(solution)/shard_map/ppermute | solution.py:74
  299.4 1.0 copy-done.18
  301.9 7.3 %collective-permute-done.51.refs_2_ = bf16[1,1,128,1280]{3,2,1,0:T(8,128)(2,1)S(1)} collective-permute-done((bf16[1,1,128,1280]{3,2,1,0:T(8,128)(2,1)S(1)}, bf16[1,1,128,1280]{3,2,1,0:T(8,128)(2,1)S(1)}, u32[]{:S(2)}, u32[]{:S(2)}) %collective-permute-start.51) | collective-permute-done | bytes 327712 | tf_op jit(solution)/shard_map/ppermute | solution.py:74
  309.2 1.3 shard_map.237
  310.5 1.2 slice_add_fusion
  316.3 1.3 pad_maximum_fusion
  317.6 1.0 collective-permute-done.53.refs_4_
  318.6 3.7 %collective-permute-done.52.refs_3_ = bf16[2,1,128,768]{3,2,1,0:T(8,128)(2,1)S(1)} collective-permute-done((bf16[2,1,128,768]{3,2,1,0:T(8,128)(2,1)S(1)}, bf16[2,1,128,768]{3,2,1,0:T(8,128)(2,1)S(1)}, u32[]{:S(2)}, u32[]{:S(2)}) %collective-permute-start.52) | collective-permute-done | bytes 393248 | tf_op jit(solution)/shard_map/ppermute | solution.py:74
  322.3 1.1 shard_map.238
  324.1 3.1 shard_map.239
  327.2 6.9 %collective-permute-done.55.refs_4_ = bf16[4,1,128,512]{3,2,1,0:T(8,128)(2,1)S(1)} collective-permute-done((bf16[4,1,128,512]{3,2,1,0:T(8,128)(2,1)S(1)}, bf16[4,1,128,512]{3,2,1,0:T(8,128)(2,1)S(1)}, u32[]{:S(2)}, u32[]{:S(2)}) %collective-permute-start.55) | collective-permute-done | bytes 524320 | tf_op jit(solution)/shard_map/ppermute | solution.py:74
  334.1 4.3 %collective-permute-done.54.refs_3_ = bf16[4,1,128,768]{3,2,1,0:T(8,128)(2,1)S(1)} collective-permute-done((bf16[4,1,128,768]{3,2,1,0:T(8,128)(2,1)S(1)}, bf16[4,1,128,768]{3,2,1,0:T(8,128)(2,1)S(1)}, u32[]{:S(2)}, u32[]{:S(2)}) %collective-permute-start.54) | collective-permute-done | bytes 786464 | tf_op jit(solution)/shard_map/ppermute | solution.py:74
  338.3 3.1 shard_map.240
  (265 shorter events, 37.5 us)
Async XLA Ops:
  0.6 14.4 %collective-permute-start.1 = (bf16[3,64,1280]{2,1,0:T(8,128)(2,1)}, bf16[3,64,1280]{2,1,0:T(8,128)(2,1)S(1)}, u32[]{:S(2)}, u32[]{:S(2)}) collective-permute-start(bf16[3,64,1280]{2,1,0:T(8,128)(2,1)} %refs_4_.1), channel_id=1, source_target_pairs={{0,2},{1,3},{2,0},{3,1},{4,6},{5,7},{6,4},{7,5},{8,10},{9,11},{10,... | collective-permute-start | bytes 1474568 | tf_op jit(solution)/shard_map/ppermute | solution.py:74
  3.6 13.2 %collective-permute-start = (bf16[3,64,1280]{2,1,0:T(8,128)(2,1)}, bf16[3,64,1280]{2,1,0:T(8,128)(2,1)S(1)}, u32[]{:S(2)}, u32[]{:S(2)}) collective-permute-start(bf16[3,64,1280]{2,1,0:T(8,128)(2,1)} %refs_4_.1), channel_id=1, source_target_pairs={{0,1},{1,0},{2,3},{3,2},{4,5},{5,4},{6,7},{7,6},{8,9},{9,8},{10,11... | collective-permute-start | bytes 1474568 | tf_op jit(solution)/shard_map/ppermute | solution.py:74
  15.1 1.9 collective-permute-start.2
  25.7 48.9 %all-to-all-start = ((bf16[8,11,80,128]{3,2,1,0:T(8,128)(2,1)}), bf16[8,11,80,128]{3,2,1,0:T(8,128)(2,1)S(1)}, u32[]{:S(2)}, u32[]{:S(2)}) async-start(bf16[8,11,80,128]{3,2,1,0:T(8,128)(2,1)} %get-tuple-element.74), calls=%async_computation | async-start | bytes 3604480 | tf_op jit(solution)/shard_map/all_to_all | solution.py:136
  32.2 3.8 %collective-permute-start.17 = (f32[1,320]{1,0:T(1,128)S(1)}, f32[1,320]{1,0:T(1,128)S(1)}, u32[]{:S(2)}, u32[]{:S(2)}) collective-permute-start(f32[1,320]{1,0:T(1,128)S(1)} %reshape.63.refs_17_), channel_id=1, source_target_pairs={{0,2},{1,3},{2,0},{3,1},{4,6},{5,7},{6,4},{7,5},{8,10},{9,11},{10,... | collective-permute-start | bytes 3848 | tf_op jit(solution)/shard_map/ppermute | solution.py:74
  33.8 3.6 %collective-permute-start.16 = (f32[1,320]{1,0:T(1,128)S(1)}, f32[1,320]{1,0:T(1,128)S(1)}, u32[]{:S(2)}, u32[]{:S(2)}) collective-permute-start(f32[1,320]{1,0:T(1,128)S(1)} %reshape.63.refs_17_), channel_id=1, source_target_pairs={{0,1},{1,0},{2,3},{3,2},{4,5},{5,4},{6,7},{7,6},{8,9},{9,8},{10,11... | collective-permute-start | bytes 3848 | tf_op jit(solution)/shard_map/ppermute | solution.py:74
  33.8 55.5 %collective-permute-start.11 = (bf16[320,1280]{1,0:T(8,128)(2,1)}, bf16[320,1280]{1,0:T(8,128)(2,1)}, u32[]{:S(2)}, u32[]{:S(2)}) collective-permute-start(bf16[320,1280]{1,0:T(8,128)(2,1)} %bitcast.5.refs_9_), channel_id=1, source_target_pairs={{0,2},{1,3},{2,0},{3,1},{4,6},{5,7},{6,4},{7,5},{8,10},{9,11},{10,... | collective-permute-start | bytes 2457608 | tf_op jit(solution)/shard_map/ppermute | solution.py:74
  34.3 66.0 %collective-permute-start.10 = (bf16[320,1280]{1,0:T(8,128)(2,1)}, bf16[320,1280]{1,0:T(8,128)(2,1)}, u32[]{:S(2)}, u32[]{:S(2)}) collective-permute-start(bf16[320,1280]{1,0:T(8,128)(2,1)} %bitcast.5.refs_9_), channel_id=1, source_target_pairs={{0,1},{1,0},{2,3},{3,2},{4,5},{5,4},{6,7},{7,6},{8,9},{9,8},{10,11... | collective-permute-start | bytes 2457608 | tf_op jit(solution)/shard_map/ppermute | solution.py:74
  34.5 54.8 %collective-permute-start.14 = (bf16[320,1280]{1,0:T(8,128)(2,1)}, bf16[320,1280]{1,0:T(8,128)(2,1)S(1)}, u32[]{:S(2)}, u32[]{:S(2)}) collective-permute-start(bf16[320,1280]{1,0:T(8,128)(2,1)} %refs_13_.1), channel_id=1, source_target_pairs={{0,2},{1,3},{2,0},{3,1},{4,6},{5,7},{6,4},{7,5},{8,10},{9,11},{10,... | collective-permute-start | bytes 2457608 | tf_op jit(solution)/shard_map/ppermute | solution.py:74
  36.0 54.2 %collective-permute-start.8 = (bf16[320,1280]{1,0:T(8,128)(2,1)}, bf16[320,1280]{1,0:T(8,128)(2,1)}, u32[]{:S(2)}, u32[]{:S(2)}) collective-permute-start(bf16[320,1280]{1,0:T(8,128)(2,1)} %refs_5_.1), channel_id=1, source_target_pairs={{0,2},{1,3},{2,0},{3,1},{4,6},{5,7},{6,4},{7,5},{8,10},{9,11},{10,... | collective-permute-start | bytes 2457608 | tf_op jit(solution)/shard_map/ppermute | solution.py:74
  37.4 62.9 %collective-permute-start.3 = (bf16[3,64,1280]{2,1,0:T(8,128)(2,1)}, bf16[3,64,1280]{2,1,0:T(8,128)(2,1)S(1)}, u32[]{:S(2)}, u32[]{:S(2)}) collective-permute-start(bf16[3,64,1280]{2,1,0:T(8,128)(2,1)} %refs_17_.1), channel_id=1, source_target_pairs={{0,2},{1,3},{2,0},{3,1},{4,6},{5,7},{6,4},{7,5},{8,10},{9,11},{10,... | collective-permute-start | bytes 1474568 | tf_op jit(solution)/shard_map/ppermute | solution.py:74
  85.3 17.9 %all-to-all-start.1 = ((bf16[8,3,80,128]{3,2,1,0:T(8,128)(2,1)}), bf16[8,3,80,128]{3,2,1,0:T(8,128)(2,1)S(1)}, u32[]{:S(2)}, u32[]{:S(2)}) async-start(bf16[8,3,80,128]{3,2,1,0:T(8,128)(2,1)} %get-tuple-element.75.refs_1_.refs_4_), calls=%async_computation.1 | async-start | bytes 983040 | tf_op jit(solution)/shard_map/all_to_all | solution.py:136
  89.3 11.5 %collective-permute-start.13 = (bf16[320,1280]{1,0:T(8,128)(2,1)}, bf16[320,1280]{1,0:T(8,128)(2,1)S(1)}, u32[]{:S(2)}, u32[]{:S(2)}) collective-permute-start(bf16[320,1280]{1,0:T(8,128)(2,1)} %refs_13_.1), channel_id=1, source_target_pairs={{0,1},{1,0},{2,3},{3,2},{4,5},{5,4},{6,7},{7,6},{8,9},{9,8},{10,11... | collective-permute-start | bytes 2457608 | tf_op jit(solution)/shard_map/ppermute | solution.py:74
  89.4 15.3 %collective-permute-start.7 = (bf16[320,1280]{1,0:T(8,128)(2,1)}, bf16[320,1280]{1,0:T(8,128)(2,1)}, u32[]{:S(2)}, u32[]{:S(2)}) collective-permute-start(bf16[320,1280]{1,0:T(8,128)(2,1)} %refs_5_.1), channel_id=1, source_target_pairs={{0,1},{1,0},{2,3},{3,2},{4,5},{5,4},{6,7},{7,6},{8,9},{9,8},{10,11... | collective-permute-start | bytes 2457608 | tf_op jit(solution)/shard_map/ppermute | solution.py:74
  90.2 16.1 %collective-permute-start.12 = (bf16[320,1280]{1,0:T(8,128)(2,1)}, bf16[320,1280]{1,0:T(8,128)(2,1)}, u32[]{:S(2)}, u32[]{:S(2)}) collective-permute-start(bf16[320,1280]{1,0:T(8,128)(2,1)} %shard_map.216.refs_11_), channel_id=1, source_target_pairs={{0,1},{1,0},{2,3},{3,2},{4,5},{5,4},{6,7},{7,6},{8,9},{9,8},{10,11... | collective-permute-start | bytes 2457608 | tf_op jit(solution)/shard_map/ppermute | solution.py:74
  100.3 6.3 %collective-permute-start.15 = (bf16[320,1280]{1,0:T(8,128)(2,1)S(1)}, bf16[320,1280]{1,0:T(8,128)(2,1)S(1)}, u32[]{:S(2)}, u32[]{:S(2)}) collective-permute-start(bf16[320,1280]{1,0:T(8,128)(2,1)S(1)} %copy-done.31), channel_id=1, source_target_pairs={{0,1},{1,0},{2,3},{3,2},{4,5},{5,4},{6,7},{7,6},{8,9},{9,8},{10,11... | collective-permute-start | bytes 2457608 | tf_op jit(solution)/shard_map/ppermute | solution.py:74
  100.3 6.3 %collective-permute-start.9 = (bf16[320,1280]{1,0:T(8,128)(2,1)}, bf16[320,1280]{1,0:T(8,128)(2,1)}, u32[]{:S(2)}, u32[]{:S(2)}) collective-permute-start(bf16[320,1280]{1,0:T(8,128)(2,1)} %shard_map.215.refs_7_), channel_id=1, source_target_pairs={{0,1},{1,0},{2,3},{3,2},{4,5},{5,4},{6,7},{7,6},{8,9},{9,8},{10,11... | collective-permute-start | bytes 2457608 | tf_op jit(solution)/shard_map/ppermute | solution.py:74
  100.8 3.9 %collective-permute-start.18 = (f32[1,320]{1,0:T(1,128)}, f32[1,320]{1,0:T(1,128)S(1)}, u32[]{:S(2)}, u32[]{:S(2)}) collective-permute-start(f32[1,320]{1,0:T(1,128)} %shard_map.218.refs_19_), channel_id=1, source_target_pairs={{0,1},{1,0},{2,3},{3,2},{4,5},{5,4},{6,7},{7,6},{8,9},{9,8},{10,11... | collective-permute-start | bytes 3848 | tf_op jit(solution)/shard_map/ppermute | solution.py:74
  104.7 2.0 collective-permute-start.4
  104.8 6.7 %collective-permute-start.5 = (bf16[3,64,320]{2,1,0:T(8,128)(2,1)S(1)}, bf16[3,64,320]{2,1,0:T(8,128)(2,1)S(1)}, u32[]{:S(2)}, u32[]{:S(2)}) collective-permute-start(bf16[3,64,320]{2,1,0:T(8,128)(2,1)S(1)} %get-tuple-element.78.refs_3_), channel_id=1, source_target_pairs={{0,2},{1,3},{2,0},{3,1},{4,6},{5,7},{6,4},{7,5},{8,10},{9,11},{10,... | collective-permute-start | bytes 368648 | tf_op jit(solution)/shard_map/ppermute | solution.py:132
  106.3 7.4 %collective-permute-start.6 = (bf16[3,64,320]{2,1,0:T(8,128)(2,1)S(1)}, bf16[3,64,320]{2,1,0:T(8,128)(2,1)S(1)}, u32[]{:S(2)}, u32[]{:S(2)}) collective-permute-start(bf16[3,64,320]{2,1,0:T(8,128)(2,1)S(1)} %get-tuple-element.79.refs_4_), channel_id=1, source_target_pairs={{0,3},{1,2},{2,1},{3,0},{4,7},{5,6},{6,5},{7,4},{8,11},{9,10},{10,... | collective-permute-start | bytes 368648 | tf_op jit(solution)/shard_map/ppermute | solution.py:132
  127.4 1.9 collective-permute-start.19
  127.8 6.9 %collective-permute-start.20 = (bf16[3,64,320]{2,1,0:T(8,128)(2,1)}, bf16[3,64,320]{2,1,0:T(8,128)(2,1)S(1)}, u32[]{:S(2)}, u32[]{:S(2)}) collective-permute-start(bf16[3,64,320]{2,1,0:T(8,128)(2,1)} %get-tuple-element.83), channel_id=1, source_target_pairs={{0,2},{1,3},{2,0},{3,1},{4,6},{5,7},{6,4},{7,5},{8,10},{9,11},{10,... | collective-permute-start | bytes 368648 | tf_op jit(solution)/shard_map/ppermute | solution.py:132
  129.3 7.1 %collective-permute-start.21 = (bf16[3,64,320]{2,1,0:T(8,128)(2,1)}, bf16[3,64,320]{2,1,0:T(8,128)(2,1)S(1)}, u32[]{:S(2)}, u32[]{:S(2)}) collective-permute-start(bf16[3,64,320]{2,1,0:T(8,128)(2,1)} %get-tuple-element.84), channel_id=1, source_target_pairs={{0,3},{1,2},{2,1},{3,0},{4,7},{5,6},{6,5},{7,4},{8,11},{9,10},{10,... | collective-permute-start | bytes 368648 | tf_op jit(solution)/shard_map/ppermute | solution.py:132
  138.9 18.9 %all-to-all-start.2 = ((bf16[8,3,80,128]{3,2,1,0:T(8,128)(2,1)}), bf16[8,3,80,128]{3,2,1,0:T(8,128)(2,1)S(1)}, u32[]{:S(2)}, u32[]{:S(2)}) async-start(bf16[8,3,80,128]{3,2,1,0:T(8,128)(2,1)} %shard_map.220), calls=%async_computation.2 | async-start | bytes 983040 | tf_op jit(solution)/shard_map/all_to_all | solution.py:136
  143.2 4.1 %collective-permute-start.22 = (bf16[2,192,320]{2,1,0:T(8,128)(2,1)S(1)}, bf16[2,192,320]{2,1,0:T(8,128)(2,1)S(1)}, u32[]{:S(2)}, u32[]{:S(2)}) collective-permute-start(bf16[2,192,320]{2,1,0:T(8,128)(2,1)S(1)} %copy-done.58), channel_id=1, source_target_pairs={{0,1},{1,0},{2,3},{3,2},{4,5},{5,4},{6,7},{7,6},{8,9},{9,8},{10,11... | collective-permute-start | bytes 737288 | tf_op jit(solution)/shard_map/ppermute | solution.py:132
  143.6 38.4 %collective-permute-start.33 = (bf16[3,64,1280]{2,1,0:T(8,128)(2,1)S(1)}, bf16[3,64,1280]{2,1,0:T(8,128)(2,1)}, u32[]{:S(2)}, u32[]{:S(2)}) collective-permute-start(bf16[3,64,1280]{2,1,0:T(8,128)(2,1)S(1)} %copy-done.48), channel_id=1, source_target_pairs={{0,1},{1,0},{2,3},{3,2},{4,5},{5,4},{6,7},{7,6},{8,9},{9,8},{10,11... | collective-permute-start | bytes 1474568 | tf_op jit(solution)/shard_map/ppermute | solution.py:74
  144.5 28.7 %collective-permute-start.25 = (bf16[3,64,1280]{2,1,0:T(8,128)(2,1)S(1)}, bf16[3,64,1280]{2,1,0:T(8,128)(2,1)S(1)}, u32[]{:S(2)}, u32[]{:S(2)}) collective-permute-start(bf16[3,64,1280]{2,1,0:T(8,128)(2,1)S(1)} %copy-done.49), channel_id=1, source_target_pairs={{0,2},{1,3},{2,0},{3,1},{4,6},{5,7},{6,4},{7,5},{8,10},{9,11},{10,... | collective-permute-start | bytes 1474568 | tf_op jit(solution)/shard_map/ppermute | solution.py:74
  145.9 27.3 %collective-permute-start.23 = (bf16[2,192,320]{2,1,0:T(8,128)(2,1)}, bf16[2,192,320]{2,1,0:T(8,128)(2,1)S(1)}, u32[]{:S(2)}, u32[]{:S(2)}) collective-permute-start(bf16[2,192,320]{2,1,0:T(8,128)(2,1)} %get-tuple-element.89), channel_id=1, source_target_pairs={{0,2},{1,3},{2,0},{3,1},{4,6},{5,7},{6,4},{7,5},{8,10},{9,11},{10,... | collective-permute-start | bytes 737288 | tf_op jit(solution)/shard_map/ppermute | solution.py:132
  146.5 26.7 %collective-permute-start.24 = (bf16[2,192,320]{2,1,0:T(8,128)(2,1)}, bf16[2,192,320]{2,1,0:T(8,128)(2,1)S(1)}, u32[]{:S(2)}, u32[]{:S(2)}) collective-permute-start(bf16[2,192,320]{2,1,0:T(8,128)(2,1)} %get-tuple-element.90), channel_id=1, source_target_pairs={{0,3},{1,2},{2,1},{3,0},{4,7},{5,6},{6,5},{7,4},{8,11},{9,10},{10,... | collective-permute-start | bytes 737288 | tf_op jit(solution)/shard_map/ppermute | solution.py:132
  147.3 33.9 %collective-permute-start.29 = (bf16[3,64,1280]{2,1,0:T(8,128)(2,1)}, bf16[3,64,1280]{2,1,0:T(8,128)(2,1)S(1)}, u32[]{:S(2)}, u32[]{:S(2)}) collective-permute-start(bf16[3,64,1280]{2,1,0:T(8,128)(2,1)} %get-tuple-element.97.refs_9_), channel_id=1, source_target_pairs={{0,2},{1,3},{2,0},{3,1},{4,6},{5,7},{6,4},{7,5},{8,10},{9,11},{10,... | collective-permute-start | bytes 1474568 | tf_op jit(solution)/shard_map/ppermute | solution.py:74
  174.1 51.9 %all-to-all-start.3 = ((bf16[8,11,80,128]{3,2,1,0:T(8,128)(2,1)}), bf16[8,11,80,128]{3,2,1,0:T(8,128)(2,1)}, u32[]{:S(2)}, u32[]{:S(2)}) async-start(bf16[8,11,80,128]{3,2,1,0:T(8,128)(2,1)} %shard_map.222), calls=%async_computation.3 | async-start | bytes 3604480 | tf_op jit(solution)/shard_map/all_to_all | solution.py:136
  178.8 3.2 collective-permute-start.34
  178.9 3.2 collective-permute-start.28
  179.4 2.9 collective-permute-start.31
  181.2 2.2 collective-permute-start.32
  182.0 2.1 collective-permute-start.30
  191.8 27.7 %collective-permute-start.35 = (bf16[4,3,40,768]{3,2,1,0:T(8,128)(2,1)}, bf16[4,3,40,768]{3,2,1,0:T(8,128)(2,1)S(1)}, u32[]{:S(2)}, u32[]{:S(2)}) collective-permute-start(bf16[4,3,40,768]{3,2,1,0:T(8,128)(2,1)} %get-tuple-element.100), channel_id=1, source_target_pairs={{0,4},{4,0},{8,12},{12,8},{16,20},{20,16},{24,28},{28,24},{1,5},{5... | collective-permute-start | bytes 2211848 | tf_op jit(solution)/shard_map/ppermute | solution.py:74
  193.6 25.9 %collective-permute-start.36 = (bf16[4,3,40,512]{3,2,1,0:T(8,128)(2,1)}, bf16[4,3,40,512]{3,2,1,0:T(8,128)(2,1)S(1)}, u32[]{:S(2)}, u32[]{:S(2)}) collective-permute-start(bf16[4,3,40,512]{3,2,1,0:T(8,128)(2,1)} %get-tuple-element.101), channel_id=1, source_target_pairs={{0,8},{4,12},{8,0},{12,4},{16,24},{20,28},{24,16},{28,20},{1,9},{5... | collective-permute-start | bytes 1474568 | tf_op jit(solution)/shard_map/ppermute | solution.py:74
  195.4 1.3 collective-permute-start.26
  196.7 4.0 %collective-permute-start.27 = (f32[8,1280]{1,0:T(8,128)S(1)}, f32[8,1280]{1,0:T(8,128)S(1)}, u32[]{:S(2)}, u32[]{:S(2)}) collective-permute-start(f32[8,1280]{1,0:T(8,128)S(1)} %add.56), channel_id=1, source_target_pairs={{0,2},{1,3},{2,0},{3,1},{4,6},{5,7},{6,4},{7,5},{8,10},{9,11},{10,... | collective-permute-start | bytes 122888 | tf_op jit(solution)/shard_map/ppermute | solution.py:74
  222.6 13.7 %collective-permute-start.40 = (bf16[2,3,40,768]{3,2,1,0:T(8,128)(2,1)S(1)}, bf16[2,3,40,768]{3,2,1,0:T(8,128)(2,1)S(1)}, u32[]{:S(2)}, u32[]{:S(2)}) collective-permute-start(bf16[2,3,40,768]{3,2,1,0:T(8,128)(2,1)S(1)} %get-tuple-element.102.refs_6_), channel_id=1, source_target_pairs={{0,8},{4,12},{8,0},{12,4},{16,24},{20,28},{24,16},{28,20},{1,9},{5... | collective-permute-start | bytes 1105928 | tf_op jit(solution)/shard_map/ppermute | solution.py:74
  225.1 11.2 %collective-permute-start.41 = (bf16[2,3,40,512]{3,2,1,0:T(8,128)(2,1)S(1)}, bf16[2,3,40,512]{3,2,1,0:T(8,128)(2,1)S(1)}, u32[]{:S(2)}, u32[]{:S(2)}) collective-permute-start(bf16[2,3,40,512]{3,2,1,0:T(8,128)(2,1)S(1)} %get-tuple-element.110), channel_id=1, source_target_pairs={{0,4},{4,0},{8,12},{12,8},{16,20},{20,16},{24,28},{28,24},{1,5},{5... | collective-permute-start | bytes 737288 | tf_op jit(solution)/shard_map/ppermute | solution.py:74
  237.8 15.2 %collective-permute-start.42 = (bf16[1,3,40,1280]{3,2,1,0:T(8,128)(2,1)S(1)}, bf16[1,3,40,1280]{3,2,1,0:T(8,128)(2,1)S(1)}, u32[]{:S(2)}, u32[]{:S(2)}) collective-permute-start(bf16[1,3,40,1280]{3,2,1,0:T(8,128)(2,1)S(1)} %get-tuple-element.113.refs_3_), channel_id=1, source_target_pairs={{0,16},{4,20},{8,24},{12,28},{16,0},{20,4},{24,8},{28,12},{1,17},{... | collective-permute-start | bytes 921608 | tf_op jit(solution)/shard_map/ppermute | solution.py:74
  239.9 21.5 %collective-permute-start.44 = (bf16[4,1,128,768]{3,2,1,0:T(8,128)(2,1)S(1)}, bf16[4,1,128,768]{3,2,1,0:T(8,128)(2,1)S(1)}, u32[]{:S(2)}, u32[]{:S(2)}) collective-permute-start(bf16[4,1,128,768]{3,2,1,0:T(8,128)(2,1)S(1)} %copy-done.46), channel_id=1, source_target_pairs={{0,4},{4,0},{8,12},{12,8},{16,20},{20,16},{24,28},{28,24},{1,5},{5... | collective-permute-start | bytes 2359304 | tf_op jit(solution)/shard_map/ppermute | solution.py:74
  241.2 20.2 %collective-permute-start.45 = (bf16[4,1,128,512]{3,2,1,0:T(8,128)(2,1)S(1)}, bf16[4,1,128,512]{3,2,1,0:T(8,128)(2,1)S(1)}, u32[]{:S(2)}, u32[]{:S(2)}) collective-permute-start(bf16[4,1,128,512]{3,2,1,0:T(8,128)(2,1)S(1)} %copy-done.47), channel_id=1, source_target_pairs={{0,8},{4,12},{8,0},{12,4},{16,24},{20,28},{24,16},{28,20},{1,9},{5... | collective-permute-start | bytes 1572872 | tf_op jit(solution)/shard_map/ppermute | solution.py:74
  242.1 11.6 %collective-permute-start.38 = (bf16[3,64,1280]{2,1,0:T(8,128)(2,1)S(1)}, bf16[3,64,1280]{2,1,0:T(8,128)(2,1)S(1)}, u32[]{:S(2)}, u32[]{:S(2)}) collective-permute-start(bf16[3,64,1280]{2,1,0:T(8,128)(2,1)S(1)} %copy-done.53), channel_id=1, source_target_pairs={{0,1},{1,0},{2,3},{3,2},{4,5},{5,4},{6,7},{7,6},{8,9},{9,8},{10,11... | collective-permute-start | bytes 1474568 | tf_op jit(solution)/shard_map/ppermute | solution.py:74
  242.1 45.1 %collective-permute-start.37 = (bf16[3,64,1280]{2,1,0:T(8,128)(2,1)S(1)}, bf16[3,64,1280]{2,1,0:T(8,128)(2,1)S(1)}, u32[]{:S(2)}, u32[]{:S(2)}) collective-permute-start(bf16[3,64,1280]{2,1,0:T(8,128)(2,1)S(1)} %copy-done.51), channel_id=1, source_target_pairs={{0,1},{1,0},{2,3},{3,2},{4,5},{5,4},{6,7},{7,6},{8,9},{9,8},{10,11... | collective-permute-start | bytes 1474568 | tf_op jit(solution)/shard_map/ppermute | solution.py:74
  253.7 16.4 %collective-permute-start.43 = (bf16[1,3,40,1280]{3,2,1,0:T(8,128)(2,1)S(1)}, bf16[1,3,40,1280]{3,2,1,0:T(8,128)(2,1)S(1)}, u32[]{:S(2)}, u32[]{:S(2)}) collective-permute-start(bf16[1,3,40,1280]{3,2,1,0:T(8,128)(2,1)S(1)} %shard_map.230.refs_5_.refs_1_), channel_id=1, source_target_pairs={{0,16},{4,20},{8,24},{12,28},{16,0},{20,4},{24,8},{28,12},{1,17},{... | collective-permute-start | bytes 921608 | tf_op jit(solution)/shard_map/ppermute | solution.py:74
  254.2 33.1 %collective-permute-start.39 = (bf16[3,64,1280]{2,1,0:T(8,128)(2,1)S(1)}, bf16[3,64,1280]{2,1,0:T(8,128)(2,1)S(1)}, u32[]{:S(2)}, u32[]{:S(2)}) collective-permute-start(bf16[3,64,1280]{2,1,0:T(8,128)(2,1)S(1)} %add_convert_fusion), channel_id=1, source_target_pairs={{0,2},{1,3},{2,0},{3,1},{4,6},{5,7},{6,4},{7,5},{8,10},{9,11},{10,... | collective-permute-start | bytes 1474568 | tf_op jit(solution)/shard_map/ppermute | solution.py:74
  262.2 16.3 %collective-permute-start.48 = (bf16[2,1,128,768]{3,2,1,0:T(8,128)(2,1)S(1)}, bf16[2,1,128,768]{3,2,1,0:T(8,128)(2,1)S(1)}, u32[]{:S(2)}, u32[]{:S(2)}) collective-permute-start(bf16[2,1,128,768]{3,2,1,0:T(8,128)(2,1)S(1)} %get-tuple-element.118.refs_3_), channel_id=1, source_target_pairs={{0,8},{4,12},{8,0},{12,4},{16,24},{20,28},{24,16},{28,20},{1,9},{5... | collective-permute-start | bytes 1179656 | tf_op jit(solution)/shard_map/ppermute | solution.py:74
  262.3 8.4 %collective-permute-start.49 = (bf16[2,1,128,512]{3,2,1,0:T(8,128)(2,1)S(1)}, bf16[2,1,128,512]{3,2,1,0:T(8,128)(2,1)S(1)}, u32[]{:S(2)}, u32[]{:S(2)}) collective-permute-start(bf16[2,1,128,512]{3,2,1,0:T(8,128)(2,1)S(1)} %get-tuple-element.123), channel_id=1, source_target_pairs={{0,4},{4,0},{8,12},{12,8},{16,20},{20,16},{24,28},{28,24},{1,5},{5... | collective-permute-start | bytes 786440 | tf_op jit(solution)/shard_map/ppermute | solution.py:74
  270.6 15.9 %collective-permute-start.46 = (bf16[2,3,40,768]{3,2,1,0:T(8,128)(2,1)S(1)}, bf16[2,3,40,768]{3,2,1,0:T(8,128)(2,1)S(1)}, u32[]{:S(2)}, u32[]{:S(2)}) collective-permute-start(bf16[2,3,40,768]{3,2,1,0:T(8,128)(2,1)S(1)} %get-tuple-element.119.refs_5_.refs_1_), channel_id=1, source_target_pairs={{0,8},{4,12},{8,0},{12,4},{16,24},{20,28},{24,16},{28,20},{1,9},{5... | collective-permute-start | bytes 1105928 | tf_op jit(solution)/shard_map/ppermute | solution.py:74
  270.7 8.6 %collective-permute-start.47 = (bf16[2,3,40,512]{3,2,1,0:T(8,128)(2,1)S(1)}, bf16[2,3,40,512]{3,2,1,0:T(8,128)(2,1)S(1)}, u32[]{:S(2)}, u32[]{:S(2)}) collective-permute-start(bf16[2,3,40,512]{3,2,1,0:T(8,128)(2,1)S(1)} %get-tuple-element.120.refs_2_), channel_id=1, source_target_pairs={{0,4},{4,0},{8,12},{12,8},{16,20},{20,16},{24,28},{28,24},{1,5},{5... | collective-permute-start | bytes 737288 | tf_op jit(solution)/shard_map/ppermute | solution.py:74
  279.3 20.1 %collective-permute-start.50 = (bf16[1,1,128,1280]{3,2,1,0:T(8,128)(2,1)S(1)}, bf16[1,1,128,1280]{3,2,1,0:T(8,128)(2,1)S(1)}, u32[]{:S(2)}, u32[]{:S(2)}) collective-permute-start(bf16[1,1,128,1280]{3,2,1,0:T(8,128)(2,1)S(1)} %get-tuple-element.124.refs_5_), channel_id=1, source_target_pairs={{0,16},{4,20},{8,24},{12,28},{16,0},{20,4},{24,8},{28,12},{1,17},{... | collective-permute-start | bytes 983048 | tf_op jit(solution)/shard_map/ppermute | solution.py:74
  301.0 8.1 %collective-permute-start.51 = (bf16[1,1,128,1280]{3,2,1,0:T(8,128)(2,1)S(1)}, bf16[1,1,128,1280]{3,2,1,0:T(8,128)(2,1)S(1)}, u32[]{:S(2)}, u32[]{:S(2)}) collective-permute-start(bf16[1,1,128,1280]{3,2,1,0:T(8,128)(2,1)S(1)} %get-tuple-element.127.refs_1_.refs_3_), channel_id=1, source_target_pairs={{0,16},{4,20},{8,24},{12,28},{16,0},{20,4},{24,8},{28,12},{1,17},{... | collective-permute-start | bytes 983048 | tf_op jit(solution)/shard_map/ppermute | solution.py:74
  301.1 23.0 %collective-permute-start.56 = (bf16[4,3,40,768]{3,2,1,0:T(8,128)(2,1)S(1)}, bf16[4,3,40,768]{3,2,1,0:T(8,128)(2,1)S(1)}, u32[]{:S(2)}, u32[]{:S(2)}) collective-permute-start(bf16[4,3,40,768]{3,2,1,0:T(8,128)(2,1)S(1)} %get-tuple-element.125.refs_7_.refs_1_), channel_id=1, source_target_pairs={{0,4},{4,0},{8,12},{12,8},{16,20},{20,16},{24,28},{28,24},{1,5},{5... | collective-permute-start | bytes 2211848 | tf_op jit(solution)/shard_map/ppermute | solution.py:74
  301.2 22.9 %collective-permute-start.57 = (bf16[4,3,40,512]{3,2,1,0:T(8,128)(2,1)S(1)}, bf16[4,3,40,512]{3,2,1,0:T(8,128)(2,1)S(1)}, u32[]{:S(2)}, u32[]{:S(2)}) collective-permute-start(bf16[4,3,40,512]{3,2,1,0:T(8,128)(2,1)S(1)} %get-tuple-element.132.refs_2_), channel_id=1, source_target_pairs={{0,8},{4,12},{8,0},{12,4},{16,24},{20,28},{24,16},{28,20},{1,9},{5... | collective-permute-start | bytes 1474568 | tf_op jit(solution)/shard_map/ppermute | solution.py:74
  301.3 9.2 %collective-permute-start.58 = (f32[1,1280]{1,0:T(1,128)S(1)}, f32[1,1280]{1,0:T(1,128)S(1)}, u32[]{:S(2)}, u32[]{:S(2)}) collective-permute-start(f32[1,1280]{1,0:T(1,128)S(1)} %slice.46), channel_id=1, source_target_pairs={{0,1},{1,0},{2,3},{3,2},{4,5},{5,4},{6,7},{7,6},{8,9},{9,8},{10,11... | collective-permute-start | bytes 15368 | tf_op jit(solution)/shard_map/ppermute | solution.py:74
  310.5 11.9 %collective-permute-start.52 = (bf16[2,1,128,768]{3,2,1,0:T(8,128)(2,1)S(1)}, bf16[2,1,128,768]{3,2,1,0:T(8,128)(2,1)S(1)}, u32[]{:S(2)}, u32[]{:S(2)}) collective-permute-start(bf16[2,1,128,768]{3,2,1,0:T(8,128)(2,1)S(1)} %get-tuple-element.128.refs_1_.refs_5_), channel_id=1, source_target_pairs={{0,8},{4,12},{8,0},{12,4},{16,24},{20,28},{24,16},{28,20},{1,9},{5... | collective-permute-start | bytes 1179656 | tf_op jit(solution)/shard_map/ppermute | solution.py:74
  311.7 3.9 %collective-permute-start.59 = (f32[1,1280]{1,0:T(1,128)}, f32[1,1280]{1,0:T(1,128)}, u32[]{:S(2)}, u32[]{:S(2)}) collective-permute-start(f32[1,1280]{1,0:T(1,128)} %get-tuple-element.137), channel_id=1, source_target_pairs={{0,2},{1,3},{2,0},{3,1},{4,6},{5,7},{6,4},{7,5},{8,10},{9,11},{10,... | collective-permute-start | bytes 15368 | tf_op jit(solution)/shard_map/ppermute | solution.py:74
  312.0 6.6 %collective-permute-start.53 = (bf16[2,1,128,512]{3,2,1,0:T(8,128)(2,1)}, bf16[2,1,128,512]{3,2,1,0:T(8,128)(2,1)S(1)}, u32[]{:S(2)}, u32[]{:S(2)}) collective-permute-start(bf16[2,1,128,512]{3,2,1,0:T(8,128)(2,1)} %get-tuple-element.129.refs_2_), channel_id=1, source_target_pairs={{0,4},{4,0},{8,12},{12,8},{16,20},{20,16},{24,28},{28,24},{1,5},{5... | collective-permute-start | bytes 786440 | tf_op jit(solution)/shard_map/ppermute | solution.py:74
  323.4 14.9 %collective-permute-start.54 = (bf16[4,1,128,768]{3,2,1,0:T(8,128)(2,1)S(1)}, bf16[4,1,128,768]{3,2,1,0:T(8,128)(2,1)S(1)}, u32[]{:S(2)}, u32[]{:S(2)}) collective-permute-start(bf16[4,1,128,768]{3,2,1,0:T(8,128)(2,1)S(1)} %get-tuple-element.130.refs_5_.refs_1_), channel_id=1, source_target_pairs={{0,4},{4,0},{8,12},{12,8},{16,20},{20,16},{24,28},{28,24},{1,5},{5... | collective-permute-start | bytes 2359304 | tf_op jit(solution)/shard_map/ppermute | solution.py:74
  324.1 10.0 %collective-permute-start.55 = (bf16[4,1,128,512]{3,2,1,0:T(8,128)(2,1)S(1)}, bf16[4,1,128,512]{3,2,1,0:T(8,128)(2,1)S(1)}, u32[]{:S(2)}, u32[]{:S(2)}) collective-permute-start(bf16[4,1,128,512]{3,2,1,0:T(8,128)(2,1)S(1)} %get-tuple-element.131.refs_2_), channel_id=1, source_target_pairs={{0,8},{4,12},{8,0},{12,4},{16,24},{20,28},{24,16},{28,20},{1,9},{5... | collective-permute-start | bytes 1572872 | tf_op jit(solution)/shard_map/ppermute | solution.py:74
  (65 other events, 709.5 us)
